TPU v7x, 512 devices: a whole 4x8x8 slice. The times are simulated.
512 devices in a mesh: dp: 64 (over y, x, z_lo), tensor: 8 (over z_hi, core).
Axes of the slice: x: 4, y: 8, z: 8 (z_hi: 4, z_lo: 2; z = z_hi * 2 + z_lo), core: 2. Of those that a mesh axis runs over, the one named last changes fastest.
Arguments:
- patches: bfloat16 [32768, 1152], P('dp'), may hold values from -6 to 6
- ln_gain: float32 [1152], replicated, may hold values from 0.1 to 1.9
- w_up: bfloat16 [1152, 4304], P(None, 'tensor'), may hold values from -0.1875 to 0.1875
- b_up: float32 [4304], P('tensor'), may hold values from -3 to 3
- w_down: bfloat16 [4304, 1152], P('tensor'), may hold values from -0.09375 to 0.09375
- b_down: float32 [1152], replicated, may hold values from -0.6 to 0.6
- head_gain: float32 [1152], replicated, may hold values from 0.1 to 1.9
- text_feats: bfloat16 [128, 1152], P('dp'), may hold values from -24 to 24
- pair_ids: int32 [128], P('dp'), may hold values from 0 to 63
- log_sharpness: float32 [1], replicated, may hold values from 1 to 2
- pairwise_logit_shift: float32 [1], replicated, may hold values from -3 to -1
Outputs:
- grad_patches: bfloat16 [32768, 1152], P('dp')
- grad_text: float32 [128, 1152], P('dp')
All inputs are finite; a program needn't handle non-finite values.
Results may differ from a plain program's by a relative error of at most 0.015.
Values may be sent and summed in bfloat16 or wider, within the bound.
No kernel may reach another device: no remote copies, remote signals or barrier semaphores. Data moves between devices by JAX's collectives and lax.ppermute only.
A program may use at most 64 MiB of HBM per device.

v0:
```python
import jax
import jax.numpy as jnp
from jax import lax
from jax.sharding import PartitionSpec as P

PATCHES = 256


epsilon = 1e-06
loss_scale = 131072.0


def norm_parts(values):
    centre = values - jnp.mean(values, axis=-1, keepdims=True)
    inverse = lax.rsqrt(jnp.mean(centre * centre, axis=-1, keepdims=True) + epsilon)
    return (centre * inverse, inverse)


def norm_back(grad_out, norm_gain, normed_vals, inverse):
    scaled = grad_out * norm_gain
    return inverse * (
        scaled
        - jnp.mean(scaled, axis=-1, keepdims=True)
        - normed_vals * jnp.mean(scaled * normed_vals, axis=-1, keepdims=True)
    )


def gelu_tanh(values):
    return jax.nn.gelu(values, approximate=True)


def on_device(
    patches,
    ln_gain,
    w_up,
    b_up,
    w_down,
    b_down,
    head_gain,
    text_feats,
    pair_ids,
    log_sharpness,
    pairwise_logit_shift,
):
    img_dev = text_feats.shape[0]
    model_width = patches.shape[1]
    batch_size = img_dev * lax.axis_size("dp")
    inputs = patches.astype(jnp.float32)
    normed_in, inverse_in = norm_parts(inputs)
    normed = (normed_in * ln_gain).astype(jnp.bfloat16)
    pre_act = jnp.dot(normed, w_up, preferred_element_type=jnp.float32) + b_up
    activation = gelu_tanh(pre_act).astype(jnp.bfloat16)
    partial_out = jnp.dot(activation, w_down, preferred_element_type=jnp.float32)
    mlp_output = lax.psum(partial_out.astype(jnp.bfloat16), "tensor").astype(jnp.float32)
    hidden = inputs + mlp_output + b_down
    pooled = hidden.reshape(img_dev, PATCHES, model_width).mean(axis=1)
    feat_n, feat_s = norm_parts(pooled)
    features = feat_n * head_gain
    feat_len = jnp.sqrt(jnp.sum(features * features, axis=-1, keepdims=True) + epsilon)
    picture_feature_vector = features / feat_len
    text_vals = text_feats.astype(jnp.float32)
    text_len = jnp.sqrt(jnp.sum(text_vals * text_vals, axis=-1, keepdims=True) + epsilon)
    unit_text = text_vals / text_len
    caption_normalized_directions = unit_text.astype(jnp.bfloat16)
    sharpness_multiplier = jnp.exp(log_sharpness[0])
    offset_bias_term = pairwise_logit_shift[0]
    text_tile_rows = lax.all_gather(caption_normalized_directions, "dp", axis=0, tiled=True).astype(
        jnp.float32
    )
    pairwise_logit_matrix = (
        sharpness_multiplier
        * jnp.dot(picture_feature_vector, text_tile_rows.T, precision=lax.Precision.HIGHEST)
        + offset_bias_term
    )
    pair_sign = jnp.where(
        pair_ids[:, None] == lax.all_gather(pair_ids, "dp", axis=0, tiled=True)[None, :], 1.0, -1.0
    ).astype(jnp.float32)
    pairwise_logit_derivative = (
        -loss_scale * pair_sign * jax.nn.sigmoid(-pair_sign * pairwise_logit_matrix) / batch_size
    )
    picture_running_total = sharpness_multiplier * jnp.dot(
        pairwise_logit_derivative, text_tile_rows, precision=lax.Precision.HIGHEST
    )
    caption_loss_derivative = lax.psum_scatter(
        sharpness_multiplier
        * jnp.dot(
            pairwise_logit_derivative.T, picture_feature_vector, precision=lax.Precision.HIGHEST
        ),
        "dp",
        scatter_dimension=0,
        tiled=True,
    )
    grad_text = (
        caption_loss_derivative
        - unit_text * jnp.sum(unit_text * caption_loss_derivative, axis=-1, keepdims=True)
    ) / text_len
    g_feat = (
        picture_running_total
        - picture_feature_vector
        * jnp.sum(picture_feature_vector * picture_running_total, axis=-1, keepdims=True)
    ) / feat_len
    g_pool = norm_back(g_feat, head_gain, feat_n, feat_s)
    g_hidden = jnp.broadcast_to(
        (g_pool / PATCHES)[:, None, :], (img_dev, PATCHES, model_width)
    ).reshape(img_dev * PATCHES, model_width)
    g_rows = g_hidden.astype(jnp.bfloat16)
    g_act = lax.dot_general(
        g_rows, w_down, (((1,), (1,)), ((), ())), preferred_element_type=jnp.float32
    )
    g_pre = jax.vjp(gelu_tanh, pre_act)[1](g_act)[0].astype(jnp.bfloat16)
    partial_back = lax.dot_general(
        g_pre, w_up, (((1,), (1,)), ((), ())), preferred_element_type=jnp.float32
    )
    g_normed = lax.psum(
        partial_back.astype(jnp.bfloat16).astype(jnp.float32).astype(jnp.bfloat16), "tensor"
    ).astype(jnp.float32)
    grad_patches = (g_hidden + norm_back(g_normed, ln_gain, normed_in, inverse_in)).astype(
        jnp.bfloat16
    )
    return (grad_patches, grad_text)


def solution(mesh):
    in_specs = (
        P("dp", None),
        P(),
        P(None, "tensor"),
        P("tensor"),
        P("tensor", None),
        P(),
        P(),
        P("dp", None),
        P("dp"),
        P(),
        P(),
    )
    out_specs = (P("dp", None), P("dp", None))
    return jax.shard_map(
        on_device, mesh=mesh, in_specs=in_specs, out_specs=out_specs, check_vma=False
    )
```

profile of v0, /device:TPU:1, one launch (start us, length us, event | category | flops | bytes accessed | tf_op | source)
XLA Modules:
  0.0 863.9 jit_solution(9174125103087682231)
XLA Ops:
  7.2 0.0 copy-start
  7.2 0.0 copy-start.1
  7.2 0.0 copy-start.4
  7.2 0.0 copy-start.8
  7.2 0.0 all-reduce.6.cloned.1.call-start
  7.3 1.6 convert_reduce_fusion
  8.9 0.0 copy-done.1
  8.9 0.4 fusion.9
  9.4 0.0 copy-done.4
  9.4 0.0 copy-done.8
  9.4 2.4 convolution_add_fusion
  11.8 0.0 copy-start.10
  11.8 1.0 copy-done.10
  12.8 0.0 copy-done
  12.8 2.3 convolution_convert_fusion.1
  15.1 0.0 copy-start.5
  15.1 0.0 copy-start.7
  15.1 0.0 copy-start.9
  15.1 0.0 copy-start.6
  15.1 0.0 all-reduce.6.cloned.1.call-update
  15.2 0.0 all-reduce.10.cloned.1.call-start
  15.2 0.6 copy-done.5
  15.8 0.1 fusion.43
  16.0 0.1 convert_bitcast_fusion
  16.0 132.0 %all-gather = bf16[64,2,1152]{2,1,0:T(2,128)(2,1)S(1)} all-gather(bf16[1,2,1152]{2,1,0:T(2,128)(2,1)S(1)} %get-tuple-element.7), channel_id=1, replica_groups=mesh['dp'=64,'tensor'=8] {'dp'}, dimensions={0}, use_global_device_ids=true | all-gather | bytes 299520 | tf_op jit(solution)/shard_map/all_gather | solution.py:67
  148.0 0.1 reshape.78
  149.5 0.0 copy-done.7
  149.5 0.6 fusion.57
  150.6 0.0 copy-done.9
  150.6 0.2 dynamic-update-slice
  150.9 12.0 %all-reduce = s32[128]{0:T(128)S(1)} all-reduce(s32[128]{0:T(128)S(1)} %dynamic-update-slice), channel_id=1, replica_groups=mesh['dp'=64,'tensor'=8] {'dp'}, use_global_device_ids=true, to_apply=%add | all-reduce | flops 128 | bytes 1024
  162.8 0.0 copy-start.3
  162.8 0.0 all-reduce.6.cloned.1.call-done
  162.9 0.0 copy-done.6
  162.9 1.7 bitcast_reduce_fusion
  164.6 0.1 multiply_reduce_fusion.5
  164.7 0.2 multiply_reduce_fusion.4
  164.9 0.0 copy-done.3
  164.9 0.2 multiply_reduce_fusion.3
  165.1 0.4 fusion.31
  165.5 1.6 convolution_multiply_fusion
  167.1 0.4 multiply_reduce_fusion.2
  167.5 0.0 all-reduce.10.cloned.1.call-update
  167.5 0.0 all-reduce.8.cloned.1.call-start
  167.6 0.2 fusion.56
  167.8 0.1 multiply_multiply_fusion.2
  167.9 1.1 bitcast_convert_fusion
  169.0 5.4 convolution_convert_fusion
  174.4 0.0 all-reduce.8.cloned.1.call-update
  175.0 563.9 %all-reduce.10.cloned.1.call-done = f32[128,1152]{1,0:T(8,128)} async-done(((f32[128,1152]{1,0:T(8,128)}), f32[128,1152]{1,0:T(8,128)}) %all-reduce.10.cloned.1.call-update) | async-done | bytes 589840
  738.9 0.9 multiply_reduce_fusion
  739.8 1.4 subtract_divide_fusion
  741.3 111.6 %all-reduce.8.cloned.1.call-done = bf16[512,1152]{1,0:T(8,128)(2,1)} async-done(((bf16[512,1152]{1,0:T(8,128)(2,1)}), bf16[512,1152]{1,0:T(8,128)(2,1)}) %all-reduce.8.cloned.1.call-update) | async-done | bytes 1179664 | tf_op jit(solution)/shard_map/psum | solution.py:114
  852.9 0.0 copy-start.2
  852.9 2.2 fusion.12
  855.2 0.0 copy-done.2
  855.2 2.1 fusion.11
  (10 shorter events, 0.1 us)
Async XLA Ops:
  7.2 5.7 copy-start
  7.2 1.7 copy-start.1
  7.2 2.2 copy-start.4
  7.2 2.2 copy-start.8
  7.2 155.6 %all-reduce.6.cloned.1.call-start = ((), (), s32[]{:S(2)}) async-start(), calls=%async_computation | async-start | bytes 2359296 | tf_op jit(solution)/shard_map/psum | solution.py:54
  11.8 1.0 copy-start.10
  15.1 0.7 copy-start.5
  15.1 134.3 %copy-start.7 = (u32[512]{0:T(512)S(1)}, u32[512]{0:T(512)}, u32[]{:S(2)}) copy-start(u32[512]{0:T(512)} %constant.48) | copy-start | bytes 6148
  15.1 135.5 %copy-start.9 = (s32[2]{0:T(128)S(1)}, s32[2]{0:T(128)}, u32[]{:S(2)}) copy-start(s32[2]{0:T(128)} %param.19) | copy-start | bytes 28
  15.1 147.7 %copy-start.6 = (f32[1152]{0:T(1024)S(1)}, f32[1152]{0:T(1024)}, u32[]{:S(2)}) copy-start(f32[1152]{0:T(1024)} %param.16) | copy-start | bytes 13828
  15.2 723.8 %all-reduce.10.cloned.1.call-start = ((), (), s32[]{:S(2)}) async-start(), calls=%async_computation.2 | async-start | bytes 1179648
  162.8 2.0 copy-start.3
  167.5 685.4 %all-reduce.8.cloned.1.call-start = ((), (), s32[]{:S(2)}) async-start(), calls=%async_computation.1 | async-start | bytes 2359296 | tf_op jit(solution)/shard_map/psum | solution.py:114
  852.9 2.2 copy-start.2
Sparse Core Ops, SparseCore 0:
  15.3 88.6 all-reduce.5
  167.7 571.2 all-reduce.9
  742.2 110.7 all-reduce.7
where the time goes:
time: 864 us
  waiting for transfers between devices  676 us (78%)
  blocking collectives  144 us (17%)
  between operations  16.4 us (2%)
  matrix products  12.5 us (1%)
  other arithmetic  11.6 us (1%)
    unnamed x4, waiting for transfers between devices  564 us
    all_gather x1, blocking collectives, on_device(): lax.all_gather(caption_normalized_directions, 'dp', axis=0, tiled=True)  132 us
    psum x1, waiting for transfers between devices, on_device(): lax.psum(partial_back.astype(jnp.bfloat16).astype(jnp.float32).astype(jnp...  112 us
  transfers between devices with their start and end apart: 3, of which 2 were waited for; matrix products, arithmetic and copies ran while one was open for 1% of the time, Pallas kernels for 0%

commit v1 on v0

v1 whole, which is shorter than its diff:
```python
import jax
import jax.numpy as jnp
from jax import lax
from jax.sharding import PartitionSpec as P

PATCHES = 256
EPS = 1e-06
LOSS_SCALE = 131072.0
HIGH = lax.Precision.HIGHEST


def norm_parts(values):
    centre = values - jnp.mean(values, axis=-1, keepdims=True)
    inverse = lax.rsqrt(jnp.mean(centre * centre, axis=-1, keepdims=True) + EPS)
    return centre * inverse, inverse


def norm_back(grad_out, gain, normed, inverse):
    scaled = grad_out * gain
    return inverse * (
        scaled
        - jnp.mean(scaled, axis=-1, keepdims=True)
        - normed * jnp.mean(scaled * normed, axis=-1, keepdims=True)
    )


def gelu_tanh(values):
    return jax.nn.gelu(values, approximate=True)


def swap(value, axis, partner):
    size = lax.axis_size(axis)
    return lax.ppermute(value, axis, [(i, partner(i)) for i in range(size)])


def swap_xor(value, axis, mask):
    return swap(value, axis, lambda i: i ^ mask)


def gather_dp(rows):
    for masks in ((16, 32, 48), (8, 1, 9), (2, 4, 6)):
        parts = [rows] + [swap_xor(rows, "dp", mask) for mask in masks]
        rows = jnp.concatenate(parts, axis=0)
    return rows


def z_next(i):
    return i ^ 2


def z_prev(i):
    return (3 - i // 2) * 2 + i % 2


def rows_at(array, start, count):
    return lax.dynamic_slice_in_dim(array, start, count, 0)


def on_device(
    patches,
    ln_gain,
    w_up,
    b_up,
    w_down,
    b_down,
    head_gain,
    text_feats,
    pair_ids,
    log_sharpness,
    pairwise_logit_shift,
):
    img_dev, width = text_feats.shape
    batch = img_dev * lax.axis_size("dp")
    position = lax.axis_index("tensor")
    core = position % 2
    ring = position // 2
    u = ((ring == 1) | (ring == 2)).astype(jnp.int32)
    v = (ring >= 2).astype(jnp.int32)

    text_vals = text_feats.astype(jnp.float32)
    text_len = jnp.sqrt(jnp.sum(text_vals * text_vals, axis=-1, keepdims=True) + EPS)
    unit_text = text_vals / text_len
    text_own = unit_text.astype(jnp.bfloat16)
    id_cols = jnp.pad(pair_ids.astype(jnp.bfloat16)[:, None], ((0, 0), (0, 127)))
    all_rows = gather_dp(jnp.concatenate([text_own, id_cols], axis=1))
    text_all = all_rows[:, :width].astype(jnp.float32)
    ids_all = all_rows[:, width].astype(jnp.int32)

    inputs = patches.astype(jnp.float32)
    normed_in, _ = norm_parts(inputs)
    normed = (normed_in * ln_gain).astype(jnp.bfloat16)
    pre_act = jnp.dot(normed, w_up, preferred_element_type=jnp.float32) + b_up
    activation = gelu_tanh(pre_act).astype(jnp.bfloat16).astype(jnp.float32)
    act_mean = activation.reshape(img_dev, PATCHES, -1).mean(axis=1)
    part = jnp.dot(act_mean, w_down.astype(jnp.float32), precision=HIGH)
    got = [part] + [swap_xor(part, "tensor", mask) for mask in range(1, 8)]
    mlp_mean = ((got[0] + got[1]) + (got[2] + got[3])) + (
        (got[4] + got[5]) + (got[6] + got[7])
    )
    pooled = inputs.reshape(img_dev, PATCHES, width).mean(axis=1) + mlp_mean + b_down

    feat_n, feat_s = norm_parts(pooled)
    features = feat_n * head_gain
    feat_len = jnp.sqrt(jnp.sum(features * features, axis=-1, keepdims=True) + EPS)
    img_emb = features / feat_len
    sharp = jnp.exp(log_sharpness[0])
    shift = pairwise_logit_shift[0]

    def logit_grad(rows, columns):
        logits = sharp * jnp.dot(rows, columns.T, precision=HIGH) + shift
        sign = jnp.where(pair_ids[:, None] == ids_all[None, :], 1.0, -1.0)
        return -LOSS_SCALE * sign * jax.nn.sigmoid(-sign * logits) / batch

    g_img = sharp * jnp.dot(logit_grad(img_emb, text_all), text_all, precision=HIGH)
    g_feat = (
        g_img - img_emb * jnp.sum(img_emb * g_img, axis=-1, keepdims=True)
    ) / feat_len
    g_hidden = norm_back(g_feat, head_gain, feat_n, feat_s) / PATCHES

    g_act = lax.dot_general(
        g_hidden.astype(jnp.bfloat16),
        w_down,
        (((1,), (1,)), ((), ())),
        preferred_element_type=jnp.float32,
    )
    g_act = jnp.broadcast_to(g_act[:, None, :], (img_dev, PATCHES, g_act.shape[1]))
    g_act = g_act.reshape(pre_act.shape)
    g_pre = jax.vjp(gelu_tanh, pre_act)[1](g_act)[0].astype(jnp.bfloat16)

    def up_back(rows):
        return lax.dot_general(
            rows, w_up, (((1,), (1,)), ((), ())), preferred_element_type=jnp.float32
        ).astype(jnp.bfloat16)

    away = up_back(rows_at(g_pre, (1 - core) * PATCHES, PATCHES))
    other = swap_xor(away, "tensor", 1)
    keep = up_back(rows_at(g_pre, core * PATCHES, PATCHES))

    def wide(array, start, count):
        return rows_at(array, start, count).astype(jnp.float32)

    def first(start):
        return wide(keep, start, 64) + wide(other, start, 64)

    send_a = first(64 * (1 - u)).astype(jnp.bfloat16)
    send_b = first(128 + 64 * (1 - v)).astype(jnp.bfloat16)
    got_a = swap(send_a, "tensor", z_next)
    got_b = swap(send_b, "tensor", z_prev)
    sum_a = first(64 * u) + got_a.astype(jnp.float32)
    sum_b = first(128 + 64 * v) + got_b.astype(jnp.float32)
    send_a = rows_at(sum_a, 32 * (1 - v), 32).astype(jnp.bfloat16)
    send_b = rows_at(sum_b, 32 * (1 - u), 32).astype(jnp.bfloat16)
    got_a = swap(send_a, "tensor", z_prev)
    got_b = swap(send_b, "tensor", z_next)
    sum_a = rows_at(sum_a, 32 * v, 32) + got_a.astype(jnp.float32)
    sum_b = rows_at(sum_b, 32 * u, 32) + got_b.astype(jnp.float32)

    def start_a(uu, vv):
        return 64 * uu + 32 * vv

    def start_b(uu, vv):
        return 128 + 64 * vv + 32 * uu

    own_x = jnp.concatenate(
        [
            rows_at(patches, core * PATCHES + start_a(u, v), 32),
            rows_at(patches, core * PATCHES + start_b(u, v), 32),
        ]
    ).astype(jnp.float32)
    own_n, own_s = norm_parts(own_x)
    g_own = rows_at(g_hidden, core, 1)
    done = norm_back(jnp.concatenate([sum_a, sum_b]), ln_gain, own_n, own_s) + g_own
    done = done.astype(jnp.bfloat16)

    from_next = swap(done, "tensor", z_next)
    from_prev = swap(done, "tensor", z_prev)
    far_a = swap(from_prev[:32], "tensor", z_next)
    far_b = swap(from_next[32:], "tensor", z_prev)
    mine = [done, from_next, from_prev, far_a, far_b]
    theirs = [swap_xor(piece, "tensor", 1) for piece in mine]
    grad_patches = jnp.zeros(patches.shape, jnp.bfloat16)
    for side, pieces in ((core, mine), (1 - core, theirs)):
        base = side * PATCHES
        blocks = [
            (pieces[0][:32], start_a(u, v)),
            (pieces[0][32:], start_b(u, v)),
            (pieces[1][:32], start_a(1 - u, v)),
            (pieces[1][32:], start_b(1 - u, v)),
            (pieces[2][:32], start_a(u, 1 - v)),
            (pieces[2][32:], start_b(u, 1 - v)),
            (pieces[3], start_a(1 - u, 1 - v)),
            (pieces[4], start_b(1 - u, 1 - v)),
        ]
        for block, start in blocks:
            grad_patches = lax.dynamic_update_slice_in_dim(
                grad_patches, block, base + start, 0
            )

    img_all = gather_dp(img_emb)
    lg_text = logit_grad(text_own.astype(jnp.float32), img_all)
    g_text = sharp * jnp.dot(lg_text, img_all, precision=HIGH)
    grad_text = (
        g_text - unit_text * jnp.sum(unit_text * g_text, axis=-1, keepdims=True)
    ) / text_len
    return grad_patches, grad_text


def solution(mesh):
    in_specs = (
        P("dp", None),
        P(),
        P(None, "tensor"),
        P("tensor"),
        P("tensor", None),
        P(),
        P(),
        P("dp", None),
        P("dp"),
        P(),
        P(),
    )
    out_specs = (P("dp", None), P("dp", None))
    return jax.shard_map(
        on_device, mesh=mesh, in_specs=in_specs, out_specs=out_specs, check_vma=False
    )
```

time: 864 us -> 199 us (0.23)
  waiting for transfers between devices: 676 us -> 11.7 us
  starting transfers between devices: 0.12 us -> 147 us
  blocking collectives: 144 us -> 0 us
  between operations: 16.4 us -> 3.35 us
  local copies, waits for them, and re-layouts: 3.69 us -> 13.8 us
    unnamed x4 -> x0, waiting for transfers between devices: 564 us -> none
    ppermute x0 -> x39, starting transfers between devices: none -> 147 us  [swap(): return lax.ppermute(value, axis, [(i, partner(i)) for i in range(size)])]
    all_gather x1 -> x0, blocking collectives: 132 us -> none  [on_device(): lax.all_gather(caption_normalized_directions, 'dp', axis=0, tiled=True)]
    psum x2 -> x0, waiting for transfers between devices: 112 us -> none  [the longest x1 112 us: on_device(): lax.psum(partial_back.astype(jnp.bfloat16).astype(jnp.float32).astype(jnp...]
    unnamed x1 -> x0, blocking collectives: 12 us -> none
    ppermute x0 -> x39, waiting for transfers between devices: none -> 11.7 us  [swap(): return lax.ppermute(value, axis, [(i, partner(i)) for i in range(size)])]
  transfers between devices with their start and end apart: 3 -> 39, of which waited for: 2 -> 4; matrix products, arithmetic and copies ran while one was open for 1% -> 11% of each run, Pallas kernels for 0% -> 0%
where the time goes in v1:
time: 199 us; the launch traced here: 197 us
  starting transfers between devices  147 us (74%)
  local copies, waits for them, and re-layouts  13.8 us (7%)
  waiting for transfers between devices  11.7 us (6%)
  matrix products  11.1 us (6%)
  other arithmetic  10.5 us (5%)
  between operations  3.35 us (2%)
    ppermute x39, starting transfers between devices, swap(): return lax.ppermute(value, axis, [(i, partner(i)) for i in range(size)])  147 us
    ppermute x39, waiting for transfers between devices, swap(): return lax.ppermute(value, axis, [(i, partner(i)) for i in range(size)])  11.7 us
    concatenate x4, local copies, waits for them, and re-layouts, gather_dp(): rows = jnp.concatenate(parts, axis=0)  6.7 us
  transfers between devices with their start and end apart: 39, of which 4 were waited for; matrix products, arithmetic and copies ran while one was open for 11% of the time, Pallas kernels for 0%

profile of v1, /device:TPU:1, one launch (start us, length us, event | category | flops | bytes accessed | tf_op | source)
XLA Modules:
  0.0 197.4 jit_solution(6337399703407655963)
XLA Ops:
  0.7 1.6 convert_reduce_fusion
  2.9 2.7 %fusion.26 = (f32[512,538]{0,1:T(8,128)}, f32[512,538]{0,1:T(8,128)}) fusion(f32[538]{0:T(1024)S(1)} %copy-done.30, bf16[1152,538]{0,1:T(8,128)(2,1)S(1)} %copy-done, bf16[512,1152]{1,0:T(8,128)(2,1)S(1)} %copy-done.1, f32[1152]{0:T(1024)S(1)} %copy-done.19, f32[512]{0:T(512)S(1)} %add_rsqrt_fusion, f32[512]{0:T(512)S(1)} %broadcast_multiply_fusion), kind=kOutput, calls=%fused_computation.40 | convolution fusion | flops 640629760 | bytes 4633704 | tf_op jit(solution)/shard_map/dot_general | solution.py:92
  5.5 2.0 reshape.101
  7.5 1.4 reduce_sum.149
  8.9 2.0 %fusion.39 = f32[2,1152]{1,0:T(2,128)S(1)} fusion(bf16[538,1152]{1,0:T(8,128)(2,1)} %param.15, f32[2,538]{0,1:T(8,128)} %reduce_sum.149), kind=kOutput, calls=%fused_computation.61 | convolution fusion | flops 14875700 | bytes 1253072 | tf_op jit(solution)/shard_map/dot_general | solution.py:95
  10.9 8.8 %collective-permute-start = (f32[2,1152]{1,0:T(2,128)S(1)}, f32[2,1152]{1,0:T(2,128)S(1)}, u32[]{:S(2)}, u32[]{:S(2)}) collective-permute-start(f32[2,1152]{1,0:T(2,128)S(1)} %fusion.39), channel_id=1, source_target_pairs={{0,1},{1,0},{2,3},{3,2},{4,5},{5,4},{6,7},{7,6},{8,9},{9,8},{10,11... | collective-permute-start | bytes 27656 | tf_op jit(solution)/shard_map/ppermute | solution.py:33
  19.7 1.9 collective-permute-start.1
  21.7 4.4 %collective-permute-start.2 = (f32[2,1152]{1,0:T(2,128)S(1)}, f32[2,1152]{1,0:T(2,128)S(1)}, u32[]{:S(2)}, u32[]{:S(2)}) collective-permute-start(f32[2,1152]{1,0:T(2,128)S(1)} %fusion.39), channel_id=1, source_target_pairs={{0,3},{1,2},{2,1},{3,0},{4,7},{5,6},{6,5},{7,4},{8,11},{9,10},{10,... | collective-permute-start | bytes 27656 | tf_op jit(solution)/shard_map/ppermute | solution.py:33
  26.1 5.3 %collective-permute-start.3 = (f32[2,1152]{1,0:T(2,128)S(1)}, f32[2,1152]{1,0:T(2,128)S(1)}, u32[]{:S(2)}, u32[]{:S(2)}) collective-permute-start(f32[2,1152]{1,0:T(2,128)S(1)} %fusion.39), channel_id=1, source_target_pairs={{0,4},{1,5},{2,6},{3,7},{4,0},{5,1},{6,2},{7,3},{8,12},{9,13},{10,... | collective-permute-start | bytes 27656 | tf_op jit(solution)/shard_map/ppermute | solution.py:33
  31.4 4.3 %collective-permute-start.4 = (f32[2,1152]{1,0:T(2,128)S(1)}, f32[2,1152]{1,0:T(2,128)S(1)}, u32[]{:S(2)}, u32[]{:S(2)}) collective-permute-start(f32[2,1152]{1,0:T(2,128)S(1)} %fusion.39), channel_id=1, source_target_pairs={{0,5},{1,4},{2,7},{3,6},{4,1},{5,0},{6,3},{7,2},{8,13},{9,12},{10,... | collective-permute-start | bytes 27656 | tf_op jit(solution)/shard_map/ppermute | solution.py:33
  35.9 0.7 fusion.55
  36.9 5.3 %collective-permute-start.5 = (f32[2,1152]{1,0:T(2,128)S(1)}, f32[2,1152]{1,0:T(2,128)S(1)}, u32[]{:S(2)}, u32[]{:S(2)}) collective-permute-start(f32[2,1152]{1,0:T(2,128)S(1)} %fusion.39), channel_id=1, source_target_pairs={{0,6},{1,7},{2,4},{3,5},{4,2},{5,3},{6,0},{7,1},{8,14},{9,15},{10,... | collective-permute-start | bytes 27656 | tf_op jit(solution)/shard_map/ppermute | solution.py:33
  42.2 2.3 %collective-permute-start.6 = (f32[2,1152]{1,0:T(2,128)S(1)}, f32[2,1152]{1,0:T(2,128)S(1)}, u32[]{:S(2)}, u32[]{:S(2)}) collective-permute-start(f32[2,1152]{1,0:T(2,128)S(1)} %fusion.39), channel_id=1, source_target_pairs={{0,7},{1,6},{2,5},{3,4},{4,3},{5,2},{6,1},{7,0},{8,15},{9,14},{10,... | collective-permute-start | bytes 27656 | tf_op jit(solution)/shard_map/ppermute | solution.py:33
  44.7 3.9 %collective-permute-start.7 = (bf16[2,1280]{1,0:T(2,128)(2,1)S(1)}, bf16[2,1280]{1,0:T(2,128)(2,1)S(1)}, u32[]{:S(2)}, u32[]{:S(2)}) collective-permute-start(bf16[2,1280]{1,0:T(2,128)(2,1)S(1)} %pad_maximum_fusion.3), channel_id=1, source_target_pairs={{0,128},{8,136},{16,144},{24,152},{32,160},{40,168},{48,176},{56,1... | collective-permute-start | bytes 15368 | tf_op jit(solution)/shard_map/ppermute | solution.py:33
  48.6 5.7 %collective-permute-start.8 = (bf16[2,1280]{1,0:T(2,128)(2,1)S(1)}, bf16[2,1280]{1,0:T(2,128)(2,1)S(1)}, u32[]{:S(2)}, u32[]{:S(2)}) collective-permute-start(bf16[2,1280]{1,0:T(2,128)(2,1)S(1)} %pad_maximum_fusion.3), channel_id=1, source_target_pairs={{0,256},{8,264},{16,272},{24,280},{32,288},{40,296},{48,304},{56,3... | collective-permute-start | bytes 15368 | tf_op jit(solution)/shard_map/ppermute | solution.py:33
  54.3 1.9 collective-permute-start.9
  56.9 3.9 %collective-permute-start.30 = (f32[2,1152]{1,0:T(2,128)S(1)}, f32[2,1152]{1,0:T(2,128)S(1)}, u32[]{:S(2)}, u32[]{:S(2)}) collective-permute-start(f32[2,1152]{1,0:T(2,128)S(1)} %multiply_divide_fusion), channel_id=1, source_target_pairs={{0,128},{8,136},{16,144},{24,152},{32,160},{40,168},{48,176},{56,1... | collective-permute-start | bytes 27656 | tf_op jit(solution)/shard_map/ppermute | solution.py:33
  60.8 5.7 %collective-permute-start.31 = (f32[2,1152]{1,0:T(2,128)S(1)}, f32[2,1152]{1,0:T(2,128)S(1)}, u32[]{:S(2)}, u32[]{:S(2)}) collective-permute-start(f32[2,1152]{1,0:T(2,128)S(1)} %multiply_divide_fusion), channel_id=1, source_target_pairs={{0,256},{8,264},{16,272},{24,280},{32,288},{40,296},{48,304},{56,3... | collective-permute-start | bytes 27656 | tf_op jit(solution)/shard_map/ppermute | solution.py:33
  66.5 1.9 collective-permute-start.32
  68.5 2.8 %collective-permute-start.10 = (bf16[8,1280]{1,0:T(8,128)(2,1)S(1)}, bf16[8,1280]{1,0:T(8,128)(2,1)S(1)}, u32[]{:S(2)}, u32[]{:S(2)}) collective-permute-start(bf16[8,1280]{1,0:T(8,128)(2,1)S(1)} %pad_maximum_fusion.2), channel_id=1, source_target_pairs={{0,64},{8,72},{16,80},{24,88},{32,96},{40,104},{48,112},{56,120},{... | collective-permute-start | bytes 61448 | tf_op jit(solution)/shard_map/ppermute | solution.py:33
  71.3 3.1 %collective-permute-start.11 = (bf16[8,1280]{1,0:T(8,128)(2,1)S(1)}, bf16[8,1280]{1,0:T(8,128)(2,1)S(1)}, u32[]{:S(2)}, u32[]{:S(2)}) collective-permute-start(bf16[8,1280]{1,0:T(8,128)(2,1)S(1)} %pad_maximum_fusion.2), channel_id=1, source_target_pairs={{0,8},{8,0},{16,24},{24,16},{32,40},{40,32},{48,56},{56,48},{64,72... | collective-permute-start | bytes 61448 | tf_op jit(solution)/shard_map/ppermute | solution.py:33
  74.5 2.5 %collective-permute-start.12 = (bf16[8,1280]{1,0:T(8,128)(2,1)S(1)}, bf16[8,1280]{1,0:T(8,128)(2,1)S(1)}, u32[]{:S(2)}, u32[]{:S(2)}) collective-permute-start(bf16[8,1280]{1,0:T(8,128)(2,1)S(1)} %pad_maximum_fusion.2), channel_id=1, source_target_pairs={{0,72},{8,64},{16,88},{24,80},{32,104},{40,96},{48,120},{56,112},{... | collective-permute-start | bytes 61448 | tf_op jit(solution)/shard_map/ppermute | solution.py:33
  77.0 2.8 %collective-permute-start.33 = (f32[8,1152]{1,0:T(8,128)S(1)}, f32[8,1152]{1,0:T(8,128)S(1)}, u32[]{:S(2)}, u32[]{:S(2)}) collective-permute-start(f32[8,1152]{1,0:T(8,128)S(1)} %pad_maximum_fusion.1), channel_id=1, source_target_pairs={{0,64},{8,72},{16,80},{24,88},{32,96},{40,104},{48,112},{56,120},{... | collective-permute-start | bytes 110600 | tf_op jit(solution)/shard_map/ppermute | solution.py:33
  80.0 3.1 %collective-permute-start.34 = (f32[8,1152]{1,0:T(8,128)S(1)}, f32[8,1152]{1,0:T(8,128)S(1)}, u32[]{:S(2)}, u32[]{:S(2)}) collective-permute-start(f32[8,1152]{1,0:T(8,128)S(1)} %pad_maximum_fusion.1), channel_id=1, source_target_pairs={{0,8},{8,0},{16,24},{24,16},{32,40},{40,32},{48,56},{56,48},{64,72... | collective-permute-start | bytes 110600 | tf_op jit(solution)/shard_map/ppermute | solution.py:33
  83.2 2.5 %collective-permute-start.35 = (f32[8,1152]{1,0:T(8,128)S(1)}, f32[8,1152]{1,0:T(8,128)S(1)}, u32[]{:S(2)}, u32[]{:S(2)}) collective-permute-start(f32[8,1152]{1,0:T(8,128)S(1)} %pad_maximum_fusion.1), channel_id=1, source_target_pairs={{0,72},{8,64},{16,88},{24,80},{32,104},{40,96},{48,120},{56,112},{... | collective-permute-start | bytes 110600 | tf_op jit(solution)/shard_map/ppermute | solution.py:33
  85.7 3.1 %collective-permute-start.13 = (bf16[32,1280]{1,0:T(8,128)(2,1)S(1)}, bf16[32,1280]{1,0:T(8,128)(2,1)S(1)}, u32[]{:S(2)}, u32[]{:S(2)}) collective-permute-start(bf16[32,1280]{1,0:T(8,128)(2,1)S(1)} %concatenate.34), channel_id=1, source_target_pairs={{0,16},{8,24},{16,0},{24,8},{32,48},{40,56},{48,32},{56,40},{64,80... | collective-permute-start | bytes 245768 | tf_op jit(solution)/shard_map/ppermute | solution.py:33
  88.8 4.4 %collective-permute-start.14 = (bf16[32,1280]{1,0:T(8,128)(2,1)S(1)}, bf16[32,1280]{1,0:T(8,128)(2,1)S(1)}, u32[]{:S(2)}, u32[]{:S(2)}) collective-permute-start(bf16[32,1280]{1,0:T(8,128)(2,1)S(1)} %concatenate.34), channel_id=1, source_target_pairs={{0,32},{8,40},{16,48},{24,56},{32,0},{40,8},{48,16},{56,24},{64,96... | collective-permute-start | bytes 245768 | tf_op jit(solution)/shard_map/ppermute | solution.py:33
  93.2 2.1 %collective-permute-start.15 = (bf16[32,1280]{1,0:T(8,128)(2,1)S(1)}, bf16[32,1280]{1,0:T(8,128)(2,1)}, u32[]{:S(2)}, u32[]{:S(2)}) collective-permute-start(bf16[32,1280]{1,0:T(8,128)(2,1)S(1)} %concatenate.34), channel_id=1, source_target_pairs={{0,48},{8,56},{16,32},{24,40},{32,16},{40,24},{48,0},{56,8},{64,11... | collective-permute-start | bytes 245768 | tf_op jit(solution)/shard_map/ppermute | solution.py:33
  97.4 2.5 %concatenate.38 = f32[32,1152]{1,0:T(8,128)} concatenate(f32[2,1152]{1,0:T(2,128)S(1)} %multiply_divide_fusion, f32[2,1152]{1,0:T(2,128)S(1)} %collective-permute-done.30, f32[2,1152]{1,0:T(2,128)S(1)} %collective-permute-done.31, f32[2,1152]{1,0:T(2,128)S(1)} %collective-permute-done.32, f32[8,1152]{1,0:T(8,128)S(1)} %collective-permute-done.33, ...), dimensions={0} | concatenate | bytes 294912 | tf_op jit(solution)/shard_map/concatenate | solution.py:43
  99.9 1.9 collective-permute-start.36
  101.8 5.6 %collective-permute-start.37 = (f32[32,1152]{1,0:T(8,128)}, f32[32,1152]{1,0:T(8,128)S(1)}, u32[]{:S(2)}, u32[]{:S(2)}) collective-permute-start(f32[32,1152]{1,0:T(8,128)} %concatenate.38), channel_id=1, source_target_pairs={{0,32},{8,40},{16,48},{24,56},{32,0},{40,8},{48,16},{56,24},{64,96... | collective-permute-start | bytes 442376 | tf_op jit(solution)/shard_map/ppermute | solution.py:33
  107.4 2.1 %collective-permute-start.38 = (f32[32,1152]{1,0:T(8,128)}, f32[32,1152]{1,0:T(8,128)}, u32[]{:S(2)}, u32[]{:S(2)}) collective-permute-start(f32[32,1152]{1,0:T(8,128)} %concatenate.38), channel_id=1, source_target_pairs={{0,48},{8,56},{16,32},{24,40},{32,16},{40,24},{48,0},{56,8},{64,11... | collective-permute-start | bytes 442376 | tf_op jit(solution)/shard_map/ppermute | solution.py:33
  109.6 1.7 concatenate.35
  111.9 1.0 fusion.17
  113.3 0.8 fusion.54
  114.1 0.7 multiply_multiply_fusion.2
  115.4 0.6 broadcast_bitcast_fusion
  116.5 1.2 copy-done.4
  117.6 0.8 fusion.9
  118.4 1.5 convolution_convert_fusion
  119.9 7.2 %collective-permute-start.16 = (bf16[256,1152]{1,0:T(8,128)(2,1)}, bf16[256,1152]{1,0:T(8,128)(2,1)S(1)}, u32[]{:S(2)}, u32[]{:S(2)}) collective-permute-start(bf16[256,1152]{1,0:T(8,128)(2,1)} %convolution_convert_fusion), channel_id=1, source_target_pairs={{0,1},{1,0},{2,3},{3,2},{4,5},{5,4},{6,7},{7,6},{8,9},{9,8},{10,11... | collective-permute-start | bytes 1769480 | tf_op jit(solution)/shard_map/ppermute | solution.py:33
  127.1 0.7 convolution_convert_fusion.1
  128.5 2.5 %concatenate.39 = f32[128,1152]{1,0:T(8,128)S(1)} concatenate(f32[2,1152]{1,0:T(2,128)S(1)} %multiply_divide_fusion, f32[2,1152]{1,0:T(2,128)} %copy-done.10, f32[2,1152]{1,0:T(2,128)} %copy-done.11, f32[2,1152]{1,0:T(2,128)} %copy-done.12, f32[8,1152]{1,0:T(8,128)S(1)} %copy-done.6, f32[8,1152]{1,0:T(8,128)S(1)} %copy-done.8, f32[8,1152]{1,0:T(8,128)} %copy-done.9, ...), dimensions={0} | concatenate | bytes 1179648 | tf_op jit(solution)/shard_map/concatenate | solution.py:43
  131.0 1.1 fusion.25
  132.1 1.2 multiply_reduce_fusion.1
  133.4 2.1 %collective-permute-start.17 = (bf16[64,1152]{1,0:T(8,128)(2,1)S(1)}, bf16[64,1152]{1,0:T(8,128)(2,1)S(1)}, u32[]{:S(2)}, u32[]{:S(2)}) collective-permute-start(bf16[64,1152]{1,0:T(8,128)(2,1)S(1)} %add_convert_fusion.1), channel_id=1, source_target_pairs={{0,2},{1,3},{2,0},{3,1},{4,6},{5,7},{6,4},{7,5},{8,10},{9,11},{10,... | collective-permute-start | bytes 442376 | tf_op jit(solution)/shard_map/ppermute | solution.py:33
  135.5 1.3 subtract_divide_fusion
  136.9 7.9 %collective-permute-done.17 = bf16[64,1152]{1,0:T(8,128)(2,1)S(1)} collective-permute-done((bf16[64,1152]{1,0:T(8,128)(2,1)S(1)}, bf16[64,1152]{1,0:T(8,128)(2,1)S(1)}, u32[]{:S(2)}, u32[]{:S(2)}) %collective-permute-start.17) | collective-permute-done | bytes 147488 | tf_op jit(solution)/shard_map/ppermute | solution.py:33
  144.9 2.6 %collective-permute-start.19 = (bf16[64,1152]{1,0:T(8,128)(2,1)S(1)}, bf16[64,1152]{1,0:T(8,128)(2,1)S(1)}, u32[]{:S(2)}, u32[]{:S(2)}) collective-permute-start(bf16[64,1152]{1,0:T(8,128)(2,1)S(1)} %get-tuple-element.16), channel_id=1, source_target_pairs={{0,6},{1,7},{2,4},{3,5},{4,2},{5,3},{6,0},{7,1},{8,14},{9,15},{10,... | collective-permute-start | bytes 442376 | tf_op jit(solution)/shard_map/ppermute | solution.py:33
  147.5 4.8 %collective-permute-start.18 = (bf16[32,1152]{1,0:T(8,128)(2,1)S(1)}, bf16[32,1152]{1,0:T(8,128)(2,1)S(1)}, u32[]{:S(2)}, u32[]{:S(2)}) collective-permute-start(bf16[32,1152]{1,0:T(8,128)(2,1)S(1)} %dynamic-slice_convert_fusion.1), channel_id=1, source_target_pairs={{0,6},{1,7},{2,4},{3,5},{4,2},{5,3},{6,0},{7,1},{8,14},{9,15},{10,... | collective-permute-start | bytes 221192 | tf_op jit(solution)/shard_map/ppermute | solution.py:33
  152.4 1.1 collective-permute-done.19
  153.6 5.6 %collective-permute-start.20 = (bf16[32,1152]{1,0:T(8,128)(2,1)S(1)}, bf16[32,1152]{1,0:T(8,128)(2,1)S(1)}, u32[]{:S(2)}, u32[]{:S(2)}) collective-permute-start(bf16[32,1152]{1,0:T(8,128)(2,1)S(1)} %dynamic-slice_convert_fusion), channel_id=1, source_target_pairs={{0,2},{1,3},{2,0},{3,1},{4,6},{5,7},{6,4},{7,5},{8,10},{9,11},{10,... | collective-permute-start | bytes 221192 | tf_op jit(solution)/shard_map/ppermute | solution.py:33
  159.2 1.7 collective-permute-done.20
  161.4 4.7 %collective-permute-start.21 = (bf16[64,1152]{1,0:T(8,128)(2,1)S(1)}, bf16[64,1152]{1,0:T(8,128)(2,1)S(1)}, u32[]{:S(2)}, u32[]{:S(2)}) collective-permute-start(bf16[64,1152]{1,0:T(8,128)(2,1)S(1)} %fusion.35), channel_id=1, source_target_pairs={{0,2},{1,3},{2,0},{3,1},{4,6},{5,7},{6,4},{7,5},{8,10},{9,11},{10,... | collective-permute-start | bytes 442376 | tf_op jit(solution)/shard_map/ppermute | solution.py:33
  166.1 3.7 %collective-permute-start.22 = (bf16[64,1152]{1,0:T(8,128)(2,1)S(1)}, bf16[64,1152]{1,0:T(8,128)(2,1)S(1)}, u32[]{:S(2)}, u32[]{:S(2)}) collective-permute-start(bf16[64,1152]{1,0:T(8,128)(2,1)S(1)} %fusion.35), channel_id=1, source_target_pairs={{0,6},{1,7},{2,4},{3,5},{4,2},{5,3},{6,0},{7,1},{8,14},{9,15},{10,... | collective-permute-start | bytes 442376 | tf_op jit(solution)/shard_map/ppermute | solution.py:33
  169.8 4.8 %collective-permute-start.25 = (bf16[64,1152]{1,0:T(8,128)(2,1)S(1)}, bf16[64,1152]{1,0:T(8,128)(2,1)S(1)}, u32[]{:S(2)}, u32[]{:S(2)}) collective-permute-start(bf16[64,1152]{1,0:T(8,128)(2,1)S(1)} %fusion.35), channel_id=1, source_target_pairs={{0,1},{1,0},{2,3},{3,2},{4,5},{5,4},{6,7},{7,6},{8,9},{9,8},{10,11... | collective-permute-start | bytes 442376 | tf_op jit(solution)/shard_map/ppermute | solution.py:33
  174.9 4.1 %collective-permute-start.23 = (bf16[32,1152]{1,0:T(8,128)(2,1)S(1)}, bf16[32,1152]{1,0:T(8,128)(2,1)S(1)}, u32[]{:S(2)}, u32[]{:S(2)}) collective-permute-start(bf16[32,1152]{1,0:T(8,128)(2,1)S(1)} %get-tuple-element.19), channel_id=1, source_target_pairs={{0,2},{1,3},{2,0},{3,1},{4,6},{5,7},{6,4},{7,5},{8,10},{9,11},{10,... | collective-permute-start | bytes 221192 | tf_op jit(solution)/shard_map/ppermute | solution.py:33
  179.0 6.2 %collective-permute-start.24 = (bf16[32,1152]{1,0:T(8,128)(2,1)S(1)}, bf16[32,1152]{1,0:T(8,128)(2,1)S(1)}, u32[]{:S(2)}, u32[]{:S(2)}) collective-permute-start(bf16[32,1152]{1,0:T(8,128)(2,1)S(1)} %get-tuple-element.17), channel_id=1, source_target_pairs={{0,6},{1,7},{2,4},{3,5},{4,2},{5,3},{6,0},{7,1},{8,14},{9,15},{10,... | collective-permute-start | bytes 221192 | tf_op jit(solution)/shard_map/ppermute | solution.py:33
  185.2 3.6 %collective-permute-start.26 = (bf16[64,1152]{1,0:T(8,128)(2,1)S(1)}, bf16[64,1152]{1,0:T(8,128)(2,1)S(1)}, u32[]{:S(2)}, u32[]{:S(2)}) collective-permute-start(bf16[64,1152]{1,0:T(8,128)(2,1)S(1)} %collective-permute-done.21), channel_id=1, source_target_pairs={{0,1},{1,0},{2,3},{3,2},{4,5},{5,4},{6,7},{7,6},{8,9},{9,8},{10,11... | collective-permute-start | bytes 442376 | tf_op jit(solution)/shard_map/ppermute | solution.py:33
  188.9 1.9 collective-permute-start.27
  190.8 2.4 %collective-permute-start.28 = (bf16[32,1152]{1,0:T(8,128)(2,1)S(1)}, bf16[32,1152]{1,0:T(8,128)(2,1)S(1)}, u32[]{:S(2)}, u32[]{:S(2)}) collective-permute-start(bf16[32,1152]{1,0:T(8,128)(2,1)S(1)} %collective-permute-done.23), channel_id=1, source_target_pairs={{0,1},{1,0},{2,3},{3,2},{4,5},{5,4},{6,7},{7,6},{8,9},{9,8},{10,11... | collective-permute-start | bytes 221192 | tf_op jit(solution)/shard_map/ppermute | solution.py:33
  193.3 2.0 %collective-permute-start.29 = (bf16[32,1152]{1,0:T(8,128)(2,1)S(1)}, bf16[32,1152]{1,0:T(8,128)(2,1)S(1)}, u32[]{:S(2)}, u32[]{:S(2)}) collective-permute-start(bf16[32,1152]{1,0:T(8,128)(2,1)S(1)} %collective-permute-done.24), channel_id=1, source_target_pairs={{0,1},{1,0},{2,3},{3,2},{4,5},{5,4},{6,7},{7,6},{8,9},{9,8},{10,11... | collective-permute-start | bytes 221192 | tf_op jit(solution)/shard_map/ppermute | solution.py:33
  195.5 0.9 collective-permute-done.29
  196.4 1.0 copy-done.3
  (155 shorter events, 6.5 us)
Async XLA Ops:
  0.6 2.2 %copy-start = (bf16[1152,538]{0,1:T(8,128)(2,1)S(1)}, bf16[1152,538]{0,1:T(8,128)(2,1)}, u32[]{:S(2)}) copy-start(bf16[1152,538]{0,1:T(8,128)(2,1)} %param.13) | copy-start | bytes 3718660
  7.5 28.3 %copy-start.22 = (bf16[2,1152]{1,0:T(2,128)(2,1)S(1)}, bf16[2,1152]{1,0:T(2,128)(2,1)}, u32[]{:S(2)}) copy-start(bf16[2,1152]{1,0:T(2,128)(2,1)} %param.18) | copy-start | bytes 13828
  7.5 29.1 %copy-start.29 = (s32[2]{0:T(128)S(1)}, s32[2]{0:T(128)}, u32[]{:S(2)}) copy-start(s32[2]{0:T(128)} %param.19) | copy-start | bytes 28
  10.9 45.3 %copy-start.23 = (f32[1152]{0:T(1024)S(1)}, f32[1152]{0:T(1024)}, u32[]{:S(2)}) copy-start(f32[1152]{0:T(1024)} %param.16) | copy-start | bytes 13828
  10.9 45.7 %copy-start.14 = (f32[1152]{0:T(1024)S(1)}, f32[1152]{0:T(1024)}, u32[]{:S(2)}) copy-start(f32[1152]{0:T(1024)} %param.17) | copy-start | bytes 13828
  10.9 26.0 %collective-permute-start = (f32[2,1152]{1,0:T(2,128)S(1)}, f32[2,1152]{1,0:T(2,128)S(1)}, u32[]{:S(2)}, u32[]{:S(2)}) collective-permute-start(f32[2,1152]{1,0:T(2,128)S(1)} %fusion.39), channel_id=1, source_target_pairs={{0,1},{1,0},{2,3},{3,2},{4,5},{5,4},{6,7},{7,6},{8,9},{9,8},{10,11... | collective-permute-start | bytes 27656 | tf_op jit(solution)/shard_map/ppermute | solution.py:33
  19.7 22.5 %collective-permute-start.1 = (f32[2,1152]{1,0:T(2,128)S(1)}, f32[2,1152]{1,0:T(2,128)S(1)}, u32[]{:S(2)}, u32[]{:S(2)}) collective-permute-start(f32[2,1152]{1,0:T(2,128)S(1)} %fusion.39), channel_id=1, source_target_pairs={{0,2},{1,3},{2,0},{3,1},{4,6},{5,7},{6,4},{7,5},{8,10},{9,11},{10,... | collective-permute-start | bytes 27656 | tf_op jit(solution)/shard_map/ppermute | solution.py:33
  21.7 23.1 %collective-permute-start.2 = (f32[2,1152]{1,0:T(2,128)S(1)}, f32[2,1152]{1,0:T(2,128)S(1)}, u32[]{:S(2)}, u32[]{:S(2)}) collective-permute-start(f32[2,1152]{1,0:T(2,128)S(1)} %fusion.39), channel_id=1, source_target_pairs={{0,3},{1,2},{2,1},{3,0},{4,7},{5,6},{6,5},{7,4},{8,11},{9,10},{10,... | collective-permute-start | bytes 27656 | tf_op jit(solution)/shard_map/ppermute | solution.py:33
  26.1 22.5 %collective-permute-start.3 = (f32[2,1152]{1,0:T(2,128)S(1)}, f32[2,1152]{1,0:T(2,128)S(1)}, u32[]{:S(2)}, u32[]{:S(2)}) collective-permute-start(f32[2,1152]{1,0:T(2,128)S(1)} %fusion.39), channel_id=1, source_target_pairs={{0,4},{1,5},{2,6},{3,7},{4,0},{5,1},{6,2},{7,3},{8,12},{9,13},{10,... | collective-permute-start | bytes 27656 | tf_op jit(solution)/shard_map/ppermute | solution.py:33
  31.4 22.9 %collective-permute-start.4 = (f32[2,1152]{1,0:T(2,128)S(1)}, f32[2,1152]{1,0:T(2,128)S(1)}, u32[]{:S(2)}, u32[]{:S(2)}) collective-permute-start(f32[2,1152]{1,0:T(2,128)S(1)} %fusion.39), channel_id=1, source_target_pairs={{0,5},{1,4},{2,7},{3,6},{4,1},{5,0},{6,3},{7,2},{8,13},{9,12},{10,... | collective-permute-start | bytes 27656 | tf_op jit(solution)/shard_map/ppermute | solution.py:33
  35.9 6.3 %copy-start.26 = (f32[2]{0:T(128)}, f32[2]{0:T(128)S(1)}, u32[]{:S(2)}) copy-start(f32[2]{0:T(128)S(1)} %add_sqrt_fusion.1) | copy-start | bytes 28
  36.6 59.3 %copy-start.15 = (bf16[2,1152]{1,0:T(2,128)(2,1)}, bf16[2,1152]{1,0:T(2,128)(2,1)S(1)}, u32[]{:S(2)}) copy-start(bf16[2,1152]{1,0:T(2,128)(2,1)S(1)} %get-tuple-element.7) | copy-start | bytes 13828
  36.7 59.2 %copy-start.18 = (bf16[2,1280]{1,0:T(2,128)(2,1)}, bf16[2,1280]{1,0:T(2,128)(2,1)S(1)}, u32[]{:S(2)}) copy-start(bf16[2,1280]{1,0:T(2,128)(2,1)S(1)} %pad_maximum_fusion.3) | copy-start | bytes 15364
  36.9 19.3 %collective-permute-start.5 = (f32[2,1152]{1,0:T(2,128)S(1)}, f32[2,1152]{1,0:T(2,128)S(1)}, u32[]{:S(2)}, u32[]{:S(2)}) collective-permute-start(f32[2,1152]{1,0:T(2,128)S(1)} %fusion.39), channel_id=1, source_target_pairs={{0,6},{1,7},{2,4},{3,5},{4,2},{5,3},{6,0},{7,1},{8,14},{9,15},{10,... | collective-permute-start | bytes 27656 | tf_op jit(solution)/shard_map/ppermute | solution.py:33
  42.2 14.0 %collective-permute-start.6 = (f32[2,1152]{1,0:T(2,128)S(1)}, f32[2,1152]{1,0:T(2,128)S(1)}, u32[]{:S(2)}, u32[]{:S(2)}) collective-permute-start(f32[2,1152]{1,0:T(2,128)S(1)} %fusion.39), channel_id=1, source_target_pairs={{0,7},{1,6},{2,5},{3,4},{4,3},{5,2},{6,1},{7,0},{8,15},{9,14},{10,... | collective-permute-start | bytes 27656 | tf_op jit(solution)/shard_map/ppermute | solution.py:33
  44.7 21.8 %collective-permute-start.7 = (bf16[2,1280]{1,0:T(2,128)(2,1)S(1)}, bf16[2,1280]{1,0:T(2,128)(2,1)S(1)}, u32[]{:S(2)}, u32[]{:S(2)}) collective-permute-start(bf16[2,1280]{1,0:T(2,128)(2,1)S(1)} %pad_maximum_fusion.3), channel_id=1, source_target_pairs={{0,128},{8,136},{16,144},{24,152},{32,160},{40,168},{48,176},{56,1... | collective-permute-start | bytes 15368 | tf_op jit(solution)/shard_map/ppermute | solution.py:33
  48.6 19.8 %collective-permute-start.8 = (bf16[2,1280]{1,0:T(2,128)(2,1)S(1)}, bf16[2,1280]{1,0:T(2,128)(2,1)S(1)}, u32[]{:S(2)}, u32[]{:S(2)}) collective-permute-start(bf16[2,1280]{1,0:T(2,128)(2,1)S(1)} %pad_maximum_fusion.3), channel_id=1, source_target_pairs={{0,256},{8,264},{16,272},{24,280},{32,288},{40,296},{48,304},{56,3... | collective-permute-start | bytes 15368 | tf_op jit(solution)/shard_map/ppermute | solution.py:33
  54.3 14.2 %collective-permute-start.9 = (bf16[2,1280]{1,0:T(2,128)(2,1)S(1)}, bf16[2,1280]{1,0:T(2,128)(2,1)S(1)}, u32[]{:S(2)}, u32[]{:S(2)}) collective-permute-start(bf16[2,1280]{1,0:T(2,128)(2,1)S(1)} %pad_maximum_fusion.3), channel_id=1, source_target_pairs={{0,384},{8,392},{16,400},{24,408},{32,416},{40,424},{48,432},{56,4... | collective-permute-start | bytes 15368 | tf_op jit(solution)/shard_map/ppermute | solution.py:33
  56.6 20.4 %copy-start.25 = (f32[2]{0:T(128)}, f32[2]{0:T(128)S(1)}, u32[]{:S(2)}) copy-start(f32[2]{0:T(128)S(1)} %add_rsqrt_fusion.1) | copy-start | bytes 28
  56.8 20.2 %copy-start.27 = (f32[2]{0:T(128)}, f32[2]{0:T(128)S(1)}, u32[]{:S(2)}) copy-start(f32[2]{0:T(128)S(1)} %add_sqrt_fusion) | copy-start | bytes 28
  56.8 58.1 %copy-start.2 = (bf16[538,1152]{1,0:T(8,128)(2,1)S(1)}, bf16[538,1152]{1,0:T(8,128)(2,1)}, u32[]{:S(2)}) copy-start(bf16[538,1152]{1,0:T(8,128)(2,1)} %param.15) | copy-start | bytes 3718660
  56.9 17.5 %collective-permute-start.30 = (f32[2,1152]{1,0:T(2,128)S(1)}, f32[2,1152]{1,0:T(2,128)S(1)}, u32[]{:S(2)}, u32[]{:S(2)}) collective-permute-start(f32[2,1152]{1,0:T(2,128)S(1)} %multiply_divide_fusion), channel_id=1, source_target_pairs={{0,128},{8,136},{16,144},{24,152},{32,160},{40,168},{48,176},{56,1... | collective-permute-start | bytes 27656 | tf_op jit(solution)/shard_map/ppermute | solution.py:33
  60.8 16.1 %collective-permute-start.31 = (f32[2,1152]{1,0:T(2,128)S(1)}, f32[2,1152]{1,0:T(2,128)S(1)}, u32[]{:S(2)}, u32[]{:S(2)}) collective-permute-start(f32[2,1152]{1,0:T(2,128)S(1)} %multiply_divide_fusion), channel_id=1, source_target_pairs={{0,256},{8,264},{16,272},{24,280},{32,288},{40,296},{48,304},{56,3... | collective-permute-start | bytes 27656 | tf_op jit(solution)/shard_map/ppermute | solution.py:33
  66.5 10.5 %collective-permute-start.32 = (f32[2,1152]{1,0:T(2,128)S(1)}, f32[2,1152]{1,0:T(2,128)S(1)}, u32[]{:S(2)}, u32[]{:S(2)}) collective-permute-start(f32[2,1152]{1,0:T(2,128)S(1)} %multiply_divide_fusion), channel_id=1, source_target_pairs={{0,384},{8,392},{16,400},{24,408},{32,416},{40,424},{48,432},{56,4... | collective-permute-start | bytes 27656 | tf_op jit(solution)/shard_map/ppermute | solution.py:33
  68.5 41.0 %copy-start.16 = (bf16[2,1280]{1,0:T(2,128)(2,1)}, bf16[2,1280]{1,0:T(2,128)(2,1)S(1)}, u32[]{:S(2)}) copy-start(bf16[2,1280]{1,0:T(2,128)(2,1)S(1)} %collective-permute-done.8) | copy-start | bytes 15364
  68.5 41.0 %copy-start.17 = (bf16[2,1280]{1,0:T(2,128)(2,1)}, bf16[2,1280]{1,0:T(2,128)(2,1)S(1)}, u32[]{:S(2)}) copy-start(bf16[2,1280]{1,0:T(2,128)(2,1)S(1)} %collective-permute-done.9) | copy-start | bytes 15364
  68.5 14.6 %collective-permute-start.10 = (bf16[8,1280]{1,0:T(8,128)(2,1)S(1)}, bf16[8,1280]{1,0:T(8,128)(2,1)S(1)}, u32[]{:S(2)}, u32[]{:S(2)}) collective-permute-start(bf16[8,1280]{1,0:T(8,128)(2,1)S(1)} %pad_maximum_fusion.2), channel_id=1, source_target_pairs={{0,64},{8,72},{16,80},{24,88},{32,96},{40,104},{48,112},{56,120},{... | collective-permute-start | bytes 61448 | tf_op jit(solution)/shard_map/ppermute | solution.py:33
  71.3 14.3 %collective-permute-start.11 = (bf16[8,1280]{1,0:T(8,128)(2,1)S(1)}, bf16[8,1280]{1,0:T(8,128)(2,1)S(1)}, u32[]{:S(2)}, u32[]{:S(2)}) collective-permute-start(bf16[8,1280]{1,0:T(8,128)(2,1)S(1)} %pad_maximum_fusion.2), channel_id=1, source_target_pairs={{0,8},{8,0},{16,24},{24,16},{32,40},{40,32},{48,56},{56,48},{64,72... | collective-permute-start | bytes 61448 | tf_op jit(solution)/shard_map/ppermute | solution.py:33
  74.4 35.1 %copy-start.10 = (f32[2,1152]{1,0:T(2,128)}, f32[2,1152]{1,0:T(2,128)S(1)}, u32[]{:S(2)}) copy-start(f32[2,1152]{1,0:T(2,128)S(1)} %collective-permute-done.30) | copy-start | bytes 27652
  74.5 11.2 %collective-permute-start.12 = (bf16[8,1280]{1,0:T(8,128)(2,1)S(1)}, bf16[8,1280]{1,0:T(8,128)(2,1)S(1)}, u32[]{:S(2)}, u32[]{:S(2)}) collective-permute-start(bf16[8,1280]{1,0:T(8,128)(2,1)S(1)} %pad_maximum_fusion.2), channel_id=1, source_target_pairs={{0,72},{8,64},{16,88},{24,80},{32,104},{40,96},{48,120},{56,112},{... | collective-permute-start | bytes 61448 | tf_op jit(solution)/shard_map/ppermute | solution.py:33
  77.0 32.5 %copy-start.11 = (f32[2,1152]{1,0:T(2,128)}, f32[2,1152]{1,0:T(2,128)S(1)}, u32[]{:S(2)}) copy-start(f32[2,1152]{1,0:T(2,128)S(1)} %collective-permute-done.31) | copy-start | bytes 27652
  77.0 32.5 %copy-start.12 = (f32[2,1152]{1,0:T(2,128)}, f32[2,1152]{1,0:T(2,128)S(1)}, u32[]{:S(2)}) copy-start(f32[2,1152]{1,0:T(2,128)S(1)} %collective-permute-done.32) | copy-start | bytes 27652
  77.0 16.2 %collective-permute-start.33 = (f32[8,1152]{1,0:T(8,128)S(1)}, f32[8,1152]{1,0:T(8,128)S(1)}, u32[]{:S(2)}, u32[]{:S(2)}) collective-permute-start(f32[8,1152]{1,0:T(8,128)S(1)} %pad_maximum_fusion.1), channel_id=1, source_target_pairs={{0,64},{8,72},{16,80},{24,88},{32,96},{40,104},{48,112},{56,120},{... | collective-permute-start | bytes 110600 | tf_op jit(solution)/shard_map/ppermute | solution.py:33
  80.0 17.3 %collective-permute-start.34 = (f32[8,1152]{1,0:T(8,128)S(1)}, f32[8,1152]{1,0:T(8,128)S(1)}, u32[]{:S(2)}, u32[]{:S(2)}) collective-permute-start(f32[8,1152]{1,0:T(8,128)S(1)} %pad_maximum_fusion.1), channel_id=1, source_target_pairs={{0,8},{8,0},{16,24},{24,16},{32,40},{40,32},{48,56},{56,48},{64,72... | collective-permute-start | bytes 110600 | tf_op jit(solution)/shard_map/ppermute | solution.py:33
  83.2 14.2 %collective-permute-start.35 = (f32[8,1152]{1,0:T(8,128)S(1)}, f32[8,1152]{1,0:T(8,128)S(1)}, u32[]{:S(2)}, u32[]{:S(2)}) collective-permute-start(f32[8,1152]{1,0:T(8,128)S(1)} %pad_maximum_fusion.1), channel_id=1, source_target_pairs={{0,72},{8,64},{16,88},{24,80},{32,104},{40,96},{48,120},{56,112},{... | collective-permute-start | bytes 110600 | tf_op jit(solution)/shard_map/ppermute | solution.py:33
  85.7 21.6 %collective-permute-start.13 = (bf16[32,1280]{1,0:T(8,128)(2,1)S(1)}, bf16[32,1280]{1,0:T(8,128)(2,1)S(1)}, u32[]{:S(2)}, u32[]{:S(2)}) collective-permute-start(bf16[32,1280]{1,0:T(8,128)(2,1)S(1)} %concatenate.34), channel_id=1, source_target_pairs={{0,16},{8,24},{16,0},{24,8},{32,48},{40,56},{48,32},{56,40},{64,80... | collective-permute-start | bytes 245768 | tf_op jit(solution)/shard_map/ppermute | solution.py:33
  88.8 20.6 %collective-permute-start.14 = (bf16[32,1280]{1,0:T(8,128)(2,1)S(1)}, bf16[32,1280]{1,0:T(8,128)(2,1)S(1)}, u32[]{:S(2)}, u32[]{:S(2)}) collective-permute-start(bf16[32,1280]{1,0:T(8,128)(2,1)S(1)} %concatenate.34), channel_id=1, source_target_pairs={{0,32},{8,40},{16,48},{24,56},{32,0},{40,8},{48,16},{56,24},{64,96... | collective-permute-start | bytes 245768 | tf_op jit(solution)/shard_map/ppermute | solution.py:33
  93.2 16.3 %copy-start.5 = (f32[8,1152]{1,0:T(8,128)}, f32[8,1152]{1,0:T(8,128)S(1)}, u32[]{:S(2)}) copy-start(f32[8,1152]{1,0:T(8,128)S(1)} %collective-permute-done.33) | copy-start | bytes 110596
  93.2 16.3 %collective-permute-start.15 = (bf16[32,1280]{1,0:T(8,128)(2,1)S(1)}, bf16[32,1280]{1,0:T(8,128)(2,1)}, u32[]{:S(2)}, u32[]{:S(2)}) collective-permute-start(bf16[32,1280]{1,0:T(8,128)(2,1)S(1)} %concatenate.34), channel_id=1, source_target_pairs={{0,48},{8,56},{16,32},{24,40},{32,16},{40,24},{48,0},{56,8},{64,11... | collective-permute-start | bytes 245768 | tf_op jit(solution)/shard_map/ppermute | solution.py:33
  97.3 12.2 %copy-start.7 = (f32[8,1152]{1,0:T(8,128)}, f32[8,1152]{1,0:T(8,128)S(1)}, u32[]{:S(2)}) copy-start(f32[8,1152]{1,0:T(8,128)S(1)} %collective-permute-done.34) | copy-start | bytes 110596
  97.4 12.2 %copy-start.9 = (f32[8,1152]{1,0:T(8,128)}, f32[8,1152]{1,0:T(8,128)S(1)}, u32[]{:S(2)}) copy-start(f32[8,1152]{1,0:T(8,128)S(1)} %collective-permute-done.35) | copy-start | bytes 110596
  99.9 28.6 %collective-permute-start.36 = (f32[32,1152]{1,0:T(8,128)}, f32[32,1152]{1,0:T(8,128)S(1)}, u32[]{:S(2)}, u32[]{:S(2)}) collective-permute-start(f32[32,1152]{1,0:T(8,128)} %concatenate.38), channel_id=1, source_target_pairs={{0,16},{8,24},{16,0},{24,8},{32,48},{40,56},{48,32},{56,40},{64,80... | collective-permute-start | bytes 442376 | tf_op jit(solution)/shard_map/ppermute | solution.py:33
  101.8 26.7 %collective-permute-start.37 = (f32[32,1152]{1,0:T(8,128)}, f32[32,1152]{1,0:T(8,128)S(1)}, u32[]{:S(2)}, u32[]{:S(2)}) collective-permute-start(f32[32,1152]{1,0:T(8,128)} %concatenate.38), channel_id=1, source_target_pairs={{0,32},{8,40},{16,48},{24,56},{32,0},{40,8},{48,16},{56,24},{64,96... | collective-permute-start | bytes 442376 | tf_op jit(solution)/shard_map/ppermute | solution.py:33
  107.4 21.1 %collective-permute-start.38 = (f32[32,1152]{1,0:T(8,128)}, f32[32,1152]{1,0:T(8,128)}, u32[]{:S(2)}, u32[]{:S(2)}) collective-permute-start(f32[32,1152]{1,0:T(8,128)} %concatenate.38), channel_id=1, source_target_pairs={{0,48},{8,56},{16,32},{24,40},{32,16},{40,24},{48,0},{56,8},{64,11... | collective-permute-start | bytes 442376 | tf_op jit(solution)/shard_map/ppermute | solution.py:33
  119.9 8.6 %copy-start.6 = (f32[8,1152]{1,0:T(8,128)S(1)}, f32[8,1152]{1,0:T(8,128)}, u32[]{:S(2)}) copy-start(f32[8,1152]{1,0:T(8,128)} %copy-done.5) | copy-start | bytes 110596
  119.9 8.6 %copy-start.8 = (f32[8,1152]{1,0:T(8,128)S(1)}, f32[8,1152]{1,0:T(8,128)}, u32[]{:S(2)}) copy-start(f32[8,1152]{1,0:T(8,128)} %copy-done.7) | copy-start | bytes 110596
  119.9 13.4 %collective-permute-start.16 = (bf16[256,1152]{1,0:T(8,128)(2,1)}, bf16[256,1152]{1,0:T(8,128)(2,1)S(1)}, u32[]{:S(2)}, u32[]{:S(2)}) collective-permute-start(bf16[256,1152]{1,0:T(8,128)(2,1)} %convolution_convert_fusion), channel_id=1, source_target_pairs={{0,1},{1,0},{2,3},{3,2},{4,5},{5,4},{6,7},{7,6},{8,9},{9,8},{10,11... | collective-permute-start | bytes 1769480 | tf_op jit(solution)/shard_map/ppermute | solution.py:33
  131.0 4.5 %copy-start.13 = (f32[2,1152]{1,0:T(2,128)S(1)}, f32[2,1152]{1,0:T(2,128)}, u32[]{:S(2)}) copy-start(f32[2,1152]{1,0:T(2,128)} %get-tuple-element.8) | copy-start | bytes 27652
  133.4 11.4 %collective-permute-start.17 = (bf16[64,1152]{1,0:T(8,128)(2,1)S(1)}, bf16[64,1152]{1,0:T(8,128)(2,1)S(1)}, u32[]{:S(2)}, u32[]{:S(2)}) collective-permute-start(bf16[64,1152]{1,0:T(8,128)(2,1)S(1)} %add_convert_fusion.1), channel_id=1, source_target_pairs={{0,2},{1,3},{2,0},{3,1},{4,6},{5,7},{6,4},{7,5},{8,10},{9,11},{10,... | collective-permute-start | bytes 442376 | tf_op jit(solution)/shard_map/ppermute | solution.py:33
  144.9 16.0 %copy-start.20 = (f32[1152]{0:T(1024)S(1)}, f32[1152]{0:T(1024)}, u32[]{:S(2)}) copy-start(f32[1152]{0:T(1024)} %param.12) | copy-start | bytes 13828
  144.9 16.0 %copy-start.24 = (f32[64]{0:T(128)S(1)}, f32[64]{0:T(128)}, u32[]{:S(2)}) copy-start(f32[64]{0:T(128)} %add_rsqrt_fusion.2) | copy-start | bytes 772
  144.9 16.2 %copy-start.21 = (f32[1152]{0:T(1024)S(1)}, f32[1152]{0:T(1024)}, u32[]{:S(2)}) copy-start(f32[1152]{0:T(1024)} %fusion.48) | copy-start | bytes 13828
  144.9 8.6 %collective-permute-start.19 = (bf16[64,1152]{1,0:T(8,128)(2,1)S(1)}, bf16[64,1152]{1,0:T(8,128)(2,1)S(1)}, u32[]{:S(2)}, u32[]{:S(2)}) collective-permute-start(bf16[64,1152]{1,0:T(8,128)(2,1)S(1)} %get-tuple-element.16), channel_id=1, source_target_pairs={{0,6},{1,7},{2,4},{3,5},{4,2},{5,3},{6,0},{7,1},{8,14},{9,15},{10,... | collective-permute-start | bytes 442376 | tf_op jit(solution)/shard_map/ppermute | solution.py:33
  147.5 11.6 %collective-permute-start.18 = (bf16[32,1152]{1,0:T(8,128)(2,1)S(1)}, bf16[32,1152]{1,0:T(8,128)(2,1)S(1)}, u32[]{:S(2)}, u32[]{:S(2)}) collective-permute-start(bf16[32,1152]{1,0:T(8,128)(2,1)S(1)} %dynamic-slice_convert_fusion.1), channel_id=1, source_target_pairs={{0,6},{1,7},{2,4},{3,5},{4,2},{5,3},{6,0},{7,1},{8,14},{9,15},{10,... | collective-permute-start | bytes 221192 | tf_op jit(solution)/shard_map/ppermute | solution.py:33
  153.6 7.3 %collective-permute-start.20 = (bf16[32,1152]{1,0:T(8,128)(2,1)S(1)}, bf16[32,1152]{1,0:T(8,128)(2,1)S(1)}, u32[]{:S(2)}, u32[]{:S(2)}) collective-permute-start(bf16[32,1152]{1,0:T(8,128)(2,1)S(1)} %dynamic-slice_convert_fusion), channel_id=1, source_target_pairs={{0,2},{1,3},{2,0},{3,1},{4,6},{5,7},{6,4},{7,5},{8,10},{9,11},{10,... | collective-permute-start | bytes 221192 | tf_op jit(solution)/shard_map/ppermute | solution.py:33
  161.4 13.4 %collective-permute-start.21 = (bf16[64,1152]{1,0:T(8,128)(2,1)S(1)}, bf16[64,1152]{1,0:T(8,128)(2,1)S(1)}, u32[]{:S(2)}, u32[]{:S(2)}) collective-permute-start(bf16[64,1152]{1,0:T(8,128)(2,1)S(1)} %fusion.35), channel_id=1, source_target_pairs={{0,2},{1,3},{2,0},{3,1},{4,6},{5,7},{6,4},{7,5},{8,10},{9,11},{10,... | collective-permute-start | bytes 442376 | tf_op jit(solution)/shard_map/ppermute | solution.py:33
  166.1 8.7 %collective-permute-start.22 = (bf16[64,1152]{1,0:T(8,128)(2,1)S(1)}, bf16[64,1152]{1,0:T(8,128)(2,1)S(1)}, u32[]{:S(2)}, u32[]{:S(2)}) collective-permute-start(bf16[64,1152]{1,0:T(8,128)(2,1)S(1)} %fusion.35), channel_id=1, source_target_pairs={{0,6},{1,7},{2,4},{3,5},{4,2},{5,3},{6,0},{7,1},{8,14},{9,15},{10,... | collective-permute-start | bytes 442376 | tf_op jit(solution)/shard_map/ppermute | solution.py:33
  169.8 25.6 %collective-permute-start.25 = (bf16[64,1152]{1,0:T(8,128)(2,1)S(1)}, bf16[64,1152]{1,0:T(8,128)(2,1)S(1)}, u32[]{:S(2)}, u32[]{:S(2)}) collective-permute-start(bf16[64,1152]{1,0:T(8,128)(2,1)S(1)} %fusion.35), channel_id=1, source_target_pairs={{0,1},{1,0},{2,3},{3,2},{4,5},{5,4},{6,7},{7,6},{8,9},{9,8},{10,11... | collective-permute-start | bytes 442376 | tf_op jit(solution)/shard_map/ppermute | solution.py:33
  174.9 16.0 %collective-permute-start.23 = (bf16[32,1152]{1,0:T(8,128)(2,1)S(1)}, bf16[32,1152]{1,0:T(8,128)(2,1)S(1)}, u32[]{:S(2)}, u32[]{:S(2)}) collective-permute-start(bf16[32,1152]{1,0:T(8,128)(2,1)S(1)} %get-tuple-element.19), channel_id=1, source_target_pairs={{0,2},{1,3},{2,0},{3,1},{4,6},{5,7},{6,4},{7,5},{8,10},{9,11},{10,... | collective-permute-start | bytes 221192 | tf_op jit(solution)/shard_map/ppermute | solution.py:33
  179.0 14.3 %collective-permute-start.24 = (bf16[32,1152]{1,0:T(8,128)(2,1)S(1)}, bf16[32,1152]{1,0:T(8,128)(2,1)S(1)}, u32[]{:S(2)}, u32[]{:S(2)}) collective-permute-start(bf16[32,1152]{1,0:T(8,128)(2,1)S(1)} %get-tuple-element.17), channel_id=1, source_target_pairs={{0,6},{1,7},{2,4},{3,5},{4,2},{5,3},{6,0},{7,1},{8,14},{9,15},{10,... | collective-permute-start | bytes 221192 | tf_op jit(solution)/shard_map/ppermute | solution.py:33
  185.2 10.2 %collective-permute-start.26 = (bf16[64,1152]{1,0:T(8,128)(2,1)S(1)}, bf16[64,1152]{1,0:T(8,128)(2,1)S(1)}, u32[]{:S(2)}, u32[]{:S(2)}) collective-permute-start(bf16[64,1152]{1,0:T(8,128)(2,1)S(1)} %collective-permute-done.21), channel_id=1, source_target_pairs={{0,1},{1,0},{2,3},{3,2},{4,5},{5,4},{6,7},{7,6},{8,9},{9,8},{10,11... | collective-permute-start | bytes 442376 | tf_op jit(solution)/shard_map/ppermute | solution.py:33
  188.9 6.6 %collective-permute-start.27 = (bf16[64,1152]{1,0:T(8,128)(2,1)S(1)}, bf16[64,1152]{1,0:T(8,128)(2,1)S(1)}, u32[]{:S(2)}, u32[]{:S(2)}) collective-permute-start(bf16[64,1152]{1,0:T(8,128)(2,1)S(1)} %collective-permute-done.22), channel_id=1, source_target_pairs={{0,1},{1,0},{2,3},{3,2},{4,5},{5,4},{6,7},{7,6},{8,9},{9,8},{10,11... | collective-permute-start | bytes 442376 | tf_op jit(solution)/shard_map/ppermute | solution.py:33
  190.8 4.7 %collective-permute-start.28 = (bf16[32,1152]{1,0:T(8,128)(2,1)S(1)}, bf16[32,1152]{1,0:T(8,128)(2,1)S(1)}, u32[]{:S(2)}, u32[]{:S(2)}) collective-permute-start(bf16[32,1152]{1,0:T(8,128)(2,1)S(1)} %collective-permute-done.23), channel_id=1, source_target_pairs={{0,1},{1,0},{2,3},{3,2},{4,5},{5,4},{6,7},{7,6},{8,9},{9,8},{10,11... | collective-permute-start | bytes 221192 | tf_op jit(solution)/shard_map/ppermute | solution.py:33
  193.3 3.2 %collective-permute-start.29 = (bf16[32,1152]{1,0:T(8,128)(2,1)S(1)}, bf16[32,1152]{1,0:T(8,128)(2,1)S(1)}, u32[]{:S(2)}, u32[]{:S(2)}) collective-permute-start(bf16[32,1152]{1,0:T(8,128)(2,1)S(1)} %collective-permute-done.24), channel_id=1, source_target_pairs={{0,1},{1,0},{2,3},{3,2},{4,5},{5,4},{6,7},{7,6},{8,9},{9,8},{10,11... | collective-permute-start | bytes 221192 | tf_op jit(solution)/shard_map/ppermute | solution.py:33
  (6 other events, 8.9 us)

commit v2 on v1

--- a/solution.py
+++ b/solution.py
@@ -37,19 +37,24 @@
     return swap(value, axis, lambda i: i ^ mask)
 
 
+def spread(value, axis, groups=None):
+    size = lax.axis_size(axis) if groups is None else len(groups[0])
+    copies = jnp.broadcast_to(value[None], (size,) + value.shape)
+    return lax.all_to_all(
+        copies, axis, split_axis=0, concat_axis=0, axis_index_groups=groups
+    )
+
+
 def gather_dp(rows):
-    for masks in ((16, 32, 48), (8, 1, 9), (2, 4, 6)):
-        parts = [rows] + [swap_xor(rows, "dp", mask) for mask in masks]
-        rows = jnp.concatenate(parts, axis=0)
-    return rows
-
-
-def z_next(i):
-    return i ^ 2
-
-
-def z_prev(i):
-    return (3 - i // 2) * 2 + i % 2
+    return spread(rows, "dp").reshape(-1, rows.shape[1])
+
+
+def step_one(i):
+    return i ^ 2 if i % 2 == 0 else (3 - i // 2) * 2 + 1
+
+
+def step_two(i):
+    return (3 - i // 2) * 2 if i % 2 == 0 else i ^ 2
 
 
 def rows_at(array, start, count):
@@ -93,10 +98,7 @@
     activation = gelu_tanh(pre_act).astype(jnp.bfloat16).astype(jnp.float32)
     act_mean = activation.reshape(img_dev, PATCHES, -1).mean(axis=1)
     part = jnp.dot(act_mean, w_down.astype(jnp.float32), precision=HIGH)
-    got = [part] + [swap_xor(part, "tensor", mask) for mask in range(1, 8)]
-    mlp_mean = ((got[0] + got[1]) + (got[2] + got[3])) + (
-        (got[4] + got[5]) + (got[6] + got[7])
-    )
+    mlp_mean = jnp.sum(spread(part, "tensor"), axis=0)
     pooled = inputs.reshape(img_dev, PATCHES, width).mean(axis=1) + mlp_mean + b_down
 
     feat_n, feat_s = norm_parts(pooled)
@@ -139,62 +141,36 @@
     def wide(array, start, count):
         return rows_at(array, start, count).astype(jnp.float32)
 
-    def first(start):
+    one = jnp.where(core == 0, u, v)
+    two = jnp.where(core == 0, v, u)
+
+    def second(start):
+        return first_rows(start) + wide(got_one, start - 128 * one, 64)
+
+    def first_rows(start):
         return wide(keep, start, 64) + wide(other, start, 64)
 
-    send_a = first(64 * (1 - u)).astype(jnp.bfloat16)
-    send_b = first(128 + 64 * (1 - v)).astype(jnp.bfloat16)
-    got_a = swap(send_a, "tensor", z_next)
-    got_b = swap(send_b, "tensor", z_prev)
-    sum_a = first(64 * u) + got_a.astype(jnp.float32)
-    sum_b = first(128 + 64 * v) + got_b.astype(jnp.float32)
-    send_a = rows_at(sum_a, 32 * (1 - v), 32).astype(jnp.bfloat16)
-    send_b = rows_at(sum_b, 32 * (1 - u), 32).astype(jnp.bfloat16)
-    got_a = swap(send_a, "tensor", z_prev)
-    got_b = swap(send_b, "tensor", z_next)
-    sum_a = rows_at(sum_a, 32 * v, 32) + got_a.astype(jnp.float32)
-    sum_b = rows_at(sum_b, 32 * u, 32) + got_b.astype(jnp.float32)
-
-    def start_a(uu, vv):
-        return 64 * uu + 32 * vv
-
-    def start_b(uu, vv):
-        return 128 + 64 * vv + 32 * uu
-
-    own_x = jnp.concatenate(
-        [
-            rows_at(patches, core * PATCHES + start_a(u, v), 32),
-            rows_at(patches, core * PATCHES + start_b(u, v), 32),
-        ]
-    ).astype(jnp.float32)
+    send_one = wide(keep, 128 * (1 - one), 128) + wide(other, 128 * (1 - one), 128)
+    got_one = swap(send_one.astype(jnp.bfloat16), "tensor", step_one)
+    send_two = second(128 * one + 64 * (1 - two)).astype(jnp.bfloat16)
+    got_two = swap(send_two, "tensor", step_two)
+    block = 128 * one + 64 * two
+    g_normed = second(block) + got_two.astype(jnp.float32)
+
+    own_x = rows_at(patches, core * PATCHES + block, 64).astype(jnp.float32)
     own_n, own_s = norm_parts(own_x)
     g_own = rows_at(g_hidden, core, 1)
-    done = norm_back(jnp.concatenate([sum_a, sum_b]), ln_gain, own_n, own_s) + g_own
-    done = done.astype(jnp.bfloat16)
-
-    from_next = swap(done, "tensor", z_next)
-    from_prev = swap(done, "tensor", z_prev)
-    far_a = swap(from_prev[:32], "tensor", z_next)
-    far_b = swap(from_next[32:], "tensor", z_prev)
-    mine = [done, from_next, from_prev, far_a, far_b]
-    theirs = [swap_xor(piece, "tensor", 1) for piece in mine]
-    grad_patches = jnp.zeros(patches.shape, jnp.bfloat16)
-    for side, pieces in ((core, mine), (1 - core, theirs)):
-        base = side * PATCHES
-        blocks = [
-            (pieces[0][:32], start_a(u, v)),
-            (pieces[0][32:], start_b(u, v)),
-            (pieces[1][:32], start_a(1 - u, v)),
-            (pieces[1][32:], start_b(1 - u, v)),
-            (pieces[2][:32], start_a(u, 1 - v)),
-            (pieces[2][32:], start_b(u, 1 - v)),
-            (pieces[3], start_a(1 - u, 1 - v)),
-            (pieces[4], start_b(1 - u, 1 - v)),
-        ]
-        for block, start in blocks:
-            grad_patches = lax.dynamic_update_slice_in_dim(
-                grad_patches, block, base + start, 0
-            )
+    done = (norm_back(g_normed, ln_gain, own_n, own_s) + g_own).astype(jnp.bfloat16)
+
+    rings = [[0, 2, 4, 6], [1, 3, 5, 7]]
+    ours = spread(done, "tensor", rings)
+    even = jnp.concatenate([ours[0], ours[3], ours[1], ours[2]])
+    odd = jnp.concatenate([ours[0], ours[1], ours[3], ours[2]])
+    ours = jnp.where(core == 0, even, odd)
+    theirs = swap_xor(ours, "tensor", 1)
+    grad_patches = jnp.where(
+        core == 0, jnp.concatenate([ours, theirs]), jnp.concatenate([theirs, ours])
+    )
 
     img_all = gather_dp(img_emb)
     lg_text = logit_grad(text_own.astype(jnp.float32), img_all)

time: 199 us -> 128 us (0.64)
  starting transfers between devices: 147 us -> 47.6 us
  waiting for transfers between devices: 11.7 us -> 44.1 us
  local copies, waits for them, and re-layouts: 13.8 us -> 9.94 us
    ppermute x39 -> x4, starting transfers between devices: 147 us -> 13.6 us  [swap(): return lax.ppermute(value, axis, [(i, partner(i)) for i in range(size)])]
    all_to_all x0 -> x4, starting transfers between devices: none -> 34.1 us  [spread(): lax.all_to_all(copies, axis, split_axis=0, concat_axis=0, axis_index_grou...]
    all_to_all x0 -> x4, waiting for transfers between devices: none -> 33.2 us  [spread(): lax.all_to_all(copies, axis, split_axis=0, concat_axis=0, axis_index_grou...]
    concatenate x4 -> x0, local copies, waits for them, and re-layouts: 6.7 us -> none  [gather_dp(): rows = jnp.concatenate(parts, axis=0)]
    broadcast_in_dim x1 -> x4, local copies, waits for them, and re-layouts: 0.09 us -> 3.37 us  [spread(): copies = jnp.broadcast_to(value[None], (size,) + value.shape)]
    convert_element_type x2 -> x3, other arithmetic: 0.21 us -> 2.77 us  [the longest x1 1.71 us: on_device(): send_two = second(128 * one + 64 * (1 - two)).astype(jnp.bfloat16)]
    ppermute x39 -> x4, waiting for transfers between devices: 11.7 us -> 10.8 us  [swap(): return lax.ppermute(value, axis, [(i, partner(i)) for i in range(size)])]
  transfers between devices with their start and end apart: 39 -> 8, of which waited for: 4 -> 7; matrix products, arithmetic and copies ran while one was open for 11% -> 7% of each run, Pallas kernels for 0% -> 0%
where the time goes in v2:
time: 128 us
  starting transfers between devices  47.6 us (37%)
  waiting for transfers between devices  44.1 us (34%)
  other arithmetic  12.3 us (10%)
  matrix products  11.3 us (9%)
  local copies, waits for them, and re-layouts  9.94 us (8%)
  between operations  2.41 us (2%)
    all_to_all x4, starting transfers between devices, spread(): lax.all_to_all(copies, axis, split_axis=0, concat_axis=0, axis_index_grou...  34.1 us
    all_to_all x4, waiting for transfers between devices, spread(): lax.all_to_all(copies, axis, split_axis=0, concat_axis=0, axis_index_grou...  33.2 us
    ppermute x4, starting transfers between devices, swap(): return lax.ppermute(value, axis, [(i, partner(i)) for i in range(size)])  13.6 us
    ppermute x4, waiting for transfers between devices, swap(): return lax.ppermute(value, axis, [(i, partner(i)) for i in range(size)])  10.8 us
    unnamed x27, local copies, waits for them, and re-layouts  3.9 us
    broadcast_in_dim x4, local copies, waits for them, and re-layouts, spread(): copies = jnp.broadcast_to(value[None], (size,) + value.shape)  3.37 us
    dot_general x2, matrix products, up_back(): lax.dot_general(rows, w_up, (((1,), (1,)), ((), ())), preferred_element_t...  3.17 us
    dot_general x1, matrix products, on_device(): pre_act = jnp.dot(normed, w_up, preferred_element_type=jnp.float32) + b_up  2.67 us
  transfers between devices with their start and end apart: 8, of which 7 were waited for; matrix products, arithmetic and copies ran while one was open for 7% of the time, Pallas kernels for 0%

profile of v2, /device:TPU:1, one launch (start us, length us, event | category | flops | bytes accessed | tf_op | source)
XLA Modules:
  0.0 127.7 jit_solution(2076653676792531771)
XLA Ops:
  0.6 0.0 copy-start
  0.7 1.6 %convert_reduce_fusion = f32[512]{0:T(512)S(1)} fusion(bf16[512,1152]{1,0:T(8,128)(2,1)} %param.11), kind=kLoop, calls=%fused_computation.5 | loop fusion | flops 1179136 | bytes 1181696 | tf_op jit(solution)/shard_map/reduce_sum | solution.py:13
  2.3 0.0 copy-done.1
  2.4 0.4 multiply_reduce_fusion
  2.9 2.7 %fusion.29 = (f32[512,538]{0,1:T(8,128)}, f32[512,538]{0,1:T(8,128)}) fusion(f32[538]{0:T(1024)S(1)} %copy-done.11, bf16[1152,538]{0,1:T(8,128)(2,1)S(1)} %copy-done, bf16[512,1152]{1,0:T(8,128)(2,1)S(1)} %copy-done.1, f32[1152]{0:T(1024)S(1)} %copy-done.8, f32[512]{0:T(512)S(1)} %add_rsqrt_fusion, f32[512]{0:T(512)S(1)} %broadcast_multiply_fusion), kind=kOutput, calls=%fused_computation.49 | convolution fusion | flops 640629760 | bytes 4633704 | tf_op jit(solution)/shard_map/dot_general | solution.py:97
  5.5 2.0 %reshape.185 = f32[2,256,538]{1,0,2:T(2,128)S(1)} reshape(f32[512,538]{0,1:T(8,128)} %get-tuple-element.18) | data formatting | bytes 2203648 | tf_op jit(solution)/shard_map/reshape | solution.py:99
  7.5 1.4 %reduce_sum.158 = f32[2,538]{0,1:T(8,128)} reduce(f32[2,256,538]{1,0,2:T(2,128)S(1)} %reshape.185, f32[]{:T(128)} %constant.74.clone.1), dimensions={1}, to_apply=%region_5.6 | reduce | flops 274380 | bytes 1106132 | tf_op jit(solution)/shard_map/reduce_sum | solution.py:99
  8.9 2.1 %fusion.42 = f32[2,1152]{1,0:T(2,128)S(1)} fusion(bf16[538,1152]{1,0:T(8,128)(2,1)} %param.15, f32[2,538]{0,1:T(8,128)} %reduce_sum.158), kind=kOutput, calls=%fused_computation.67 | convolution fusion | flops 14875700 | bytes 1253072 | tf_op jit(solution)/shard_map/dot_general | solution.py:100
  10.9 0.7 broadcast_in_dim.20
  11.6 11.8 %all-to-all-start = ((f32[8,2,1152]{2,1,0:T(2,128)}), f32[8,2,1152]{2,1,0:T(2,128)S(1)}, u32[]{:S(2)}, u32[]{:S(2)}) async-start(f32[8,2,1152]{2,1,0:T(2,128)} %broadcast_in_dim.20), calls=%async_computation | async-start | bytes 147456 | tf_op jit(solution)/shard_map/all_to_all | solution.py:43
  23.4 0.1 fusion.47
  23.5 0.1 fusion.58
  23.6 0.0 copy-done.10
  23.6 0.1 copy.25
  25.1 0.2 bitcast_reduce_fusion
  25.3 5.8 %all-to-all-done = f32[8,2,1152]{2,1,0:T(2,128)S(1)} async-done(((f32[8,2,1152]{2,1,0:T(2,128)}), f32[8,2,1152]{2,1,0:T(2,128)S(1)}, u32[]{:S(2)}, u32[]{:S(2)}) %all-to-all-start) | async-done | bytes 73760 | tf_op jit(solution)/shard_map/all_to_all | solution.py:43
  31.1 0.9 broadcast_in_dim.22
  32.0 10.8 %all-to-all-start.1 = ((bf16[64,2,1280]{2,1,0:T(2,128)(2,1)}), bf16[64,2,1280]{2,1,0:T(2,128)(2,1)S(1)}, u32[]{:S(2)}, u32[]{:S(2)}) async-start(bf16[64,2,1280]{2,1,0:T(2,128)(2,1)} %broadcast_in_dim.22), calls=%async_computation.1 | async-start | bytes 655360 | tf_op jit(solution)/shard_map/all_to_all | solution.py:43
  42.9 0.1 fusion.59
  43.0 0.2 multiply_reduce_fusion.5
  43.2 0.2 multiply_reduce_fusion.4
  43.4 0.1 multiply_divide_fusion
  43.5 10.6 %all-to-all-done.1 = bf16[64,2,1280]{2,1,0:T(2,128)(2,1)S(1)} async-done(((bf16[64,2,1280]{2,1,0:T(2,128)(2,1)}), bf16[64,2,1280]{2,1,0:T(2,128)(2,1)S(1)}, u32[]{:S(2)}, u32[]{:S(2)}) %all-to-all-start.1) | async-done | bytes 327712 | tf_op jit(solution)/shard_map/all_to_all | solution.py:43
  54.0 0.1 reshape.181
  54.2 0.1 convert_reduce_fusion.2
  54.3 0.4 fusion.17
  54.7 0.4 multiply_reduce_fusion.3
  55.1 0.2 fusion.57
  55.3 0.1 multiply_multiply_fusion.2
  55.4 1.8 %fusion.49 = f32[2,538]{0,1:T(8,128)S(1)} fusion(bf16[538,1152]{1,0:T(8,128)(2,1)} %param.15, f32[2,1152]{1,0:T(2,128)S(1)} %multiply_multiply_fusion.2), kind=kOutput, calls=%fused_computation.94 | convolution fusion | flops 2481408 | bytes 1253072 | tf_op jit(solution)/shard_map/dot_general | solution.py:122
  57.1 0.6 broadcast_bitcast_fusion
  57.8 0.4 pad.20
  58.2 0.1 copy.29
  58.3 1.2 copy-done.2
  59.4 0.8 fusion.9
  60.2 0.8 copy-done.5
  61.0 1.5 %convolution_convert_fusion = bf16[256,1152]{1,0:T(8,128)(2,1)} fusion(bf16[1152,538]{0,1:T(8,128)(2,1)S(1)} %copy-done, bf16[512,538]{0,1:T(8,128)(2,1)S(1)} %fusion.9, s32[]{:T(128)S(6)} %select_n.78), kind=kOutput, calls=%fused_computation | convolution fusion | flops 317620224 | bytes 2121732 | tf_op jit(solution)/shard_map/dot_general | solution.py:133
  62.5 5.7 %collective-permute-start = (bf16[256,1152]{1,0:T(8,128)(2,1)}, bf16[256,1152]{1,0:T(8,128)(2,1)S(1)}, u32[]{:S(2)}, u32[]{:S(2)}) collective-permute-start(bf16[256,1152]{1,0:T(8,128)(2,1)} %convolution_convert_fusion), channel_id=1, source_target_pairs={{0,1},{1,0},{2,3},{3,2},{4,5},{5,4},{6,7},{7,6},{8,9},{9,8},{10,11... | collective-permute-start | bytes 1769480 | tf_op jit(solution)/shard_map/ppermute | solution.py:33
  68.3 0.1 convert_reduce_fusion.1
  68.4 1.6 %convolution_convert_fusion.1 = bf16[256,1152]{1,0:T(8,128)(2,1)S(1)} fusion(bf16[1152,538]{0,1:T(8,128)(2,1)S(1)} %copy-done, bf16[512,538]{0,1:T(8,128)(2,1)} %copy-done.5, s32[]{:T(128)S(6)} %select_n.76), kind=kOutput, calls=%fused_computation.1 | convolution fusion | flops 317620224 | bytes 2107908 | tf_op jit(solution)/shard_map/dot_general | solution.py:133
  70.1 0.8 copy-done.4
  70.9 0.9 add_convert_fusion
  71.8 2.4 %collective-permute-start.1 = (bf16[128,1152]{1,0:T(8,128)(2,1)}, bf16[128,1152]{1,0:T(8,128)(2,1)S(1)}, u32[]{:S(2)}, u32[]{:S(2)}) collective-permute-start(bf16[128,1152]{1,0:T(8,128)(2,1)} %add_convert_fusion), channel_id=1, source_target_pairs={{0,2},{1,7},{2,0},{3,5},{4,6},{5,3},{6,4},{7,1},{8,10},{9,15},{10,... | collective-permute-start | bytes 884744 | tf_op jit(solution)/shard_map/ppermute | solution.py:33
  74.2 0.2 fusion.39
  74.4 1.0 broadcast_in_dim.29
  75.4 4.9 %all-to-all-start.3 = ((f32[64,2,1152]{2,1,0:T(2,128)}), f32[64,2,1152]{2,1,0:T(2,128)S(1)}, u32[]{:S(2)}, u32[]{:S(2)}) async-start(f32[64,2,1152]{2,1,0:T(2,128)} %broadcast_in_dim.29), calls=%async_computation.3 | async-start | bytes 1179648 | tf_op jit(solution)/shard_map/all_to_all | solution.py:43
  80.3 4.6 %collective-permute-done.1 = bf16[128,1152]{1,0:T(8,128)(2,1)S(1)} collective-permute-done((bf16[128,1152]{1,0:T(8,128)(2,1)}, bf16[128,1152]{1,0:T(8,128)(2,1)S(1)}, u32[]{:S(2)}, u32[]{:S(2)}) %collective-permute-start.1) | collective-permute-done | bytes 294944 | tf_op jit(solution)/shard_map/ppermute | solution.py:33
  84.9 1.7 %add_convert_fusion.1 = bf16[64,1152]{1,0:T(8,128)(2,1)} fusion(bf16[128,1152]{1,0:T(8,128)(2,1)S(1)} %collective-permute-done.1, s32[]{:T(128)S(6)} %select_n.82, bf16[256,1152]{1,0:T(8,128)(2,1)} %copy-done.3, s32[]{:T(128)S(6)} %select_n.81, bf16[256,1152]{1,0:T(8,128)(2,1)} %copy-done.4), kind=kLoop, calls=%fused_computation.64 | loop fusion | flops 442368 | bytes 589832 | tf_op jit(solution)/shard_map/convert_element_type | solution.py:155
  86.6 1.9 %collective-permute-start.2 = (bf16[64,1152]{1,0:T(8,128)(2,1)}, bf16[64,1152]{1,0:T(8,128)(2,1)S(1)}, u32[]{:S(2)}, u32[]{:S(2)}) collective-permute-start(bf16[64,1152]{1,0:T(8,128)(2,1)} %add_convert_fusion.1), channel_id=1, source_target_pairs={{0,6},{1,3},{2,4},{3,1},{4,2},{5,7},{6,0},{7,5},{8,14},{9,11},{10,... | collective-permute-start | bytes 442376 | tf_op jit(solution)/shard_map/ppermute | solution.py:33
  88.6 5.8 %collective-permute-done.2 = bf16[64,1152]{1,0:T(8,128)(2,1)S(1)} collective-permute-done((bf16[64,1152]{1,0:T(8,128)(2,1)}, bf16[64,1152]{1,0:T(8,128)(2,1)S(1)}, u32[]{:S(2)}, u32[]{:S(2)}) %collective-permute-start.2) | collective-permute-done | bytes 147488 | tf_op jit(solution)/shard_map/ppermute | solution.py:33
  94.4 1.3 fusion.56
  95.7 0.2 fusion.38
  95.9 1.9 %all-to-all-done.3 = f32[64,2,1152]{2,1,0:T(2,128)S(1)} async-done(((f32[64,2,1152]{2,1,0:T(2,128)}), f32[64,2,1152]{2,1,0:T(2,128)S(1)}, u32[]{:S(2)}, u32[]{:S(2)}) %all-to-all-start.3) | async-done | bytes 589856 | tf_op jit(solution)/shard_map/all_to_all | solution.py:43
  97.7 0.9 broadcast_in_dim.28
  98.6 6.6 %all-to-all-start.2 = ((bf16[4,64,1152]{2,1,0:T(8,128)(2,1)}), bf16[4,64,1152]{2,1,0:T(8,128)(2,1)S(1)}, u32[]{:S(2)}, u32[]{:S(2)}) async-start(bf16[4,64,1152]{2,1,0:T(8,128)(2,1)} %broadcast_in_dim.28), calls=%async_computation.2 | async-start | bytes 1179648 | tf_op jit(solution)/shard_map/all_to_all | solution.py:43
  105.1 0.4 reshape.183
  105.5 0.4 fusion.25
  105.9 15.0 %all-to-all-done.2 = bf16[4,64,1152]{2,1,0:T(8,128)(2,1)S(1)} async-done(((bf16[4,64,1152]{2,1,0:T(8,128)(2,1)}), bf16[4,64,1152]{2,1,0:T(8,128)(2,1)S(1)}, u32[]{:S(2)}, u32[]{:S(2)}) %all-to-all-start.2) | async-done | bytes 589856 | tf_op jit(solution)/shard_map/all_to_all | solution.py:43
  121.0 0.1 fusion.28
  121.1 3.5 %collective-permute-start.3 = (bf16[256,1152]{1,0:T(8,128)(2,1)S(1)}, bf16[256,1152]{1,0:T(8,128)(2,1)S(1)}, u32[]{:S(2)}, u32[]{:S(2)}) collective-permute-start(bf16[256,1152]{1,0:T(8,128)(2,1)S(1)} %fusion.28), channel_id=1, source_target_pairs={{0,1},{1,0},{2,3},{3,2},{4,5},{5,4},{6,7},{7,6},{8,9},{9,8},{10,11... | collective-permute-start | bytes 1769480 | tf_op jit(solution)/shard_map/ppermute | solution.py:33
  124.6 0.5 multiply_reduce_fusion.1
  125.1 0.7 subtract_divide_fusion
  125.8 0.4 collective-permute-done.3
  126.2 1.5 %maximum_select_fusion = bf16[512,1152]{1,0:T(8,128)(2,1)} fusion(bf16[256,1152]{1,0:T(8,128)(2,1)S(1)} %collective-permute-done.3, bf16[256,1152]{1,0:T(8,128)(2,1)S(1)} %fusion.28, pred[]{:T(512)S(6)} %eq.14), kind=kLoop, calls=%fused_computation.11 | loop fusion | flops 5308416 | bytes 2359297 | tf_op jit(solution)/shard_map/jit(_where)/select_n | solution.py:171
  (35 shorter events, 0.2 us)
Async XLA Ops:
  0.6 2.2 %copy-start = (bf16[1152,538]{0,1:T(8,128)(2,1)S(1)}, bf16[1152,538]{0,1:T(8,128)(2,1)}, u32[]{:S(2)}) copy-start(bf16[1152,538]{0,1:T(8,128)(2,1)} %param.13) | copy-start | bytes 3718660
  0.6 1.7 %copy-start.1 = (bf16[512,1152]{1,0:T(8,128)(2,1)S(1)}, bf16[512,1152]{1,0:T(8,128)(2,1)}, u32[]{:S(2)}) copy-start(bf16[512,1152]{1,0:T(8,128)(2,1)} %param.11) | copy-start | bytes 3538948
  0.7 2.2 %copy-start.8 = (f32[1152]{0:T(1024)S(1)}, f32[1152]{0:T(1024)}, u32[]{:S(2)}) copy-start(f32[1152]{0:T(1024)} %param.12) | copy-start | bytes 13828
  0.7 2.2 %copy-start.11 = (f32[538]{0:T(1024)S(1)}, f32[538]{0:T(1024)}, u32[]{:S(2)}) copy-start(f32[538]{0:T(1024)} %param.14) | copy-start | bytes 6460
  8.8 14.5 %copy-start.7 = (bf16[2,1152]{1,0:T(2,128)(2,1)S(1)}, bf16[2,1152]{1,0:T(2,128)(2,1)}, u32[]{:S(2)}) copy-start(bf16[2,1152]{1,0:T(2,128)(2,1)} %param.18) | copy-start | bytes 13828
  8.8 14.7 %copy-start.10 = (s32[2]{0:T(128)S(1)}, s32[2]{0:T(128)}, u32[]{:S(2)}) copy-start(s32[2]{0:T(128)} %param.19) | copy-start | bytes 28
  11.6 19.5 %all-to-all-start = ((f32[8,2,1152]{2,1,0:T(2,128)}), f32[8,2,1152]{2,1,0:T(2,128)S(1)}, u32[]{:S(2)}, u32[]{:S(2)}) async-start(f32[8,2,1152]{2,1,0:T(2,128)} %broadcast_in_dim.20), calls=%async_computation | async-start | bytes 147456 | tf_op jit(solution)/shard_map/all_to_all | solution.py:43
  23.4 19.5 %copy-start.9 = (f32[1152]{0:T(1024)S(1)}, f32[1152]{0:T(1024)}, u32[]{:S(2)}) copy-start(f32[1152]{0:T(1024)} %param.16) | copy-start | bytes 13828
  23.6 19.6 %copy-start.6 = (f32[1152]{0:T(1024)S(1)}, f32[1152]{0:T(1024)}, u32[]{:S(2)}) copy-start(f32[1152]{0:T(1024)} %param.17) | copy-start | bytes 13828
  32.0 22.1 %all-to-all-start.1 = ((bf16[64,2,1280]{2,1,0:T(2,128)(2,1)}), bf16[64,2,1280]{2,1,0:T(2,128)(2,1)S(1)}, u32[]{:S(2)}, u32[]{:S(2)}) async-start(bf16[64,2,1280]{2,1,0:T(2,128)(2,1)} %broadcast_in_dim.22), calls=%async_computation.1 | async-start | bytes 655360 | tf_op jit(solution)/shard_map/all_to_all | solution.py:43
  58.2 1.2 copy-start.2
  60.2 0.8 copy-start.5
  62.5 7.6 %collective-permute-start = (bf16[256,1152]{1,0:T(8,128)(2,1)}, bf16[256,1152]{1,0:T(8,128)(2,1)S(1)}, u32[]{:S(2)}, u32[]{:S(2)}) collective-permute-start(bf16[256,1152]{1,0:T(8,128)(2,1)} %convolution_convert_fusion), channel_id=1, source_target_pairs={{0,1},{1,0},{2,3},{3,2},{4,5},{5,4},{6,7},{7,6},{8,9},{9,8},{10,11... | collective-permute-start | bytes 1769480 | tf_op jit(solution)/shard_map/ppermute | solution.py:33
  70.1 0.8 copy-start.4
  70.9 4.5 %copy-start.3 = (bf16[256,1152]{1,0:T(8,128)(2,1)}, bf16[256,1152]{1,0:T(8,128)(2,1)S(1)}, u32[]{:S(2)}) copy-start(bf16[256,1152]{1,0:T(8,128)(2,1)S(1)} %collective-permute-done) | copy-start | bytes 1769476
  71.8 13.1 %collective-permute-start.1 = (bf16[128,1152]{1,0:T(8,128)(2,1)}, bf16[128,1152]{1,0:T(8,128)(2,1)S(1)}, u32[]{:S(2)}, u32[]{:S(2)}) collective-permute-start(bf16[128,1152]{1,0:T(8,128)(2,1)} %add_convert_fusion), channel_id=1, source_target_pairs={{0,2},{1,7},{2,0},{3,5},{4,6},{5,3},{6,4},{7,1},{8,10},{9,15},{10,... | collective-permute-start | bytes 884744 | tf_op jit(solution)/shard_map/ppermute | solution.py:33
  75.4 22.3 %all-to-all-start.3 = ((f32[64,2,1152]{2,1,0:T(2,128)}), f32[64,2,1152]{2,1,0:T(2,128)S(1)}, u32[]{:S(2)}, u32[]{:S(2)}) async-start(f32[64,2,1152]{2,1,0:T(2,128)} %broadcast_in_dim.29), calls=%async_computation.3 | async-start | bytes 1179648 | tf_op jit(solution)/shard_map/all_to_all | solution.py:43
  86.6 7.8 %collective-permute-start.2 = (bf16[64,1152]{1,0:T(8,128)(2,1)}, bf16[64,1152]{1,0:T(8,128)(2,1)S(1)}, u32[]{:S(2)}, u32[]{:S(2)}) collective-permute-start(bf16[64,1152]{1,0:T(8,128)(2,1)} %add_convert_fusion.1), channel_id=1, source_target_pairs={{0,6},{1,3},{2,4},{3,1},{4,2},{5,7},{6,0},{7,5},{8,14},{9,11},{10,... | collective-permute-start | bytes 442376 | tf_op jit(solution)/shard_map/ppermute | solution.py:33
  98.6 22.4 %all-to-all-start.2 = ((bf16[4,64,1152]{2,1,0:T(8,128)(2,1)}), bf16[4,64,1152]{2,1,0:T(8,128)(2,1)S(1)}, u32[]{:S(2)}, u32[]{:S(2)}) async-start(bf16[4,64,1152]{2,1,0:T(8,128)(2,1)} %broadcast_in_dim.28), calls=%async_computation.2 | async-start | bytes 1179648 | tf_op jit(solution)/shard_map/all_to_all | solution.py:43
  121.1 5.1 %collective-permute-start.3 = (bf16[256,1152]{1,0:T(8,128)(2,1)S(1)}, bf16[256,1152]{1,0:T(8,128)(2,1)S(1)}, u32[]{:S(2)}, u32[]{:S(2)}) collective-permute-start(bf16[256,1152]{1,0:T(8,128)(2,1)S(1)} %fusion.28), channel_id=1, source_target_pairs={{0,1},{1,0},{2,3},{3,2},{4,5},{5,4},{6,7},{7,6},{8,9},{9,8},{10,11... | collective-permute-start | bytes 1769480 | tf_op jit(solution)/shard_map/ppermute | solution.py:33

commit v3 on v2

v3 whole, which is shorter than its diff:
```python
import functools
import math

import jax
import jax.numpy as jnp
from jax import lax
from jax.experimental import pallas as pl
from jax.experimental.pallas import tpu as pltpu
from jax.sharding import PartitionSpec as P

PATCHES = 256
BLOCK = 64
EPS = 1e-06
LOSS_SCALE = 131072.0
HIGH = lax.Precision.HIGHEST
F32 = jnp.float32
BF16 = jnp.bfloat16
LAST = (((1,), (1,)), ((), ()))
SMEM = pl.BlockSpec(memory_space=pltpu.SMEM)
HBM = pl.BlockSpec(memory_space=pltpu.HBM)
VMEM = pl.BlockSpec(memory_space=pltpu.VMEM)
LARGE = pltpu.CompilerParams(vmem_limit_bytes=60 * 1024 * 1024)
SMALL = pltpu.CompilerParams(vmem_limit_bytes=16 * 1024 * 1024)


def norm_parts(values):
    centre = values - jnp.mean(values, axis=-1, keepdims=True)
    inverse = lax.rsqrt(jnp.mean(centre * centre, axis=-1, keepdims=True) + EPS)
    return centre * inverse, inverse


def norm_back(grad_out, gain, normed, inverse):
    scaled = grad_out * gain
    return inverse * (
        scaled
        - jnp.mean(scaled, axis=-1, keepdims=True)
        - normed * jnp.mean(scaled * normed, axis=-1, keepdims=True)
    )


def split_stack(values):
    high = values.astype(BF16).astype(F32)
    rest = values - high
    mid = rest.astype(BF16).astype(F32)
    low = rest - mid
    return jnp.concatenate([high, mid, low, jnp.zeros_like(high)], axis=0).astype(BF16)


def unstack(sums):
    return (sums[0:8] + sums[8:16]) + sums[16:24]


def pack_kernel(ids_ref, text_ref, pack_ref, unit_ref, len_ref):
    text = text_ref[...].astype(F32)
    length = jnp.sqrt(jnp.sum(text * text, axis=-1, keepdims=True) + EPS)
    unit = text / length
    unit_ref[...] = unit
    len_ref[...] = jnp.broadcast_to(length, len_ref.shape)
    row = lax.broadcasted_iota(jnp.int32, (2, 128), 0)
    lane = lax.broadcasted_iota(jnp.int32, (2, 128), 1)
    ids = jnp.where(row == 0, ids_ref[0], ids_ref[1])
    ids = jnp.where(lane == 0, ids, 0).astype(F32)
    packed = jnp.concatenate([unit, ids], axis=1).astype(BF16)
    for copy in range(pack_ref.shape[0]):
        pack_ref[copy] = packed


def pack_text(pair_ids, text_feats, copies):
    width = text_feats.shape[1]
    return pl.pallas_call(
        pack_kernel,
        in_specs=[SMEM, pl.BlockSpec(memory_space=pltpu.VMEM)],
        out_shape=[
            jax.ShapeDtypeStruct((copies, 2, width + 128), BF16),
            jax.ShapeDtypeStruct((2, width), F32),
            jax.ShapeDtypeStruct((2, 128), F32),
        ],
        compiler_params=SMALL,
        name="pack_text",
    )(pair_ids, text_feats)


def forward_kernel(
    n_tensor, x_ref, gain_ref, bias_ref, b_down_ref, up_hbm, down_hbm,
    slope_ref, part_ref, up_ref, down_ref, act_sum, x_sum, sems,
):
    step = pl.program_id(0)
    image = step // 2
    up_copy = pltpu.make_async_copy(up_hbm, up_ref, sems.at[0])
    down_copy = pltpu.make_async_copy(down_hbm, down_ref, sems.at[1])

    @pl.when(step == 0)
    def _():
        up_copy.start()
        down_copy.start()
        act_sum[...] = jnp.zeros_like(act_sum)
        x_sum[...] = jnp.zeros_like(x_sum)

    x = x_ref[...].astype(F32)
    normed, _ = norm_parts(x)
    normed = (normed * gain_ref[...][None, :]).astype(BF16)

    @pl.when(step == 0)
    def _():
        up_copy.wait()

    pre = lax.dot_general(normed, up_ref[...], LAST, preferred_element_type=F32)
    pre = pre + bias_ref[...][None, :]
    root = math.sqrt(2.0 / math.pi)
    square = pre * pre
    tanh = jnp.tanh(root * (pre + 0.044715 * (square * pre)))
    half = 0.5 * (1.0 + tanh)
    act = (pre * half).astype(BF16).astype(F32)
    slope_ref[...] = half + (0.5 * root) * pre * (1.0 - tanh * tanh) * (
        1.0 + (3.0 * 0.044715) * square
    )

    def add(total, values):
        row = lax.broadcasted_iota(jnp.int32, total.shape, 0)
        sums = jnp.sum(values, axis=0, keepdims=True)
        total[...] += jnp.where(row == image, sums, 0.0)

    add(act_sum, act)
    add(x_sum, x)

    @pl.when(step == pl.num_programs(0) - 1)
    def _():
        down_copy.wait()
        stack = split_stack(act_sum[...] * (1.0 / PATCHES))
        mlp = unstack(jnp.dot(stack, down_ref[...], preferred_element_type=F32))
        rest = x_sum[...] * (1.0 / PATCHES) + b_down_ref[...][None, :]
        part_ref[...] = (mlp + rest * (1.0 / n_tensor))[0:2]


def forward(patches, ln_gain, up_t, b_up, w_down, b_down, n_tensor):
    tokens, width = patches.shape
    units = up_t.shape[0]
    rows = 128
    vector = lambda size: pl.BlockSpec((size,), lambda i: (0,))
    return pl.pallas_call(
        functools.partial(forward_kernel, n_tensor),
        grid=(tokens // rows,),
        in_specs=[
            pl.BlockSpec((rows, width), lambda i: (i, 0)),
            vector(width),
            vector(units),
            vector(width),
            HBM,
            HBM,
        ],
        out_specs=[
            pl.BlockSpec((rows, units), lambda i: (i, 0)),
            pl.BlockSpec((2, width), lambda i: (0, 0)),
        ],
        out_shape=[
            jax.ShapeDtypeStruct((tokens, units), F32),
            jax.ShapeDtypeStruct((2, width), F32),
        ],
        scratch_shapes=[
            pltpu.VMEM((units, width), BF16),
            pltpu.VMEM((units, width), BF16),
            pltpu.VMEM((8, units), F32),
            pltpu.VMEM((8, width), F32),
            pltpu.SemaphoreType.DMA((2,)),
        ],
        compiler_params=LARGE,
        cost_estimate=pl.CostEstimate(
            flops=2 * tokens * width * units,
            bytes_accessed=2 * tokens * width + 4 * units * width + 4 * tokens * units,
            transcendentals=tokens * units,
        ),
        name="forward",
    )(patches, ln_gain, b_up, b_down, up_t, w_down)


def back_rows(blocks, slope_ref, g_act, up_ref, g_pre, out_ref):
    for place, block in enumerate(blocks):
        start = pl.multiple_of(block * BLOCK, BLOCK)
        g_pre[place * BLOCK : (place + 1) * BLOCK, :] = (
            slope_ref[pl.ds(start, BLOCK), :] * g_act
        ).astype(BF16)
    out_ref[...] = jnp.dot(
        g_pre[...], up_ref[...], preferred_element_type=F32
    ).astype(BF16)


def pick_row(rows, index):
    row = lax.broadcasted_iota(jnp.int32, rows.shape, 0)
    return jnp.sum(jnp.where(row == index, rows, 0.0), axis=0, keepdims=True)


def loss_kernel(
    place_ref, scale_ref, ids_ref, pooled_ref, gain_ref, text_ref, down_hbm, up_hbm,
    slope_hbm, img_ref, spread_ref, hidden_ref, g_act_ref, away_ref, pooled, g_pre,
    down_ref, up_ref, slope_ref, sems,
):
    image = 1 - place_ref[0]
    rows = pl.ds(pl.multiple_of(image * PATCHES, PATCHES), PATCHES)
    down_copy = pltpu.make_async_copy(down_hbm, down_ref, sems.at[0])
    slope_copy = pltpu.make_async_copy(slope_hbm.at[rows, :], slope_ref, sems.at[1])
    up_copy = pltpu.make_async_copy(up_hbm, up_ref, sems.at[2])
    down_copy.start()
    slope_copy.start()
    up_copy.start()
    gain = gain_ref[...][None, :]
    batch, width = text_ref.shape[0], pooled_ref.shape[1]
    sharp, shift = scale_ref[0], scale_ref[1]
    pooled[...] = jnp.zeros_like(pooled)
    pooled[0:2, :] = pooled_ref[...]
    feat_n, feat_s = norm_parts(pooled[...])
    features = feat_n * gain
    feat_len = jnp.sqrt(jnp.sum(features * features, axis=-1, keepdims=True) + EPS)
    img_emb = features / feat_len
    img_ref[...] = img_emb[0:2]
    own_img = pick_row(img_emb, place_ref[0])
    for copy in range(spread_ref.shape[0]):
        spread_ref[copy] = own_img

    text = text_ref[:, 0:width]
    logits = sharp * unstack(
        lax.dot_general(split_stack(img_emb), text, LAST, preferred_element_type=F32)
    ) + shift
    lane = lax.broadcasted_iota(jnp.int32, (16, 128), 1)
    first_lane = jnp.where(lane == 0, 1.0, 0.0).astype(BF16)
    ids = lax.dot_general(
        first_lane, text_ref[:, width:], LAST, preferred_element_type=F32
    )[0:8]
    row = lax.broadcasted_iota(jnp.int32, (8, batch), 0)
    own = jnp.where(row == 0, ids_ref[0], ids_ref[1]).astype(F32)
    sign = jnp.where(ids == own, 1.0, -1.0)
    logit_grad = -LOSS_SCALE * sign * jax.nn.sigmoid(-sign * logits) / batch
    logit_grad = jnp.where(row < 2, logit_grad, 0.0)
    g_img = sharp * unstack(
        jnp.dot(split_stack(logit_grad), text, preferred_element_type=F32)
    )
    g_feat = (
        g_img - img_emb * jnp.sum(img_emb * g_img, axis=-1, keepdims=True)
    ) / feat_len
    g_hidden = norm_back(g_feat, gain, feat_n, feat_s) * (1.0 / PATCHES)
    hidden_ref[...] = g_hidden[0:2]
    g_rows = jnp.concatenate([g_hidden, jnp.zeros_like(g_hidden)], axis=0).astype(BF16)
    down_copy.wait()
    g_act = lax.dot_general(g_rows, down_ref[...], LAST, preferred_element_type=F32)
    g_act_ref[...] = g_act[0:2]
    blocks = [place_ref[5 + i] for i in range(4)]
    slope_copy.wait()
    up_copy.wait()
    back_rows(blocks, slope_ref, pick_row(g_act[0:8], image), up_ref, g_pre, away_ref)


def keep_kernel(place_ref, g_act_ref, up_hbm, slope_hbm, out_ref, g_pre, up_ref, slope_ref, sems):
    image = place_ref[0]
    rows = pl.ds(pl.multiple_of(image * PATCHES, PATCHES), PATCHES)
    slope_copy = pltpu.make_async_copy(slope_hbm.at[rows, :], slope_ref, sems.at[0])
    up_copy = pltpu.make_async_copy(up_hbm, up_ref, sems.at[1])
    slope_copy.start()
    up_copy.start()
    blocks = [place_ref[1 + i] for i in range(4)]
    slope_copy.wait()
    up_copy.wait()
    back_rows(
        blocks, slope_ref, pick_row(g_act_ref[...], image), up_ref, g_pre, out_ref
    )


def loss_and_away(place, scale, ids, pooled, gain, text, w_down, up_t, slope, copies):
    units, width = up_t.shape
    return pl.pallas_call(
        loss_kernel,
        in_specs=[SMEM] * 3 + [VMEM] * 3 + [HBM] * 3,
        out_shape=[
            jax.ShapeDtypeStruct((2, width), F32),
            jax.ShapeDtypeStruct((copies, 1, width), F32),
            jax.ShapeDtypeStruct((2, width), F32),
            jax.ShapeDtypeStruct((2, units), F32),
            jax.ShapeDtypeStruct((PATCHES, width), BF16),
        ],
        scratch_shapes=[
            pltpu.VMEM((8, width), F32),
            pltpu.VMEM((PATCHES, units), BF16),
            pltpu.VMEM((units, width), BF16),
            pltpu.VMEM((units, width), BF16),
            pltpu.VMEM((PATCHES, units), F32),
            pltpu.SemaphoreType.DMA((3,)),
        ],
        compiler_params=LARGE,
        cost_estimate=pl.CostEstimate(
            flops=2 * PATCHES * width * units,
            bytes_accessed=6 * units * width + 4 * PATCHES * units,
            transcendentals=0,
        ),
        name="loss_and_away",
    )(place, scale, ids, pooled, gain, text, w_down, up_t, slope)


def keep_rows(place, g_act, up_t, slope):
    units, width = up_t.shape
    return pl.pallas_call(
        keep_kernel,
        in_specs=[SMEM, VMEM, HBM, HBM],
        out_shape=jax.ShapeDtypeStruct((PATCHES, width), BF16),
        scratch_shapes=[
            pltpu.VMEM((PATCHES, units), BF16),
            pltpu.VMEM((units, width), BF16),
            pltpu.VMEM((PATCHES, units), F32),
            pltpu.SemaphoreType.DMA((2,)),
        ],
        compiler_params=LARGE,
        cost_estimate=pl.CostEstimate(
            flops=2 * PATCHES * width * units,
            bytes_accessed=4 * units * width + 4 * PATCHES * units,
            transcendentals=0,
        ),
        name="keep_rows",
    )(place, g_act, up_t, slope)


def finish_kernel(
    place_ref, keep_ref, other_ref, one_ref, two_ref, x_ref, hidden_ref, gain_ref, out_ref
):
    g_normed = keep_ref[...].astype(F32) + other_ref[...].astype(F32)
    g_normed = g_normed + one_ref[...].astype(F32) + two_ref[...].astype(F32)
    normed, inverse = norm_parts(x_ref[...].astype(F32))
    grad = norm_back(g_normed, gain_ref[...][None, :], normed, inverse)
    out_ref[...] = (grad + pick_row(hidden_ref[...], place_ref[0])).astype(BF16)


def finish(place, keep, other, got_one, got_two, patches, g_hidden, ln_gain):
    width = patches.shape[1]
    block = lambda index: pl.BlockSpec((BLOCK, width), index)
    return pl.pallas_call(
        finish_kernel,
        grid_spec=pltpu.PrefetchScalarGridSpec(
            num_scalar_prefetch=1,
            grid=(1,),
            in_specs=[
                block(lambda i, place: (3, 0)),
                block(lambda i, place: (3, 0)),
                block(lambda i, place: (1, 0)),
                block(lambda i, place: (0, 0)),
                block(lambda i, place: (place[0] * (PATCHES // BLOCK) + place[4], 0)),
                pl.BlockSpec((2, width), lambda i, place: (0, 0)),
                pl.BlockSpec((width,), lambda i, place: (0,)),
            ],
            out_specs=block(lambda i, place: (0, 0)),
        ),
        out_shape=jax.ShapeDtypeStruct((BLOCK, width), BF16),
        compiler_params=SMALL,
        name="finish",
    )(place, keep, other, got_one, got_two, patches, g_hidden, ln_gain)


def place_kernel(place_ref, own, two, one, far, near, rest, out_ref):
    core = place_ref[0]
    low, high = slice(0, BLOCK), slice(BLOCK, 2 * BLOCK)
    moves = [
        (far, low, core, place_ref[1]),
        (one, low, core, place_ref[2]),
        (two, low, core, place_ref[3]),
        (own, low, core, place_ref[4]),
        (rest, high, 1 - core, place_ref[5]),
        (rest, low, 1 - core, place_ref[6]),
        (near, high, 1 - core, place_ref[7]),
        (near, low, 1 - core, place_ref[8]),
    ]
    for ref, rows, image, block in moves:
        start = pl.multiple_of(image * PATCHES + block * BLOCK, BLOCK)
        out_ref[pl.ds(start, BLOCK), :] = ref[rows, :]


def put_in_place(place, pieces, tokens):
    width = pieces[0].shape[1]
    return pl.pallas_call(
        place_kernel,
        in_specs=[SMEM] + [VMEM] * 6,
        out_shape=jax.ShapeDtypeStruct((tokens, width), BF16),
        compiler_params=SMALL,
        name="put_in_place",
    )(place, *pieces)


def swap(value, axis, partner):
    size = lax.axis_size(axis)
    return lax.ppermute(value, axis, [(i, partner(i)) for i in range(size)])


def swap_core(value):
    return swap(value, "tensor", lambda i: i ^ 1)


def step_one(i):
    return i ^ 2 if i % 2 == 0 else (3 - i // 2) * 2 + 1


def step_two(i):
    return (3 - i // 2) * 2 if i % 2 == 0 else i ^ 2


def exchange(copies, groups):
    return lax.all_to_all(
        copies, "dp", split_axis=0, concat_axis=0, axis_index_groups=groups
    )


def spread(rows, groups):
    copies = jnp.broadcast_to(rows[None], (len(groups[0]),) + rows.shape)
    return exchange(copies, groups)


def on_device(
    patches,
    ln_gain,
    w_up,
    b_up,
    w_down,
    b_down,
    head_gain,
    text_feats,
    pair_ids,
    log_sharpness,
    pairwise_logit_shift,
):
    width = text_feats.shape[1]
    batch = text_feats.shape[0] * lax.axis_size("dp")
    position = lax.axis_index("tensor")
    core = position % 2
    ring = position // 2
    u = ((ring == 1) | (ring == 2)).astype(jnp.int32)
    v = (ring >= 2).astype(jnp.int32)
    one, two = jnp.where(core == 0, u, v), jnp.where(core == 0, v, u)

    def order(hi, lo):
        return [3 - 2 * hi - lo, 2 - 2 * hi + lo, 2 * hi + 1 - lo, 2 * hi + lo]

    place = jnp.stack([core] + order(one, two) + order(two, one)).astype(jnp.int32)

    count = lax.axis_size("dp")
    side = math.isqrt(count)
    along_y = [[y * side + k for y in range(side)] for k in range(side)]
    along_xz = [[y * side + k for k in range(side)] for y in range(side)]

    packed, unit_text, text_len = pack_text(pair_ids, text_feats, side)
    text_len = text_len[:, :1]
    text_own = unit_text.astype(BF16)
    some_text = exchange(packed, along_y).reshape(2 * side, -1)

    up_t = w_up.T
    slope, part = forward(
        patches, ln_gain, up_t, b_up, w_down, b_down, lax.axis_size("tensor")
    )
    some_text, part = lax.optimization_barrier((some_text, part))
    text_all = spread(some_text, along_xz).reshape(batch, -1)
    pooled = lax.psum(part, "tensor")

    sharp = jnp.exp(log_sharpness[0])
    shift = pairwise_logit_shift[0]
    img_emb, img_copies, g_hidden, g_act, away = loss_and_away(
        place,
        jnp.stack([sharp, shift]),
        pair_ids,
        pooled,
        head_gain,
        text_all,
        w_down,
        up_t,
        slope,
        side,
    )

    other = swap_core(away)
    keep = keep_rows(place, g_act, up_t, slope)

    def both(start, count):
        rows = slice(start, start + count)
        return keep[rows].astype(F32) + other[rows].astype(F32)

    send_one = both(0, 128).astype(BF16)
    got_one = swap(send_one, "tensor", step_one)
    send_two = (both(128, 64) + got_one[:64].astype(F32)).astype(BF16)
    got_two = swap(send_two, "tensor", step_two)
    done = finish(place, keep, other, got_one, got_two, patches, g_hidden, ln_gain)

    from_two = swap(done, "tensor", step_two)
    from_one = swap(done, "tensor", step_one)
    far = swap(from_two, "tensor", step_one)
    near = swap_core(jnp.concatenate([done, from_two]))
    rest = swap_core(jnp.concatenate([from_one, far]))
    grad_patches = put_in_place(
        place, (done, from_two, from_one, far, near, rest), patches.shape[0]
    )

    img_copies, _ = lax.optimization_barrier((img_copies, send_one))
    some_img = exchange(img_copies, along_y).reshape(side, width)
    some_img, _ = lax.optimization_barrier((some_img, send_two))
    img_all = spread(some_img, along_xz).reshape(count, width)
    img_all, _ = lax.optimization_barrier((img_all, done))
    ids_all = text_all[:, width].astype(jnp.int32).reshape(count, 2)
    ids_all = jnp.where(core == 0, ids_all[:, 0], ids_all[:, 1])
    logits = sharp * jnp.dot(text_own.astype(F32), img_all.T, precision=HIGH) + shift
    sign = jnp.where(pair_ids[:, None] == ids_all[None, :], 1.0, -1.0)
    logit_grad = -LOSS_SCALE * sign * jax.nn.sigmoid(-sign * logits) / batch
    g_text = sharp * jnp.dot(logit_grad, img_all, precision=HIGH)
    g_text = g_text + swap_core(g_text)
    grad_text = (
        g_text - unit_text * jnp.sum(unit_text * g_text, axis=-1, keepdims=True)
    ) / text_len
    return grad_patches, grad_text


def solution(mesh):
    in_specs = (
        P("dp", None),
        P(),
        P(None, "tensor"),
        P("tensor"),
        P("tensor", None),
        P(),
        P(),
        P("dp", None),
        P("dp"),
        P(),
        P(),
    )
    out_specs = (P("dp", None), P("dp", None))
    return jax.shard_map(
        on_device, mesh=mesh, in_specs=in_specs, out_specs=out_specs, check_vma=False
    )
```

time: 128 us -> 118 us (0.922)
  waiting for transfers between devices: 44.1 us -> 5.07 us
  blocking collectives: 0 us -> 21.3 us
  Pallas kernels: 0 us -> 19 us
  starting transfers between devices: 47.6 us -> 59 us
  matrix products: 11.3 us -> 0.55 us
  other arithmetic: 12.3 us -> 4.7 us
  local copies, waits for them, and re-layouts: 9.94 us -> 4.53 us
    all_to_all x4, waiting for transfers between devices: 33.2 us -> 0.01 us  [exchange(): lax.all_to_all(copies, 'dp', split_axis=0, concat_axis=0, axis_index_grou...]
    psum x0 -> x1, blocking collectives: none -> 21.3 us  [on_device(): pooled = lax.psum(part, 'tensor')]
    ppermute x4 -> x9, starting transfers between devices: 13.6 us -> 33.9 us  [swap(): return lax.ppermute(value, axis, [(i, partner(i)) for i in range(size)])]
    pallas_call x0 -> x6, Pallas kernels: none -> 19 us  [the longest x1 7.1 us: forward(): pl.pallas_call(functools.partial(forward_kernel, n_tensor), grid=(tokens...]
    dot_general x9 -> x2, matrix products: 11.3 us -> 0.55 us  [the longest x1 0.29 us: on_device(): g_text = sharp * jnp.dot(logit_grad, img_all, precision=HIGH)]
    all_to_all x4, starting transfers between devices: 34.1 us -> 25.1 us  [exchange(): lax.all_to_all(copies, 'dp', split_axis=0, concat_axis=0, axis_index_grou...]
    reduce_sum x13 -> x1, other arithmetic: 6.15 us -> 0.13 us  [on_device(): jnp.sum(unit_text * g_text, axis=-1, keepdims=True)]
    ppermute x4 -> x9, waiting for transfers between devices: 10.8 us -> 5.06 us  [swap(): return lax.ppermute(value, axis, [(i, partner(i)) for i in range(size)])]
  transfers between devices with their start and end apart: 8 -> 13, of which waited for: 7 -> 3; matrix products, arithmetic and copies ran while one was open for 7% -> 5% of each run, Pallas kernels for 0% -> 10%
where the time goes in v3:
time: 118 us; the launch traced here: 116 us
  starting transfers between devices  59 us (50%)
  blocking collectives  21.3 us (18%)
  Pallas kernels  19 us (16%)
  waiting for transfers between devices  5.07 us (4%)
  other arithmetic  4.7 us (4%)
  local copies, waits for them, and re-layouts  4.53 us (4%)
  between operations  2.29 us (2%)
    ppermute x9, starting transfers between devices, swap(): return lax.ppermute(value, axis, [(i, partner(i)) for i in range(size)])  33.9 us
    all_to_all x4, starting transfers between devices, exchange(): lax.all_to_all(copies, 'dp', split_axis=0, concat_axis=0, axis_index_grou...  25.1 us
    psum x1, blocking collectives, on_device(): pooled = lax.psum(part, 'tensor')  21.3 us
    pallas_call x1, Pallas kernels, forward(): pl.pallas_call(functools.partial(forward_kernel, n_tensor), grid=(tokens...  7.1 us
    ppermute x9, waiting for transfers between devices, swap(): return lax.ppermute(value, axis, [(i, partner(i)) for i in range(size)])  5.06 us
    pallas_call x1, Pallas kernels, loss_and_away(): pl.pallas_call(loss_kernel, in_specs=[SMEM] * 3 + [VMEM] * 3 + [HBM] * 3,...  4.4 us
    pallas_call x1, Pallas kernels, keep_rows(): pl.pallas_call(keep_kernel, in_specs=[SMEM, VMEM, HBM, HBM], out_shape=ja...  3.71 us
  transfers between devices with their start and end apart: 13, of which 3 were waited for; matrix products, arithmetic and copies ran while one was open for 5% of the time, Pallas kernels for 10%

profile of v3, /device:TPU:1, one launch (start us, length us, event | category | flops | bytes accessed | tf_op | source)
XLA Modules:
  0.0 116.5 jit_solution(17349620795471701457)
XLA Ops:
  0.6 0.0 copy-start.5
  0.6 0.6 copy-done.5
  1.3 0.0 copy-start.7
  1.3 0.7 copy-done.7
  2.0 1.3 %pack_text.1 = (bf16[8,2,1280]{2,1,0:T(2,128)(2,1)}, f32[2,1152]{1,0:T(2,128)S(1)}, f32[2,128]{1,0:T(2,128)S(1)}) custom-call(s32[2]{0:T(128)S(1)} %copy-done.5, bf16[2,1152]{1,0:T(2,128)(2,1)S(1)} %copy-done.7), custom_call_target="tpu_custom_call" | custom-call | tf_op jit(solution)/shard_map/pack_text/pallas_call | solution.py:70
  3.2 7.7 %all-to-all-start = ((bf16[8,2,1280]{2,1,0:T(2,128)(2,1)}), bf16[8,2,1280]{2,1,0:T(2,128)(2,1)S(1)}, u32[]{:S(2)}, u32[]{:S(2)}) async-start(bf16[8,2,1280]{2,1,0:T(2,128)(2,1)} %get-tuple-element.16), calls=%async_computation | async-start | bytes 81920 | tf_op jit(solution)/shard_map/all_to_all | solution.py:400
  10.9 7.1 %forward.1 = (f32[512,538]{1,0:T(8,128)}, f32[2,1152]{1,0:T(2,128)}) custom-call(bf16[512,1152]{1,0:T(8,128)(2,1)} %x_ref.3, f32[1152]{0:T(1024)} %gain_ref.5, f32[538]{0:T(1024)} %bias_ref.1, f32[1152]{0:T(1024)} %b_down_ref.1, bf16[538,1152]{1,0:T(8,128)(2,1)} %bitcast.21, bf16[538,1152]{1,0:T(8,128)(2,1)} %down_hbm.3), custom_call_target="tpu_custom_call" | custom-call | flops 634650624 | bytes 4760576 | tf_op jit(solution)/shard_map/forward/pallas_call | solution.py:140
  18.0 0.0 all-to-all-done
  18.1 0.7 broadcast_in_dim.10
  18.8 5.8 %all-to-all-start.1 = ((bf16[8,16,1280]{2,1,0:T(8,128)(2,1)}), bf16[8,16,1280]{2,1,0:T(8,128)(2,1)S(1)}, u32[]{:S(2)}, u32[]{:S(2)}) async-start(bf16[8,16,1280]{2,1,0:T(8,128)(2,1)} %broadcast_in_dim.10), calls=%async_computation.1 | async-start | bytes 655360 | tf_op jit(solution)/shard_map/all_to_all | solution.py:400
  26.0 0.7 stack.43.place_ref
  26.6 0.7 pad_maximum_fusion.2.scale_ref
  27.3 21.3 %psum.7.pooled_ref = f32[2,1152]{1,0:T(2,128)} all-reduce(f32[2,1152]{1,0:T(2,128)} %get-tuple-element.18), channel_id=1, replica_groups=mesh['dp'=64,'tensor'=8] {'tensor'}, use_global_device_ids=true, to_apply=%region_0.1 | all-reduce | flops 2304 | bytes 18432 | tf_op jit(solution)/shard_map/psum | solution.py:453
  48.6 0.0 all-to-all-done.1
  48.6 0.7 copy-done.8
  49.3 4.4 %loss_and_away.1 = (f32[2,1152]{1,0:T(2,128)}, f32[8,1,1152]{2,1,0:T(1,128)}, f32[2,1152]{1,0:T(2,128)}, f32[2,538]{1,0:T(2,128)}, bf16[256,1152]{1,0:T(8,128)(2,1)}) custom-call(s32[9]{0:T(128)} %stack.43.place_ref, f32[2]{0:T(128)} %pad_maximum_fusion.2.scale_ref, s32[2]{0:T(128)} %ids_ref.3, f32[2,1152]{1,0:T(2,128)} %psum.7.pooled_ref, f32[1152]{0:T(1024)} %gain_ref.4, ...), custom_call_target="tpu_custom_call" | custom-call | flops 317325312 | bytes 4269568 | tf_op jit(solution)/shard_map/loss_and_away/pallas_call | solution.py:268
  53.7 4.4 %collective-permute-start = (bf16[256,1152]{1,0:T(8,128)(2,1)}, bf16[256,1152]{1,0:T(8,128)(2,1)S(1)}, u32[]{:S(2)}, u32[]{:S(2)}) collective-permute-start(bf16[256,1152]{1,0:T(8,128)(2,1)} %get-tuple-element.22), channel_id=1, source_target_pairs={{0,1},{1,0},{2,3},{3,2},{4,5},{5,4},{6,7},{7,6},{8,9},{9,8},{10,11... | collective-permute-start | bytes 1769480 | tf_op jit(solution)/shard_map/ppermute | solution.py:384
  58.1 3.7 %keep_rows.1.keep_ref = bf16[256,1152]{1,0:T(8,128)(2,1)} custom-call(s32[9]{0:T(128)} %stack.43.place_ref, f32[2,538]{1,0:T(2,128)} %get-tuple-element.21.g_act_ref, bf16[538,1152]{1,0:T(8,128)(2,1)} %bitcast.23, f32[512,538]{1,0:T(8,128)} %get-tuple-element.20.slope_hbm), custom_call_target="tpu_custom_call" | custom-call | flops 317325312 | bytes 3030016 | tf_op jit(solution)/shard_map/keep_rows/pallas_call | solution.py:298
  61.8 0.0 copy-start
  61.8 0.0 copy-start.1
  61.8 0.0 copy-start.2
  61.8 0.0 copy-start.3
  61.9 0.0 copy-start.4
  61.9 0.0 collective-permute-done.other_ref
  61.9 1.2 %add_convert_fusion = bf16[128,1152]{1,0:T(8,128)(2,1)S(1)} fusion(bf16[256,1152]{1,0:T(8,128)(2,1)S(1)} %collective-permute-done.other_ref, bf16[256,1152]{1,0:T(8,128)(2,1)} %keep_rows.1.keep_ref), kind=kLoop, calls=%fused_computation.10 | loop fusion | flops 589824 | bytes 884736 | tf_op jit(solution)/shard_map/convert_element_type | solution.py:477
  63.1 1.9 %collective-permute-start.1 = (bf16[128,1152]{1,0:T(8,128)(2,1)S(1)}, bf16[128,1152]{1,0:T(8,128)(2,1)S(1)}, u32[]{:S(2)}, u32[]{:S(2)}) collective-permute-start(bf16[128,1152]{1,0:T(8,128)(2,1)S(1)} %add_convert_fusion), channel_id=1, source_target_pairs={{0,2},{1,7},{2,0},{3,5},{4,6},{5,3},{6,4},{7,1},{8,10},{9,15},{10,... | collective-permute-start | bytes 884744 | tf_op jit(solution)/shard_map/ppermute | solution.py:384
  65.0 6.5 %all-to-all-start.2 = ((f32[8,1,1152]{2,1,0:T(1,128)}), f32[8,1,1152]{2,1,0:T(1,128)S(1)}, u32[]{:S(2)}, u32[]{:S(2)}) async-start(f32[8,1,1152]{2,1,0:T(1,128)} %get-tuple-element.26), calls=%async_computation.2 | async-start | bytes 73728 | tf_op jit(solution)/shard_map/all_to_all | solution.py:400
  71.5 4.3 %collective-permute-done.1.one_ref = bf16[128,1152]{1,0:T(8,128)(2,1)S(1)} collective-permute-done((bf16[128,1152]{1,0:T(8,128)(2,1)S(1)}, bf16[128,1152]{1,0:T(8,128)(2,1)S(1)}, u32[]{:S(2)}, u32[]{:S(2)}) %collective-permute-start.1) | collective-permute-done | bytes 294944 | tf_op jit(solution)/shard_map/ppermute | solution.py:384
  75.8 1.0 add_convert_fusion.1
  76.8 1.9 %collective-permute-start.2 = (bf16[64,1152]{1,0:T(8,128)(2,1)S(1)}, bf16[64,1152]{1,0:T(8,128)(2,1)S(1)}, u32[]{:S(2)}, u32[]{:S(2)}) collective-permute-start(bf16[64,1152]{1,0:T(8,128)(2,1)S(1)} %add_convert_fusion.1), channel_id=1, source_target_pairs={{0,6},{1,3},{2,4},{3,1},{4,2},{5,7},{6,0},{7,5},{8,14},{9,11},{10,... | collective-permute-start | bytes 442376 | tf_op jit(solution)/shard_map/ppermute | solution.py:384
  78.7 0.0 all-to-all-done.2
  78.7 0.7 broadcast_in_dim.26
  79.4 5.1 %all-to-all-start.3 = ((f32[8,8,1152]{2,1,0:T(8,128)}), f32[8,8,1152]{2,1,0:T(8,128)S(1)}, u32[]{:S(2)}, u32[]{:S(2)}) async-start(f32[8,8,1152]{2,1,0:T(8,128)} %broadcast_in_dim.26), calls=%async_computation.3 | async-start | bytes 589824 | tf_op jit(solution)/shard_map/all_to_all | solution.py:400
  84.5 0.1 slice_reduce_fusion
  84.7 0.4 collective-permute-done.2.two_ref
  85.1 0.0 copy-done
  85.1 0.0 copy-done.1
  85.1 0.0 copy-done.2
  85.1 0.0 copy-done.3
  85.1 0.0 copy-done.4
  85.1 0.0 copy-start.6
  85.1 0.9 finish.1.own
  86.0 3.0 %collective-permute-start.3 = (bf16[64,1152]{1,0:T(8,128)(2,1)S(1)}, bf16[64,1152]{1,0:T(8,128)(2,1)S(1)}, u32[]{:S(2)}, u32[]{:S(2)}) collective-permute-start(bf16[64,1152]{1,0:T(8,128)(2,1)S(1)} %finish.1.own), channel_id=1, source_target_pairs={{0,6},{1,3},{2,4},{3,1},{4,2},{5,7},{6,0},{7,5},{8,14},{9,11},{10,... | collective-permute-start | bytes 442376 | tf_op jit(solution)/shard_map/ppermute | solution.py:384
  89.0 0.9 convert_reduce_fusion
  89.9 0.1 reshape.41
  90.0 0.2 fusion.8
  90.2 4.0 %collective-permute-start.4 = (bf16[64,1152]{1,0:T(8,128)(2,1)S(1)}, bf16[64,1152]{1,0:T(8,128)(2,1)S(1)}, u32[]{:S(2)}, u32[]{:S(2)}) collective-permute-start(bf16[64,1152]{1,0:T(8,128)(2,1)S(1)} %finish.1.own), channel_id=1, source_target_pairs={{0,2},{1,7},{2,0},{3,5},{4,6},{5,3},{6,4},{7,1},{8,10},{9,15},{10,... | collective-permute-start | bytes 442376 | tf_op jit(solution)/shard_map/ppermute | solution.py:384
  94.2 0.0 collective-permute-done.3.two
  94.3 6.2 %collective-permute-start.6 = (bf16[128,1152]{1,0:T(8,128)(2,1)S(1)}, bf16[128,1152]{1,0:T(8,128)(2,1)S(1)}, u32[]{:S(2)}, u32[]{:S(2)}) collective-permute-start(bf16[128,1152]{1,0:T(8,128)(2,1)S(1)} %pad_maximum_fusion), channel_id=1, source_target_pairs={{0,1},{1,0},{2,3},{3,2},{4,5},{5,4},{6,7},{7,6},{8,9},{9,8},{10,11... | collective-permute-start | bytes 884744 | tf_op jit(solution)/shard_map/ppermute | solution.py:384
  100.5 3.2 %collective-permute-start.5 = (bf16[64,1152]{1,0:T(8,128)(2,1)S(1)}, bf16[64,1152]{1,0:T(8,128)(2,1)S(1)}, u32[]{:S(2)}, u32[]{:S(2)}) collective-permute-start(bf16[64,1152]{1,0:T(8,128)(2,1)S(1)} %collective-permute-done.3.two), channel_id=1, source_target_pairs={{0,2},{1,7},{2,0},{3,5},{4,6},{5,3},{6,4},{7,1},{8,10},{9,15},{10,... | collective-permute-start | bytes 442376 | tf_op jit(solution)/shard_map/ppermute | solution.py:384
  103.7 0.0 all-to-all-done.3
  103.7 0.0 copy-done.6
  103.7 0.3 fusion.7
  104.0 0.3 convolution_multiply_fusion
  104.3 5.2 %collective-permute-start.8 = (f32[2,1152]{1,0:T(2,128)S(1)}, f32[2,1152]{1,0:T(2,128)S(1)}, u32[]{:S(2)}, u32[]{:S(2)}) collective-permute-start(f32[2,1152]{1,0:T(2,128)S(1)} %convolution_multiply_fusion), channel_id=1, source_target_pairs={{0,1},{1,0},{2,3},{3,2},{4,5},{5,4},{6,7},{7,6},{8,9},{9,8},{10,11... | collective-permute-start | bytes 27656 | tf_op jit(solution)/shard_map/ppermute | solution.py:384
  109.5 0.0 collective-permute-done.4.one
  109.5 0.0 collective-permute-done.5.far
  109.5 4.1 %collective-permute-start.7 = (bf16[128,1152]{1,0:T(8,128)(2,1)S(1)}, bf16[128,1152]{1,0:T(8,128)(2,1)S(1)}, u32[]{:S(2)}, u32[]{:S(2)}) collective-permute-start(bf16[128,1152]{1,0:T(8,128)(2,1)S(1)} %pad_maximum_fusion.1), channel_id=1, source_target_pairs={{0,1},{1,0},{2,3},{3,2},{4,5},{5,4},{6,7},{7,6},{8,9},{9,8},{10,11... | collective-permute-start | bytes 884744 | tf_op jit(solution)/shard_map/ppermute | solution.py:384
  113.7 0.0 collective-permute-done.8
  113.7 0.1 multiply_reduce_fusion
  113.8 0.7 subtract_divide_fusion
  114.5 0.0 collective-permute-done.6.near
  114.5 0.4 collective-permute-done.7.rest
  114.8 1.6 %put_in_place.1 = bf16[512,1152]{1,0:T(8,128)(2,1)} custom-call(s32[9]{0:T(128)S(1)} %copy-done.3, bf16[64,1152]{1,0:T(8,128)(2,1)S(1)} %finish.1.own, bf16[64,1152]{1,0:T(8,128)(2,1)S(1)} %collective-permute-done.3.two, bf16[64,1152]{1,0:T(8,128)(2,1)S(1)} %collective-permute-done.4.one, bf16[64,1152]{1,0:T(8,128)(2,1)S(1)} %collective-permute-done.5.far, ...), custom_call_target="tpu_custom_call" | custom-call | tf_op jit(solution)/shard_map/put_in_place/pallas_call | solution.py:373
  (5 shorter events, 0.1 us)
Async XLA Ops:
  0.6 0.7 copy-start.5
  1.3 0.7 copy-start.7
  3.2 14.8 %all-to-all-start = ((bf16[8,2,1280]{2,1,0:T(2,128)(2,1)}), bf16[8,2,1280]{2,1,0:T(2,128)(2,1)S(1)}, u32[]{:S(2)}, u32[]{:S(2)}) async-start(bf16[8,2,1280]{2,1,0:T(2,128)(2,1)} %get-tuple-element.16), calls=%async_computation | async-start | bytes 81920 | tf_op jit(solution)/shard_map/all_to_all | solution.py:400
  18.8 29.8 %all-to-all-start.1 = ((bf16[8,16,1280]{2,1,0:T(8,128)(2,1)}), bf16[8,16,1280]{2,1,0:T(8,128)(2,1)S(1)}, u32[]{:S(2)}, u32[]{:S(2)}) async-start(bf16[8,16,1280]{2,1,0:T(8,128)(2,1)} %broadcast_in_dim.10), calls=%async_computation.1 | async-start | bytes 655360 | tf_op jit(solution)/shard_map/all_to_all | solution.py:400
  48.6 0.7 copy-start.8
  53.7 8.2 %collective-permute-start = (bf16[256,1152]{1,0:T(8,128)(2,1)}, bf16[256,1152]{1,0:T(8,128)(2,1)S(1)}, u32[]{:S(2)}, u32[]{:S(2)}) collective-permute-start(bf16[256,1152]{1,0:T(8,128)(2,1)} %get-tuple-element.22), channel_id=1, source_target_pairs={{0,1},{1,0},{2,3},{3,2},{4,5},{5,4},{6,7},{7,6},{8,9},{9,8},{10,11... | collective-permute-start | bytes 1769480 | tf_op jit(solution)/shard_map/ppermute | solution.py:384
  61.8 23.2 %copy-start = (bf16[512,1152]{1,0:T(8,128)(2,1)S(1)}, bf16[512,1152]{1,0:T(8,128)(2,1)}, u32[]{:S(2)}) copy-start(bf16[512,1152]{1,0:T(8,128)(2,1)} %x_ref.3) | copy-start | bytes 3538948
  61.8 23.2 %copy-start.1 = (bf16[256,1152]{1,0:T(8,128)(2,1)S(1)}, bf16[256,1152]{1,0:T(8,128)(2,1)}, u32[]{:S(2)}) copy-start(bf16[256,1152]{1,0:T(8,128)(2,1)} %keep_rows.1.keep_ref) | copy-start | bytes 1769476
  61.8 23.2 %copy-start.2 = (f32[1152]{0:T(1024)S(1)}, f32[1152]{0:T(1024)}, u32[]{:S(2)}) copy-start(f32[1152]{0:T(1024)} %gain_ref.5) | copy-start | bytes 13828
  61.8 23.2 %copy-start.3 = (s32[9]{0:T(128)S(1)}, s32[9]{0:T(128)}, u32[]{:S(2)}) copy-start(s32[9]{0:T(128)} %stack.43.place_ref) | copy-start | bytes 112
  61.9 23.2 %copy-start.4 = (f32[2,1152]{1,0:T(2,128)S(1)}, f32[2,1152]{1,0:T(2,128)}, u32[]{:S(2)}) copy-start(f32[2,1152]{1,0:T(2,128)} %get-tuple-element.23.hidden_ref) | copy-start | bytes 27652
  63.1 12.7 %collective-permute-start.1 = (bf16[128,1152]{1,0:T(8,128)(2,1)S(1)}, bf16[128,1152]{1,0:T(8,128)(2,1)S(1)}, u32[]{:S(2)}, u32[]{:S(2)}) collective-permute-start(bf16[128,1152]{1,0:T(8,128)(2,1)S(1)} %add_convert_fusion), channel_id=1, source_target_pairs={{0,2},{1,7},{2,0},{3,5},{4,6},{5,3},{6,4},{7,1},{8,10},{9,15},{10,... | collective-permute-start | bytes 884744 | tf_op jit(solution)/shard_map/ppermute | solution.py:384
  65.0 13.7 %all-to-all-start.2 = ((f32[8,1,1152]{2,1,0:T(1,128)}), f32[8,1,1152]{2,1,0:T(1,128)S(1)}, u32[]{:S(2)}, u32[]{:S(2)}) async-start(f32[8,1,1152]{2,1,0:T(1,128)} %get-tuple-element.26), calls=%async_computation.2 | async-start | bytes 73728 | tf_op jit(solution)/shard_map/all_to_all | solution.py:400
  76.8 8.3 %collective-permute-start.2 = (bf16[64,1152]{1,0:T(8,128)(2,1)S(1)}, bf16[64,1152]{1,0:T(8,128)(2,1)S(1)}, u32[]{:S(2)}, u32[]{:S(2)}) collective-permute-start(bf16[64,1152]{1,0:T(8,128)(2,1)S(1)} %add_convert_fusion.1), channel_id=1, source_target_pairs={{0,6},{1,3},{2,4},{3,1},{4,2},{5,7},{6,0},{7,5},{8,14},{9,11},{10,... | collective-permute-start | bytes 442376 | tf_op jit(solution)/shard_map/ppermute | solution.py:384
  79.4 24.2 %all-to-all-start.3 = ((f32[8,8,1152]{2,1,0:T(8,128)}), f32[8,8,1152]{2,1,0:T(8,128)S(1)}, u32[]{:S(2)}, u32[]{:S(2)}) async-start(f32[8,8,1152]{2,1,0:T(8,128)} %broadcast_in_dim.26), calls=%async_computation.3 | async-start | bytes 589824 | tf_op jit(solution)/shard_map/all_to_all | solution.py:400
  85.1 18.6 %copy-start.6 = (s32[2]{0:T(128)S(1)}, s32[2]{0:T(128)}, u32[]{:S(2)}) copy-start(s32[2]{0:T(128)} %ids_ref.3) | copy-start | bytes 28
  86.0 8.2 %collective-permute-start.3 = (bf16[64,1152]{1,0:T(8,128)(2,1)S(1)}, bf16[64,1152]{1,0:T(8,128)(2,1)S(1)}, u32[]{:S(2)}, u32[]{:S(2)}) collective-permute-start(bf16[64,1152]{1,0:T(8,128)(2,1)S(1)} %finish.1.own), channel_id=1, source_target_pairs={{0,6},{1,3},{2,4},{3,1},{4,2},{5,7},{6,0},{7,5},{8,14},{9,11},{10,... | collective-permute-start | bytes 442376 | tf_op jit(solution)/shard_map/ppermute | solution.py:384
  90.2 19.3 %collective-permute-start.4 = (bf16[64,1152]{1,0:T(8,128)(2,1)S(1)}, bf16[64,1152]{1,0:T(8,128)(2,1)S(1)}, u32[]{:S(2)}, u32[]{:S(2)}) collective-permute-start(bf16[64,1152]{1,0:T(8,128)(2,1)S(1)} %finish.1.own), channel_id=1, source_target_pairs={{0,2},{1,7},{2,0},{3,5},{4,6},{5,3},{6,4},{7,1},{8,10},{9,15},{10,... | collective-permute-start | bytes 442376 | tf_op jit(solution)/shard_map/ppermute | solution.py:384
  94.3 20.2 %collective-permute-start.6 = (bf16[128,1152]{1,0:T(8,128)(2,1)S(1)}, bf16[128,1152]{1,0:T(8,128)(2,1)S(1)}, u32[]{:S(2)}, u32[]{:S(2)}) collective-permute-start(bf16[128,1152]{1,0:T(8,128)(2,1)S(1)} %pad_maximum_fusion), channel_id=1, source_target_pairs={{0,1},{1,0},{2,3},{3,2},{4,5},{5,4},{6,7},{7,6},{8,9},{9,8},{10,11... | collective-permute-start | bytes 884744 | tf_op jit(solution)/shard_map/ppermute | solution.py:384
  100.5 9.0 %collective-permute-start.5 = (bf16[64,1152]{1,0:T(8,128)(2,1)S(1)}, bf16[64,1152]{1,0:T(8,128)(2,1)S(1)}, u32[]{:S(2)}, u32[]{:S(2)}) collective-permute-start(bf16[64,1152]{1,0:T(8,128)(2,1)S(1)} %collective-permute-done.3.two), channel_id=1, source_target_pairs={{0,2},{1,7},{2,0},{3,5},{4,6},{5,3},{6,4},{7,1},{8,10},{9,15},{10,... | collective-permute-start | bytes 442376 | tf_op jit(solution)/shard_map/ppermute | solution.py:384
  104.3 9.4 %collective-permute-start.8 = (f32[2,1152]{1,0:T(2,128)S(1)}, f32[2,1152]{1,0:T(2,128)S(1)}, u32[]{:S(2)}, u32[]{:S(2)}) collective-permute-start(f32[2,1152]{1,0:T(2,128)S(1)} %convolution_multiply_fusion), channel_id=1, source_target_pairs={{0,1},{1,0},{2,3},{3,2},{4,5},{5,4},{6,7},{7,6},{8,9},{9,8},{10,11... | collective-permute-start | bytes 27656 | tf_op jit(solution)/shard_map/ppermute | solution.py:384
  109.5 5.3 %collective-permute-start.7 = (bf16[128,1152]{1,0:T(8,128)(2,1)S(1)}, bf16[128,1152]{1,0:T(8,128)(2,1)S(1)}, u32[]{:S(2)}, u32[]{:S(2)}) collective-permute-start(bf16[128,1152]{1,0:T(8,128)(2,1)S(1)} %pad_maximum_fusion.1), channel_id=1, source_target_pairs={{0,1},{1,0},{2,3},{3,2},{4,5},{5,4},{6,7},{7,6},{8,9},{9,8},{10,11... | collective-permute-start | bytes 884744 | tf_op jit(solution)/shard_map/ppermute | solution.py:384

commit v4 on v3

v4 whole, which is shorter than its diff:
```python
import functools
import math

import jax
import jax.numpy as jnp
from jax import lax
from jax.experimental import pallas as pl
from jax.experimental.pallas import tpu as pltpu
from jax.sharding import PartitionSpec as P

PATCHES = 256
BLOCK = 64
EPS = 1e-06
LOSS_SCALE = 131072.0
F32 = jnp.float32
BF16 = jnp.bfloat16
LAST = (((1,), (1,)), ((), ()))
SMEM = pl.BlockSpec(memory_space=pltpu.SMEM)
HBM = pl.BlockSpec(memory_space=pltpu.HBM)
VMEM = pl.BlockSpec(memory_space=pltpu.VMEM)
LARGE = pltpu.CompilerParams(vmem_limit_bytes=60 * 1024 * 1024)
SMALL = pltpu.CompilerParams(vmem_limit_bytes=16 * 1024 * 1024)


def places(position):
    core, ring = position & 1, position >> 1
    u, v = (ring ^ (ring >> 1)) & 1, ring >> 1
    swap = core * (u ^ v)
    return core, u ^ swap, v ^ swap


def order(one, two):
    return [3 - 2 * one - two, 2 - 2 * one + two, 2 * one + 1 - two, 2 * one + two]


def norm_parts(values):
    centre = values - jnp.mean(values, axis=-1, keepdims=True)
    inverse = lax.rsqrt(jnp.mean(centre * centre, axis=-1, keepdims=True) + EPS)
    return centre * inverse, inverse


def norm_back(grad_out, gain, normed, inverse):
    scaled = grad_out * gain
    return inverse * (
        scaled
        - jnp.mean(scaled, axis=-1, keepdims=True)
        - normed * jnp.mean(scaled * normed, axis=-1, keepdims=True)
    )


def split_stack(values):
    high = values.astype(BF16).astype(F32)
    rest = values - high
    mid = rest.astype(BF16).astype(F32)
    low = rest - mid
    return jnp.concatenate([high, mid, low, jnp.zeros_like(high)], axis=0).astype(BF16)


def unstack(sums):
    return (sums[0:8] + sums[8:16]) + sums[16:24]


def image_features(pooled_ref, gain):
    rows = pooled_ref[...]
    pooled = jnp.concatenate([rows] * 4, axis=0)
    feat_n, feat_s = norm_parts(pooled)
    features = feat_n * gain
    feat_len = jnp.sqrt(jnp.sum(features * features, axis=-1, keepdims=True) + EPS)
    return feat_n, feat_s, feat_len, features / feat_len


def pack_kernel(ids_ref, text_ref, pooled_ref, gain_ref, pack_ref, unit_ref, len_ref):
    text = text_ref[...].astype(F32)
    length = jnp.sqrt(jnp.sum(text * text, axis=-1, keepdims=True) + EPS)
    unit = text / length
    unit_ref[...] = unit
    len_ref[...] = jnp.broadcast_to(length, len_ref.shape)
    row = lax.broadcasted_iota(jnp.int32, (2, 128), 0)
    lane = lax.broadcasted_iota(jnp.int32, (2, 128), 1)
    ids = jnp.where(row == 0, ids_ref[0], ids_ref[1])
    ids = jnp.where(lane == 0, ids, 0).astype(F32)
    img_emb = image_features(pooled_ref, gain_ref[...][None, :])[3][0:2]
    packed = jnp.concatenate([unit, ids, img_emb], axis=1).astype(BF16)
    for copy in range(pack_ref.shape[0]):
        pack_ref[copy] = packed


def pack(pair_ids, text_feats, pooled, head_gain, copies):
    width = text_feats.shape[1]
    return pl.pallas_call(
        pack_kernel,
        in_specs=[SMEM] + [VMEM] * 3,
        out_shape=[
            jax.ShapeDtypeStruct((copies, 2, 2 * width + 128), BF16),
            jax.ShapeDtypeStruct((2, width), F32),
            jax.ShapeDtypeStruct((2, 128), F32),
        ],
        compiler_params=SMALL,
        cost_estimate=pl.CostEstimate(
            flops=30_000_000_000, bytes_accessed=100_000, transcendentals=0
        ),
        name="pack",
    )(pair_ids, text_feats, pooled, head_gain)


def forward_kernel(
    n_tensor, x_ref, gain_ref, bias_ref, b_down_ref, up_hbm, down_hbm,
    slope_ref, part_ref, up_ref, down_ref, act_sum, x_sum, sems,
):
    step = pl.program_id(0)
    image = step // 2
    up_copy = pltpu.make_async_copy(up_hbm, up_ref, sems.at[0])
    down_copy = pltpu.make_async_copy(down_hbm, down_ref, sems.at[1])

    @pl.when(step == 0)
    def _():
        up_copy.start()
        act_sum[...] = jnp.zeros_like(act_sum)
        x_sum[...] = jnp.zeros_like(x_sum)

    x = x_ref[...].astype(F32)
    normed, _ = norm_parts(x)
    normed = (normed * gain_ref[...][None, :]).astype(BF16)

    @pl.when(step == 0)
    def _():
        up_copy.wait()
        down_copy.start()

    pre = lax.dot_general(normed, up_ref[...], LAST, preferred_element_type=F32)
    pre = pre + bias_ref[...][None, :]
    root = math.sqrt(2.0 / math.pi)
    square = pre * pre
    tanh = jnp.tanh(root * (pre + 0.044715 * (square * pre)))
    half = 0.5 * (1.0 + tanh)
    act = (pre * half).astype(BF16).astype(F32)
    slope_ref[...] = half + (0.5 * root) * pre * (1.0 - tanh * tanh) * (
        1.0 + (3.0 * 0.044715) * square
    )

    def add(total, values):
        row = lax.broadcasted_iota(jnp.int32, total.shape, 0)
        sums = jnp.sum(values, axis=0, keepdims=True)
        total[...] += jnp.where(row == image, sums, 0.0)

    add(act_sum, act)
    add(x_sum, x)

    @pl.when(step == pl.num_programs(0) - 1)
    def _():
        down_copy.wait()
        stack = split_stack(act_sum[...] * (1.0 / PATCHES))
        mlp = unstack(jnp.dot(stack, down_ref[...], preferred_element_type=F32))
        rest = x_sum[...] * (1.0 / PATCHES) + b_down_ref[...][None, :]
        part_ref[...] = (mlp + rest * (1.0 / n_tensor))[0:2]


def forward(patches, ln_gain, up_t, b_up, w_down, b_down, n_tensor):
    tokens, width = patches.shape
    units = up_t.shape[0]
    rows = 128
    vector = lambda size: pl.BlockSpec((size,), lambda i: (0,))
    return pl.pallas_call(
        functools.partial(forward_kernel, n_tensor),
        grid=(tokens // rows,),
        in_specs=[
            pl.BlockSpec((rows, width), lambda i: (i, 0)),
            vector(width),
            vector(units),
            vector(width),
            HBM,
            HBM,
        ],
        out_specs=[
            pl.BlockSpec((rows, units), lambda i: (i, 0)),
            pl.BlockSpec((2, width), lambda i: (0, 0)),
        ],
        out_shape=[
            jax.ShapeDtypeStruct((tokens, units), F32),
            jax.ShapeDtypeStruct((2, width), F32),
        ],
        scratch_shapes=[
            pltpu.VMEM((units, width), BF16),
            pltpu.VMEM((units, width), BF16),
            pltpu.VMEM((8, units), F32),
            pltpu.VMEM((8, width), F32),
            pltpu.SemaphoreType.DMA((2,)),
        ],
        compiler_params=LARGE,
        cost_estimate=pl.CostEstimate(
            flops=2 * tokens * width * units,
            bytes_accessed=2 * tokens * width + 4 * units * width + 4 * tokens * units,
            transcendentals=tokens * units,
        ),
        name="forward",
    )(patches, ln_gain, b_up, b_down, up_t, w_down)


def pick_row(rows, index):
    row = lax.broadcasted_iota(jnp.int32, rows.shape, 0)
    return jnp.sum(jnp.where(row == index, rows, 0.0), axis=0, keepdims=True)


def pair_grad(queries, keys, ids_ref, id_columns, sharp, shift):
    batch = keys.shape[0]
    logits = sharp * unstack(
        lax.dot_general(split_stack(queries), keys, LAST, preferred_element_type=F32)
    ) + shift
    lane = lax.broadcasted_iota(jnp.int32, (16, 128), 1)
    first_lane = jnp.where(lane == 0, 1.0, 0.0).astype(BF16)
    ids = lax.dot_general(first_lane, id_columns, LAST, preferred_element_type=F32)[0:8]
    row = lax.broadcasted_iota(jnp.int32, (8, batch), 0)
    own = jnp.where(row == 0, ids_ref[0], ids_ref[1]).astype(F32)
    sign = jnp.where(ids == own, 1.0, -1.0)
    logit_grad = -LOSS_SCALE * sign * jax.nn.sigmoid(-sign * logits) / batch
    logit_grad = jnp.where(row < 2, logit_grad, 0.0)
    return sharp * unstack(
        jnp.dot(split_stack(logit_grad), keys, preferred_element_type=F32)
    )


def scalars(sharp_ref, shift_ref):
    return jnp.exp(jnp.full((8, 1), sharp_ref[0], F32)), shift_ref[0]


def loss_kernel(
    place_ref, sharp_ref, shift_ref, ids_ref, pooled_ref, gain_ref, rows_ref, down_ref,
    up_ref, slope_ref, hidden_ref, away_ref, keep_ref, g_pre,
):
    width = pooled_ref.shape[1]
    core, one, two = places(place_ref[0])
    gain = gain_ref[...][None, :]
    feat_n, feat_s, feat_len, img_emb = image_features(pooled_ref, gain)
    g_img = pair_grad(
        img_emb, rows_ref[:, 0:width], ids_ref, rows_ref[:, width : width + 128],
        *scalars(sharp_ref, shift_ref),
    )
    g_feat = (
        g_img - img_emb * jnp.sum(img_emb * g_img, axis=-1, keepdims=True)
    ) / feat_len
    g_hidden = norm_back(g_feat, gain, feat_n, feat_s) * (1.0 / PATCHES)
    hidden_ref[...] = g_hidden[0:2]
    g_rows = jnp.concatenate([g_hidden, jnp.zeros_like(g_hidden)], axis=0).astype(BF16)
    g_act = lax.dot_general(g_rows, down_ref[...], LAST, preferred_element_type=F32)[0:8]
    for image, blocks, out_ref in (
        (1 - core, order(two, one), away_ref),
        (core, order(one, two), keep_ref),
    ):
        row = pick_row(g_act, image)
        for spot, block in enumerate(blocks):
            start = pl.multiple_of(image * PATCHES + block * BLOCK, BLOCK)
            g_pre[spot * BLOCK : (spot + 1) * BLOCK, :] = (
                slope_ref[pl.ds(start, BLOCK), :] * row
            ).astype(BF16)
        out_ref[...] = jnp.dot(
            g_pre[...], up_ref[...], preferred_element_type=F32
        ).astype(BF16)


def loss_and_back(place, sharp, shift, ids, pooled, gain, rows, w_down, up_t, slope):
    units, width = up_t.shape
    return pl.pallas_call(
        loss_kernel,
        in_specs=[SMEM] * 4 + [VMEM] * 6,
        out_shape=[
            jax.ShapeDtypeStruct((2, width), F32),
            jax.ShapeDtypeStruct((PATCHES, width), BF16),
            jax.ShapeDtypeStruct((PATCHES, width), BF16),
        ],
        scratch_shapes=[pltpu.VMEM((PATCHES, units), BF16)],
        compiler_params=SMALL,
        cost_estimate=pl.CostEstimate(
            flops=4 * PATCHES * width * units,
            bytes_accessed=6 * units * width + 8 * PATCHES * units,
            transcendentals=0,
        ),
        name="loss_and_back",
    )(place, sharp, shift, ids, pooled, gain, rows, w_down, up_t, slope)


def text_kernel(sharp_ref, shift_ref, ids_ref, unit_ref, len_ref, rows_ref, out_ref):
    width = unit_ref.shape[1]
    unit = unit_ref[...]
    queries = jnp.concatenate([unit] * 4, axis=0).astype(BF16).astype(F32)
    g_text = pair_grad(
        queries, rows_ref[:, width + 128 :], ids_ref, rows_ref[:, width : width + 128],
        *scalars(sharp_ref, shift_ref),
    )[0:2]
    along = jnp.sum(unit * g_text, axis=-1, keepdims=True)
    out_ref[...] = (g_text - unit * along) / len_ref[:, 0:1]


def text_grad(sharp, shift, ids, unit, length, rows):
    return pl.pallas_call(
        text_kernel,
        in_specs=[SMEM] * 3 + [VMEM] * 3,
        out_shape=jax.ShapeDtypeStruct(unit.shape, F32),
        compiler_params=SMALL,
        cost_estimate=pl.CostEstimate(
            flops=1_000_000_000, bytes_accessed=600_000, transcendentals=0
        ),
        name="text_grad",
    )(sharp, shift, ids, unit, length, rows)


def finish_kernel(
    place_ref, keep_ref, other_ref, one_ref, two_ref, x_ref, hidden_ref, gain_ref, out_ref
):
    g_normed = keep_ref[...].astype(F32) + other_ref[...].astype(F32)
    g_normed = g_normed + one_ref[...].astype(F32) + two_ref[...].astype(F32)
    normed, inverse = norm_parts(x_ref[...].astype(F32))
    grad = norm_back(g_normed, gain_ref[...][None, :], normed, inverse)
    out_ref[...] = (grad + pick_row(hidden_ref[...], place_ref[0] & 1)).astype(BF16)


def finish(place, keep, other, got_one, got_two, patches, g_hidden, ln_gain):
    width = patches.shape[1]
    block = lambda index: pl.BlockSpec((BLOCK, width), index)

    def own_block(i, place):
        core, one, two = places(place[0])
        return core * (PATCHES // BLOCK) + 2 * one + two, 0

    return pl.pallas_call(
        finish_kernel,
        grid_spec=pltpu.PrefetchScalarGridSpec(
            num_scalar_prefetch=1,
            grid=(1,),
            in_specs=[
                block(lambda i, place: (3, 0)),
                block(lambda i, place: (3, 0)),
                block(lambda i, place: (1, 0)),
                block(lambda i, place: (0, 0)),
                block(own_block),
                pl.BlockSpec((2, width), lambda i, place: (0, 0)),
                pl.BlockSpec((width,), lambda i, place: (0,)),
            ],
            out_specs=block(lambda i, place: (0, 0)),
        ),
        out_shape=jax.ShapeDtypeStruct((BLOCK, width), BF16),
        compiler_params=SMALL,
        name="finish",
    )(place, keep, other, got_one, got_two, patches, g_hidden, ln_gain)


def place_kernel(place_ref, own, two, one, far, near, rest, out_ref):
    core, one_bit, two_bit = places(place_ref[0])
    low, high = slice(0, BLOCK), slice(BLOCK, 2 * BLOCK)
    mine, theirs = order(one_bit, two_bit), order(two_bit, one_bit)
    moves = [
        (far, low, core, mine[0]),
        (one, low, core, mine[1]),
        (two, low, core, mine[2]),
        (own, low, core, mine[3]),
        (rest, high, 1 - core, theirs[0]),
        (rest, low, 1 - core, theirs[1]),
        (near, high, 1 - core, theirs[2]),
        (near, low, 1 - core, theirs[3]),
    ]
    for ref, rows, image, block in moves:
        start = pl.multiple_of(image * PATCHES + block * BLOCK, BLOCK)
        out_ref[pl.ds(start, BLOCK), :] = ref[rows, :]


def put_in_place(place, pieces, tokens):
    width = pieces[0].shape[1]
    return pl.pallas_call(
        place_kernel,
        in_specs=[SMEM] + [VMEM] * 6,
        out_shape=jax.ShapeDtypeStruct((tokens, width), BF16),
        compiler_params=SMALL,
        name="put_in_place",
    )(place, *pieces)


def swap(value, axis, partner):
    size = lax.axis_size(axis)
    return lax.ppermute(value, axis, [(i, partner(i)) for i in range(size)])


def swap_core(value):
    return swap(value, "tensor", lambda i: i ^ 1)


def step_one(i):
    return i ^ 2 if i % 2 == 0 else (3 - i // 2) * 2 + 1


def step_two(i):
    return (3 - i // 2) * 2 if i % 2 == 0 else i ^ 2


def exchange(copies, groups):
    return lax.all_to_all(
        copies, "dp", split_axis=0, concat_axis=0, axis_index_groups=groups
    )


def spread(rows, groups):
    copies = jnp.broadcast_to(rows[None], (len(groups[0]),) + rows.shape)
    return exchange(copies, groups)


def on_device(
    patches,
    ln_gain,
    w_up,
    b_up,
    w_down,
    b_down,
    head_gain,
    text_feats,
    pair_ids,
    log_sharpness,
    pairwise_logit_shift,
):
    batch = text_feats.shape[0] * lax.axis_size("dp")
    place = lax.axis_index("tensor").astype(jnp.int32).reshape(1)

    up_t = w_up.T
    slope, part = forward(
        patches, ln_gain, up_t, b_up, w_down, b_down, lax.axis_size("tensor")
    )
    pooled = part + swap_core(part)
    pooled = pooled + swap(pooled, "tensor", step_one)
    pooled = pooled + swap(pooled, "tensor", step_two)

    side = math.isqrt(lax.axis_size("dp"))
    along_y = [[y * side + k for y in range(side)] for k in range(side)]
    along_xz = [[y * side + k for k in range(side)] for y in range(side)]
    packed, unit_text, text_len = pack(pair_ids, text_feats, pooled, head_gain, side)
    some_rows = exchange(packed, along_y).reshape(2 * side, -1)
    rows = spread(some_rows, along_xz).reshape(batch, -1)

    g_hidden, away, keep = loss_and_back(
        place,
        log_sharpness,
        pairwise_logit_shift,
        pair_ids,
        pooled,
        head_gain,
        rows,
        w_down,
        up_t,
        slope,
    )

    other = swap_core(away)

    def both(start, count):
        rows = slice(start, start + count)
        return keep[rows].astype(F32) + other[rows].astype(F32)

    send_one = both(0, 128).astype(BF16)
    got_one = swap(send_one, "tensor", step_one)
    send_two = (both(128, 64) + got_one[:64].astype(F32)).astype(BF16)
    got_two = swap(send_two, "tensor", step_two)
    done = finish(place, keep, other, got_one, got_two, patches, g_hidden, ln_gain)

    from_two = swap(done, "tensor", step_two)
    from_one = swap(done, "tensor", step_one)
    far = swap(from_two, "tensor", step_one)
    near = swap_core(jnp.concatenate([done, from_two]))
    rest = swap_core(jnp.concatenate([from_one, far]))
    grad_patches = put_in_place(
        place, (done, from_two, from_one, far, near, rest), patches.shape[0]
    )

    rows, _ = lax.optimization_barrier((rows, send_one))
    grad_text = text_grad(
        log_sharpness, pairwise_logit_shift, pair_ids, unit_text, text_len, rows
    )
    return grad_patches, grad_text


def solution(mesh):
    in_specs = (
        P("dp", None),
        P(),
        P(None, "tensor"),
        P("tensor"),
        P("tensor", None),
        P(),
        P(),
        P("dp", None),
        P("dp"),
        P(),
        P(),
    )
    out_specs = (P("dp", None), P("dp", None))
    return jax.shard_map(
        on_device, mesh=mesh, in_specs=in_specs, out_specs=out_specs, check_vma=False
    )
```

time: 118 us -> 123 us (1.042)
  waiting for transfers between devices: 5.07 us -> 27.2 us
  blocking collectives: 21.3 us -> 13.9 us
  Pallas kernels: 19 us -> 14.1 us
  other arithmetic: 4.7 us -> 0.91 us
  starting transfers between devices: 59 us -> 61.6 us
  local copies, waits for them, and re-layouts: 4.53 us -> 2.26 us
    ppermute x9 -> x11, starting transfers between devices: 33.9 us -> 56.6 us  [swap(): return lax.ppermute(value, axis, [(i, partner(i)) for i in range(size)])]
    psum x1 -> x0, blocking collectives: 21.3 us -> none  [on_device(): pooled = lax.psum(part, 'tensor')]
    all_to_all x4 -> x1, starting transfers between devices: 25.1 us -> 5.01 us  [exchange(): lax.all_to_all(copies, 'dp', split_axis=0, concat_axis=0, axis_index_grou...]
    ppermute x9 -> x11, waiting for transfers between devices: 5.06 us -> 20.5 us  [swap(): return lax.ppermute(value, axis, [(i, partner(i)) for i in range(size)])]
    all_to_all x0 -> x1, blocking collectives: none -> 13.9 us  [exchange(): lax.all_to_all(copies, 'dp', split_axis=0, concat_axis=0, axis_index_grou...]
    all_to_all x4 -> x1, waiting for transfers between devices: 0.01 us -> 6.77 us  [exchange(): lax.all_to_all(copies, 'dp', split_axis=0, concat_axis=0, axis_index_grou...]
    pallas_call x3, Pallas kernels: 9.38 us -> 5.44 us  [the longest x1 2.92 us: loss_and_back(): pl.pallas_call(loss_kernel, in_specs=[SMEM] * 4 + [VMEM] * 6, out_shape=[...]
  transfers between devices with their start and end apart: 13 -> 12, of which waited for: 3 -> 8; matrix products, arithmetic and copies ran while one was open for 5% -> 0% of each run, Pallas kernels for 10% -> 1%
where the time goes in v4:
time: 123 us; the launch traced here: 122 us
  starting transfers between devices  61.6 us (50%)
  waiting for transfers between devices  27.2 us (22%)
  Pallas kernels  14.1 us (11%)
  blocking collectives  13.9 us (11%)
  local copies, waits for them, and re-layouts  2.26 us (2%)
  between operations  2.17 us (2%)
    ppermute x11, starting transfers between devices, swap(): return lax.ppermute(value, axis, [(i, partner(i)) for i in range(size)])  56.6 us
    ppermute x11, waiting for transfers between devices, swap(): return lax.ppermute(value, axis, [(i, partner(i)) for i in range(size)])  20.5 us
    all_to_all x1, blocking collectives, exchange(): lax.all_to_all(copies, 'dp', split_axis=0, concat_axis=0, axis_index_grou...  13.9 us
    pallas_call x1, Pallas kernels, forward(): pl.pallas_call(functools.partial(forward_kernel, n_tensor), grid=(tokens...  7.18 us
    all_to_all x1, waiting for transfers between devices, exchange(): lax.all_to_all(copies, 'dp', split_axis=0, concat_axis=0, axis_index_grou...  6.77 us
    all_to_all x1, starting transfers between devices, exchange(): lax.all_to_all(copies, 'dp', split_axis=0, concat_axis=0, axis_index_grou...  5.01 us
    pallas_call x1, Pallas kernels, loss_and_back(): pl.pallas_call(loss_kernel, in_specs=[SMEM] * 4 + [VMEM] * 6, out_shape=[...  2.92 us
  transfers between devices with their start and end apart: 12, of which 8 were waited for; matrix products, arithmetic and copies ran while one was open for 0% of the time, Pallas kernels for 1%

profile of v4, /device:TPU:1, one launch (start us, length us, event | category | flops | bytes accessed | tf_op | source)
XLA Modules:
  0.0 122.2 jit_solution(1166362547944472601)
XLA Ops:
  0.6 0.0 copy-start.5
  0.6 0.0 copy-start.6
  0.7 0.0 copy-start.7
  0.7 7.2 %forward.1 = (f32[512,538]{1,0:T(8,128)}, f32[2,1152]{1,0:T(2,128)}) custom-call(bf16[512,1152]{1,0:T(8,128)(2,1)} %x_ref.3, f32[1152]{0:T(1024)} %gain_ref.7, f32[538]{0:T(1024)} %bias_ref.1, f32[1152]{0:T(1024)} %b_down_ref.1, bf16[538,1152]{1,0:T(8,128)(2,1)} %bitcast.3, bf16[538,1152]{1,0:T(8,128)(2,1)} %down_ref.1), custom_call_target="tpu_custom_call" | custom-call | flops 634650624 | bytes 4760576 | tf_op jit(solution)/shard_map/forward/pallas_call | solution.py:163
  7.9 8.8 %collective-permute-start = (f32[2,1152]{1,0:T(2,128)}, f32[2,1152]{1,0:T(2,128)S(1)}, u32[]{:S(2)}, u32[]{:S(2)}) collective-permute-start(f32[2,1152]{1,0:T(2,128)} %get-tuple-element.11), channel_id=1, source_target_pairs={{0,1},{1,0},{2,3},{3,2},{4,5},{5,4},{6,7},{7,6},{8,9},{9,8},{10,11... | collective-permute-start | bytes 27656 | tf_op jit(solution)/shard_map/ppermute | solution.py:378
  16.6 1.0 collective-permute-done
  17.7 0.7 add.18
  18.4 5.3 %collective-permute-start.1 = (f32[2,1152]{1,0:T(2,128)S(1)}, f32[2,1152]{1,0:T(2,128)S(1)}, u32[]{:S(2)}, u32[]{:S(2)}) collective-permute-start(f32[2,1152]{1,0:T(2,128)S(1)} %add.18), channel_id=1, source_target_pairs={{0,2},{1,7},{2,0},{3,5},{4,6},{5,3},{6,4},{7,1},{8,10},{9,15},{10,... | collective-permute-start | bytes 27656 | tf_op jit(solution)/shard_map/ppermute | solution.py:378
  23.6 1.2 %collective-permute-done.1 = f32[2,1152]{1,0:T(2,128)S(1)} collective-permute-done((f32[2,1152]{1,0:T(2,128)S(1)}, f32[2,1152]{1,0:T(2,128)S(1)}, u32[]{:S(2)}, u32[]{:S(2)}) %collective-permute-start.1) | collective-permute-done | bytes 9248 | tf_op jit(solution)/shard_map/ppermute | solution.py:378
  24.9 2.0 %collective-permute-start.2 = (f32[2,1152]{1,0:T(2,128)S(1)}, f32[2,1152]{1,0:T(2,128)S(1)}, u32[]{:S(2)}, u32[]{:S(2)}) collective-permute-start(f32[2,1152]{1,0:T(2,128)S(1)} %add.19), channel_id=1, source_target_pairs={{0,6},{1,3},{2,4},{3,1},{4,2},{5,7},{6,0},{7,5},{8,14},{9,11},{10,... | collective-permute-start | bytes 27656 | tf_op jit(solution)/shard_map/ppermute | solution.py:378
  26.9 3.3 %collective-permute-done.2 = f32[2,1152]{1,0:T(2,128)S(1)} collective-permute-done((f32[2,1152]{1,0:T(2,128)S(1)}, f32[2,1152]{1,0:T(2,128)S(1)}, u32[]{:S(2)}, u32[]{:S(2)}) %collective-permute-start.2) | collective-permute-done | bytes 9248 | tf_op jit(solution)/shard_map/ppermute | solution.py:378
  30.2 0.0 copy-done.5
  30.2 0.0 copy-done.6
  30.2 0.0 copy-done.7
  30.2 0.0 copy-start.1
  30.2 0.8 pack.1
  31.1 0.0 copy-start
  31.1 13.9 %all_to_all.10 = bf16[8,2,2432]{2,1,0:T(2,128)(2,1)S(1)} all-to-all(bf16[8,2,2432]{2,1,0:T(2,128)(2,1)S(1)} %get-tuple-element.12), channel_id=1, replica_groups={{0,64,128,192,256,320,384,448},{8,72,136,200,264,328,392,456},{16,80,14..., dimensions={0} | all-to-all | bytes 155648 | tf_op jit(solution)/shard_map/all_to_all | solution.py:394
  45.0 0.9 broadcast_in_dim.8
  45.9 5.0 %all-to-all-start.1 = ((bf16[8,16,2432]{2,1,0:T(8,128)(2,1)}), bf16[8,16,2432]{2,1,0:T(8,128)(2,1)S(1)}, u32[]{:S(2)}, u32[]{:S(2)}) async-start(bf16[8,16,2432]{2,1,0:T(8,128)(2,1)} %broadcast_in_dim.8), calls=%async_computation.1 | async-start | bytes 1245184 | tf_op jit(solution)/shard_map/all_to_all | solution.py:394
  52.2 6.8 %all-to-all-done.1 = bf16[8,16,2432]{2,1,0:T(8,128)(2,1)S(1)} async-done(((bf16[8,16,2432]{2,1,0:T(8,128)(2,1)}), bf16[8,16,2432]{2,1,0:T(8,128)(2,1)S(1)}, u32[]{:S(2)}, u32[]{:S(2)}) %all-to-all-start.1) | async-done | bytes 622624 | tf_op jit(solution)/shard_map/all_to_all | solution.py:394
  59.0 0.0 copy-done.1
  59.0 0.0 copy-done
  59.0 0.0 copy-start.3
  59.0 1.3 %copy-done.3 = f32[512,538]{1,0:T(8,128)S(1)} copy-done((f32[512,538]{1,0:T(8,128)S(1)}, f32[512,538]{1,0:T(8,128)}, u32[]{:S(2)}) %copy-start.3) | copy-done | bytes 1101848
  60.3 2.9 %loss_and_back.1 = (f32[2,1152]{1,0:T(2,128)S(1)}, bf16[256,1152]{1,0:T(8,128)(2,1)S(1)}, bf16[256,1152]{1,0:T(8,128)(2,1)S(1)}) custom-call(s32[1]{0:T(128)} %bitcast.place_ref, f32[1]{0:T(128)S(6)} %copy.13.sharp_ref, f32[1]{0:T(128)S(6)} %copy.14.shift_ref, s32[2]{0:T(128)S(1)} %copy-done.6, f32[2,1152]{1,0:T(2,128)S(1)} %add.20.pooled_ref, ...), custom_call_target="tpu_custom_call" | custom-call | flops 634650624 | bytes 4820480 | tf_op jit(solution)/shard_map/loss_and_back/pallas_call | solution.py:262
  63.2 0.0 copy-start.2
  63.2 0.0 copy-start.4
  63.3 7.3 %collective-permute-start.3 = (bf16[256,1152]{1,0:T(8,128)(2,1)S(1)}, bf16[256,1152]{1,0:T(8,128)(2,1)S(1)}, u32[]{:S(2)}, u32[]{:S(2)}) collective-permute-start(bf16[256,1152]{1,0:T(8,128)(2,1)S(1)} %get-tuple-element.15), channel_id=1, source_target_pairs={{0,1},{1,0},{2,3},{3,2},{4,5},{5,4},{6,7},{7,6},{8,9},{9,8},{10,11... | collective-permute-start | bytes 1769480 | tf_op jit(solution)/shard_map/ppermute | solution.py:378
  70.5 1.6 %collective-permute-done.3.other_ref = bf16[256,1152]{1,0:T(8,128)(2,1)S(1)} collective-permute-done((bf16[256,1152]{1,0:T(8,128)(2,1)S(1)}, bf16[256,1152]{1,0:T(8,128)(2,1)S(1)}, u32[]{:S(2)}, u32[]{:S(2)}) %collective-permute-start.3) | collective-permute-done | bytes 589856 | tf_op jit(solution)/shard_map/ppermute | solution.py:378
  72.1 0.1 add_convert_fusion
  72.2 5.7 %collective-permute-start.4 = (bf16[128,1152]{1,0:T(8,128)(2,1)S(1)}, bf16[128,1152]{1,0:T(8,128)(2,1)S(1)}, u32[]{:S(2)}, u32[]{:S(2)}) collective-permute-start(bf16[128,1152]{1,0:T(8,128)(2,1)S(1)} %add_convert_fusion), channel_id=1, source_target_pairs={{0,2},{1,7},{2,0},{3,5},{4,6},{5,3},{6,4},{7,1},{8,10},{9,15},{10,... | collective-permute-start | bytes 884744 | tf_op jit(solution)/shard_map/ppermute | solution.py:378
  78.0 6.8 %collective-permute-done.4.one_ref = bf16[128,1152]{1,0:T(8,128)(2,1)S(1)} collective-permute-done((bf16[128,1152]{1,0:T(8,128)(2,1)S(1)}, bf16[128,1152]{1,0:T(8,128)(2,1)S(1)}, u32[]{:S(2)}, u32[]{:S(2)}) %collective-permute-start.4) | collective-permute-done | bytes 294944 | tf_op jit(solution)/shard_map/ppermute | solution.py:378
  84.8 0.1 add_convert_fusion.1
  84.8 2.6 %collective-permute-start.5 = (bf16[64,1152]{1,0:T(8,128)(2,1)S(1)}, bf16[64,1152]{1,0:T(8,128)(2,1)S(1)}, u32[]{:S(2)}, u32[]{:S(2)}) collective-permute-start(bf16[64,1152]{1,0:T(8,128)(2,1)S(1)} %add_convert_fusion.1), channel_id=1, source_target_pairs={{0,6},{1,3},{2,4},{3,1},{4,2},{5,7},{6,0},{7,5},{8,14},{9,11},{10,... | collective-permute-start | bytes 442376 | tf_op jit(solution)/shard_map/ppermute | solution.py:378
  87.5 6.0 %collective-permute-done.5.two_ref = bf16[64,1152]{1,0:T(8,128)(2,1)S(1)} collective-permute-done((bf16[64,1152]{1,0:T(8,128)(2,1)S(1)}, bf16[64,1152]{1,0:T(8,128)(2,1)S(1)}, u32[]{:S(2)}, u32[]{:S(2)}) %collective-permute-start.5) | collective-permute-done | bytes 147488 | tf_op jit(solution)/shard_map/ppermute | solution.py:378
  93.5 0.0 copy-done.2
  93.5 0.0 copy-done.4
  93.5 0.4 finish.1.own
  93.9 1.9 %collective-permute-start.6 = (bf16[64,1152]{1,0:T(8,128)(2,1)S(1)}, bf16[64,1152]{1,0:T(8,128)(2,1)S(1)}, u32[]{:S(2)}, u32[]{:S(2)}) collective-permute-start(bf16[64,1152]{1,0:T(8,128)(2,1)S(1)} %finish.1.own), channel_id=1, source_target_pairs={{0,6},{1,3},{2,4},{3,1},{4,2},{5,7},{6,0},{7,5},{8,14},{9,11},{10,... | collective-permute-start | bytes 442376 | tf_op jit(solution)/shard_map/ppermute | solution.py:378
  95.8 5.7 %collective-permute-start.7 = (bf16[64,1152]{1,0:T(8,128)(2,1)S(1)}, bf16[64,1152]{1,0:T(8,128)(2,1)S(1)}, u32[]{:S(2)}, u32[]{:S(2)}) collective-permute-start(bf16[64,1152]{1,0:T(8,128)(2,1)S(1)} %finish.1.own), channel_id=1, source_target_pairs={{0,2},{1,7},{2,0},{3,5},{4,6},{5,3},{6,4},{7,1},{8,10},{9,15},{10,... | collective-permute-start | bytes 442376 | tf_op jit(solution)/shard_map/ppermute | solution.py:378
  101.5 0.4 collective-permute-done.6.two
  101.9 5.7 %collective-permute-start.8 = (bf16[64,1152]{1,0:T(8,128)(2,1)S(1)}, bf16[64,1152]{1,0:T(8,128)(2,1)S(1)}, u32[]{:S(2)}, u32[]{:S(2)}) collective-permute-start(bf16[64,1152]{1,0:T(8,128)(2,1)S(1)} %collective-permute-done.6.two), channel_id=1, source_target_pairs={{0,2},{1,7},{2,0},{3,5},{4,6},{5,3},{6,4},{7,1},{8,10},{9,15},{10,... | collective-permute-start | bytes 442376 | tf_op jit(solution)/shard_map/ppermute | solution.py:378
  107.7 5.9 %collective-permute-start.9 = (bf16[128,1152]{1,0:T(8,128)(2,1)S(1)}, bf16[128,1152]{1,0:T(8,128)(2,1)S(1)}, u32[]{:S(2)}, u32[]{:S(2)}) collective-permute-start(bf16[128,1152]{1,0:T(8,128)(2,1)S(1)} %pad_maximum_fusion), channel_id=1, source_target_pairs={{0,1},{1,0},{2,3},{3,2},{4,5},{5,4},{6,7},{7,6},{8,9},{9,8},{10,11... | collective-permute-start | bytes 884744 | tf_op jit(solution)/shard_map/ppermute | solution.py:378
  113.5 0.0 collective-permute-done.7.one
  113.6 0.0 collective-permute-done.8.far
  113.6 5.8 %collective-permute-start.10 = (bf16[128,1152]{1,0:T(8,128)(2,1)S(1)}, bf16[128,1152]{1,0:T(8,128)(2,1)S(1)}, u32[]{:S(2)}, u32[]{:S(2)}) collective-permute-start(bf16[128,1152]{1,0:T(8,128)(2,1)S(1)} %pad_maximum_fusion.1), channel_id=1, source_target_pairs={{0,1},{1,0},{2,3},{3,2},{4,5},{5,4},{6,7},{7,6},{8,9},{9,8},{10,11... | collective-permute-start | bytes 884744 | tf_op jit(solution)/shard_map/ppermute | solution.py:378
  119.4 1.7 %text_grad.1 = f32[2,1152]{1,0:T(2,128)} custom-call(f32[1]{0:T(128)S(6)} %copy.13.sharp_ref, f32[1]{0:T(128)S(6)} %copy.14.shift_ref, s32[2]{0:T(128)S(1)} %copy-done.6, f32[2,1152]{1,0:T(2,128)S(1)} %get-tuple-element.17.unit_ref, f32[2,128]{1,0:T(2,128)S(1)} %get-tuple-element.18.len_ref, bf16[128,2432]{1,0:T(8,128)(2,1)S(1)} %bitcast.6), custom_call_target="tpu_custom_call" | custom-call | flops 1000000000 | bytes 600000 | tf_op jit(solution)/shard_map/text_grad/pallas_call | solution.py:294
  121.0 0.0 collective-permute-done.9.near
  121.0 0.0 collective-permute-done.10.rest
  121.1 1.1 put_in_place.1
  (5 shorter events, 0.1 us)
Async XLA Ops:
  0.6 29.5 %copy-start.5 = (f32[1152]{0:T(1024)S(1)}, f32[1152]{0:T(1024)}, u32[]{:S(2)}) copy-start(f32[1152]{0:T(1024)} %gain_ref.6) | copy-start | bytes 13828
  0.6 29.5 %copy-start.6 = (s32[2]{0:T(128)S(1)}, s32[2]{0:T(128)}, u32[]{:S(2)}) copy-start(s32[2]{0:T(128)} %ids_ref.5) | copy-start | bytes 28
  0.7 29.5 %copy-start.7 = (bf16[2,1152]{1,0:T(2,128)(2,1)S(1)}, bf16[2,1152]{1,0:T(2,128)(2,1)}, u32[]{:S(2)}) copy-start(bf16[2,1152]{1,0:T(2,128)(2,1)} %text_ref.1) | copy-start | bytes 13828
  7.9 9.8 %collective-permute-start = (f32[2,1152]{1,0:T(2,128)}, f32[2,1152]{1,0:T(2,128)S(1)}, u32[]{:S(2)}, u32[]{:S(2)}) collective-permute-start(f32[2,1152]{1,0:T(2,128)} %get-tuple-element.11), channel_id=1, source_target_pairs={{0,1},{1,0},{2,3},{3,2},{4,5},{5,4},{6,7},{7,6},{8,9},{9,8},{10,11... | collective-permute-start | bytes 27656 | tf_op jit(solution)/shard_map/ppermute | solution.py:378
  18.4 6.5 %collective-permute-start.1 = (f32[2,1152]{1,0:T(2,128)S(1)}, f32[2,1152]{1,0:T(2,128)S(1)}, u32[]{:S(2)}, u32[]{:S(2)}) collective-permute-start(f32[2,1152]{1,0:T(2,128)S(1)} %add.18), channel_id=1, source_target_pairs={{0,2},{1,7},{2,0},{3,5},{4,6},{5,3},{6,4},{7,1},{8,10},{9,15},{10,... | collective-permute-start | bytes 27656 | tf_op jit(solution)/shard_map/ppermute | solution.py:378
  24.9 5.3 %collective-permute-start.2 = (f32[2,1152]{1,0:T(2,128)S(1)}, f32[2,1152]{1,0:T(2,128)S(1)}, u32[]{:S(2)}, u32[]{:S(2)}) collective-permute-start(f32[2,1152]{1,0:T(2,128)S(1)} %add.19), channel_id=1, source_target_pairs={{0,6},{1,3},{2,4},{3,1},{4,2},{5,7},{6,0},{7,5},{8,14},{9,11},{10,... | collective-permute-start | bytes 27656 | tf_op jit(solution)/shard_map/ppermute | solution.py:378
  30.2 28.8 %copy-start.1 = (bf16[538,1152]{1,0:T(8,128)(2,1)S(1)}, bf16[538,1152]{1,0:T(8,128)(2,1)}, u32[]{:S(2)}) copy-start(bf16[538,1152]{1,0:T(8,128)(2,1)} %down_ref.1) | copy-start | bytes 3718660
  31.1 27.9 %copy-start = (bf16[1152,538]{0,1:T(8,128)(2,1)S(1)}, bf16[1152,538]{0,1:T(8,128)(2,1)}, u32[]{:S(2)}) copy-start(bf16[1152,538]{0,1:T(8,128)(2,1)} %param.13) | copy-start | bytes 3718660
  45.9 13.1 %all-to-all-start.1 = ((bf16[8,16,2432]{2,1,0:T(8,128)(2,1)}), bf16[8,16,2432]{2,1,0:T(8,128)(2,1)S(1)}, u32[]{:S(2)}, u32[]{:S(2)}) async-start(bf16[8,16,2432]{2,1,0:T(8,128)(2,1)} %broadcast_in_dim.8), calls=%async_computation.1 | async-start | bytes 1245184 | tf_op jit(solution)/shard_map/all_to_all | solution.py:394
  59.0 1.3 %copy-start.3 = (f32[512,538]{1,0:T(8,128)S(1)}, f32[512,538]{1,0:T(8,128)}, u32[]{:S(2)}) copy-start(f32[512,538]{1,0:T(8,128)} %get-tuple-element.13.slope_ref) | copy-start | bytes 3305476
  63.2 30.3 %copy-start.2 = (bf16[512,1152]{1,0:T(8,128)(2,1)S(1)}, bf16[512,1152]{1,0:T(8,128)(2,1)}, u32[]{:S(2)}) copy-start(bf16[512,1152]{1,0:T(8,128)(2,1)} %x_ref.3) | copy-start | bytes 3538948
  63.2 30.3 %copy-start.4 = (f32[1152]{0:T(1024)S(1)}, f32[1152]{0:T(1024)}, u32[]{:S(2)}) copy-start(f32[1152]{0:T(1024)} %gain_ref.7) | copy-start | bytes 13828
  63.3 8.9 %collective-permute-start.3 = (bf16[256,1152]{1,0:T(8,128)(2,1)S(1)}, bf16[256,1152]{1,0:T(8,128)(2,1)S(1)}, u32[]{:S(2)}, u32[]{:S(2)}) collective-permute-start(bf16[256,1152]{1,0:T(8,128)(2,1)S(1)} %get-tuple-element.15), channel_id=1, source_target_pairs={{0,1},{1,0},{2,3},{3,2},{4,5},{5,4},{6,7},{7,6},{8,9},{9,8},{10,11... | collective-permute-start | bytes 1769480 | tf_op jit(solution)/shard_map/ppermute | solution.py:378
  72.2 12.6 %collective-permute-start.4 = (bf16[128,1152]{1,0:T(8,128)(2,1)S(1)}, bf16[128,1152]{1,0:T(8,128)(2,1)S(1)}, u32[]{:S(2)}, u32[]{:S(2)}) collective-permute-start(bf16[128,1152]{1,0:T(8,128)(2,1)S(1)} %add_convert_fusion), channel_id=1, source_target_pairs={{0,2},{1,7},{2,0},{3,5},{4,6},{5,3},{6,4},{7,1},{8,10},{9,15},{10,... | collective-permute-start | bytes 884744 | tf_op jit(solution)/shard_map/ppermute | solution.py:378
  84.8 8.7 %collective-permute-start.5 = (bf16[64,1152]{1,0:T(8,128)(2,1)S(1)}, bf16[64,1152]{1,0:T(8,128)(2,1)S(1)}, u32[]{:S(2)}, u32[]{:S(2)}) collective-permute-start(bf16[64,1152]{1,0:T(8,128)(2,1)S(1)} %add_convert_fusion.1), channel_id=1, source_target_pairs={{0,6},{1,3},{2,4},{3,1},{4,2},{5,7},{6,0},{7,5},{8,14},{9,11},{10,... | collective-permute-start | bytes 442376 | tf_op jit(solution)/shard_map/ppermute | solution.py:378
  93.9 8.1 %collective-permute-start.6 = (bf16[64,1152]{1,0:T(8,128)(2,1)S(1)}, bf16[64,1152]{1,0:T(8,128)(2,1)S(1)}, u32[]{:S(2)}, u32[]{:S(2)}) collective-permute-start(bf16[64,1152]{1,0:T(8,128)(2,1)S(1)} %finish.1.own), channel_id=1, source_target_pairs={{0,6},{1,3},{2,4},{3,1},{4,2},{5,7},{6,0},{7,5},{8,14},{9,11},{10,... | collective-permute-start | bytes 442376 | tf_op jit(solution)/shard_map/ppermute | solution.py:378
  95.8 17.7 %collective-permute-start.7 = (bf16[64,1152]{1,0:T(8,128)(2,1)S(1)}, bf16[64,1152]{1,0:T(8,128)(2,1)S(1)}, u32[]{:S(2)}, u32[]{:S(2)}) collective-permute-start(bf16[64,1152]{1,0:T(8,128)(2,1)S(1)} %finish.1.own), channel_id=1, source_target_pairs={{0,2},{1,7},{2,0},{3,5},{4,6},{5,3},{6,4},{7,1},{8,10},{9,15},{10,... | collective-permute-start | bytes 442376 | tf_op jit(solution)/shard_map/ppermute | solution.py:378
  101.9 11.6 %collective-permute-start.8 = (bf16[64,1152]{1,0:T(8,128)(2,1)S(1)}, bf16[64,1152]{1,0:T(8,128)(2,1)S(1)}, u32[]{:S(2)}, u32[]{:S(2)}) collective-permute-start(bf16[64,1152]{1,0:T(8,128)(2,1)S(1)} %collective-permute-done.6.two), channel_id=1, source_target_pairs={{0,2},{1,7},{2,0},{3,5},{4,6},{5,3},{6,4},{7,1},{8,10},{9,15},{10,... | collective-permute-start | bytes 442376 | tf_op jit(solution)/shard_map/ppermute | solution.py:378
  107.7 13.4 %collective-permute-start.9 = (bf16[128,1152]{1,0:T(8,128)(2,1)S(1)}, bf16[128,1152]{1,0:T(8,128)(2,1)S(1)}, u32[]{:S(2)}, u32[]{:S(2)}) collective-permute-start(bf16[128,1152]{1,0:T(8,128)(2,1)S(1)} %pad_maximum_fusion), channel_id=1, source_target_pairs={{0,1},{1,0},{2,3},{3,2},{4,5},{5,4},{6,7},{7,6},{8,9},{9,8},{10,11... | collective-permute-start | bytes 884744 | tf_op jit(solution)/shard_map/ppermute | solution.py:378
  113.6 7.5 %collective-permute-start.10 = (bf16[128,1152]{1,0:T(8,128)(2,1)S(1)}, bf16[128,1152]{1,0:T(8,128)(2,1)S(1)}, u32[]{:S(2)}, u32[]{:S(2)}) collective-permute-start(bf16[128,1152]{1,0:T(8,128)(2,1)S(1)} %pad_maximum_fusion.1), channel_id=1, source_target_pairs={{0,1},{1,0},{2,3},{3,2},{4,5},{5,4},{6,7},{7,6},{8,9},{9,8},{10,11... | collective-permute-start | bytes 884744 | tf_op jit(solution)/shard_map/ppermute | solution.py:378

commit v5 on v4

--- a/solution.py
+++ b/solution.py
@@ -69,7 +69,7 @@
     return feat_n, feat_s, feat_len, features / feat_len
 
 
-def pack_kernel(ids_ref, text_ref, pooled_ref, gain_ref, pack_ref, unit_ref, len_ref):
+def pack_kernel(ids_ref, text_ref, pack_ref, unit_ref, len_ref):
     text = text_ref[...].astype(F32)
     length = jnp.sqrt(jnp.sum(text * text, axis=-1, keepdims=True) + EPS)
     unit = text / length
@@ -79,28 +79,24 @@
     lane = lax.broadcasted_iota(jnp.int32, (2, 128), 1)
     ids = jnp.where(row == 0, ids_ref[0], ids_ref[1])
     ids = jnp.where(lane == 0, ids, 0).astype(F32)
-    img_emb = image_features(pooled_ref, gain_ref[...][None, :])[3][0:2]
-    packed = jnp.concatenate([unit, ids, img_emb], axis=1).astype(BF16)
+    packed = jnp.concatenate([unit, ids], axis=1).astype(BF16)
     for copy in range(pack_ref.shape[0]):
         pack_ref[copy] = packed
 
 
-def pack(pair_ids, text_feats, pooled, head_gain, copies):
+def pack(pair_ids, text_feats, copies):
     width = text_feats.shape[1]
     return pl.pallas_call(
         pack_kernel,
-        in_specs=[SMEM] + [VMEM] * 3,
+        in_specs=[SMEM, VMEM],
         out_shape=[
-            jax.ShapeDtypeStruct((copies, 2, 2 * width + 128), BF16),
+            jax.ShapeDtypeStruct((copies, 2, width + 128), BF16),
             jax.ShapeDtypeStruct((2, width), F32),
             jax.ShapeDtypeStruct((2, 128), F32),
         ],
         compiler_params=SMALL,
-        cost_estimate=pl.CostEstimate(
-            flops=30_000_000_000, bytes_accessed=100_000, transcendentals=0
-        ),
         name="pack",
-    )(pair_ids, text_feats, pooled, head_gain)
+    )(pair_ids, text_feats)
 
 
 def forward_kernel(
@@ -109,12 +105,22 @@
 ):
     step = pl.program_id(0)
     image = step // 2
-    up_copy = pltpu.make_async_copy(up_hbm, up_ref, sems.at[0])
-    down_copy = pltpu.make_async_copy(down_hbm, down_ref, sems.at[1])
+    third = x_ref.shape[1] // 3
+
+    def copies(source, target, first):
+        parts = [pl.ds(part * third, third) for part in range(3)]
+        return [
+            pltpu.make_async_copy(source.at[:, part], target.at[:, part], sems.at[first + i])
+            for i, part in enumerate(parts)
+        ]
+
+    up_copies = copies(up_hbm, up_ref, 0)
+    down_copies = copies(down_hbm, down_ref, 3)
 
     @pl.when(step == 0)
     def _():
-        up_copy.start()
+        for copy in up_copies:
+            copy.start()
         act_sum[...] = jnp.zeros_like(act_sum)
         x_sum[...] = jnp.zeros_like(x_sum)
 
@@ -124,8 +130,10 @@
 
     @pl.when(step == 0)
     def _():
-        up_copy.wait()
-        down_copy.start()
+        for copy in up_copies:
+            copy.wait()
+        for copy in down_copies:
+            copy.start()
 
     pre = lax.dot_general(normed, up_ref[...], LAST, preferred_element_type=F32)
     pre = pre + bias_ref[...][None, :]
@@ -134,9 +142,10 @@
     tanh = jnp.tanh(root * (pre + 0.044715 * (square * pre)))
     half = 0.5 * (1.0 + tanh)
     act = (pre * half).astype(BF16).astype(F32)
-    slope_ref[...] = half + (0.5 * root) * pre * (1.0 - tanh * tanh) * (
+    slope = half + (0.5 * root) * pre * (1.0 - tanh * tanh) * (
         1.0 + (3.0 * 0.044715) * square
     )
+    slope_ref[...] = slope.astype(BF16)
 
     def add(total, values):
         row = lax.broadcasted_iota(jnp.int32, total.shape, 0)
@@ -148,7 +157,8 @@
 
     @pl.when(step == pl.num_programs(0) - 1)
     def _():
-        down_copy.wait()
+        for copy in down_copies:
+            copy.wait()
         stack = split_stack(act_sum[...] * (1.0 / PATCHES))
         mlp = unstack(jnp.dot(stack, down_ref[...], preferred_element_type=F32))
         rest = x_sum[...] * (1.0 / PATCHES) + b_down_ref[...][None, :]
@@ -176,7 +186,7 @@
             pl.BlockSpec((2, width), lambda i: (0, 0)),
         ],
         out_shape=[
-            jax.ShapeDtypeStruct((tokens, units), F32),
+            jax.ShapeDtypeStruct((tokens, units), BF16),
             jax.ShapeDtypeStruct((2, width), F32),
         ],
         scratch_shapes=[
@@ -184,7 +194,7 @@
             pltpu.VMEM((units, width), BF16),
             pltpu.VMEM((8, units), F32),
             pltpu.VMEM((8, width), F32),
-            pltpu.SemaphoreType.DMA((2,)),
+            pltpu.SemaphoreType.DMA((6,)),
         ],
         compiler_params=LARGE,
         cost_estimate=pl.CostEstimate(
@@ -199,6 +209,13 @@
 def pick_row(rows, index):
     row = lax.broadcasted_iota(jnp.int32, rows.shape, 0)
     return jnp.sum(jnp.where(row == index, rows, 0.0), axis=0, keepdims=True)
+
+
+def image_features(rows, gain):
+    feat_n, feat_s = norm_parts(jnp.concatenate([rows] * 4, axis=0))
+    features = feat_n * gain
+    feat_len = jnp.sqrt(jnp.sum(features * features, axis=-1, keepdims=True) + EPS)
+    return feat_n, feat_s, feat_len, features / feat_len
 
 
 def pair_grad(queries, keys, ids_ref, id_columns, sharp, shift):
@@ -225,12 +242,14 @@
 
 def loss_kernel(
     place_ref, sharp_ref, shift_ref, ids_ref, pooled_ref, gain_ref, rows_ref, down_ref,
-    up_ref, slope_ref, hidden_ref, away_ref, keep_ref, g_pre,
+    up_ref, slope_ref, img_ref, hidden_ref, away_ref, keep_ref, g_pre,
 ):
-    width = pooled_ref.shape[1]
+    width = gain_ref.shape[0]
     core, one, two = places(place_ref[0])
     gain = gain_ref[...][None, :]
-    feat_n, feat_s, feat_len, img_emb = image_features(pooled_ref, gain)
+    feat_n, feat_s, feat_len, img_emb = image_features(pooled_ref[...], gain)
+    for copy in range(img_ref.shape[0]):
+        img_ref[copy] = img_emb[0:2].astype(BF16)
     g_img = pair_grad(
         img_emb, rows_ref[:, 0:width], ids_ref, rows_ref[:, width : width + 128],
         *scalars(sharp_ref, shift_ref),
@@ -250,19 +269,22 @@
         for spot, block in enumerate(blocks):
             start = pl.multiple_of(image * PATCHES + block * BLOCK, BLOCK)
             g_pre[spot * BLOCK : (spot + 1) * BLOCK, :] = (
-                slope_ref[pl.ds(start, BLOCK), :] * row
+                slope_ref[pl.ds(start, BLOCK), :].astype(F32) * row
             ).astype(BF16)
         out_ref[...] = jnp.dot(
             g_pre[...], up_ref[...], preferred_element_type=F32
         ).astype(BF16)
 
 
-def loss_and_back(place, sharp, shift, ids, pooled, gain, rows, w_down, up_t, slope):
+def loss_and_back(
+    place, sharp, shift, ids, pooled, gain, rows, w_down, up_t, slope, copies
+):
     units, width = up_t.shape
     return pl.pallas_call(
         loss_kernel,
         in_specs=[SMEM] * 4 + [VMEM] * 6,
         out_shape=[
+            jax.ShapeDtypeStruct((copies, 2, width), BF16),
             jax.ShapeDtypeStruct((2, width), F32),
             jax.ShapeDtypeStruct((PATCHES, width), BF16),
             jax.ShapeDtypeStruct((PATCHES, width), BF16),
@@ -278,29 +300,31 @@
     )(place, sharp, shift, ids, pooled, gain, rows, w_down, up_t, slope)
 
 
-def text_kernel(sharp_ref, shift_ref, ids_ref, unit_ref, len_ref, rows_ref, out_ref):
+def text_kernel(
+    sharp_ref, shift_ref, ids_ref, unit_ref, len_ref, img_ref, rows_ref, out_ref
+):
     width = unit_ref.shape[1]
     unit = unit_ref[...]
     queries = jnp.concatenate([unit] * 4, axis=0).astype(BF16).astype(F32)
     g_text = pair_grad(
-        queries, rows_ref[:, width + 128 :], ids_ref, rows_ref[:, width : width + 128],
+        queries, img_ref[...], ids_ref, rows_ref[:, width : width + 128],
         *scalars(sharp_ref, shift_ref),
     )[0:2]
     along = jnp.sum(unit * g_text, axis=-1, keepdims=True)
     out_ref[...] = (g_text - unit * along) / len_ref[:, 0:1]
 
 
-def text_grad(sharp, shift, ids, unit, length, rows):
+def text_grad(sharp, shift, ids, unit, length, images, rows):
     return pl.pallas_call(
         text_kernel,
-        in_specs=[SMEM] * 3 + [VMEM] * 3,
+        in_specs=[SMEM] * 3 + [VMEM] * 4,
         out_shape=jax.ShapeDtypeStruct(unit.shape, F32),
         compiler_params=SMALL,
         cost_estimate=pl.CostEstimate(
             flops=1_000_000_000, bytes_accessed=600_000, transcendentals=0
         ),
         name="text_grad",
-    )(sharp, shift, ids, unit, length, rows)
+    )(sharp, shift, ids, unit, length, images, rows)
 
 
 def finish_kernel(
@@ -417,22 +441,20 @@
     batch = text_feats.shape[0] * lax.axis_size("dp")
     place = lax.axis_index("tensor").astype(jnp.int32).reshape(1)
 
+    side = math.isqrt(lax.axis_size("dp"))
+    along_y = [[y * side + k for y in range(side)] for k in range(side)]
+    along_xz = [[y * side + k for k in range(side)] for y in range(side)]
+    packed, unit_text, text_len = pack(pair_ids, text_feats, side)
+    some_text = exchange(packed, along_y).reshape(2 * side, -1)
+
     up_t = w_up.T
     slope, part = forward(
         patches, ln_gain, up_t, b_up, w_down, b_down, lax.axis_size("tensor")
     )
-    pooled = part + swap_core(part)
-    pooled = pooled + swap(pooled, "tensor", step_one)
-    pooled = pooled + swap(pooled, "tensor", step_two)
-
-    side = math.isqrt(lax.axis_size("dp"))
-    along_y = [[y * side + k for y in range(side)] for k in range(side)]
-    along_xz = [[y * side + k for k in range(side)] for y in range(side)]
-    packed, unit_text, text_len = pack(pair_ids, text_feats, pooled, head_gain, side)
-    some_rows = exchange(packed, along_y).reshape(2 * side, -1)
-    rows = spread(some_rows, along_xz).reshape(batch, -1)
-
-    g_hidden, away, keep = loss_and_back(
+    some_text, part = lax.optimization_barrier((some_text, part))
+    rows = spread(some_text, along_xz).reshape(batch, -1)
+    pooled = lax.psum(part, "tensor")
+    img_copies, g_hidden, away, keep = loss_and_back(
         place,
         log_sharpness,
         pairwise_logit_shift,
@@ -443,32 +465,43 @@
         w_down,
         up_t,
         slope,
+        side,
     )
 
     other = swap_core(away)
 
     def both(start, count):
-        rows = slice(start, start + count)
-        return keep[rows].astype(F32) + other[rows].astype(F32)
+        part = slice(start, start + count)
+        return keep[part].astype(F32) + other[part].astype(F32)
 
     send_one = both(0, 128).astype(BF16)
     got_one = swap(send_one, "tensor", step_one)
+    img_copies, _ = lax.optimization_barrier((img_copies, send_one))
+    some_img = exchange(img_copies, along_y).reshape(2 * side, -1)
+    got_one, some_img = lax.optimization_barrier((got_one, some_img))
     send_two = (both(128, 64) + got_one[:64].astype(F32)).astype(BF16)
     got_two = swap(send_two, "tensor", step_two)
+    images = spread(some_img, along_xz).reshape(batch, -1)
     done = finish(place, keep, other, got_one, got_two, patches, g_hidden, ln_gain)
 
     from_two = swap(done, "tensor", step_two)
     from_one = swap(done, "tensor", step_one)
     far = swap(from_two, "tensor", step_one)
     near = swap_core(jnp.concatenate([done, from_two]))
+    from_one, images = lax.optimization_barrier((from_one, images))
     rest = swap_core(jnp.concatenate([from_one, far]))
     grad_patches = put_in_place(
         place, (done, from_two, from_one, far, near, rest), patches.shape[0]
     )
 
-    rows, _ = lax.optimization_barrier((rows, send_one))
     grad_text = text_grad(
-        log_sharpness, pairwise_logit_shift, pair_ids, unit_text, text_len, rows
+        log_sharpness,
+        pairwise_logit_shift,
+        pair_ids,
+        unit_text,
+        text_len,
+        images,
+        rows,
     )
     return grad_patches, grad_text
 

time: 123 us -> 115 us (0.935)
  the two profiles are of different devices: /device:TPU:1 before, /device:TPU:5 now
where the time goes in v5:
time: 115 us
  starting transfers between devices  57.1 us (50%)
  blocking collectives  34.3 us (30%)
  Pallas kernels  15.2 us (13%)
  local copies, waits for them, and re-layouts  3.96 us (3%)
  between operations  2.2 us (2%)
  waiting for transfers between devices  1.63 us (1%)
    ppermute x8, starting transfers between devices, swap(): return lax.ppermute(value, axis, [(i, partner(i)) for i in range(size)])  39.3 us
    psum x1, blocking collectives, on_device(): pooled = lax.psum(part, 'tensor')  20.8 us
    all_to_all x3, starting transfers between devices, exchange(): lax.all_to_all(copies, 'dp', split_axis=0, concat_axis=0, axis_index_grou...  17.8 us
    all_to_all x1, blocking collectives, exchange(): lax.all_to_all(copies, 'dp', split_axis=0, concat_axis=0, axis_index_grou...  13.5 us
    pallas_call x1, Pallas kernels, forward(): pl.pallas_call(functools.partial(forward_kernel, n_tensor), grid=(tokens...  7.34 us
    pallas_call x1, Pallas kernels, loss_and_back(): pl.pallas_call(loss_kernel, in_specs=[SMEM] * 4 + [VMEM] * 6, out_shape=[...  2.96 us
    unnamed x18, local copies, waits for them, and re-layouts  2.45 us
  transfers between devices with their start and end apart: 11, of which 1 were waited for; matrix products, arithmetic and copies ran while one was open for 1% of the time, Pallas kernels for 9%

profile of v5, /device:TPU:5, one launch (start us, length us, event | category | flops | bytes accessed | tf_op | source)
XLA Modules:
  0.0 114.6 jit_solution(10783508958468371354)
XLA Ops:
  0.6 0.0 copy-start.6
  0.6 0.7 copy-done.6
  1.3 0.0 copy-start.7
  1.3 0.7 copy-done.7
  2.0 1.3 %pack.1 = (bf16[8,2,1280]{2,1,0:T(2,128)(2,1)}, f32[2,1152]{1,0:T(2,128)S(1)}, f32[2,128]{1,0:T(2,128)S(1)}) custom-call(s32[2]{0:T(128)S(1)} %copy-done.7, bf16[2,1152]{1,0:T(2,128)(2,1)S(1)} %copy-done.6), custom_call_target="tpu_custom_call" | custom-call | tf_op jit(solution)/shard_map/pack/pallas_call | solution.py:89
  3.2 6.8 %all-to-all-start = ((bf16[8,2,1280]{2,1,0:T(2,128)(2,1)}), bf16[8,2,1280]{2,1,0:T(2,128)(2,1)S(1)}, u32[]{:S(2)}, u32[]{:S(2)}) async-start(bf16[8,2,1280]{2,1,0:T(2,128)(2,1)} %get-tuple-element.18), calls=%async_computation | async-start | bytes 81920 | tf_op jit(solution)/shard_map/all_to_all | solution.py:418
  10.1 0.0 copy-start
  10.1 0.0 copy-start.1
  10.1 0.0 copy-start.5
  10.1 0.0 copy-start.8
  10.1 7.3 %forward.1 = (bf16[512,538]{1,0:T(8,128)(2,1)}, f32[2,1152]{1,0:T(2,128)}) custom-call(bf16[512,1152]{1,0:T(8,128)(2,1)} %x_ref.3, f32[1152]{0:T(1024)} %gain_ref.5, f32[538]{0:T(1024)} %bias_ref.1, f32[1152]{0:T(1024)} %b_down_ref.1, bf16[538,1152]{1,0:T(8,128)(2,1)} %bitcast.4, bf16[538,1152]{1,0:T(8,128)(2,1)} %down_ref.1), custom_call_target="tpu_custom_call" | custom-call | flops 634650624 | bytes 4760576 | tf_op jit(solution)/shard_map/forward/pallas_call | solution.py:173
  17.5 0.0 all-to-all-done
  17.5 0.7 broadcast_in_dim.4
  18.2 6.1 %all-to-all-start.1 = ((bf16[8,16,1280]{2,1,0:T(8,128)(2,1)}), bf16[8,16,1280]{2,1,0:T(8,128)(2,1)S(1)}, u32[]{:S(2)}, u32[]{:S(2)}) async-start(bf16[8,16,1280]{2,1,0:T(8,128)(2,1)} %broadcast_in_dim.4), calls=%async_computation.1 | async-start | bytes 655360 | tf_op jit(solution)/shard_map/all_to_all | solution.py:418
  25.6 20.8 %psum.7.pooled_ref = f32[2,1152]{1,0:T(2,128)S(1)} all-reduce(f32[2,1152]{1,0:T(2,128)} %get-tuple-element.20), channel_id=1, replica_groups=mesh['dp'=64,'tensor'=8] {'tensor'}, use_global_device_ids=true, to_apply=%region_0.0 | all-reduce | flops 2304 | bytes 18432 | tf_op jit(solution)/shard_map/psum | solution.py:456
  46.4 0.0 all-to-all-done.1
  46.4 0.0 copy-done
  46.5 0.0 copy-done.1
  46.5 0.0 copy-done.5
  46.5 0.0 copy-done.8
  46.5 0.0 copy-start.3
  46.5 1.1 copy-done.3
  47.6 3.0 %loss_and_back.1 = (bf16[8,2,1152]{2,1,0:T(2,128)(2,1)S(1)}, f32[2,1152]{1,0:T(2,128)S(1)}, bf16[256,1152]{1,0:T(8,128)(2,1)S(1)}, bf16[256,1152]{1,0:T(8,128)(2,1)S(1)}) custom-call(s32[1]{0:T(128)} %bitcast.place_ref, f32[1]{0:T(128)S(6)} %copy.13.sharp_ref, f32[1]{0:T(128)S(6)} %copy.14.shift_ref, s32[2]{0:T(128)S(1)} %copy-done.8, ...), custom_call_target="tpu_custom_call" | custom-call | flops 634650624 | bytes 4820480 | tf_op jit(solution)/shard_map/loss_and_back/pallas_call | solution.py:283
  50.5 4.1 %collective-permute-start = (bf16[256,1152]{1,0:T(8,128)(2,1)S(1)}, bf16[256,1152]{1,0:T(8,128)(2,1)S(1)}, u32[]{:S(2)}, u32[]{:S(2)}) collective-permute-start(bf16[256,1152]{1,0:T(8,128)(2,1)S(1)} %get-tuple-element.24), channel_id=1, source_target_pairs={{0,1},{1,0},{2,3},{3,2},{4,5},{5,4},{6,7},{7,6},{8,9},{9,8},{10,11... | collective-permute-start | bytes 1769480 | tf_op jit(solution)/shard_map/ppermute | solution.py:402
  54.7 1.6 %collective-permute-done.other_ref = bf16[256,1152]{1,0:T(8,128)(2,1)S(1)} collective-permute-done((bf16[256,1152]{1,0:T(8,128)(2,1)S(1)}, bf16[256,1152]{1,0:T(8,128)(2,1)S(1)}, u32[]{:S(2)}, u32[]{:S(2)}) %collective-permute-start) | collective-permute-done | bytes 589856 | tf_op jit(solution)/shard_map/ppermute | solution.py:402
  56.3 0.0 copy-start.2
  56.3 0.0 copy-start.4
  56.3 0.1 add_convert_fusion
  56.4 2.1 %collective-permute-start.1 = (bf16[128,1152]{1,0:T(8,128)(2,1)S(1)}, bf16[128,1152]{1,0:T(8,128)(2,1)S(1)}, u32[]{:S(2)}, u32[]{:S(2)}) collective-permute-start(bf16[128,1152]{1,0:T(8,128)(2,1)S(1)} %add_convert_fusion), channel_id=1, source_target_pairs={{0,2},{1,7},{2,0},{3,5},{4,6},{5,3},{6,4},{7,1},{8,10},{9,15},{10,... | collective-permute-start | bytes 884744 | tf_op jit(solution)/shard_map/ppermute | solution.py:402
  58.4 13.5 %all_to_all.20 = bf16[8,2,1152]{2,1,0:T(2,128)(2,1)S(1)} all-to-all(bf16[8,2,1152]{2,1,0:T(2,128)(2,1)S(1)} %get-tuple-element.26), channel_id=1, replica_groups={{0,64,128,192,256,320,384,448},{8,72,136,200,264,328,392,456},{16,80,14..., dimensions={0} | all-to-all | bytes 73728 | tf_op jit(solution)/shard_map/all_to_all | solution.py:418
  72.0 0.0 collective-permute-done.1.one_ref
  72.0 0.1 add_convert_fusion.1
  72.1 3.6 %collective-permute-start.2 = (bf16[64,1152]{1,0:T(8,128)(2,1)S(1)}, bf16[64,1152]{1,0:T(8,128)(2,1)S(1)}, u32[]{:S(2)}, u32[]{:S(2)}) collective-permute-start(bf16[64,1152]{1,0:T(8,128)(2,1)S(1)} %add_convert_fusion.1), channel_id=1, source_target_pairs={{0,6},{1,3},{2,4},{3,1},{4,2},{5,7},{6,0},{7,5},{8,14},{9,11},{10,... | collective-permute-start | bytes 442376 | tf_op jit(solution)/shard_map/ppermute | solution.py:402
  75.7 0.7 broadcast_in_dim.5
  76.4 4.9 %all-to-all-start.3 = ((bf16[8,16,1152]{2,1,0:T(8,128)(2,1)}), bf16[8,16,1152]{2,1,0:T(8,128)(2,1)}, u32[]{:S(2)}, u32[]{:S(2)}) async-start(bf16[8,16,1152]{2,1,0:T(8,128)(2,1)} %broadcast_in_dim.5), calls=%async_computation.3 | async-start | bytes 589824 | tf_op jit(solution)/shard_map/all_to_all | solution.py:418
  81.4 0.0 collective-permute-done.2.two_ref
  81.4 0.0 copy-done.2
  81.4 0.0 copy-done.4
  81.4 0.4 finish.1.own
  81.7 2.9 %collective-permute-start.3 = (bf16[64,1152]{1,0:T(8,128)(2,1)S(1)}, bf16[64,1152]{1,0:T(8,128)(2,1)S(1)}, u32[]{:S(2)}, u32[]{:S(2)}) collective-permute-start(bf16[64,1152]{1,0:T(8,128)(2,1)S(1)} %finish.1.own), channel_id=1, source_target_pairs={{0,6},{1,3},{2,4},{3,1},{4,2},{5,7},{6,0},{7,5},{8,14},{9,11},{10,... | collective-permute-start | bytes 442376 | tf_op jit(solution)/shard_map/ppermute | solution.py:402
  84.6 5.4 %collective-permute-start.4 = (bf16[64,1152]{1,0:T(8,128)(2,1)S(1)}, bf16[64,1152]{1,0:T(8,128)(2,1)S(1)}, u32[]{:S(2)}, u32[]{:S(2)}) collective-permute-start(bf16[64,1152]{1,0:T(8,128)(2,1)S(1)} %finish.1.own), channel_id=1, source_target_pairs={{0,2},{1,7},{2,0},{3,5},{4,6},{5,3},{6,4},{7,1},{8,10},{9,15},{10,... | collective-permute-start | bytes 442376 | tf_op jit(solution)/shard_map/ppermute | solution.py:402
  90.1 0.0 collective-permute-done.3.two
  90.1 3.6 %collective-permute-start.5 = (bf16[64,1152]{1,0:T(8,128)(2,1)S(1)}, bf16[64,1152]{1,0:T(8,128)(2,1)S(1)}, u32[]{:S(2)}, u32[]{:S(2)}) collective-permute-start(bf16[64,1152]{1,0:T(8,128)(2,1)S(1)} %collective-permute-done.3.two), channel_id=1, source_target_pairs={{0,2},{1,7},{2,0},{3,5},{4,6},{5,3},{6,4},{7,1},{8,10},{9,15},{10,... | collective-permute-start | bytes 442376 | tf_op jit(solution)/shard_map/ppermute | solution.py:402
  93.7 12.9 %collective-permute-start.6 = (bf16[128,1152]{1,0:T(8,128)(2,1)S(1)}, bf16[128,1152]{1,0:T(8,128)(2,1)S(1)}, u32[]{:S(2)}, u32[]{:S(2)}) collective-permute-start(bf16[128,1152]{1,0:T(8,128)(2,1)S(1)} %pad_maximum_fusion), channel_id=1, source_target_pairs={{0,1},{1,0},{2,3},{3,2},{4,5},{5,4},{6,7},{7,6},{8,9},{9,8},{10,11... | collective-permute-start | bytes 884744 | tf_op jit(solution)/shard_map/ppermute | solution.py:402
  106.7 0.0 collective-permute-done.4.one
  106.7 0.0 all-to-all-done.3
  106.7 0.0 collective-permute-done.5.far
  106.7 4.6 %collective-permute-start.7 = (bf16[128,1152]{1,0:T(8,128)(2,1)S(1)}, bf16[128,1152]{1,0:T(8,128)(2,1)S(1)}, u32[]{:S(2)}, u32[]{:S(2)}) collective-permute-start(bf16[128,1152]{1,0:T(8,128)(2,1)S(1)} %pad_maximum_fusion.1), channel_id=1, source_target_pairs={{0,1},{1,0},{2,3},{3,2},{4,5},{5,4},{6,7},{7,6},{8,9},{9,8},{10,11... | collective-permute-start | bytes 884744 | tf_op jit(solution)/shard_map/ppermute | solution.py:402
  111.3 2.1 %text_grad.1 = f32[2,1152]{1,0:T(2,128)} custom-call(f32[1]{0:T(128)S(6)} %copy.13.sharp_ref, f32[1]{0:T(128)S(6)} %copy.14.shift_ref, s32[2]{0:T(128)S(1)} %copy-done.8, f32[2,1152]{1,0:T(2,128)S(1)} %get-tuple-element.31.unit_ref, f32[2,128]{1,0:T(2,128)S(1)} %get-tuple-element.32.len_ref, bf16[128,1152]{1,0:T(8,128)(2,1)} %bitcast.3.img_ref, ...), custom_call_target="tpu_custom_call" | custom-call | flops 1000000000 | bytes 600000 | tf_op jit(solution)/shard_map/text_grad/pallas_call | solution.py:318
  113.5 0.0 collective-permute-done.6.near
  113.5 0.0 collective-permute-done.7.rest
  113.5 1.1 put_in_place.1
  (4 shorter events, 0.1 us)
Async XLA Ops:
  0.6 0.7 copy-start.6
  1.3 0.7 copy-start.7
  3.2 14.2 %all-to-all-start = ((bf16[8,2,1280]{2,1,0:T(2,128)(2,1)}), bf16[8,2,1280]{2,1,0:T(2,128)(2,1)S(1)}, u32[]{:S(2)}, u32[]{:S(2)}) async-start(bf16[8,2,1280]{2,1,0:T(2,128)(2,1)} %get-tuple-element.18), calls=%async_computation | async-start | bytes 81920 | tf_op jit(solution)/shard_map/all_to_all | solution.py:418
  10.1 36.4 %copy-start = (bf16[1152,538]{0,1:T(8,128)(2,1)S(1)}, bf16[1152,538]{0,1:T(8,128)(2,1)}, u32[]{:S(2)}) copy-start(bf16[1152,538]{0,1:T(8,128)(2,1)} %param.13) | copy-start | bytes 3718660
  10.1 36.4 %copy-start.1 = (bf16[538,1152]{1,0:T(8,128)(2,1)S(1)}, bf16[538,1152]{1,0:T(8,128)(2,1)}, u32[]{:S(2)}) copy-start(bf16[538,1152]{1,0:T(8,128)(2,1)} %down_ref.1) | copy-start | bytes 3718660
  10.1 36.4 %copy-start.5 = (f32[1152]{0:T(1024)S(1)}, f32[1152]{0:T(1024)}, u32[]{:S(2)}) copy-start(f32[1152]{0:T(1024)} %gain_ref.4) | copy-start | bytes 13828
  10.1 36.4 %copy-start.8 = (s32[2]{0:T(128)S(1)}, s32[2]{0:T(128)}, u32[]{:S(2)}) copy-start(s32[2]{0:T(128)} %ids_ref.5) | copy-start | bytes 28
  18.2 28.2 %all-to-all-start.1 = ((bf16[8,16,1280]{2,1,0:T(8,128)(2,1)}), bf16[8,16,1280]{2,1,0:T(8,128)(2,1)S(1)}, u32[]{:S(2)}, u32[]{:S(2)}) async-start(bf16[8,16,1280]{2,1,0:T(8,128)(2,1)} %broadcast_in_dim.4), calls=%async_computation.1 | async-start | bytes 655360 | tf_op jit(solution)/shard_map/all_to_all | solution.py:418
  46.5 1.1 copy-start.3
  50.5 5.8 %collective-permute-start = (bf16[256,1152]{1,0:T(8,128)(2,1)S(1)}, bf16[256,1152]{1,0:T(8,128)(2,1)S(1)}, u32[]{:S(2)}, u32[]{:S(2)}) collective-permute-start(bf16[256,1152]{1,0:T(8,128)(2,1)S(1)} %get-tuple-element.24), channel_id=1, source_target_pairs={{0,1},{1,0},{2,3},{3,2},{4,5},{5,4},{6,7},{7,6},{8,9},{9,8},{10,11... | collective-permute-start | bytes 1769480 | tf_op jit(solution)/shard_map/ppermute | solution.py:402
  56.3 25.1 %copy-start.2 = (bf16[512,1152]{1,0:T(8,128)(2,1)S(1)}, bf16[512,1152]{1,0:T(8,128)(2,1)}, u32[]{:S(2)}) copy-start(bf16[512,1152]{1,0:T(8,128)(2,1)} %x_ref.3) | copy-start | bytes 3538948
  56.3 25.1 %copy-start.4 = (f32[1152]{0:T(1024)S(1)}, f32[1152]{0:T(1024)}, u32[]{:S(2)}) copy-start(f32[1152]{0:T(1024)} %gain_ref.5) | copy-start | bytes 13828
  56.4 15.6 %collective-permute-start.1 = (bf16[128,1152]{1,0:T(8,128)(2,1)S(1)}, bf16[128,1152]{1,0:T(8,128)(2,1)S(1)}, u32[]{:S(2)}, u32[]{:S(2)}) collective-permute-start(bf16[128,1152]{1,0:T(8,128)(2,1)S(1)} %add_convert_fusion), channel_id=1, source_target_pairs={{0,2},{1,7},{2,0},{3,5},{4,6},{5,3},{6,4},{7,1},{8,10},{9,15},{10,... | collective-permute-start | bytes 884744 | tf_op jit(solution)/shard_map/ppermute | solution.py:402
  72.1 9.3 %collective-permute-start.2 = (bf16[64,1152]{1,0:T(8,128)(2,1)S(1)}, bf16[64,1152]{1,0:T(8,128)(2,1)S(1)}, u32[]{:S(2)}, u32[]{:S(2)}) collective-permute-start(bf16[64,1152]{1,0:T(8,128)(2,1)S(1)} %add_convert_fusion.1), channel_id=1, source_target_pairs={{0,6},{1,3},{2,4},{3,1},{4,2},{5,7},{6,0},{7,5},{8,14},{9,11},{10,... | collective-permute-start | bytes 442376 | tf_op jit(solution)/shard_map/ppermute | solution.py:402
  76.4 30.2 %all-to-all-start.3 = ((bf16[8,16,1152]{2,1,0:T(8,128)(2,1)}), bf16[8,16,1152]{2,1,0:T(8,128)(2,1)}, u32[]{:S(2)}, u32[]{:S(2)}) async-start(bf16[8,16,1152]{2,1,0:T(8,128)(2,1)} %broadcast_in_dim.5), calls=%async_computation.3 | async-start | bytes 589824 | tf_op jit(solution)/shard_map/all_to_all | solution.py:418
  81.7 8.3 %collective-permute-start.3 = (bf16[64,1152]{1,0:T(8,128)(2,1)S(1)}, bf16[64,1152]{1,0:T(8,128)(2,1)S(1)}, u32[]{:S(2)}, u32[]{:S(2)}) collective-permute-start(bf16[64,1152]{1,0:T(8,128)(2,1)S(1)} %finish.1.own), channel_id=1, source_target_pairs={{0,6},{1,3},{2,4},{3,1},{4,2},{5,7},{6,0},{7,5},{8,14},{9,11},{10,... | collective-permute-start | bytes 442376 | tf_op jit(solution)/shard_map/ppermute | solution.py:402
  84.6 22.0 %collective-permute-start.4 = (bf16[64,1152]{1,0:T(8,128)(2,1)S(1)}, bf16[64,1152]{1,0:T(8,128)(2,1)S(1)}, u32[]{:S(2)}, u32[]{:S(2)}) collective-permute-start(bf16[64,1152]{1,0:T(8,128)(2,1)S(1)} %finish.1.own), channel_id=1, source_target_pairs={{0,2},{1,7},{2,0},{3,5},{4,6},{5,3},{6,4},{7,1},{8,10},{9,15},{10,... | collective-permute-start | bytes 442376 | tf_op jit(solution)/shard_map/ppermute | solution.py:402
  90.1 16.6 %collective-permute-start.5 = (bf16[64,1152]{1,0:T(8,128)(2,1)S(1)}, bf16[64,1152]{1,0:T(8,128)(2,1)S(1)}, u32[]{:S(2)}, u32[]{:S(2)}) collective-permute-start(bf16[64,1152]{1,0:T(8,128)(2,1)S(1)} %collective-permute-done.3.two), channel_id=1, source_target_pairs={{0,2},{1,7},{2,0},{3,5},{4,6},{5,3},{6,4},{7,1},{8,10},{9,15},{10,... | collective-permute-start | bytes 442376 | tf_op jit(solution)/shard_map/ppermute | solution.py:402
  93.7 19.7 %collective-permute-start.6 = (bf16[128,1152]{1,0:T(8,128)(2,1)S(1)}, bf16[128,1152]{1,0:T(8,128)(2,1)S(1)}, u32[]{:S(2)}, u32[]{:S(2)}) collective-permute-start(bf16[128,1152]{1,0:T(8,128)(2,1)S(1)} %pad_maximum_fusion), channel_id=1, source_target_pairs={{0,1},{1,0},{2,3},{3,2},{4,5},{5,4},{6,7},{7,6},{8,9},{9,8},{10,11... | collective-permute-start | bytes 884744 | tf_op jit(solution)/shard_map/ppermute | solution.py:402
  106.7 6.7 %collective-permute-start.7 = (bf16[128,1152]{1,0:T(8,128)(2,1)S(1)}, bf16[128,1152]{1,0:T(8,128)(2,1)S(1)}, u32[]{:S(2)}, u32[]{:S(2)}) collective-permute-start(bf16[128,1152]{1,0:T(8,128)(2,1)S(1)} %pad_maximum_fusion.1), channel_id=1, source_target_pairs={{0,1},{1,0},{2,3},{3,2},{4,5},{5,4},{6,7},{7,6},{8,9},{9,8},{10,11... | collective-permute-start | bytes 884744 | tf_op jit(solution)/shard_map/ppermute | solution.py:402

commit v6 on v5

--- a/solution.py
+++ b/solution.py
@@ -16,9 +16,7 @@
 BF16 = jnp.bfloat16
 LAST = (((1,), (1,)), ((), ()))
 SMEM = pl.BlockSpec(memory_space=pltpu.SMEM)
-HBM = pl.BlockSpec(memory_space=pltpu.HBM)
 VMEM = pl.BlockSpec(memory_space=pltpu.VMEM)
-LARGE = pltpu.CompilerParams(vmem_limit_bytes=60 * 1024 * 1024)
 SMALL = pltpu.CompilerParams(vmem_limit_bytes=16 * 1024 * 1024)
 
 
@@ -95,45 +93,27 @@
             jax.ShapeDtypeStruct((2, 128), F32),
         ],
         compiler_params=SMALL,
+        cost_estimate=pl.CostEstimate(
+            flops=30_000_000_000, bytes_accessed=100_000, transcendentals=0
+        ),
         name="pack",
     )(pair_ids, text_feats)
 
 
 def forward_kernel(
-    n_tensor, x_ref, gain_ref, bias_ref, b_down_ref, up_hbm, down_hbm,
-    slope_ref, part_ref, up_ref, down_ref, act_sum, x_sum, sems,
+    n_tensor, x_ref, gain_ref, bias_ref, b_down_ref, up_ref, down_ref,
+    slope_ref, part_ref, act_sum, x_sum,
 ):
     step = pl.program_id(0)
     image = step // 2
-    third = x_ref.shape[1] // 3
-
-    def copies(source, target, first):
-        parts = [pl.ds(part * third, third) for part in range(3)]
-        return [
-            pltpu.make_async_copy(source.at[:, part], target.at[:, part], sems.at[first + i])
-            for i, part in enumerate(parts)
-        ]
-
-    up_copies = copies(up_hbm, up_ref, 0)
-    down_copies = copies(down_hbm, down_ref, 3)
-
     @pl.when(step == 0)
     def _():
-        for copy in up_copies:
-            copy.start()
         act_sum[...] = jnp.zeros_like(act_sum)
         x_sum[...] = jnp.zeros_like(x_sum)
 
     x = x_ref[...].astype(F32)
     normed, _ = norm_parts(x)
     normed = (normed * gain_ref[...][None, :]).astype(BF16)
-
-    @pl.when(step == 0)
-    def _():
-        for copy in up_copies:
-            copy.wait()
-        for copy in down_copies:
-            copy.start()
 
     pre = lax.dot_general(normed, up_ref[...], LAST, preferred_element_type=F32)
     pre = pre + bias_ref[...][None, :]
@@ -157,12 +137,12 @@
 
     @pl.when(step == pl.num_programs(0) - 1)
     def _():
-        for copy in down_copies:
-            copy.wait()
         stack = split_stack(act_sum[...] * (1.0 / PATCHES))
         mlp = unstack(jnp.dot(stack, down_ref[...], preferred_element_type=F32))
         rest = x_sum[...] * (1.0 / PATCHES) + b_down_ref[...][None, :]
-        part_ref[...] = (mlp + rest * (1.0 / n_tensor))[0:2]
+        part = (mlp + rest * (1.0 / n_tensor))[0:2]
+        for copy in range(n_tensor):
+            part_ref[copy] = part
 
 
 def forward(patches, ln_gain, up_t, b_up, w_down, b_down, n_tensor):
@@ -178,25 +158,22 @@
             vector(width),
             vector(units),
             vector(width),
-            HBM,
-            HBM,
+            pl.BlockSpec((units, width), lambda i: (0, 0)),
+            pl.BlockSpec((units, width), lambda i: (0, 0)),
         ],
         out_specs=[
             pl.BlockSpec((rows, units), lambda i: (i, 0)),
-            pl.BlockSpec((2, width), lambda i: (0, 0)),
+            pl.BlockSpec((n_tensor, 2, width), lambda i: (0, 0, 0)),
         ],
         out_shape=[
             jax.ShapeDtypeStruct((tokens, units), BF16),
-            jax.ShapeDtypeStruct((2, width), F32),
+            jax.ShapeDtypeStruct((n_tensor, 2, width), F32),
         ],
         scratch_shapes=[
-            pltpu.VMEM((units, width), BF16),
-            pltpu.VMEM((units, width), BF16),
             pltpu.VMEM((8, units), F32),
             pltpu.VMEM((8, width), F32),
-            pltpu.SemaphoreType.DMA((6,)),
         ],
-        compiler_params=LARGE,
+        compiler_params=SMALL,
         cost_estimate=pl.CostEstimate(
             flops=2 * tokens * width * units,
             bytes_accessed=2 * tokens * width + 4 * units * width + 4 * tokens * units,
@@ -237,17 +214,20 @@
 
 
 def scalars(sharp_ref, shift_ref):
-    return jnp.exp(jnp.full((8, 1), sharp_ref[0], F32)), shift_ref[0]
+    return jnp.exp(sharp_ref[...][None, :]), shift_ref[...][None, :]
 
 
 def loss_kernel(
-    place_ref, sharp_ref, shift_ref, ids_ref, pooled_ref, gain_ref, rows_ref, down_ref,
+    place_ref, ids_ref, sharp_ref, shift_ref, parts_ref, gain_ref, rows_ref, down_ref,
     up_ref, slope_ref, img_ref, hidden_ref, away_ref, keep_ref, g_pre,
 ):
     width = gain_ref.shape[0]
     core, one, two = places(place_ref[0])
     gain = gain_ref[...][None, :]
-    feat_n, feat_s, feat_len, img_emb = image_features(pooled_ref[...], gain)
+    pooled = parts_ref[0]
+    for part in range(1, parts_ref.shape[0]):
+        pooled = pooled + parts_ref[part]
+    feat_n, feat_s, feat_len, img_emb = image_features(pooled, gain)
     for copy in range(img_ref.shape[0]):
         img_ref[copy] = img_emb[0:2].astype(BF16)
     g_img = pair_grad(
@@ -277,12 +257,12 @@
 
 
 def loss_and_back(
-    place, sharp, shift, ids, pooled, gain, rows, w_down, up_t, slope, copies
+    place, sharp, shift, ids, parts, gain, rows, w_down, up_t, slope, copies
 ):
     units, width = up_t.shape
     return pl.pallas_call(
         loss_kernel,
-        in_specs=[SMEM] * 4 + [VMEM] * 6,
+        in_specs=[SMEM] * 2 + [VMEM] * 8,
         out_shape=[
             jax.ShapeDtypeStruct((copies, 2, width), BF16),
             jax.ShapeDtypeStruct((2, width), F32),
@@ -297,11 +277,11 @@
             transcendentals=0,
         ),
         name="loss_and_back",
-    )(place, sharp, shift, ids, pooled, gain, rows, w_down, up_t, slope)
+    )(place, ids, sharp, shift, parts, gain, rows, w_down, up_t, slope)
 
 
 def text_kernel(
-    sharp_ref, shift_ref, ids_ref, unit_ref, len_ref, img_ref, rows_ref, out_ref
+    ids_ref, sharp_ref, shift_ref, unit_ref, len_ref, img_ref, rows_ref, out_ref
 ):
     width = unit_ref.shape[1]
     unit = unit_ref[...]
@@ -317,14 +297,14 @@
 def text_grad(sharp, shift, ids, unit, length, images, rows):
     return pl.pallas_call(
         text_kernel,
-        in_specs=[SMEM] * 3 + [VMEM] * 4,
+        in_specs=[SMEM] + [VMEM] * 6,
         out_shape=jax.ShapeDtypeStruct(unit.shape, F32),
         compiler_params=SMALL,
         cost_estimate=pl.CostEstimate(
             flops=1_000_000_000, bytes_accessed=600_000, transcendentals=0
         ),
         name="text_grad",
-    )(sharp, shift, ids, unit, length, images, rows)
+    )(ids, sharp, shift, unit, length, images, rows)
 
 
 def finish_kernel(
@@ -414,9 +394,9 @@
     return (3 - i // 2) * 2 if i % 2 == 0 else i ^ 2
 
 
-def exchange(copies, groups):
+def exchange(copies, groups, axis="dp"):
     return lax.all_to_all(
-        copies, "dp", split_axis=0, concat_axis=0, axis_index_groups=groups
+        copies, axis, split_axis=0, concat_axis=0, axis_index_groups=groups
     )
 
 
@@ -448,18 +428,19 @@
     some_text = exchange(packed, along_y).reshape(2 * side, -1)
 
     up_t = w_up.T
-    slope, part = forward(
-        patches, ln_gain, up_t, b_up, w_down, b_down, lax.axis_size("tensor")
-    )
-    some_text, part = lax.optimization_barrier((some_text, part))
+    some_text, first_gain = lax.optimization_barrier((some_text, ln_gain))
     rows = spread(some_text, along_xz).reshape(batch, -1)
-    pooled = lax.psum(part, "tensor")
+    slope, parts = forward(
+        patches, first_gain, up_t, b_up, w_down, b_down, lax.axis_size("tensor")
+    )
+    parts, rows = lax.optimization_barrier((parts, rows))
+    parts = exchange(parts, None, "tensor")
     img_copies, g_hidden, away, keep = loss_and_back(
         place,
         log_sharpness,
         pairwise_logit_shift,
         pair_ids,
-        pooled,
+        parts,
         head_gain,
         rows,
         w_down,

time: 115 us -> 112 us (0.974)
  the two profiles are of different devices: /device:TPU:5 before, /device:TPU:1 now
where the time goes in v6:
time: 112 us; the launch traced here: 111 us
  starting transfers between devices  54.6 us (49%)
  blocking collectives  23.8 us (21%)
  waiting for transfers between devices  12.8 us (11%)
  Pallas kernels  11.6 us (10%)
  local copies, waits for them, and re-layouts  6.09 us (5%)
  between operations  2.16 us (2%)
    ppermute x8, starting transfers between devices, swap(): return lax.ppermute(value, axis, [(i, partner(i)) for i in range(size)])  31.9 us
    all_to_all x2, blocking collectives, exchange(): lax.all_to_all(copies, axis, split_axis=0, concat_axis=0, axis_index_grou...  23.8 us
    all_to_all x3, starting transfers between devices, exchange(): lax.all_to_all(copies, axis, split_axis=0, concat_axis=0, axis_index_grou...  22.7 us
    ppermute x8, waiting for transfers between devices, swap(): return lax.ppermute(value, axis, [(i, partner(i)) for i in range(size)])  6.71 us
    all_to_all x3, waiting for transfers between devices, exchange(): lax.all_to_all(copies, axis, split_axis=0, concat_axis=0, axis_index_grou...  6.14 us
    unnamed x26, local copies, waits for them, and re-layouts  4.57 us
    pallas_call x1, Pallas kernels, forward(): pl.pallas_call(functools.partial(forward_kernel, n_tensor), grid=(tokens...  4.41 us
    pallas_call x1, Pallas kernels, loss_and_back(): pl.pallas_call(loss_kernel, in_specs=[SMEM] * 2 + [VMEM] * 8, out_shape=[...  3 us
  transfers between devices with their start and end apart: 11, of which 5 were waited for; matrix products, arithmetic and copies ran while one was open for 1% of the time, Pallas kernels for 6%

profile of v6, /device:TPU:1, one launch (start us, length us, event | category | flops | bytes accessed | tf_op | source)
XLA Modules:
  0.0 111.4 jit_solution(11770928617610183668)
XLA Ops:
  0.6 0.0 copy-start.6
  0.6 0.0 copy-start.7
  0.7 0.0 copy-start.9
  0.7 0.0 copy-start.10
  0.7 0.7 copy-done.10
  1.3 0.0 copy-start.12
  1.3 0.7 copy-done.12
  2.0 0.0 copy-start
  2.0 0.0 copy-start.1
  2.0 0.7 pack.1
  2.7 14.5 %all_to_all.25 = bf16[8,2,1280]{2,1,0:T(2,128)(2,1)S(1)} all-to-all(bf16[8,2,1280]{2,1,0:T(2,128)(2,1)S(1)} %get-tuple-element.20), channel_id=1, replica_groups={{0,64,128,192,256,320,384,448},{8,72,136,200,264,328,392,456},{16,80,14..., dimensions={0} | all-to-all | bytes 81920 | tf_op jit(solution)/shard_map/all_to_all | solution.py:398
  17.3 0.7 broadcast_in_dim.4
  18.0 5.8 %all-to-all-start.1 = ((bf16[8,16,1280]{2,1,0:T(8,128)(2,1)}), bf16[8,16,1280]{2,1,0:T(8,128)(2,1)S(1)}, u32[]{:S(2)}, u32[]{:S(2)}) async-start(bf16[8,16,1280]{2,1,0:T(8,128)(2,1)} %broadcast_in_dim.4), calls=%async_computation.1 | async-start | bytes 655360 | tf_op jit(solution)/shard_map/all_to_all | solution.py:398
  23.8 0.0 copy-done.6
  23.8 0.0 copy-done.7
  23.8 0.0 copy-done.9
  23.9 0.0 copy-done
  23.9 0.0 copy-done.1
  23.9 0.0 copy-start.2
  23.9 1.3 %copy-done.2 = bf16[512,1152]{1,0:T(8,128)(2,1)S(1)} copy-done((bf16[512,1152]{1,0:T(8,128)(2,1)S(1)}, bf16[512,1152]{1,0:T(8,128)(2,1)}, u32[]{:S(2)}) %copy-start.2) | copy-done | bytes 1179672
  25.1 0.0 copy-start.8
  25.1 0.0 copy-start.11
  25.1 4.4 %forward.1 = (bf16[512,538]{1,0:T(8,128)(2,1)S(1)}, f32[8,2,1152]{2,1,0:T(2,128)}) custom-call(bf16[512,1152]{1,0:T(8,128)(2,1)S(1)} %copy-done.2, f32[1152]{0:T(1024)S(1)} %copy-done.6, f32[538]{0:T(1024)S(1)} %copy-done.9, f32[1152]{0:T(1024)S(1)} %copy-done.7, bf16[538,1152]{1,0:T(8,128)(2,1)S(1)} %bitcast.4, bf16[538,1152]{1,0:T(8,128)(2,1)S(1)} %copy-done.1), custom_call_target="tpu_custom_call" | custom-call | flops 634650624 | bytes 4760576 | tf_op jit(solution)/shard_map/forward/pallas_call | solution.py:153
  29.6 0.0 copy-start.4
  29.6 0.8 copy-done.4
  30.4 0.0 all-to-all-done.1
  30.4 12.9 %all-to-all-start.2 = ((f32[8,2,1152]{2,1,0:T(2,128)}), f32[8,2,1152]{2,1,0:T(2,128)S(1)}, u32[]{:S(2)}, u32[]{:S(2)}) async-start(f32[8,2,1152]{2,1,0:T(2,128)} %get-tuple-element.24), calls=%async_computation.2 | async-start | bytes 147456 | tf_op jit(solution)/shard_map/all_to_all | solution.py:398
  44.5 6.1 %all-to-all-done.2.parts_ref = f32[8,2,1152]{2,1,0:T(2,128)S(1)} async-done(((f32[8,2,1152]{2,1,0:T(2,128)}), f32[8,2,1152]{2,1,0:T(2,128)S(1)}, u32[]{:S(2)}, u32[]{:S(2)}) %all-to-all-start.2) | async-done | bytes 73760 | tf_op jit(solution)/shard_map/all_to_all | solution.py:398
  50.7 0.0 copy-done.8
  50.7 0.0 copy-done.11
  50.7 0.0 copy-start.5
  50.7 1.1 copy-done.5
  51.8 3.0 %loss_and_back.1 = (bf16[8,2,1152]{2,1,0:T(2,128)(2,1)S(1)}, f32[2,1152]{1,0:T(2,128)S(1)}, bf16[256,1152]{1,0:T(8,128)(2,1)S(1)}, bf16[256,1152]{1,0:T(8,128)(2,1)S(1)}) custom-call(s32[1]{0:T(128)} %bitcast.place_ref, s32[2]{0:T(128)S(1)} %copy-done.11, f32[1]{0:T(128)S(6)} %copy.13.sharp_ref, f32[1]{0:T(128)S(6)} %copy.14.shift_ref, ...), custom_call_target="tpu_custom_call" | custom-call | flops 634650624 | bytes 4820480 | tf_op jit(solution)/shard_map/loss_and_back/pallas_call | solution.py:263
  54.8 3.0 %collective-permute-start = (bf16[256,1152]{1,0:T(8,128)(2,1)S(1)}, bf16[256,1152]{1,0:T(8,128)(2,1)S(1)}, u32[]{:S(2)}, u32[]{:S(2)}) collective-permute-start(bf16[256,1152]{1,0:T(8,128)(2,1)S(1)} %get-tuple-element.28), channel_id=1, source_target_pairs={{0,1},{1,0},{2,3},{3,2},{4,5},{5,4},{6,7},{7,6},{8,9},{9,8},{10,11... | collective-permute-start | bytes 1769480 | tf_op jit(solution)/shard_map/ppermute | solution.py:382
  57.8 1.6 %collective-permute-done.other_ref = bf16[256,1152]{1,0:T(8,128)(2,1)S(1)} collective-permute-done((bf16[256,1152]{1,0:T(8,128)(2,1)S(1)}, bf16[256,1152]{1,0:T(8,128)(2,1)S(1)}, u32[]{:S(2)}, u32[]{:S(2)}) %collective-permute-start) | collective-permute-done | bytes 589856 | tf_op jit(solution)/shard_map/ppermute | solution.py:382
  59.4 0.0 copy-start.3
  59.4 0.1 add_convert_fusion
  59.5 2.1 %collective-permute-start.1 = (bf16[128,1152]{1,0:T(8,128)(2,1)S(1)}, bf16[128,1152]{1,0:T(8,128)(2,1)S(1)}, u32[]{:S(2)}, u32[]{:S(2)}) collective-permute-start(bf16[128,1152]{1,0:T(8,128)(2,1)S(1)} %add_convert_fusion), channel_id=1, source_target_pairs={{0,2},{1,7},{2,0},{3,5},{4,6},{5,3},{6,4},{7,1},{8,10},{9,15},{10,... | collective-permute-start | bytes 884744 | tf_op jit(solution)/shard_map/ppermute | solution.py:382
  61.6 9.3 %all_to_all.26 = bf16[8,2,1152]{2,1,0:T(2,128)(2,1)S(1)} all-to-all(bf16[8,2,1152]{2,1,0:T(2,128)(2,1)S(1)} %get-tuple-element.30), channel_id=1, replica_groups={{0,64,128,192,256,320,384,448},{8,72,136,200,264,328,392,456},{16,80,14..., dimensions={0} | all-to-all | bytes 73728 | tf_op jit(solution)/shard_map/all_to_all | solution.py:398
  70.9 1.7 %collective-permute-done.1.one_ref = bf16[128,1152]{1,0:T(8,128)(2,1)S(1)} collective-permute-done((bf16[128,1152]{1,0:T(8,128)(2,1)S(1)}, bf16[128,1152]{1,0:T(8,128)(2,1)S(1)}, u32[]{:S(2)}, u32[]{:S(2)}) %collective-permute-start.1) | collective-permute-done | bytes 294944 | tf_op jit(solution)/shard_map/ppermute | solution.py:382
  72.6 0.1 add_convert_fusion.1
  72.6 2.5 %collective-permute-start.2 = (bf16[64,1152]{1,0:T(8,128)(2,1)S(1)}, bf16[64,1152]{1,0:T(8,128)(2,1)S(1)}, u32[]{:S(2)}, u32[]{:S(2)}) collective-permute-start(bf16[64,1152]{1,0:T(8,128)(2,1)S(1)} %add_convert_fusion.1), channel_id=1, source_target_pairs={{0,6},{1,3},{2,4},{3,1},{4,2},{5,7},{6,0},{7,5},{8,14},{9,11},{10,... | collective-permute-start | bytes 442376 | tf_op jit(solution)/shard_map/ppermute | solution.py:382
  75.2 0.7 broadcast_in_dim.5
  75.9 4.1 %all-to-all-start.4 = ((bf16[8,16,1152]{2,1,0:T(8,128)(2,1)}), bf16[8,16,1152]{2,1,0:T(8,128)(2,1)}, u32[]{:S(2)}, u32[]{:S(2)}) async-start(bf16[8,16,1152]{2,1,0:T(8,128)(2,1)} %broadcast_in_dim.5), calls=%async_computation.4 | async-start | bytes 589824 | tf_op jit(solution)/shard_map/all_to_all | solution.py:398
  80.0 1.3 %collective-permute-done.2.two_ref = bf16[64,1152]{1,0:T(8,128)(2,1)S(1)} collective-permute-done((bf16[64,1152]{1,0:T(8,128)(2,1)S(1)}, bf16[64,1152]{1,0:T(8,128)(2,1)S(1)}, u32[]{:S(2)}, u32[]{:S(2)}) %collective-permute-start.2) | collective-permute-done | bytes 147488 | tf_op jit(solution)/shard_map/ppermute | solution.py:382
  81.3 0.0 copy-done.3
  81.3 0.4 finish.1.own
  81.7 2.4 %collective-permute-start.3 = (bf16[64,1152]{1,0:T(8,128)(2,1)S(1)}, bf16[64,1152]{1,0:T(8,128)(2,1)S(1)}, u32[]{:S(2)}, u32[]{:S(2)}) collective-permute-start(bf16[64,1152]{1,0:T(8,128)(2,1)S(1)} %finish.1.own), channel_id=1, source_target_pairs={{0,6},{1,3},{2,4},{3,1},{4,2},{5,7},{6,0},{7,5},{8,14},{9,11},{10,... | collective-permute-start | bytes 442376 | tf_op jit(solution)/shard_map/ppermute | solution.py:382
  84.0 3.8 %collective-permute-start.4 = (bf16[64,1152]{1,0:T(8,128)(2,1)S(1)}, bf16[64,1152]{1,0:T(8,128)(2,1)S(1)}, u32[]{:S(2)}, u32[]{:S(2)}) collective-permute-start(bf16[64,1152]{1,0:T(8,128)(2,1)S(1)} %finish.1.own), channel_id=1, source_target_pairs={{0,2},{1,7},{2,0},{3,5},{4,6},{5,3},{6,4},{7,1},{8,10},{9,15},{10,... | collective-permute-start | bytes 442376 | tf_op jit(solution)/shard_map/ppermute | solution.py:382
  87.9 2.1 %collective-permute-done.3.two = bf16[64,1152]{1,0:T(8,128)(2,1)S(1)} collective-permute-done((bf16[64,1152]{1,0:T(8,128)(2,1)S(1)}, bf16[64,1152]{1,0:T(8,128)(2,1)S(1)}, u32[]{:S(2)}, u32[]{:S(2)}) %collective-permute-start.3) | collective-permute-done | bytes 147488 | tf_op jit(solution)/shard_map/ppermute | solution.py:382
  89.9 2.8 %collective-permute-start.5 = (bf16[64,1152]{1,0:T(8,128)(2,1)S(1)}, bf16[64,1152]{1,0:T(8,128)(2,1)S(1)}, u32[]{:S(2)}, u32[]{:S(2)}) collective-permute-start(bf16[64,1152]{1,0:T(8,128)(2,1)S(1)} %collective-permute-done.3.two), channel_id=1, source_target_pairs={{0,2},{1,7},{2,0},{3,5},{4,6},{5,3},{6,4},{7,1},{8,10},{9,15},{10,... | collective-permute-start | bytes 442376 | tf_op jit(solution)/shard_map/ppermute | solution.py:382
  92.8 10.6 %collective-permute-start.6 = (bf16[128,1152]{1,0:T(8,128)(2,1)S(1)}, bf16[128,1152]{1,0:T(8,128)(2,1)S(1)}, u32[]{:S(2)}, u32[]{:S(2)}) collective-permute-start(bf16[128,1152]{1,0:T(8,128)(2,1)S(1)} %pad_maximum_fusion), channel_id=1, source_target_pairs={{0,1},{1,0},{2,3},{3,2},{4,5},{5,4},{6,7},{7,6},{8,9},{9,8},{10,11... | collective-permute-start | bytes 884744 | tf_op jit(solution)/shard_map/ppermute | solution.py:382
  103.5 0.0 collective-permute-done.4.one
  103.5 0.0 all-to-all-done.4
  103.5 0.0 collective-permute-done.5.far
  103.5 4.6 %collective-permute-start.7 = (bf16[128,1152]{1,0:T(8,128)(2,1)S(1)}, bf16[128,1152]{1,0:T(8,128)(2,1)S(1)}, u32[]{:S(2)}, u32[]{:S(2)}) collective-permute-start(bf16[128,1152]{1,0:T(8,128)(2,1)S(1)} %pad_maximum_fusion.1), channel_id=1, source_target_pairs={{0,1},{1,0},{2,3},{3,2},{4,5},{5,4},{6,7},{7,6},{8,9},{9,8},{10,11... | collective-permute-start | bytes 884744 | tf_op jit(solution)/shard_map/ppermute | solution.py:382
  108.2 2.1 %text_grad.1 = f32[2,1152]{1,0:T(2,128)} custom-call(s32[2]{0:T(128)S(1)} %copy-done.11, f32[1]{0:T(128)S(6)} %copy.13.sharp_ref, f32[1]{0:T(128)S(6)} %copy.14.shift_ref, f32[2,1152]{1,0:T(2,128)S(1)} %get-tuple-element.35.unit_ref, f32[2,128]{1,0:T(2,128)S(1)} %get-tuple-element.36.len_ref, bf16[128,1152]{1,0:T(8,128)(2,1)} %bitcast.3.img_ref, ...), custom_call_target="tpu_custom_call" | custom-call | flops 1000000000 | bytes 600000 | tf_op jit(solution)/shard_map/text_grad/pallas_call | solution.py:298
  110.3 0.0 collective-permute-done.6.near
  110.3 0.0 collective-permute-done.7.rest
  110.3 1.1 put_in_place.1
  (4 shorter events, 0.1 us)
Async XLA Ops:
  0.6 23.2 %copy-start.6 = (f32[1152]{0:T(1024)S(1)}, f32[1152]{0:T(1024)}, u32[]{:S(2)}) copy-start(f32[1152]{0:T(1024)} %gain_ref.4) | copy-start | bytes 13828
  0.6 23.2 %copy-start.7 = (f32[1152]{0:T(1024)S(1)}, f32[1152]{0:T(1024)}, u32[]{:S(2)}) copy-start(f32[1152]{0:T(1024)} %b_down_ref.1) | copy-start | bytes 13828
  0.7 23.2 %copy-start.9 = (f32[538]{0:T(1024)S(1)}, f32[538]{0:T(1024)}, u32[]{:S(2)}) copy-start(f32[538]{0:T(1024)} %bias_ref.1) | copy-start | bytes 6460
  0.7 0.7 copy-start.10
  1.3 0.7 copy-start.12
  2.0 21.8 %copy-start = (bf16[1152,538]{0,1:T(8,128)(2,1)S(1)}, bf16[1152,538]{0,1:T(8,128)(2,1)}, u32[]{:S(2)}) copy-start(bf16[1152,538]{0,1:T(8,128)(2,1)} %param.13) | copy-start | bytes 3718660
  2.0 21.8 %copy-start.1 = (bf16[538,1152]{1,0:T(8,128)(2,1)S(1)}, bf16[538,1152]{1,0:T(8,128)(2,1)}, u32[]{:S(2)}) copy-start(bf16[538,1152]{1,0:T(8,128)(2,1)} %down_ref.3) | copy-start | bytes 3718660
  18.0 12.4 %all-to-all-start.1 = ((bf16[8,16,1280]{2,1,0:T(8,128)(2,1)}), bf16[8,16,1280]{2,1,0:T(8,128)(2,1)S(1)}, u32[]{:S(2)}, u32[]{:S(2)}) async-start(bf16[8,16,1280]{2,1,0:T(8,128)(2,1)} %broadcast_in_dim.4), calls=%async_computation.1 | async-start | bytes 655360 | tf_op jit(solution)/shard_map/all_to_all | solution.py:398
  23.9 1.3 %copy-start.2 = (bf16[512,1152]{1,0:T(8,128)(2,1)S(1)}, bf16[512,1152]{1,0:T(8,128)(2,1)}, u32[]{:S(2)}) copy-start(bf16[512,1152]{1,0:T(8,128)(2,1)} %x_ref.3) | copy-start | bytes 3538948
  25.1 25.5 %copy-start.8 = (f32[1152]{0:T(1024)S(1)}, f32[1152]{0:T(1024)}, u32[]{:S(2)}) copy-start(f32[1152]{0:T(1024)} %gain_ref.3) | copy-start | bytes 13828
  25.1 25.5 %copy-start.11 = (s32[2]{0:T(128)S(1)}, s32[2]{0:T(128)}, u32[]{:S(2)}) copy-start(s32[2]{0:T(128)} %ids_ref.5) | copy-start | bytes 28
  29.6 0.8 copy-start.4
  30.4 20.3 %all-to-all-start.2 = ((f32[8,2,1152]{2,1,0:T(2,128)}), f32[8,2,1152]{2,1,0:T(2,128)S(1)}, u32[]{:S(2)}, u32[]{:S(2)}) async-start(f32[8,2,1152]{2,1,0:T(2,128)} %get-tuple-element.24), calls=%async_computation.2 | async-start | bytes 147456 | tf_op jit(solution)/shard_map/all_to_all | solution.py:398
  50.7 1.1 copy-start.5
  54.8 4.6 %collective-permute-start = (bf16[256,1152]{1,0:T(8,128)(2,1)S(1)}, bf16[256,1152]{1,0:T(8,128)(2,1)S(1)}, u32[]{:S(2)}, u32[]{:S(2)}) collective-permute-start(bf16[256,1152]{1,0:T(8,128)(2,1)S(1)} %get-tuple-element.28), channel_id=1, source_target_pairs={{0,1},{1,0},{2,3},{3,2},{4,5},{5,4},{6,7},{7,6},{8,9},{9,8},{10,11... | collective-permute-start | bytes 1769480 | tf_op jit(solution)/shard_map/ppermute | solution.py:382
  59.4 21.9 %copy-start.3 = (bf16[512,1152]{1,0:T(8,128)(2,1)S(1)}, bf16[512,1152]{1,0:T(8,128)(2,1)}, u32[]{:S(2)}) copy-start(bf16[512,1152]{1,0:T(8,128)(2,1)} %x_ref.3) | copy-start | bytes 3538948
  59.5 13.1 %collective-permute-start.1 = (bf16[128,1152]{1,0:T(8,128)(2,1)S(1)}, bf16[128,1152]{1,0:T(8,128)(2,1)S(1)}, u32[]{:S(2)}, u32[]{:S(2)}) collective-permute-start(bf16[128,1152]{1,0:T(8,128)(2,1)S(1)} %add_convert_fusion), channel_id=1, source_target_pairs={{0,2},{1,7},{2,0},{3,5},{4,6},{5,3},{6,4},{7,1},{8,10},{9,15},{10,... | collective-permute-start | bytes 884744 | tf_op jit(solution)/shard_map/ppermute | solution.py:382
  72.6 8.7 %collective-permute-start.2 = (bf16[64,1152]{1,0:T(8,128)(2,1)S(1)}, bf16[64,1152]{1,0:T(8,128)(2,1)S(1)}, u32[]{:S(2)}, u32[]{:S(2)}) collective-permute-start(bf16[64,1152]{1,0:T(8,128)(2,1)S(1)} %add_convert_fusion.1), channel_id=1, source_target_pairs={{0,6},{1,3},{2,4},{3,1},{4,2},{5,7},{6,0},{7,5},{8,14},{9,11},{10,... | collective-permute-start | bytes 442376 | tf_op jit(solution)/shard_map/ppermute | solution.py:382
  75.9 27.6 %all-to-all-start.4 = ((bf16[8,16,1152]{2,1,0:T(8,128)(2,1)}), bf16[8,16,1152]{2,1,0:T(8,128)(2,1)}, u32[]{:S(2)}, u32[]{:S(2)}) async-start(bf16[8,16,1152]{2,1,0:T(8,128)(2,1)} %broadcast_in_dim.5), calls=%async_computation.4 | async-start | bytes 589824 | tf_op jit(solution)/shard_map/all_to_all | solution.py:398
  81.7 8.3 %collective-permute-start.3 = (bf16[64,1152]{1,0:T(8,128)(2,1)S(1)}, bf16[64,1152]{1,0:T(8,128)(2,1)S(1)}, u32[]{:S(2)}, u32[]{:S(2)}) collective-permute-start(bf16[64,1152]{1,0:T(8,128)(2,1)S(1)} %finish.1.own), channel_id=1, source_target_pairs={{0,6},{1,3},{2,4},{3,1},{4,2},{5,7},{6,0},{7,5},{8,14},{9,11},{10,... | collective-permute-start | bytes 442376 | tf_op jit(solution)/shard_map/ppermute | solution.py:382
  84.0 19.4 %collective-permute-start.4 = (bf16[64,1152]{1,0:T(8,128)(2,1)S(1)}, bf16[64,1152]{1,0:T(8,128)(2,1)S(1)}, u32[]{:S(2)}, u32[]{:S(2)}) collective-permute-start(bf16[64,1152]{1,0:T(8,128)(2,1)S(1)} %finish.1.own), channel_id=1, source_target_pairs={{0,2},{1,7},{2,0},{3,5},{4,6},{5,3},{6,4},{7,1},{8,10},{9,15},{10,... | collective-permute-start | bytes 442376 | tf_op jit(solution)/shard_map/ppermute | solution.py:382
  89.9 13.6 %collective-permute-start.5 = (bf16[64,1152]{1,0:T(8,128)(2,1)S(1)}, bf16[64,1152]{1,0:T(8,128)(2,1)S(1)}, u32[]{:S(2)}, u32[]{:S(2)}) collective-permute-start(bf16[64,1152]{1,0:T(8,128)(2,1)S(1)} %collective-permute-done.3.two), channel_id=1, source_target_pairs={{0,2},{1,7},{2,0},{3,5},{4,6},{5,3},{6,4},{7,1},{8,10},{9,15},{10,... | collective-permute-start | bytes 442376 | tf_op jit(solution)/shard_map/ppermute | solution.py:382
  92.8 17.4 %collective-permute-start.6 = (bf16[128,1152]{1,0:T(8,128)(2,1)S(1)}, bf16[128,1152]{1,0:T(8,128)(2,1)S(1)}, u32[]{:S(2)}, u32[]{:S(2)}) collective-permute-start(bf16[128,1152]{1,0:T(8,128)(2,1)S(1)} %pad_maximum_fusion), channel_id=1, source_target_pairs={{0,1},{1,0},{2,3},{3,2},{4,5},{5,4},{6,7},{7,6},{8,9},{9,8},{10,11... | collective-permute-start | bytes 884744 | tf_op jit(solution)/shard_map/ppermute | solution.py:382
  103.5 6.7 %collective-permute-start.7 = (bf16[128,1152]{1,0:T(8,128)(2,1)S(1)}, bf16[128,1152]{1,0:T(8,128)(2,1)S(1)}, u32[]{:S(2)}, u32[]{:S(2)}) collective-permute-start(bf16[128,1152]{1,0:T(8,128)(2,1)S(1)} %pad_maximum_fusion.1), channel_id=1, source_target_pairs={{0,1},{1,0},{2,3},{3,2},{4,5},{5,4},{6,7},{7,6},{8,9},{9,8},{10,11... | collective-permute-start | bytes 884744 | tf_op jit(solution)/shard_map/ppermute | solution.py:382

commit v7 on v6

--- a/solution.py
+++ b/solution.py
@@ -281,20 +281,19 @@
 
 
 def text_kernel(
-    ids_ref, sharp_ref, shift_ref, unit_ref, len_ref, img_ref, rows_ref, out_ref
+    ids_ref, sharp_ref, shift_ref, unit_ref, len_ref, img_ref, columns_ref, out_ref
 ):
-    width = unit_ref.shape[1]
     unit = unit_ref[...]
     queries = jnp.concatenate([unit] * 4, axis=0).astype(BF16).astype(F32)
     g_text = pair_grad(
-        queries, img_ref[...], ids_ref, rows_ref[:, width : width + 128],
+        queries, img_ref[...], ids_ref, columns_ref[...],
         *scalars(sharp_ref, shift_ref),
     )[0:2]
     along = jnp.sum(unit * g_text, axis=-1, keepdims=True)
     out_ref[...] = (g_text - unit * along) / len_ref[:, 0:1]
 
 
-def text_grad(sharp, shift, ids, unit, length, images, rows):
+def text_grad(sharp, shift, ids, unit, length, images, columns):
     return pl.pallas_call(
         text_kernel,
         in_specs=[SMEM] + [VMEM] * 6,
@@ -304,7 +303,7 @@
             flops=1_000_000_000, bytes_accessed=600_000, transcendentals=0
         ),
         name="text_grad",
-    )(ids, sharp, shift, unit, length, images, rows)
+    )(ids, sharp, shift, unit, length, images, columns)
 
 
 def finish_kernel(
@@ -347,12 +346,12 @@
     )(place, keep, other, got_one, got_two, patches, g_hidden, ln_gain)
 
 
-def place_kernel(place_ref, own, two, one, far, near, rest, out_ref):
+def place_kernel(place_ref, own, two, one, near, rest, out_ref):
     core, one_bit, two_bit = places(place_ref[0])
     low, high = slice(0, BLOCK), slice(BLOCK, 2 * BLOCK)
     mine, theirs = order(one_bit, two_bit), order(two_bit, one_bit)
     moves = [
-        (far, low, core, mine[0]),
+        (one, high, core, mine[0]),
         (one, low, core, mine[1]),
         (two, low, core, mine[2]),
         (own, low, core, mine[3]),
@@ -370,7 +369,7 @@
     width = pieces[0].shape[1]
     return pl.pallas_call(
         place_kernel,
-        in_specs=[SMEM] + [VMEM] * 6,
+        in_specs=[SMEM] + [VMEM] * 5,
         out_shape=jax.ShapeDtypeStruct((tokens, width), BF16),
         compiler_params=SMALL,
         name="put_in_place",
@@ -458,23 +457,23 @@
     send_one = both(0, 128).astype(BF16)
     got_one = swap(send_one, "tensor", step_one)
     img_copies, _ = lax.optimization_barrier((img_copies, send_one))
-    some_img = exchange(img_copies, along_y).reshape(2 * side, -1)
+    some_img = exchange(img_copies, along_xz).reshape(2 * side, -1)
     got_one, some_img = lax.optimization_barrier((got_one, some_img))
     send_two = (both(128, 64) + got_one[:64].astype(F32)).astype(BF16)
     got_two = swap(send_two, "tensor", step_two)
-    images = spread(some_img, along_xz).reshape(batch, -1)
+    images = spread(some_img, along_y).reshape(batch, -1)
     done = finish(place, keep, other, got_one, got_two, patches, g_hidden, ln_gain)
 
     from_two = swap(done, "tensor", step_two)
-    from_one = swap(done, "tensor", step_one)
-    far = swap(from_two, "tensor", step_one)
-    near = swap_core(jnp.concatenate([done, from_two]))
-    from_one, images = lax.optimization_barrier((from_one, images))
-    rest = swap_core(jnp.concatenate([from_one, far]))
+    pair = jnp.concatenate([done, from_two])
+    from_one = swap(pair, "tensor", step_one)
+    near = swap_core(pair)
+    rest = swap_core(from_one)
     grad_patches = put_in_place(
-        place, (done, from_two, from_one, far, near, rest), patches.shape[0]
-    )
-
+        place, (done, from_two, from_one, near, rest), patches.shape[0]
+    )
+
+    ids = rows[:, -128:].reshape(side, side, 2, 128).swapaxes(0, 1).reshape(batch, 128)
     grad_text = text_grad(
         log_sharpness,
         pairwise_logit_shift,
@@ -482,7 +481,7 @@
         unit_text,
         text_len,
         images,
-        rows,
+        ids,
     )
     return grad_patches, grad_text
 

time: 112 us -> 112 us (level)
  the two profiles are of different devices: /device:TPU:1 before, /device:TPU:65 now
where the time goes in v7:
time: 112 us; the launch traced here: 111 us
  starting transfers between devices  54.7 us (49%)
  blocking collectives  22.4 us (20%)
  waiting for transfers between devices  14.6 us (13%)
  Pallas kernels  11.1 us (10%)
  local copies, waits for them, and re-layouts  6.14 us (5%)
  between operations  2.15 us (2%)
    ppermute x7, starting transfers between devices, swap(): return lax.ppermute(value, axis, [(i, partner(i)) for i in range(size)])  34 us
    all_to_all x2, blocking collectives, exchange(): lax.all_to_all(copies, axis, split_axis=0, concat_axis=0, axis_index_grou...  22.4 us
    all_to_all x3, starting transfers between devices, exchange(): lax.all_to_all(copies, axis, split_axis=0, concat_axis=0, axis_index_grou...  20.7 us
    ppermute x7, waiting for transfers between devices, swap(): return lax.ppermute(value, axis, [(i, partner(i)) for i in range(size)])  8.44 us
    all_to_all x3, waiting for transfers between devices, exchange(): lax.all_to_all(copies, axis, split_axis=0, concat_axis=0, axis_index_grou...  6.14 us
    unnamed x26, local copies, waits for them, and re-layouts  4.58 us
    pallas_call x1, Pallas kernels, forward(): pl.pallas_call(functools.partial(forward_kernel, n_tensor), grid=(tokens...  4.37 us
    pallas_call x1, Pallas kernels, loss_and_back(): pl.pallas_call(loss_kernel, in_specs=[SMEM] * 2 + [VMEM] * 8, out_shape=[...  2.97 us
  transfers between devices with their start and end apart: 10, of which 5 were waited for; matrix products, arithmetic and copies ran while one was open for 1% of the time, Pallas kernels for 5%

profile of v7, /device:TPU:65, one launch (start us, length us, event | category | flops | bytes accessed | tf_op | source)
XLA Modules:
  0.0 111.2 jit_solution(10846219889475863419)
XLA Ops:
  0.6 0.0 copy-start.6
  0.6 0.0 copy-start.7
  0.7 0.0 copy-start.9
  0.7 0.0 copy-start.10
  0.7 0.7 copy-done.10
  1.3 0.0 copy-start.12
  1.3 0.7 copy-done.12
  2.0 0.0 copy-start
  2.0 0.0 copy-start.1
  2.0 0.7 pack.1
  2.7 13.7 %all_to_all.25 = bf16[8,2,1280]{2,1,0:T(2,128)(2,1)S(1)} all-to-all(bf16[8,2,1280]{2,1,0:T(2,128)(2,1)S(1)} %get-tuple-element.18), channel_id=1, replica_groups={{0,64,128,192,256,320,384,448},{8,72,136,200,264,328,392,456},{16,80,14..., dimensions={0} | all-to-all | bytes 81920 | tf_op jit(solution)/shard_map/all_to_all | solution.py:397
  16.4 0.8 broadcast_in_dim.4
  17.2 5.2 %all-to-all-start.1 = ((bf16[8,16,1280]{2,1,0:T(8,128)(2,1)}), bf16[8,16,1280]{2,1,0:T(8,128)(2,1)S(1)}, u32[]{:S(2)}, u32[]{:S(2)}) async-start(bf16[8,16,1280]{2,1,0:T(8,128)(2,1)} %broadcast_in_dim.4), calls=%async_computation.1 | async-start | bytes 655360 | tf_op jit(solution)/shard_map/all_to_all | solution.py:397
  22.4 0.0 copy-done.6
  22.4 0.0 copy-done.7
  22.4 0.0 copy-done.9
  22.4 0.0 copy-done
  22.4 0.0 copy-done.1
  22.4 0.0 copy-start.2
  22.4 1.3 %copy-done.2 = bf16[512,1152]{1,0:T(8,128)(2,1)S(1)} copy-done((bf16[512,1152]{1,0:T(8,128)(2,1)S(1)}, bf16[512,1152]{1,0:T(8,128)(2,1)}, u32[]{:S(2)}) %copy-start.2) | copy-done | bytes 1179672
  23.7 0.0 copy-start.8
  23.7 0.0 copy-start.11
  23.7 4.4 %forward.1 = (bf16[512,538]{1,0:T(8,128)(2,1)S(1)}, f32[8,2,1152]{2,1,0:T(2,128)}) custom-call(bf16[512,1152]{1,0:T(8,128)(2,1)S(1)} %copy-done.2, f32[1152]{0:T(1024)S(1)} %copy-done.6, f32[538]{0:T(1024)S(1)} %copy-done.9, f32[1152]{0:T(1024)S(1)} %copy-done.7, bf16[538,1152]{1,0:T(8,128)(2,1)S(1)} %bitcast.8, bf16[538,1152]{1,0:T(8,128)(2,1)S(1)} %copy-done.1), custom_call_target="tpu_custom_call" | custom-call | flops 634650624 | bytes 4760576 | tf_op jit(solution)/shard_map/forward/pallas_call | solution.py:153
  28.1 0.0 copy-start.4
  28.1 0.8 copy-done.4
  28.9 0.0 all-to-all-done.1
  28.9 12.1 %all-to-all-start.2 = ((f32[8,2,1152]{2,1,0:T(2,128)}), f32[8,2,1152]{2,1,0:T(2,128)S(1)}, u32[]{:S(2)}, u32[]{:S(2)}) async-start(f32[8,2,1152]{2,1,0:T(2,128)} %get-tuple-element.22), calls=%async_computation.2 | async-start | bytes 147456 | tf_op jit(solution)/shard_map/all_to_all | solution.py:397
  42.3 6.1 %all-to-all-done.2.parts_ref = f32[8,2,1152]{2,1,0:T(2,128)S(1)} async-done(((f32[8,2,1152]{2,1,0:T(2,128)}), f32[8,2,1152]{2,1,0:T(2,128)S(1)}, u32[]{:S(2)}, u32[]{:S(2)}) %all-to-all-start.2) | async-done | bytes 73760 | tf_op jit(solution)/shard_map/all_to_all | solution.py:397
  48.4 0.0 copy-done.8
  48.4 0.0 copy-done.11
  48.4 0.0 copy-start.5
  48.4 1.1 copy-done.5
  49.5 3.0 %loss_and_back.1 = (bf16[8,2,1152]{2,1,0:T(2,128)(2,1)S(1)}, f32[2,1152]{1,0:T(2,128)S(1)}, bf16[256,1152]{1,0:T(8,128)(2,1)S(1)}, bf16[256,1152]{1,0:T(8,128)(2,1)S(1)}) custom-call(s32[1]{0:T(128)} %bitcast.place_ref, s32[2]{0:T(128)S(1)} %copy-done.11, f32[1]{0:T(128)S(6)} %copy.14.sharp_ref, f32[1]{0:T(128)S(6)} %copy.15.shift_ref, ...), custom_call_target="tpu_custom_call" | custom-call | flops 634650624 | bytes 4820480 | tf_op jit(solution)/shard_map/loss_and_back/pallas_call | solution.py:263
  52.5 0.0 copy-start.3
  52.5 3.1 %collective-permute-start = (bf16[256,1152]{1,0:T(8,128)(2,1)S(1)}, bf16[256,1152]{1,0:T(8,128)(2,1)S(1)}, u32[]{:S(2)}, u32[]{:S(2)}) collective-permute-start(bf16[256,1152]{1,0:T(8,128)(2,1)S(1)} %get-tuple-element.26), channel_id=1, source_target_pairs={{0,1},{1,0},{2,3},{3,2},{4,5},{5,4},{6,7},{7,6},{8,9},{9,8},{10,11... | collective-permute-start | bytes 1769480 | tf_op jit(solution)/shard_map/ppermute | solution.py:381
  55.6 1.6 %collective-permute-done.other_ref = bf16[256,1152]{1,0:T(8,128)(2,1)S(1)} collective-permute-done((bf16[256,1152]{1,0:T(8,128)(2,1)S(1)}, bf16[256,1152]{1,0:T(8,128)(2,1)S(1)}, u32[]{:S(2)}, u32[]{:S(2)}) %collective-permute-start) | collective-permute-done | bytes 589856 | tf_op jit(solution)/shard_map/ppermute | solution.py:381
  57.2 0.1 add_convert_fusion
  57.3 2.6 %collective-permute-start.1 = (bf16[128,1152]{1,0:T(8,128)(2,1)S(1)}, bf16[128,1152]{1,0:T(8,128)(2,1)S(1)}, u32[]{:S(2)}, u32[]{:S(2)}) collective-permute-start(bf16[128,1152]{1,0:T(8,128)(2,1)S(1)} %add_convert_fusion), channel_id=1, source_target_pairs={{0,2},{1,7},{2,0},{3,5},{4,6},{5,3},{6,4},{7,1},{8,10},{9,15},{10,... | collective-permute-start | bytes 884744 | tf_op jit(solution)/shard_map/ppermute | solution.py:381
  59.9 8.6 %all_to_all.26 = bf16[8,2,1152]{2,1,0:T(2,128)(2,1)S(1)} all-to-all(bf16[8,2,1152]{2,1,0:T(2,128)(2,1)S(1)} %get-tuple-element.28), channel_id=1, replica_groups={{0,8,16,24,32,40,48,56},{64,72,80,88,96,104,112,120},{128,136,144,152,1..., dimensions={0} | all-to-all | bytes 73728 | tf_op jit(solution)/shard_map/all_to_all | solution.py:397
  68.6 0.8 collective-permute-done.1.one_ref
  69.4 0.1 add_convert_fusion.1
  69.5 1.9 %collective-permute-start.2 = (bf16[64,1152]{1,0:T(8,128)(2,1)S(1)}, bf16[64,1152]{1,0:T(8,128)(2,1)S(1)}, u32[]{:S(2)}, u32[]{:S(2)}) collective-permute-start(bf16[64,1152]{1,0:T(8,128)(2,1)S(1)} %add_convert_fusion.1), channel_id=1, source_target_pairs={{0,6},{1,3},{2,4},{3,1},{4,2},{5,7},{6,0},{7,5},{8,14},{9,11},{10,... | collective-permute-start | bytes 442376 | tf_op jit(solution)/shard_map/ppermute | solution.py:381
  71.4 5.0 %collective-permute-done.2.two_ref = bf16[64,1152]{1,0:T(8,128)(2,1)S(1)} collective-permute-done((bf16[64,1152]{1,0:T(8,128)(2,1)S(1)}, bf16[64,1152]{1,0:T(8,128)(2,1)S(1)}, u32[]{:S(2)}, u32[]{:S(2)}) %collective-permute-start.2) | collective-permute-done | bytes 147488 | tf_op jit(solution)/shard_map/ppermute | solution.py:381
  76.4 0.0 copy-done.3
  76.4 0.4 finish.1.own
  76.7 1.9 %collective-permute-start.3 = (bf16[64,1152]{1,0:T(8,128)(2,1)S(1)}, bf16[64,1152]{1,0:T(8,128)(2,1)S(1)}, u32[]{:S(2)}, u32[]{:S(2)}) collective-permute-start(bf16[64,1152]{1,0:T(8,128)(2,1)S(1)} %finish.1.own), channel_id=1, source_target_pairs={{0,6},{1,3},{2,4},{3,1},{4,2},{5,7},{6,0},{7,5},{8,14},{9,11},{10,... | collective-permute-start | bytes 442376 | tf_op jit(solution)/shard_map/ppermute | solution.py:381
  78.7 0.7 broadcast_in_dim.5
  79.4 3.4 %all-to-all-start.4 = ((bf16[8,16,1152]{2,1,0:T(8,128)(2,1)}), bf16[8,16,1152]{2,1,0:T(8,128)(2,1)S(1)}, u32[]{:S(2)}, u32[]{:S(2)}) async-start(bf16[8,16,1152]{2,1,0:T(8,128)(2,1)} %broadcast_in_dim.5), calls=%async_computation.4 | async-start | bytes 589824 | tf_op jit(solution)/shard_map/all_to_all | solution.py:397
  82.8 1.0 collective-permute-done.3.two
  83.9 6.8 %collective-permute-start.4 = (bf16[128,1152]{1,0:T(8,128)(2,1)S(1)}, bf16[128,1152]{1,0:T(8,128)(2,1)S(1)}, u32[]{:S(2)}, u32[]{:S(2)}) collective-permute-start(bf16[128,1152]{1,0:T(8,128)(2,1)S(1)} %pad_maximum_fusion), channel_id=1, source_target_pairs={{0,2},{1,7},{2,0},{3,5},{4,6},{5,3},{6,4},{7,1},{8,10},{9,15},{10,... | collective-permute-start | bytes 884744 | tf_op jit(solution)/shard_map/ppermute | solution.py:381
  90.7 10.0 %collective-permute-start.5 = (bf16[128,1152]{1,0:T(8,128)(2,1)S(1)}, bf16[128,1152]{1,0:T(8,128)(2,1)S(1)}, u32[]{:S(2)}, u32[]{:S(2)}) collective-permute-start(bf16[128,1152]{1,0:T(8,128)(2,1)S(1)} %pad_maximum_fusion), channel_id=1, source_target_pairs={{0,1},{1,0},{2,3},{3,2},{4,5},{5,4},{6,7},{7,6},{8,9},{9,8},{10,11... | collective-permute-start | bytes 884744 | tf_op jit(solution)/shard_map/ppermute | solution.py:381
  100.8 0.0 collective-permute-done.4.one
  100.8 7.6 %collective-permute-start.6 = (bf16[128,1152]{1,0:T(8,128)(2,1)S(1)}, bf16[128,1152]{1,0:T(8,128)(2,1)S(1)}, u32[]{:S(2)}, u32[]{:S(2)}) collective-permute-start(bf16[128,1152]{1,0:T(8,128)(2,1)S(1)} %collective-permute-done.4.one), channel_id=1, source_target_pairs={{0,1},{1,0},{2,3},{3,2},{4,5},{5,4},{6,7},{7,6},{8,9},{9,8},{10,11... | collective-permute-start | bytes 884744 | tf_op jit(solution)/shard_map/ppermute | solution.py:381
  108.4 0.0 all-to-all-done.4
  108.4 1.7 %text_grad.1 = f32[2,1152]{1,0:T(2,128)} custom-call(s32[2]{0:T(128)S(1)} %copy-done.11, f32[1]{0:T(128)S(6)} %copy.14.sharp_ref, f32[1]{0:T(128)S(6)} %copy.15.shift_ref, f32[2,1152]{1,0:T(2,128)S(1)} %get-tuple-element.31.unit_ref, f32[2,128]{1,0:T(2,128)S(1)} %get-tuple-element.32.len_ref, bf16[128,1152]{1,0:T(8,128)(2,1)S(1)} %bitcast.12, ...), custom_call_target="tpu_custom_call" | custom-call | flops 1000000000 | bytes 600000 | tf_op jit(solution)/shard_map/text_grad/pallas_call | solution.py:297
  110.1 0.0 collective-permute-done.5.near
  110.1 0.0 collective-permute-done.6.rest
  110.1 1.1 put_in_place.1
  (5 shorter events, 0.1 us)
Async XLA Ops:
  0.6 21.7 %copy-start.6 = (f32[1152]{0:T(1024)S(1)}, f32[1152]{0:T(1024)}, u32[]{:S(2)}) copy-start(f32[1152]{0:T(1024)} %gain_ref.4) | copy-start | bytes 13828
  0.6 21.7 %copy-start.7 = (f32[1152]{0:T(1024)S(1)}, f32[1152]{0:T(1024)}, u32[]{:S(2)}) copy-start(f32[1152]{0:T(1024)} %b_down_ref.1) | copy-start | bytes 13828
  0.7 21.7 %copy-start.9 = (f32[538]{0:T(1024)S(1)}, f32[538]{0:T(1024)}, u32[]{:S(2)}) copy-start(f32[538]{0:T(1024)} %bias_ref.1) | copy-start | bytes 6460
  0.7 0.7 copy-start.10
  1.3 0.7 copy-start.12
  2.0 20.4 %copy-start = (bf16[1152,538]{0,1:T(8,128)(2,1)S(1)}, bf16[1152,538]{0,1:T(8,128)(2,1)}, u32[]{:S(2)}) copy-start(bf16[1152,538]{0,1:T(8,128)(2,1)} %param.13) | copy-start | bytes 3718660
  2.0 20.4 %copy-start.1 = (bf16[538,1152]{1,0:T(8,128)(2,1)S(1)}, bf16[538,1152]{1,0:T(8,128)(2,1)}, u32[]{:S(2)}) copy-start(bf16[538,1152]{1,0:T(8,128)(2,1)} %down_ref.3) | copy-start | bytes 3718660
  17.2 11.7 %all-to-all-start.1 = ((bf16[8,16,1280]{2,1,0:T(8,128)(2,1)}), bf16[8,16,1280]{2,1,0:T(8,128)(2,1)S(1)}, u32[]{:S(2)}, u32[]{:S(2)}) async-start(bf16[8,16,1280]{2,1,0:T(8,128)(2,1)} %broadcast_in_dim.4), calls=%async_computation.1 | async-start | bytes 655360 | tf_op jit(solution)/shard_map/all_to_all | solution.py:397
  22.4 1.3 %copy-start.2 = (bf16[512,1152]{1,0:T(8,128)(2,1)S(1)}, bf16[512,1152]{1,0:T(8,128)(2,1)}, u32[]{:S(2)}) copy-start(bf16[512,1152]{1,0:T(8,128)(2,1)} %x_ref.3) | copy-start | bytes 3538948
  23.7 24.7 %copy-start.8 = (f32[1152]{0:T(1024)S(1)}, f32[1152]{0:T(1024)}, u32[]{:S(2)}) copy-start(f32[1152]{0:T(1024)} %gain_ref.3) | copy-start | bytes 13828
  23.7 24.7 %copy-start.11 = (s32[2]{0:T(128)S(1)}, s32[2]{0:T(128)}, u32[]{:S(2)}) copy-start(s32[2]{0:T(128)} %ids_ref.5) | copy-start | bytes 28
  28.1 0.8 copy-start.4
  28.9 19.5 %all-to-all-start.2 = ((f32[8,2,1152]{2,1,0:T(2,128)}), f32[8,2,1152]{2,1,0:T(2,128)S(1)}, u32[]{:S(2)}, u32[]{:S(2)}) async-start(f32[8,2,1152]{2,1,0:T(2,128)} %get-tuple-element.22), calls=%async_computation.2 | async-start | bytes 147456 | tf_op jit(solution)/shard_map/all_to_all | solution.py:397
  48.4 1.1 copy-start.5
  52.5 23.9 %copy-start.3 = (bf16[512,1152]{1,0:T(8,128)(2,1)S(1)}, bf16[512,1152]{1,0:T(8,128)(2,1)}, u32[]{:S(2)}) copy-start(bf16[512,1152]{1,0:T(8,128)(2,1)} %x_ref.3) | copy-start | bytes 3538948
  52.5 4.7 %collective-permute-start = (bf16[256,1152]{1,0:T(8,128)(2,1)S(1)}, bf16[256,1152]{1,0:T(8,128)(2,1)S(1)}, u32[]{:S(2)}, u32[]{:S(2)}) collective-permute-start(bf16[256,1152]{1,0:T(8,128)(2,1)S(1)} %get-tuple-element.26), channel_id=1, source_target_pairs={{0,1},{1,0},{2,3},{3,2},{4,5},{5,4},{6,7},{7,6},{8,9},{9,8},{10,11... | collective-permute-start | bytes 1769480 | tf_op jit(solution)/shard_map/ppermute | solution.py:381
  57.3 12.1 %collective-permute-start.1 = (bf16[128,1152]{1,0:T(8,128)(2,1)S(1)}, bf16[128,1152]{1,0:T(8,128)(2,1)S(1)}, u32[]{:S(2)}, u32[]{:S(2)}) collective-permute-start(bf16[128,1152]{1,0:T(8,128)(2,1)S(1)} %add_convert_fusion), channel_id=1, source_target_pairs={{0,2},{1,7},{2,0},{3,5},{4,6},{5,3},{6,4},{7,1},{8,10},{9,15},{10,... | collective-permute-start | bytes 884744 | tf_op jit(solution)/shard_map/ppermute | solution.py:381
  69.5 6.9 %collective-permute-start.2 = (bf16[64,1152]{1,0:T(8,128)(2,1)S(1)}, bf16[64,1152]{1,0:T(8,128)(2,1)S(1)}, u32[]{:S(2)}, u32[]{:S(2)}) collective-permute-start(bf16[64,1152]{1,0:T(8,128)(2,1)S(1)} %add_convert_fusion.1), channel_id=1, source_target_pairs={{0,6},{1,3},{2,4},{3,1},{4,2},{5,7},{6,0},{7,5},{8,14},{9,11},{10,... | collective-permute-start | bytes 442376 | tf_op jit(solution)/shard_map/ppermute | solution.py:381
  76.7 7.1 %collective-permute-start.3 = (bf16[64,1152]{1,0:T(8,128)(2,1)S(1)}, bf16[64,1152]{1,0:T(8,128)(2,1)S(1)}, u32[]{:S(2)}, u32[]{:S(2)}) collective-permute-start(bf16[64,1152]{1,0:T(8,128)(2,1)S(1)} %finish.1.own), channel_id=1, source_target_pairs={{0,6},{1,3},{2,4},{3,1},{4,2},{5,7},{6,0},{7,5},{8,14},{9,11},{10,... | collective-permute-start | bytes 442376 | tf_op jit(solution)/shard_map/ppermute | solution.py:381
  79.4 29.0 %all-to-all-start.4 = ((bf16[8,16,1152]{2,1,0:T(8,128)(2,1)}), bf16[8,16,1152]{2,1,0:T(8,128)(2,1)S(1)}, u32[]{:S(2)}, u32[]{:S(2)}) async-start(bf16[8,16,1152]{2,1,0:T(8,128)(2,1)} %broadcast_in_dim.5), calls=%async_computation.4 | async-start | bytes 589824 | tf_op jit(solution)/shard_map/all_to_all | solution.py:397
  83.9 16.9 %collective-permute-start.4 = (bf16[128,1152]{1,0:T(8,128)(2,1)S(1)}, bf16[128,1152]{1,0:T(8,128)(2,1)S(1)}, u32[]{:S(2)}, u32[]{:S(2)}) collective-permute-start(bf16[128,1152]{1,0:T(8,128)(2,1)S(1)} %pad_maximum_fusion), channel_id=1, source_target_pairs={{0,2},{1,7},{2,0},{3,5},{4,6},{5,3},{6,4},{7,1},{8,10},{9,15},{10,... | collective-permute-start | bytes 884744 | tf_op jit(solution)/shard_map/ppermute | solution.py:381
  90.7 19.4 %collective-permute-start.5 = (bf16[128,1152]{1,0:T(8,128)(2,1)S(1)}, bf16[128,1152]{1,0:T(8,128)(2,1)S(1)}, u32[]{:S(2)}, u32[]{:S(2)}) collective-permute-start(bf16[128,1152]{1,0:T(8,128)(2,1)S(1)} %pad_maximum_fusion), channel_id=1, source_target_pairs={{0,1},{1,0},{2,3},{3,2},{4,5},{5,4},{6,7},{7,6},{8,9},{9,8},{10,11... | collective-permute-start | bytes 884744 | tf_op jit(solution)/shard_map/ppermute | solution.py:381
  100.8 9.3 %collective-permute-start.6 = (bf16[128,1152]{1,0:T(8,128)(2,1)S(1)}, bf16[128,1152]{1,0:T(8,128)(2,1)S(1)}, u32[]{:S(2)}, u32[]{:S(2)}) collective-permute-start(bf16[128,1152]{1,0:T(8,128)(2,1)S(1)} %collective-permute-done.4.one), channel_id=1, source_target_pairs={{0,1},{1,0},{2,3},{3,2},{4,5},{5,4},{6,7},{7,6},{8,9},{9,8},{10,11... | collective-permute-start | bytes 884744 | tf_op jit(solution)/shard_map/ppermute | solution.py:381

commit v8 on v7

--- a/solution.py
+++ b/solution.py
@@ -399,9 +399,8 @@
     )
 
 
-def spread(rows, groups):
-    copies = jnp.broadcast_to(rows[None], (len(groups[0]),) + rows.shape)
-    return exchange(copies, groups)
+def copies_of(rows, count):
+    return jnp.broadcast_to(rows[None], (count,) + rows.shape)
 
 
 def on_device(
@@ -420,15 +419,18 @@
     batch = text_feats.shape[0] * lax.axis_size("dp")
     place = lax.axis_index("tensor").astype(jnp.int32).reshape(1)
 
-    side = math.isqrt(lax.axis_size("dp"))
-    along_y = [[y * side + k for y in range(side)] for k in range(side)]
-    along_xz = [[y * side + k for k in range(side)] for y in range(side)]
-    packed, unit_text, text_len = pack(pair_ids, text_feats, side)
-    some_text = exchange(packed, along_y).reshape(2 * side, -1)
+    count = lax.axis_size("dp")
+    n_x, n_lo = 4, 2
+    n_yz = count // n_x
+    rest_of = [y * n_x * n_lo + lo for y in range(n_yz // n_lo) for lo in range(n_lo)]
+    along_x = [[place + x * n_lo for x in range(n_x)] for place in rest_of]
+    along_yz = [[place + x * n_lo for place in rest_of] for x in range(n_x)]
+    packed, unit_text, text_len = pack(pair_ids, text_feats, n_yz)
+    some_text = exchange(packed, along_yz).reshape(2 * n_yz, -1)
 
     up_t = w_up.T
     some_text, first_gain = lax.optimization_barrier((some_text, ln_gain))
-    rows = spread(some_text, along_xz).reshape(batch, -1)
+    rows = exchange(copies_of(some_text, n_x), along_x).reshape(batch, -1)
     slope, parts = forward(
         patches, first_gain, up_t, b_up, w_down, b_down, lax.axis_size("tensor")
     )
@@ -445,7 +447,7 @@
         w_down,
         up_t,
         slope,
-        side,
+        n_x,
     )
 
     other = swap_core(away)
@@ -457,23 +459,27 @@
     send_one = both(0, 128).astype(BF16)
     got_one = swap(send_one, "tensor", step_one)
     img_copies, _ = lax.optimization_barrier((img_copies, send_one))
-    some_img = exchange(img_copies, along_xz).reshape(2 * side, -1)
+    some_img = exchange(img_copies, along_x).reshape(2 * n_x, -1)
     got_one, some_img = lax.optimization_barrier((got_one, some_img))
     send_two = (both(128, 64) + got_one[:64].astype(F32)).astype(BF16)
     got_two = swap(send_two, "tensor", step_two)
-    images = spread(some_img, along_y).reshape(batch, -1)
+    some_img, _ = lax.optimization_barrier((some_img, send_two))
+    img_copies = copies_of(some_img, n_yz)
+    got_two, img_copies = lax.optimization_barrier((got_two, img_copies))
+    images = exchange(img_copies, along_yz).reshape(batch, -1)
     done = finish(place, keep, other, got_one, got_two, patches, g_hidden, ln_gain)
 
     from_two = swap(done, "tensor", step_two)
     pair = jnp.concatenate([done, from_two])
     from_one = swap(pair, "tensor", step_one)
     near = swap_core(pair)
+    from_one, images = lax.optimization_barrier((from_one, images))
     rest = swap_core(from_one)
     grad_patches = put_in_place(
         place, (done, from_two, from_one, near, rest), patches.shape[0]
     )
 
-    ids = rows[:, -128:].reshape(side, side, 2, 128).swapaxes(0, 1).reshape(batch, 128)
+    ids = rows[:, -128:].reshape(n_x, n_yz, 2, 128).swapaxes(0, 1).reshape(batch, 128)
     grad_text = text_grad(
         log_sharpness,
         pairwise_logit_shift,

time: 112 us -> 112 us (level)
  the two profiles are of different devices: /device:TPU:65 before, /device:TPU:1 now
where the time goes in v8:
time: 112 us
  starting transfers between devices  47.3 us (42%)
  blocking collectives  25.7 us (23%)
  waiting for transfers between devices  19.1 us (17%)
  Pallas kernels  11.2 us (10%)
  local copies, waits for them, and re-layouts  6.14 us (5%)
  between operations  2.13 us (2%)
    ppermute x7, starting transfers between devices, swap(): return lax.ppermute(value, axis, [(i, partner(i)) for i in range(size)])  27.6 us
    all_to_all x2, blocking collectives, exchange(): lax.all_to_all(copies, axis, split_axis=0, concat_axis=0, axis_index_grou...  25.7 us
    all_to_all x3, starting transfers between devices, exchange(): lax.all_to_all(copies, axis, split_axis=0, concat_axis=0, axis_index_grou...  19.7 us
    ppermute x7, waiting for transfers between devices, swap(): return lax.ppermute(value, axis, [(i, partner(i)) for i in range(size)])  13 us
    all_to_all x3, waiting for transfers between devices, exchange(): lax.all_to_all(copies, axis, split_axis=0, concat_axis=0, axis_index_grou...  6.05 us
    unnamed x26, local copies, waits for them, and re-layouts  4.57 us
    pallas_call x1, Pallas kernels, forward(): pl.pallas_call(functools.partial(forward_kernel, n_tensor), grid=(tokens...  4.4 us
    pallas_call x1, Pallas kernels, loss_and_back(): pl.pallas_call(loss_kernel, in_specs=[SMEM] * 2 + [VMEM] * 8, out_shape=[...  2.99 us
  transfers between devices with their start and end apart: 10, of which 6 were waited for; matrix products, arithmetic and copies ran while one was open for 0% of the time, Pallas kernels for 5%

profile of v8, /device:TPU:1, one launch (start us, length us, event | category | flops | bytes accessed | tf_op | source)
XLA Modules:
  0.0 111.7 jit_solution(1535867251350929176)
XLA Ops:
  0.6 0.0 copy-start.10
  0.6 0.6 copy-done.10
  1.3 0.0 copy-start.12
  1.3 0.7 copy-done.12
  2.0 0.0 copy-start.1
  2.0 0.7 pack.1
  2.6 0.0 copy-start
  2.7 0.0 copy-start.6
  2.7 0.0 copy-start.7
  2.7 0.0 copy-start.9
  2.7 17.6 %all_to_all.25 = bf16[16,2,1280]{2,1,0:T(2,128)(2,1)S(1)} all-to-all(bf16[16,2,1280]{2,1,0:T(2,128)(2,1)S(1)} %get-tuple-element.23), channel_id=1, replica_groups={{0,8,64,72,128,136,192,200,256,264,320,328,384,392,448,456},{16,24,80,8..., dimensions={0} | all-to-all | bytes 163840 | tf_op jit(solution)/shard_map/all_to_all | solution.py:397
  20.4 0.8 broadcast_in_dim.4
  21.1 4.0 %all-to-all-start.1 = ((bf16[4,32,1280]{2,1,0:T(8,128)(2,1)}), bf16[4,32,1280]{2,1,0:T(8,128)(2,1)S(1)}, u32[]{:S(2)}, u32[]{:S(2)}) async-start(bf16[4,32,1280]{2,1,0:T(8,128)(2,1)} %broadcast_in_dim.4), calls=%async_computation.1 | async-start | bytes 655360 | tf_op jit(solution)/shard_map/all_to_all | solution.py:397
  25.1 0.0 copy-done.1
  25.1 0.0 copy-done
  25.1 0.0 copy-done.6
  25.1 0.0 copy-done.7
  25.2 0.0 copy-done.9
  25.2 0.0 copy-start.2
  25.2 1.3 %copy-done.2 = bf16[512,1152]{1,0:T(8,128)(2,1)S(1)} copy-done((bf16[512,1152]{1,0:T(8,128)(2,1)S(1)}, bf16[512,1152]{1,0:T(8,128)(2,1)}, u32[]{:S(2)}) %copy-start.2) | copy-done | bytes 1179672
  26.4 0.0 copy-start.8
  26.4 0.0 copy-start.11
  26.4 4.4 %forward.1 = (bf16[512,538]{1,0:T(8,128)(2,1)S(1)}, f32[8,2,1152]{2,1,0:T(2,128)}) custom-call(bf16[512,1152]{1,0:T(8,128)(2,1)S(1)} %copy-done.2, f32[1152]{0:T(1024)S(1)} %copy-done.6, f32[538]{0:T(1024)S(1)} %copy-done.9, f32[1152]{0:T(1024)S(1)} %copy-done.7, bf16[538,1152]{1,0:T(8,128)(2,1)S(1)} %bitcast.8, bf16[538,1152]{1,0:T(8,128)(2,1)S(1)} %copy-done.1), custom_call_target="tpu_custom_call" | custom-call | flops 634650624 | bytes 4760576 | tf_op jit(solution)/shard_map/forward/pallas_call | solution.py:153
  30.8 0.0 copy-start.4
  30.8 0.8 copy-done.4
  31.7 0.0 all-to-all-done.1
  31.7 12.2 %all-to-all-start.2 = ((f32[8,2,1152]{2,1,0:T(2,128)}), f32[8,2,1152]{2,1,0:T(2,128)S(1)}, u32[]{:S(2)}, u32[]{:S(2)}) async-start(f32[8,2,1152]{2,1,0:T(2,128)} %get-tuple-element.27), calls=%async_computation.2 | async-start | bytes 147456 | tf_op jit(solution)/shard_map/all_to_all | solution.py:397
  45.2 6.0 %all-to-all-done.2.parts_ref = f32[8,2,1152]{2,1,0:T(2,128)S(1)} async-done(((f32[8,2,1152]{2,1,0:T(2,128)}), f32[8,2,1152]{2,1,0:T(2,128)S(1)}, u32[]{:S(2)}, u32[]{:S(2)}) %all-to-all-start.2) | async-done | bytes 73760 | tf_op jit(solution)/shard_map/all_to_all | solution.py:397
  51.2 0.0 copy-done.8
  51.2 0.0 copy-done.11
  51.2 0.0 copy-start.5
  51.2 1.1 copy-done.5
  52.3 3.0 %loss_and_back.1 = (bf16[4,2,1152]{2,1,0:T(2,128)(2,1)S(1)}, f32[2,1152]{1,0:T(2,128)S(1)}, bf16[256,1152]{1,0:T(8,128)(2,1)S(1)}, bf16[256,1152]{1,0:T(8,128)(2,1)S(1)}) custom-call(s32[1]{0:T(128)} %bitcast.place_ref, s32[2]{0:T(128)S(1)} %copy-done.11, f32[1]{0:T(128)S(6)} %copy.14.sharp_ref, f32[1]{0:T(128)S(6)} %copy.15.shift_ref, ...), custom_call_target="tpu_custom_call" | custom-call | flops 634650624 | bytes 4820480 | tf_op jit(solution)/shard_map/loss_and_back/pallas_call | solution.py:263
  55.3 0.0 copy-start.3
  55.3 3.1 %collective-permute-start = (bf16[256,1152]{1,0:T(8,128)(2,1)S(1)}, bf16[256,1152]{1,0:T(8,128)(2,1)S(1)}, u32[]{:S(2)}, u32[]{:S(2)}) collective-permute-start(bf16[256,1152]{1,0:T(8,128)(2,1)S(1)} %get-tuple-element.31), channel_id=1, source_target_pairs={{0,1},{1,0},{2,3},{3,2},{4,5},{5,4},{6,7},{7,6},{8,9},{9,8},{10,11... | collective-permute-start | bytes 1769480 | tf_op jit(solution)/shard_map/ppermute | solution.py:381
  58.4 1.6 %collective-permute-done.other_ref = bf16[256,1152]{1,0:T(8,128)(2,1)S(1)} collective-permute-done((bf16[256,1152]{1,0:T(8,128)(2,1)S(1)}, bf16[256,1152]{1,0:T(8,128)(2,1)S(1)}, u32[]{:S(2)}, u32[]{:S(2)}) %collective-permute-start) | collective-permute-done | bytes 589856 | tf_op jit(solution)/shard_map/ppermute | solution.py:381
  60.0 0.1 add_convert_fusion
  60.0 2.0 %collective-permute-start.1 = (bf16[128,1152]{1,0:T(8,128)(2,1)S(1)}, bf16[128,1152]{1,0:T(8,128)(2,1)S(1)}, u32[]{:S(2)}, u32[]{:S(2)}) collective-permute-start(bf16[128,1152]{1,0:T(8,128)(2,1)S(1)} %add_convert_fusion), channel_id=1, source_target_pairs={{0,2},{1,7},{2,0},{3,5},{4,6},{5,3},{6,4},{7,1},{8,10},{9,15},{10,... | collective-permute-start | bytes 884744 | tf_op jit(solution)/shard_map/ppermute | solution.py:381
  62.1 8.1 %all_to_all.26 = bf16[4,2,1152]{2,1,0:T(2,128)(2,1)S(1)} all-to-all(bf16[4,2,1152]{2,1,0:T(2,128)(2,1)S(1)} %get-tuple-element.33), channel_id=1, replica_groups={{0,16,32,48},{8,24,40,56},{64,80,96,112},{72,88,104,120},{128,144,160,1..., dimensions={0} | all-to-all | bytes 36864 | tf_op jit(solution)/shard_map/all_to_all | solution.py:397
  70.2 1.6 %collective-permute-done.1.one_ref = bf16[128,1152]{1,0:T(8,128)(2,1)S(1)} collective-permute-done((bf16[128,1152]{1,0:T(8,128)(2,1)S(1)}, bf16[128,1152]{1,0:T(8,128)(2,1)S(1)}, u32[]{:S(2)}, u32[]{:S(2)}) %collective-permute-start.1) | collective-permute-done | bytes 294944 | tf_op jit(solution)/shard_map/ppermute | solution.py:381
  71.8 0.1 add_convert_fusion.1
  71.8 3.5 %collective-permute-start.2 = (bf16[64,1152]{1,0:T(8,128)(2,1)S(1)}, bf16[64,1152]{1,0:T(8,128)(2,1)S(1)}, u32[]{:S(2)}, u32[]{:S(2)}) collective-permute-start(bf16[64,1152]{1,0:T(8,128)(2,1)S(1)} %add_convert_fusion.1), channel_id=1, source_target_pairs={{0,6},{1,3},{2,4},{3,1},{4,2},{5,7},{6,0},{7,5},{8,14},{9,11},{10,... | collective-permute-start | bytes 442376 | tf_op jit(solution)/shard_map/ppermute | solution.py:381
  75.4 5.1 %collective-permute-done.2.two_ref = bf16[64,1152]{1,0:T(8,128)(2,1)S(1)} collective-permute-done((bf16[64,1152]{1,0:T(8,128)(2,1)S(1)}, bf16[64,1152]{1,0:T(8,128)(2,1)S(1)}, u32[]{:S(2)}, u32[]{:S(2)}) %collective-permute-start.2) | collective-permute-done | bytes 147488 | tf_op jit(solution)/shard_map/ppermute | solution.py:381
  80.5 0.7 broadcast_in_dim.5
  81.2 0.0 copy-done.3
  81.2 0.4 finish.1.own
  81.6 1.9 %collective-permute-start.3 = (bf16[64,1152]{1,0:T(8,128)(2,1)S(1)}, bf16[64,1152]{1,0:T(8,128)(2,1)S(1)}, u32[]{:S(2)}, u32[]{:S(2)}) collective-permute-start(bf16[64,1152]{1,0:T(8,128)(2,1)S(1)} %finish.1.own), channel_id=1, source_target_pairs={{0,6},{1,3},{2,4},{3,1},{4,2},{5,7},{6,0},{7,5},{8,14},{9,11},{10,... | collective-permute-start | bytes 442376 | tf_op jit(solution)/shard_map/ppermute | solution.py:381
  83.5 3.5 %all-to-all-start.4 = ((bf16[16,8,1152]{2,1,0:T(8,128)(2,1)}), bf16[16,8,1152]{2,1,0:T(8,128)(2,1)S(1)}, u32[]{:S(2)}, u32[]{:S(2)}) async-start(bf16[16,8,1152]{2,1,0:T(8,128)(2,1)} %broadcast_in_dim.5), calls=%async_computation.4 | async-start | bytes 589824 | tf_op jit(solution)/shard_map/all_to_all | solution.py:397
  87.1 2.8 %collective-permute-done.3.two = bf16[64,1152]{1,0:T(8,128)(2,1)S(1)} collective-permute-done((bf16[64,1152]{1,0:T(8,128)(2,1)S(1)}, bf16[64,1152]{1,0:T(8,128)(2,1)S(1)}, u32[]{:S(2)}, u32[]{:S(2)}) %collective-permute-start.3) | collective-permute-done | bytes 147488 | tf_op jit(solution)/shard_map/ppermute | solution.py:381
  89.9 2.0 %collective-permute-start.4 = (bf16[128,1152]{1,0:T(8,128)(2,1)S(1)}, bf16[128,1152]{1,0:T(8,128)(2,1)S(1)}, u32[]{:S(2)}, u32[]{:S(2)}) collective-permute-start(bf16[128,1152]{1,0:T(8,128)(2,1)S(1)} %pad_maximum_fusion), channel_id=1, source_target_pairs={{0,2},{1,7},{2,0},{3,5},{4,6},{5,3},{6,4},{7,1},{8,10},{9,15},{10,... | collective-permute-start | bytes 884744 | tf_op jit(solution)/shard_map/ppermute | solution.py:381
  92.0 9.8 %collective-permute-start.5 = (bf16[128,1152]{1,0:T(8,128)(2,1)S(1)}, bf16[128,1152]{1,0:T(8,128)(2,1)S(1)}, u32[]{:S(2)}, u32[]{:S(2)}) collective-permute-start(bf16[128,1152]{1,0:T(8,128)(2,1)S(1)} %pad_maximum_fusion), channel_id=1, source_target_pairs={{0,1},{1,0},{2,3},{3,2},{4,5},{5,4},{6,7},{7,6},{8,9},{9,8},{10,11... | collective-permute-start | bytes 884744 | tf_op jit(solution)/shard_map/ppermute | solution.py:381
  101.8 1.9 %collective-permute-done.4.one = bf16[128,1152]{1,0:T(8,128)(2,1)S(1)} collective-permute-done((bf16[128,1152]{1,0:T(8,128)(2,1)S(1)}, bf16[128,1152]{1,0:T(8,128)(2,1)S(1)}, u32[]{:S(2)}, u32[]{:S(2)}) %collective-permute-start.4) | collective-permute-done | bytes 294944 | tf_op jit(solution)/shard_map/ppermute | solution.py:381
  103.7 0.0 all-to-all-done.4
  103.7 5.1 %collective-permute-start.6 = (bf16[128,1152]{1,0:T(8,128)(2,1)S(1)}, bf16[128,1152]{1,0:T(8,128)(2,1)S(1)}, u32[]{:S(2)}, u32[]{:S(2)}) collective-permute-start(bf16[128,1152]{1,0:T(8,128)(2,1)S(1)} %collective-permute-done.4.one), channel_id=1, source_target_pairs={{0,1},{1,0},{2,3},{3,2},{4,5},{5,4},{6,7},{7,6},{8,9},{9,8},{10,11... | collective-permute-start | bytes 884744 | tf_op jit(solution)/shard_map/ppermute | solution.py:381
  108.9 1.7 %text_grad.1 = f32[2,1152]{1,0:T(2,128)} custom-call(s32[2]{0:T(128)S(1)} %copy-done.11, f32[1]{0:T(128)S(6)} %copy.14.sharp_ref, f32[1]{0:T(128)S(6)} %copy.15.shift_ref, f32[2,1152]{1,0:T(2,128)S(1)} %get-tuple-element.41.unit_ref, f32[2,128]{1,0:T(2,128)S(1)} %get-tuple-element.42.len_ref, bf16[128,1152]{1,0:T(8,128)(2,1)S(1)} %bitcast.12, ...), custom_call_target="tpu_custom_call" | custom-call | flops 1000000000 | bytes 600000 | tf_op jit(solution)/shard_map/text_grad/pallas_call | solution.py:297
  110.6 0.0 collective-permute-done.5.near
  110.6 0.0 collective-permute-done.6.rest
  110.6 1.1 put_in_place.1
  (5 shorter events, 0.1 us)
Async XLA Ops:
  0.6 0.7 copy-start.10
  1.3 0.7 copy-start.12
  2.0 23.2 %copy-start.1 = (bf16[538,1152]{1,0:T(8,128)(2,1)S(1)}, bf16[538,1152]{1,0:T(8,128)(2,1)}, u32[]{:S(2)}) copy-start(bf16[538,1152]{1,0:T(8,128)(2,1)} %down_ref.3) | copy-start | bytes 3718660
  2.6 22.5 %copy-start = (bf16[1152,538]{0,1:T(8,128)(2,1)S(1)}, bf16[1152,538]{0,1:T(8,128)(2,1)}, u32[]{:S(2)}) copy-start(bf16[1152,538]{0,1:T(8,128)(2,1)} %param.13) | copy-start | bytes 3718660
  2.7 22.5 %copy-start.6 = (f32[1152]{0:T(1024)S(1)}, f32[1152]{0:T(1024)}, u32[]{:S(2)}) copy-start(f32[1152]{0:T(1024)} %gain_ref.4) | copy-start | bytes 13828
  2.7 22.5 %copy-start.7 = (f32[1152]{0:T(1024)S(1)}, f32[1152]{0:T(1024)}, u32[]{:S(2)}) copy-start(f32[1152]{0:T(1024)} %b_down_ref.1) | copy-start | bytes 13828
  2.7 22.5 %copy-start.9 = (f32[538]{0:T(1024)S(1)}, f32[538]{0:T(1024)}, u32[]{:S(2)}) copy-start(f32[538]{0:T(1024)} %bias_ref.1) | copy-start | bytes 6460
  21.1 10.6 %all-to-all-start.1 = ((bf16[4,32,1280]{2,1,0:T(8,128)(2,1)}), bf16[4,32,1280]{2,1,0:T(8,128)(2,1)S(1)}, u32[]{:S(2)}, u32[]{:S(2)}) async-start(bf16[4,32,1280]{2,1,0:T(8,128)(2,1)} %broadcast_in_dim.4), calls=%async_computation.1 | async-start | bytes 655360 | tf_op jit(solution)/shard_map/all_to_all | solution.py:397
  25.2 1.3 %copy-start.2 = (bf16[512,1152]{1,0:T(8,128)(2,1)S(1)}, bf16[512,1152]{1,0:T(8,128)(2,1)}, u32[]{:S(2)}) copy-start(bf16[512,1152]{1,0:T(8,128)(2,1)} %x_ref.3) | copy-start | bytes 3538948
  26.4 24.8 %copy-start.8 = (f32[1152]{0:T(1024)S(1)}, f32[1152]{0:T(1024)}, u32[]{:S(2)}) copy-start(f32[1152]{0:T(1024)} %gain_ref.3) | copy-start | bytes 13828
  26.4 24.8 %copy-start.11 = (s32[2]{0:T(128)S(1)}, s32[2]{0:T(128)}, u32[]{:S(2)}) copy-start(s32[2]{0:T(128)} %ids_ref.5) | copy-start | bytes 28
  30.8 0.8 copy-start.4
  31.7 19.5 %all-to-all-start.2 = ((f32[8,2,1152]{2,1,0:T(2,128)}), f32[8,2,1152]{2,1,0:T(2,128)S(1)}, u32[]{:S(2)}, u32[]{:S(2)}) async-start(f32[8,2,1152]{2,1,0:T(2,128)} %get-tuple-element.27), calls=%async_computation.2 | async-start | bytes 147456 | tf_op jit(solution)/shard_map/all_to_all | solution.py:397
  51.2 1.1 copy-start.5
  55.3 25.9 %copy-start.3 = (bf16[512,1152]{1,0:T(8,128)(2,1)S(1)}, bf16[512,1152]{1,0:T(8,128)(2,1)}, u32[]{:S(2)}) copy-start(bf16[512,1152]{1,0:T(8,128)(2,1)} %x_ref.3) | copy-start | bytes 3538948
  55.3 4.7 %collective-permute-start = (bf16[256,1152]{1,0:T(8,128)(2,1)S(1)}, bf16[256,1152]{1,0:T(8,128)(2,1)S(1)}, u32[]{:S(2)}, u32[]{:S(2)}) collective-permute-start(bf16[256,1152]{1,0:T(8,128)(2,1)S(1)} %get-tuple-element.31), channel_id=1, source_target_pairs={{0,1},{1,0},{2,3},{3,2},{4,5},{5,4},{6,7},{7,6},{8,9},{9,8},{10,11... | collective-permute-start | bytes 1769480 | tf_op jit(solution)/shard_map/ppermute | solution.py:381
  60.0 11.7 %collective-permute-start.1 = (bf16[128,1152]{1,0:T(8,128)(2,1)S(1)}, bf16[128,1152]{1,0:T(8,128)(2,1)S(1)}, u32[]{:S(2)}, u32[]{:S(2)}) collective-permute-start(bf16[128,1152]{1,0:T(8,128)(2,1)S(1)} %add_convert_fusion), channel_id=1, source_target_pairs={{0,2},{1,7},{2,0},{3,5},{4,6},{5,3},{6,4},{7,1},{8,10},{9,15},{10,... | collective-permute-start | bytes 884744 | tf_op jit(solution)/shard_map/ppermute | solution.py:381
  71.8 8.7 %collective-permute-start.2 = (bf16[64,1152]{1,0:T(8,128)(2,1)S(1)}, bf16[64,1152]{1,0:T(8,128)(2,1)S(1)}, u32[]{:S(2)}, u32[]{:S(2)}) collective-permute-start(bf16[64,1152]{1,0:T(8,128)(2,1)S(1)} %add_convert_fusion.1), channel_id=1, source_target_pairs={{0,6},{1,3},{2,4},{3,1},{4,2},{5,7},{6,0},{7,5},{8,14},{9,11},{10,... | collective-permute-start | bytes 442376 | tf_op jit(solution)/shard_map/ppermute | solution.py:381
  81.6 8.3 %collective-permute-start.3 = (bf16[64,1152]{1,0:T(8,128)(2,1)S(1)}, bf16[64,1152]{1,0:T(8,128)(2,1)S(1)}, u32[]{:S(2)}, u32[]{:S(2)}) collective-permute-start(bf16[64,1152]{1,0:T(8,128)(2,1)S(1)} %finish.1.own), channel_id=1, source_target_pairs={{0,6},{1,3},{2,4},{3,1},{4,2},{5,7},{6,0},{7,5},{8,14},{9,11},{10,... | collective-permute-start | bytes 442376 | tf_op jit(solution)/shard_map/ppermute | solution.py:381
  83.5 20.2 %all-to-all-start.4 = ((bf16[16,8,1152]{2,1,0:T(8,128)(2,1)}), bf16[16,8,1152]{2,1,0:T(8,128)(2,1)S(1)}, u32[]{:S(2)}, u32[]{:S(2)}) async-start(bf16[16,8,1152]{2,1,0:T(8,128)(2,1)} %broadcast_in_dim.5), calls=%async_computation.4 | async-start | bytes 589824 | tf_op jit(solution)/shard_map/all_to_all | solution.py:397
  89.9 13.8 %collective-permute-start.4 = (bf16[128,1152]{1,0:T(8,128)(2,1)S(1)}, bf16[128,1152]{1,0:T(8,128)(2,1)S(1)}, u32[]{:S(2)}, u32[]{:S(2)}) collective-permute-start(bf16[128,1152]{1,0:T(8,128)(2,1)S(1)} %pad_maximum_fusion), channel_id=1, source_target_pairs={{0,2},{1,7},{2,0},{3,5},{4,6},{5,3},{6,4},{7,1},{8,10},{9,15},{10,... | collective-permute-start | bytes 884744 | tf_op jit(solution)/shard_map/ppermute | solution.py:381
  92.0 18.6 %collective-permute-start.5 = (bf16[128,1152]{1,0:T(8,128)(2,1)S(1)}, bf16[128,1152]{1,0:T(8,128)(2,1)S(1)}, u32[]{:S(2)}, u32[]{:S(2)}) collective-permute-start(bf16[128,1152]{1,0:T(8,128)(2,1)S(1)} %pad_maximum_fusion), channel_id=1, source_target_pairs={{0,1},{1,0},{2,3},{3,2},{4,5},{5,4},{6,7},{7,6},{8,9},{9,8},{10,11... | collective-permute-start | bytes 884744 | tf_op jit(solution)/shard_map/ppermute | solution.py:381
  103.7 6.9 %collective-permute-start.6 = (bf16[128,1152]{1,0:T(8,128)(2,1)S(1)}, bf16[128,1152]{1,0:T(8,128)(2,1)S(1)}, u32[]{:S(2)}, u32[]{:S(2)}) collective-permute-start(bf16[128,1152]{1,0:T(8,128)(2,1)S(1)} %collective-permute-done.4.one), channel_id=1, source_target_pairs={{0,1},{1,0},{2,3},{3,2},{4,5},{5,4},{6,7},{7,6},{8,9},{9,8},{10,11... | collective-permute-start | bytes 884744 | tf_op jit(solution)/shard_map/ppermute | solution.py:381

commit v9 on v7

--- a/solution.py
+++ b/solution.py
@@ -342,6 +342,9 @@
         ),
         out_shape=jax.ShapeDtypeStruct((BLOCK, width), BF16),
         compiler_params=SMALL,
+        cost_estimate=pl.CostEstimate(
+            flops=5_000_000_000, bytes_accessed=1_000_000, transcendentals=0
+        ),
         name="finish",
     )(place, keep, other, got_one, got_two, patches, g_hidden, ln_gain)
 
@@ -461,18 +464,11 @@
     got_one, some_img = lax.optimization_barrier((got_one, some_img))
     send_two = (both(128, 64) + got_one[:64].astype(F32)).astype(BF16)
     got_two = swap(send_two, "tensor", step_two)
+    some_img, _ = lax.optimization_barrier((some_img, send_two))
     images = spread(some_img, along_y).reshape(batch, -1)
     done = finish(place, keep, other, got_one, got_two, patches, g_hidden, ln_gain)
 
     from_two = swap(done, "tensor", step_two)
-    pair = jnp.concatenate([done, from_two])
-    from_one = swap(pair, "tensor", step_one)
-    near = swap_core(pair)
-    rest = swap_core(from_one)
-    grad_patches = put_in_place(
-        place, (done, from_two, from_one, near, rest), patches.shape[0]
-    )
-
     ids = rows[:, -128:].reshape(side, side, 2, 128).swapaxes(0, 1).reshape(batch, 128)
     grad_text = text_grad(
         log_sharpness,
@@ -483,6 +479,15 @@
         images,
         ids,
     )
+    from_two, grad_text = lax.optimization_barrier((from_two, grad_text))
+    pair = jnp.concatenate([done, from_two])
+    from_one = swap(pair, "tensor", step_one)
+    near = swap_core(pair)
+    rest = swap_core(from_one)
+    grad_patches = put_in_place(
+        place, (done, from_two, from_one, near, rest), patches.shape[0]
+    )
+
     return grad_patches, grad_text
 
 

time: 112 us -> 113 us (level)
  other arithmetic: 0.15 us -> 1.72 us
    all_to_all x3, waiting for transfers between devices: 6.14 us -> 9.67 us  [exchange(): lax.all_to_all(copies, axis, split_axis=0, concat_axis=0, axis_index_grou...]
    ppermute x7, waiting for transfers between devices: 8.44 us -> 5.59 us  [swap(): return lax.ppermute(value, axis, [(i, partner(i)) for i in range(size)])]
    ppermute x7, starting transfers between devices: 34 us -> 32.3 us  [swap(): return lax.ppermute(value, axis, [(i, partner(i)) for i in range(size)])]
    convert_element_type x1, other arithmetic: 0.06 us -> 1.63 us  [on_device(): send_two = (both(128, 64) + got_one[:64].astype(F32)).astype(BF16)]
    unnamed x26 -> x32, local copies, waits for them, and re-layouts: 4.58 us -> 4.85 us
  transfers between devices with their start and end apart: 10 -> 10, of which waited for: 5 -> 6; matrix products, arithmetic and copies ran while one was open for 1% -> 1% of each run, Pallas kernels for 5% -> 5%
where the time goes in v9:
time: 113 us; the launch traced here: 112 us
  starting transfers between devices  53.8 us (48%)
  blocking collectives  21.6 us (19%)
  waiting for transfers between devices  15.3 us (14%)
  Pallas kernels  10.9 us (10%)
  local copies, waits for them, and re-layouts  6.39 us (6%)
  between operations  2.17 us (2%)
  other arithmetic  1.72 us (2%)
    ppermute x7, starting transfers between devices, swap(): return lax.ppermute(value, axis, [(i, partner(i)) for i in range(size)])  32.3 us
    all_to_all x2, blocking collectives, exchange(): lax.all_to_all(copies, axis, split_axis=0, concat_axis=0, axis_index_grou...  21.6 us
    all_to_all x3, starting transfers between devices, exchange(): lax.all_to_all(copies, axis, split_axis=0, concat_axis=0, axis_index_grou...  21.4 us
    all_to_all x3, waiting for transfers between devices, exchange(): lax.all_to_all(copies, axis, split_axis=0, concat_axis=0, axis_index_grou...  9.67 us
    ppermute x7, waiting for transfers between devices, swap(): return lax.ppermute(value, axis, [(i, partner(i)) for i in range(size)])  5.59 us
    unnamed x32, local copies, waits for them, and re-layouts  4.85 us
    pallas_call x1, Pallas kernels, forward(): pl.pallas_call(functools.partial(forward_kernel, n_tensor), grid=(tokens...  3.76 us
    pallas_call x1, Pallas kernels, loss_and_back(): pl.pallas_call(loss_kernel, in_specs=[SMEM] * 2 + [VMEM] * 8, out_shape=[...  3.34 us
  transfers between devices with their start and end apart: 10, of which 6 were waited for; matrix products, arithmetic and copies ran while one was open for 1% of the time, Pallas kernels for 5%

profile of v9, /device:TPU:65, one launch (start us, length us, event | category | flops | bytes accessed | tf_op | source)
XLA Modules:
  0.0 111.8 jit_solution(5148218893852390285)
XLA Ops:
  0.6 0.0 copy-start.9
  0.6 0.0 copy-start.7
  0.7 0.0 copy-start.10
  0.7 0.0 copy-start.11
  0.7 0.7 copy-done.11
  1.3 0.0 copy-start.15
  1.3 0.7 copy-done.15
  2.0 0.0 copy-start
  2.0 0.0 copy-start.1
  2.0 0.7 pack.1
  2.7 13.7 %all_to_all.25 = bf16[8,2,1280]{2,1,0:T(2,128)(2,1)S(1)} all-to-all(bf16[8,2,1280]{2,1,0:T(2,128)(2,1)S(1)} %get-tuple-element.21), channel_id=1, replica_groups={{0,64,128,192,256,320,384,448},{8,72,136,200,264,328,392,456},{16,80,14..., dimensions={0} | all-to-all | bytes 81920 | tf_op jit(solution)/shard_map/all_to_all | solution.py:400
  16.4 0.7 broadcast_in_dim.4
  17.2 5.2 %all-to-all-start.1 = ((bf16[8,16,1280]{2,1,0:T(8,128)(2,1)}), bf16[8,16,1280]{2,1,0:T(8,128)(2,1)S(1)}, u32[]{:S(2)}, u32[]{:S(2)}) async-start(bf16[8,16,1280]{2,1,0:T(8,128)(2,1)} %broadcast_in_dim.4), calls=%async_computation.1 | async-start | bytes 655360 | tf_op jit(solution)/shard_map/all_to_all | solution.py:400
  22.4 0.0 copy-done.9
  22.4 0.0 copy-done.7
  22.4 0.0 copy-done.10
  22.4 0.0 copy-done
  22.4 0.0 copy-done.1
  22.4 0.0 copy-start.2
  22.4 1.3 %copy-done.2 = bf16[512,1152]{1,0:T(8,128)(2,1)S(1)} copy-done((bf16[512,1152]{1,0:T(8,128)(2,1)S(1)}, bf16[512,1152]{1,0:T(8,128)(2,1)}, u32[]{:S(2)}) %copy-start.2) | copy-done | bytes 1179672
  23.7 0.0 copy-start.8
  23.7 0.0 copy-start.12
  23.7 3.8 %forward.1 = (bf16[512,538]{1,0:T(8,128)(2,1)S(1)}, f32[8,2,1152]{2,1,0:T(2,128)S(1)}) custom-call(bf16[512,1152]{1,0:T(8,128)(2,1)S(1)} %copy-done.2, f32[1152]{0:T(1024)S(1)} %copy-done.9, f32[538]{0:T(1024)S(1)} %copy-done.10, f32[1152]{0:T(1024)S(1)} %copy-done.7, bf16[538,1152]{1,0:T(8,128)(2,1)S(1)} %bitcast.8, bf16[538,1152]{1,0:T(8,128)(2,1)S(1)} %copy-done.1), custom_call_target="tpu_custom_call" | custom-call | flops 634650624 | bytes 4760576 | tf_op jit(solution)/shard_map/forward/pallas_call | solution.py:153
  27.5 0.0 copy-start.6
  27.5 0.6 copy-done.6
  28.1 0.0 all-to-all-done.1
  28.1 12.8 %all-to-all-start.2 = ((f32[8,2,1152]{2,1,0:T(2,128)}), f32[8,2,1152]{2,1,0:T(2,128)}, u32[]{:S(2)}, u32[]{:S(2)}) async-start(f32[8,2,1152]{2,1,0:T(2,128)} %copy-done.6), calls=%async_computation.2 | async-start | bytes 147456 | tf_op jit(solution)/shard_map/all_to_all | solution.py:400
  42.2 6.2 %all-to-all-done.2.parts_ref = f32[8,2,1152]{2,1,0:T(2,128)} async-done(((f32[8,2,1152]{2,1,0:T(2,128)}), f32[8,2,1152]{2,1,0:T(2,128)}, u32[]{:S(2)}, u32[]{:S(2)}) %all-to-all-start.2) | async-done | bytes 73760 | tf_op jit(solution)/shard_map/all_to_all | solution.py:400
  48.4 0.0 copy-done.8
  48.4 0.0 copy-done.12
  48.4 3.3 %loss_and_back.1 = (bf16[8,2,1152]{2,1,0:T(2,128)(2,1)S(1)}, f32[2,1152]{1,0:T(2,128)S(1)}, bf16[256,1152]{1,0:T(8,128)(2,1)S(1)}, bf16[256,1152]{1,0:T(8,128)(2,1)S(1)}) custom-call(s32[1]{0:T(128)} %bitcast.place_ref, s32[2]{0:T(128)S(1)} %copy-done.12, f32[1]{0:T(128)S(6)} %copy.14.sharp_ref, f32[1]{0:T(128)S(6)} %copy.15.shift_ref, ...), custom_call_target="tpu_custom_call" | custom-call | flops 634650624 | bytes 4820480 | tf_op jit(solution)/shard_map/loss_and_back/pallas_call | solution.py:263
  51.8 0.0 copy-start.4
  51.8 3.0 %collective-permute-start = (bf16[256,1152]{1,0:T(8,128)(2,1)S(1)}, bf16[256,1152]{1,0:T(8,128)(2,1)S(1)}, u32[]{:S(2)}, u32[]{:S(2)}) collective-permute-start(bf16[256,1152]{1,0:T(8,128)(2,1)S(1)} %get-tuple-element.29), channel_id=1, source_target_pairs={{0,1},{1,0},{2,3},{3,2},{4,5},{5,4},{6,7},{7,6},{8,9},{9,8},{10,11... | collective-permute-start | bytes 1769480 | tf_op jit(solution)/shard_map/ppermute | solution.py:384
  54.8 1.6 %collective-permute-done.other_ref = bf16[256,1152]{1,0:T(8,128)(2,1)S(1)} collective-permute-done((bf16[256,1152]{1,0:T(8,128)(2,1)S(1)}, bf16[256,1152]{1,0:T(8,128)(2,1)S(1)}, u32[]{:S(2)}, u32[]{:S(2)}) %collective-permute-start) | collective-permute-done | bytes 589856 | tf_op jit(solution)/shard_map/ppermute | solution.py:384
  56.4 0.0 copy-done.4
  56.4 0.0 copy-start.3
  56.4 0.1 add_convert_fusion
  56.5 0.0 copy-start.5
  56.5 2.8 %collective-permute-start.1 = (bf16[128,1152]{1,0:T(8,128)(2,1)S(1)}, bf16[128,1152]{1,0:T(8,128)(2,1)S(1)}, u32[]{:S(2)}, u32[]{:S(2)}) collective-permute-start(bf16[128,1152]{1,0:T(8,128)(2,1)S(1)} %add_convert_fusion), channel_id=1, source_target_pairs={{0,2},{1,7},{2,0},{3,5},{4,6},{5,3},{6,4},{7,1},{8,10},{9,15},{10,... | collective-permute-start | bytes 884744 | tf_op jit(solution)/shard_map/ppermute | solution.py:384
  59.3 7.9 %all_to_all.26 = bf16[8,2,1152]{2,1,0:T(2,128)(2,1)S(1)} all-to-all(bf16[8,2,1152]{2,1,0:T(2,128)(2,1)S(1)} %get-tuple-element.31), channel_id=1, replica_groups={{0,8,16,24,32,40,48,56},{64,72,80,88,96,104,112,120},{128,136,144,152,1..., dimensions={0} | all-to-all | bytes 73728 | tf_op jit(solution)/shard_map/all_to_all | solution.py:400
  67.2 1.8 %collective-permute-done.1.one_ref = bf16[128,1152]{1,0:T(8,128)(2,1)S(1)} collective-permute-done((bf16[128,1152]{1,0:T(8,128)(2,1)S(1)}, bf16[128,1152]{1,0:T(8,128)(2,1)S(1)}, u32[]{:S(2)}, u32[]{:S(2)}) %collective-permute-start.1) | collective-permute-done | bytes 294944 | tf_op jit(solution)/shard_map/ppermute | solution.py:384
  69.0 1.6 %add_convert_fusion.1 = bf16[64,1152]{1,0:T(8,128)(2,1)} fusion(bf16[256,1152]{1,0:T(8,128)(2,1)S(1)} %collective-permute-done.other_ref, bf16[128,1152]{1,0:T(8,128)(2,1)S(1)} %collective-permute-done.1.one_ref, bf16[256,1152]{1,0:T(8,128)(2,1)} %copy-done.4), kind=kLoop, calls=%fused_computation.2 | loop fusion | flops 442368 | bytes 589824 | tf_op jit(solution)/shard_map/convert_element_type | solution.py:465
  70.6 1.9 %collective-permute-start.2 = (bf16[64,1152]{1,0:T(8,128)(2,1)}, bf16[64,1152]{1,0:T(8,128)(2,1)S(1)}, u32[]{:S(2)}, u32[]{:S(2)}) collective-permute-start(bf16[64,1152]{1,0:T(8,128)(2,1)} %add_convert_fusion.1), channel_id=1, source_target_pairs={{0,6},{1,3},{2,4},{3,1},{4,2},{5,7},{6,0},{7,5},{8,14},{9,11},{10,... | collective-permute-start | bytes 442376 | tf_op jit(solution)/shard_map/ppermute | solution.py:384
  72.5 0.7 broadcast_in_dim.5
  73.3 3.4 %all-to-all-start.4 = ((bf16[8,16,1152]{2,1,0:T(8,128)(2,1)}), bf16[8,16,1152]{2,1,0:T(8,128)(2,1)S(1)}, u32[]{:S(2)}, u32[]{:S(2)}) async-start(bf16[8,16,1152]{2,1,0:T(8,128)(2,1)} %broadcast_in_dim.5), calls=%async_computation.4 | async-start | bytes 589824 | tf_op jit(solution)/shard_map/all_to_all | solution.py:400
  76.7 1.0 collective-permute-done.2.two_ref
  77.7 0.0 copy-start.13
  77.7 0.6 copy-done.13
  78.4 0.0 copy-done.3
  78.4 0.0 copy-done.5
  78.4 0.0 copy-start.14
  78.4 0.9 copy-done.14
  79.3 0.4 finish.1.own
  79.6 3.3 %collective-permute-start.3 = (bf16[64,1152]{1,0:T(8,128)(2,1)S(1)}, bf16[64,1152]{1,0:T(8,128)(2,1)S(1)}, u32[]{:S(2)}, u32[]{:S(2)}) collective-permute-start(bf16[64,1152]{1,0:T(8,128)(2,1)S(1)} %finish.1.own), channel_id=1, source_target_pairs={{0,6},{1,3},{2,4},{3,1},{4,2},{5,7},{6,0},{7,5},{8,14},{9,11},{10,... | collective-permute-start | bytes 442376 | tf_op jit(solution)/shard_map/ppermute | solution.py:384
  83.0 3.5 %all-to-all-done.4 = bf16[8,16,1152]{2,1,0:T(8,128)(2,1)S(1)} async-done(((bf16[8,16,1152]{2,1,0:T(8,128)(2,1)}), bf16[8,16,1152]{2,1,0:T(8,128)(2,1)S(1)}, u32[]{:S(2)}, u32[]{:S(2)}) %all-to-all-start.4) | async-done | bytes 294944 | tf_op jit(solution)/shard_map/all_to_all | solution.py:400
  86.4 1.7 %text_grad.1 = f32[2,1152]{1,0:T(2,128)} custom-call(s32[2]{0:T(128)S(1)} %copy-done.12, f32[1]{0:T(128)S(6)} %copy.14.sharp_ref, f32[1]{0:T(128)S(6)} %copy.15.shift_ref, f32[2,1152]{1,0:T(2,128)S(1)} %get-tuple-element.34.unit_ref, f32[2,128]{1,0:T(2,128)S(1)} %get-tuple-element.35.len_ref, bf16[128,1152]{1,0:T(8,128)(2,1)S(1)} %bitcast.12, ...), custom_call_target="tpu_custom_call" | custom-call | flops 1000000000 | bytes 600000 | tf_op jit(solution)/shard_map/text_grad/pallas_call | solution.py:297
  88.1 0.0 collective-permute-done.3.two
  88.1 4.8 %collective-permute-start.4 = (bf16[128,1152]{1,0:T(8,128)(2,1)S(1)}, bf16[128,1152]{1,0:T(8,128)(2,1)S(1)}, u32[]{:S(2)}, u32[]{:S(2)}) collective-permute-start(bf16[128,1152]{1,0:T(8,128)(2,1)S(1)} %pad_maximum_fusion), channel_id=1, source_target_pairs={{0,2},{1,7},{2,0},{3,5},{4,6},{5,3},{6,4},{7,1},{8,10},{9,15},{10,... | collective-permute-start | bytes 884744 | tf_op jit(solution)/shard_map/ppermute | solution.py:384
  92.9 6.7 %collective-permute-start.5 = (bf16[128,1152]{1,0:T(8,128)(2,1)S(1)}, bf16[128,1152]{1,0:T(8,128)(2,1)S(1)}, u32[]{:S(2)}, u32[]{:S(2)}) collective-permute-start(bf16[128,1152]{1,0:T(8,128)(2,1)S(1)} %pad_maximum_fusion), channel_id=1, source_target_pairs={{0,1},{1,0},{2,3},{3,2},{4,5},{5,4},{6,7},{7,6},{8,9},{9,8},{10,11... | collective-permute-start | bytes 884744 | tf_op jit(solution)/shard_map/ppermute | solution.py:384
  99.6 0.0 collective-permute-done.4.one
  99.6 9.9 %collective-permute-start.6 = (bf16[128,1152]{1,0:T(8,128)(2,1)S(1)}, bf16[128,1152]{1,0:T(8,128)(2,1)S(1)}, u32[]{:S(2)}, u32[]{:S(2)}) collective-permute-start(bf16[128,1152]{1,0:T(8,128)(2,1)S(1)} %collective-permute-done.4.one), channel_id=1, source_target_pairs={{0,1},{1,0},{2,3},{3,2},{4,5},{5,4},{6,7},{7,6},{8,9},{9,8},{10,11... | collective-permute-start | bytes 884744 | tf_op jit(solution)/shard_map/ppermute | solution.py:384
  109.5 0.0 collective-permute-done.5.near
  109.6 1.2 %collective-permute-done.6.rest = bf16[128,1152]{1,0:T(8,128)(2,1)S(1)} collective-permute-done((bf16[128,1152]{1,0:T(8,128)(2,1)S(1)}, bf16[128,1152]{1,0:T(8,128)(2,1)S(1)}, u32[]{:S(2)}, u32[]{:S(2)}) %collective-permute-start.6) | collective-permute-done | bytes 294944 | tf_op jit(solution)/shard_map/ppermute | solution.py:384
  110.7 1.1 put_in_place.1
  (5 shorter events, 0.1 us)
Async XLA Ops:
  0.6 21.7 %copy-start.9 = (f32[1152]{0:T(1024)S(1)}, f32[1152]{0:T(1024)}, u32[]{:S(2)}) copy-start(f32[1152]{0:T(1024)} %gain_ref.4) | copy-start | bytes 13828
  0.6 21.7 %copy-start.7 = (f32[1152]{0:T(1024)S(1)}, f32[1152]{0:T(1024)}, u32[]{:S(2)}) copy-start(f32[1152]{0:T(1024)} %b_down_ref.1) | copy-start | bytes 13828
  0.7 21.7 %copy-start.10 = (f32[538]{0:T(1024)S(1)}, f32[538]{0:T(1024)}, u32[]{:S(2)}) copy-start(f32[538]{0:T(1024)} %bias_ref.1) | copy-start | bytes 6460
  0.7 0.7 copy-start.11
  1.3 0.7 copy-start.15
  2.0 20.4 %copy-start = (bf16[1152,538]{0,1:T(8,128)(2,1)S(1)}, bf16[1152,538]{0,1:T(8,128)(2,1)}, u32[]{:S(2)}) copy-start(bf16[1152,538]{0,1:T(8,128)(2,1)} %param.13) | copy-start | bytes 3718660
  2.0 20.4 %copy-start.1 = (bf16[538,1152]{1,0:T(8,128)(2,1)S(1)}, bf16[538,1152]{1,0:T(8,128)(2,1)}, u32[]{:S(2)}) copy-start(bf16[538,1152]{1,0:T(8,128)(2,1)} %down_ref.3) | copy-start | bytes 3718660
  17.2 10.9 %all-to-all-start.1 = ((bf16[8,16,1280]{2,1,0:T(8,128)(2,1)}), bf16[8,16,1280]{2,1,0:T(8,128)(2,1)S(1)}, u32[]{:S(2)}, u32[]{:S(2)}) async-start(bf16[8,16,1280]{2,1,0:T(8,128)(2,1)} %broadcast_in_dim.4), calls=%async_computation.1 | async-start | bytes 655360 | tf_op jit(solution)/shard_map/all_to_all | solution.py:400
  22.4 1.3 %copy-start.2 = (bf16[512,1152]{1,0:T(8,128)(2,1)S(1)}, bf16[512,1152]{1,0:T(8,128)(2,1)}, u32[]{:S(2)}) copy-start(bf16[512,1152]{1,0:T(8,128)(2,1)} %x_ref.3) | copy-start | bytes 3538948
  23.7 24.7 %copy-start.8 = (f32[1152]{0:T(1024)S(1)}, f32[1152]{0:T(1024)}, u32[]{:S(2)}) copy-start(f32[1152]{0:T(1024)} %gain_ref.3) | copy-start | bytes 13828
  23.7 24.7 %copy-start.12 = (s32[2]{0:T(128)S(1)}, s32[2]{0:T(128)}, u32[]{:S(2)}) copy-start(s32[2]{0:T(128)} %ids_ref.5) | copy-start | bytes 28
  27.5 0.6 copy-start.6
  28.1 20.3 %all-to-all-start.2 = ((f32[8,2,1152]{2,1,0:T(2,128)}), f32[8,2,1152]{2,1,0:T(2,128)}, u32[]{:S(2)}, u32[]{:S(2)}) async-start(f32[8,2,1152]{2,1,0:T(2,128)} %copy-done.6), calls=%async_computation.2 | async-start | bytes 147456 | tf_op jit(solution)/shard_map/all_to_all | solution.py:400
  51.8 4.7 %copy-start.4 = (bf16[256,1152]{1,0:T(8,128)(2,1)}, bf16[256,1152]{1,0:T(8,128)(2,1)S(1)}, u32[]{:S(2)}) copy-start(bf16[256,1152]{1,0:T(8,128)(2,1)S(1)} %get-tuple-element.28.keep_ref) | copy-start | bytes 1769476
  51.8 4.6 %collective-permute-start = (bf16[256,1152]{1,0:T(8,128)(2,1)S(1)}, bf16[256,1152]{1,0:T(8,128)(2,1)S(1)}, u32[]{:S(2)}, u32[]{:S(2)}) collective-permute-start(bf16[256,1152]{1,0:T(8,128)(2,1)S(1)} %get-tuple-element.29), channel_id=1, source_target_pairs={{0,1},{1,0},{2,3},{3,2},{4,5},{5,4},{6,7},{7,6},{8,9},{9,8},{10,11... | collective-permute-start | bytes 1769480 | tf_op jit(solution)/shard_map/ppermute | solution.py:384
  56.4 21.9 %copy-start.3 = (bf16[512,1152]{1,0:T(8,128)(2,1)S(1)}, bf16[512,1152]{1,0:T(8,128)(2,1)}, u32[]{:S(2)}) copy-start(bf16[512,1152]{1,0:T(8,128)(2,1)} %x_ref.3) | copy-start | bytes 3538948
  56.5 21.9 %copy-start.5 = (bf16[256,1152]{1,0:T(8,128)(2,1)S(1)}, bf16[256,1152]{1,0:T(8,128)(2,1)}, u32[]{:S(2)}) copy-start(bf16[256,1152]{1,0:T(8,128)(2,1)} %copy-done.4) | copy-start | bytes 1769476
  56.5 12.5 %collective-permute-start.1 = (bf16[128,1152]{1,0:T(8,128)(2,1)S(1)}, bf16[128,1152]{1,0:T(8,128)(2,1)S(1)}, u32[]{:S(2)}, u32[]{:S(2)}) collective-permute-start(bf16[128,1152]{1,0:T(8,128)(2,1)S(1)} %add_convert_fusion), channel_id=1, source_target_pairs={{0,2},{1,7},{2,0},{3,5},{4,6},{5,3},{6,4},{7,1},{8,10},{9,15},{10,... | collective-permute-start | bytes 884744 | tf_op jit(solution)/shard_map/ppermute | solution.py:384
  70.6 7.1 %collective-permute-start.2 = (bf16[64,1152]{1,0:T(8,128)(2,1)}, bf16[64,1152]{1,0:T(8,128)(2,1)S(1)}, u32[]{:S(2)}, u32[]{:S(2)}) collective-permute-start(bf16[64,1152]{1,0:T(8,128)(2,1)} %add_convert_fusion.1), channel_id=1, source_target_pairs={{0,6},{1,3},{2,4},{3,1},{4,2},{5,7},{6,0},{7,5},{8,14},{9,11},{10,... | collective-permute-start | bytes 442376 | tf_op jit(solution)/shard_map/ppermute | solution.py:384
  73.3 13.1 %all-to-all-start.4 = ((bf16[8,16,1152]{2,1,0:T(8,128)(2,1)}), bf16[8,16,1152]{2,1,0:T(8,128)(2,1)S(1)}, u32[]{:S(2)}, u32[]{:S(2)}) async-start(bf16[8,16,1152]{2,1,0:T(8,128)(2,1)} %broadcast_in_dim.5), calls=%async_computation.4 | async-start | bytes 589824 | tf_op jit(solution)/shard_map/all_to_all | solution.py:400
  77.7 0.7 copy-start.13
  78.4 0.9 copy-start.14
  79.6 8.5 %collective-permute-start.3 = (bf16[64,1152]{1,0:T(8,128)(2,1)S(1)}, bf16[64,1152]{1,0:T(8,128)(2,1)S(1)}, u32[]{:S(2)}, u32[]{:S(2)}) collective-permute-start(bf16[64,1152]{1,0:T(8,128)(2,1)S(1)} %finish.1.own), channel_id=1, source_target_pairs={{0,6},{1,3},{2,4},{3,1},{4,2},{5,7},{6,0},{7,5},{8,14},{9,11},{10,... | collective-permute-start | bytes 442376 | tf_op jit(solution)/shard_map/ppermute | solution.py:384
  88.1 11.5 %collective-permute-start.4 = (bf16[128,1152]{1,0:T(8,128)(2,1)S(1)}, bf16[128,1152]{1,0:T(8,128)(2,1)S(1)}, u32[]{:S(2)}, u32[]{:S(2)}) collective-permute-start(bf16[128,1152]{1,0:T(8,128)(2,1)S(1)} %pad_maximum_fusion), channel_id=1, source_target_pairs={{0,2},{1,7},{2,0},{3,5},{4,6},{5,3},{6,4},{7,1},{8,10},{9,15},{10,... | collective-permute-start | bytes 884744 | tf_op jit(solution)/shard_map/ppermute | solution.py:384
  92.9 16.6 %collective-permute-start.5 = (bf16[128,1152]{1,0:T(8,128)(2,1)S(1)}, bf16[128,1152]{1,0:T(8,128)(2,1)S(1)}, u32[]{:S(2)}, u32[]{:S(2)}) collective-permute-start(bf16[128,1152]{1,0:T(8,128)(2,1)S(1)} %pad_maximum_fusion), channel_id=1, source_target_pairs={{0,1},{1,0},{2,3},{3,2},{4,5},{5,4},{6,7},{7,6},{8,9},{9,8},{10,11... | collective-permute-start | bytes 884744 | tf_op jit(solution)/shard_map/ppermute | solution.py:384
  99.6 11.1 %collective-permute-start.6 = (bf16[128,1152]{1,0:T(8,128)(2,1)S(1)}, bf16[128,1152]{1,0:T(8,128)(2,1)S(1)}, u32[]{:S(2)}, u32[]{:S(2)}) collective-permute-start(bf16[128,1152]{1,0:T(8,128)(2,1)S(1)} %collective-permute-done.4.one), channel_id=1, source_target_pairs={{0,1},{1,0},{2,3},{3,2},{4,5},{5,4},{6,7},{7,6},{8,9},{9,8},{10,11... | collective-permute-start | bytes 884744 | tf_op jit(solution)/shard_map/ppermute | solution.py:384

commit v10 on v9

--- a/solution.py
+++ b/solution.py
@@ -306,47 +306,24 @@
     )(ids, sharp, shift, unit, length, images, columns)
 
 
-def finish_kernel(
-    place_ref, keep_ref, other_ref, one_ref, two_ref, x_ref, hidden_ref, gain_ref, out_ref
-):
-    g_normed = keep_ref[...].astype(F32) + other_ref[...].astype(F32)
-    g_normed = g_normed + one_ref[...].astype(F32) + two_ref[...].astype(F32)
+def finish_kernel(place_ref, mine_ref, one_ref, two_ref, x_ref, hidden_ref, gain_ref, out_ref):
+    g_normed = mine_ref[...] + one_ref[BLOCK:, :].astype(F32) + two_ref[...].astype(F32)
     normed, inverse = norm_parts(x_ref[...].astype(F32))
     grad = norm_back(g_normed, gain_ref[...][None, :], normed, inverse)
     out_ref[...] = (grad + pick_row(hidden_ref[...], place_ref[0] & 1)).astype(BF16)
 
 
-def finish(place, keep, other, got_one, got_two, patches, g_hidden, ln_gain):
-    width = patches.shape[1]
-    block = lambda index: pl.BlockSpec((BLOCK, width), index)
-
-    def own_block(i, place):
-        core, one, two = places(place[0])
-        return core * (PATCHES // BLOCK) + 2 * one + two, 0
-
+def finish(place, mine, got_one, got_two, own_x, g_hidden, ln_gain):
     return pl.pallas_call(
         finish_kernel,
-        grid_spec=pltpu.PrefetchScalarGridSpec(
-            num_scalar_prefetch=1,
-            grid=(1,),
-            in_specs=[
-                block(lambda i, place: (3, 0)),
-                block(lambda i, place: (3, 0)),
-                block(lambda i, place: (1, 0)),
-                block(lambda i, place: (0, 0)),
-                block(own_block),
-                pl.BlockSpec((2, width), lambda i, place: (0, 0)),
-                pl.BlockSpec((width,), lambda i, place: (0,)),
-            ],
-            out_specs=block(lambda i, place: (0, 0)),
-        ),
-        out_shape=jax.ShapeDtypeStruct((BLOCK, width), BF16),
+        in_specs=[SMEM] + [VMEM] * 6,
+        out_shape=jax.ShapeDtypeStruct(mine.shape, BF16),
         compiler_params=SMALL,
         cost_estimate=pl.CostEstimate(
             flops=5_000_000_000, bytes_accessed=1_000_000, transcendentals=0
         ),
         name="finish",
-    )(place, keep, other, got_one, got_two, patches, g_hidden, ln_gain)
+    )(place, mine, got_one, got_two, own_x, g_hidden, ln_gain)
 
 
 def place_kernel(place_ref, own, two, one, near, rest, out_ref):
@@ -461,12 +438,17 @@
     got_one = swap(send_one, "tensor", step_one)
     img_copies, _ = lax.optimization_barrier((img_copies, send_one))
     some_img = exchange(img_copies, along_xz).reshape(2 * side, -1)
-    got_one, some_img = lax.optimization_barrier((got_one, some_img))
-    send_two = (both(128, 64) + got_one[:64].astype(F32)).astype(BF16)
+    core, one, two = places(place[0])
+    own_start = core * PATCHES + (2 * one + two) * BLOCK
+    own_x = lax.dynamic_slice_in_dim(patches, own_start, BLOCK, 0)
+    got_one, some_img, travels, mine, own_x = lax.optimization_barrier(
+        (got_one, some_img, both(128, 64), both(192, 64), own_x)
+    )
+    send_two = (travels + got_one[:BLOCK].astype(F32)).astype(BF16)
     got_two = swap(send_two, "tensor", step_two)
     some_img, _ = lax.optimization_barrier((some_img, send_two))
     images = spread(some_img, along_y).reshape(batch, -1)
-    done = finish(place, keep, other, got_one, got_two, patches, g_hidden, ln_gain)
+    done = finish(place, mine, got_one, got_two, own_x, g_hidden, ln_gain)
 
     from_two = swap(done, "tensor", step_two)
     ids = rows[:, -128:].reshape(side, side, 2, 128).swapaxes(0, 1).reshape(batch, 128)

time: 113 us -> 112 us (level)
  the two profiles are of different devices: /device:TPU:65 before, /device:TPU:1 now
where the time goes in v10:
time: 112 us; the launch traced here: 111 us
  starting transfers between devices  45.3 us (40%)
  waiting for transfers between devices  30.4 us (27%)
  blocking collectives  14.5 us (13%)
  Pallas kernels  11.2 us (10%)
  local copies, waits for them, and re-layouts  6.56 us (6%)
  between operations  2.18 us (2%)
  other arithmetic  1.14 us (1%)
    all_to_all x4, starting transfers between devices, exchange(): lax.all_to_all(copies, axis, split_axis=0, concat_axis=0, axis_index_grou...  26 us
    all_to_all x4, waiting for transfers between devices, exchange(): lax.all_to_all(copies, axis, split_axis=0, concat_axis=0, axis_index_grou...  20.9 us
    ppermute x7, starting transfers between devices, swap(): return lax.ppermute(value, axis, [(i, partner(i)) for i in range(size)])  19.3 us
    all_to_all x1, blocking collectives, exchange(): lax.all_to_all(copies, axis, split_axis=0, concat_axis=0, axis_index_grou...  14.5 us
    ppermute x7, waiting for transfers between devices, swap(): return lax.ppermute(value, axis, [(i, partner(i)) for i in range(size)])  9.43 us
    unnamed x26, local copies, waits for them, and re-layouts  4.08 us
    pallas_call x1, Pallas kernels, forward(): pl.pallas_call(functools.partial(forward_kernel, n_tensor), grid=(tokens...  3.74 us
    pallas_call x1, Pallas kernels, loss_and_back(): pl.pallas_call(loss_kernel, in_specs=[SMEM] * 2 + [VMEM] * 8, out_shape=[...  3.67 us
  transfers between devices with their start and end apart: 11, of which 9 were waited for; matrix products, arithmetic and copies ran while one was open for 2% of the time, Pallas kernels for 5%

profile of v10, /device:TPU:1, one launch (start us, length us, event | category | flops | bytes accessed | tf_op | source)
XLA Modules:
  0.0 111.2 jit_solution(13704117876573395302)
XLA Ops:
  0.6 0.0 copy-start.10
  0.6 0.6 copy-done.10
  1.3 0.0 copy-start.12
  1.3 0.7 copy-done.12
  2.0 0.0 copy-start
  2.0 0.0 copy-start.1
  2.0 0.7 pack.1
  2.6 0.0 copy-start.6
  2.7 0.0 copy-start.8
  2.7 0.0 copy-start.9
  2.7 14.5 %all_to_all.25 = bf16[8,2,1280]{2,1,0:T(2,128)(2,1)S(1)} all-to-all(bf16[8,2,1280]{2,1,0:T(2,128)(2,1)S(1)} %get-tuple-element.24), channel_id=1, replica_groups={{0,64,128,192,256,320,384,448},{8,72,136,200,264,328,392,456},{16,80,14..., dimensions={0} | all-to-all | bytes 81920 | tf_op jit(solution)/shard_map/all_to_all | solution.py:377
  17.2 0.7 broadcast_in_dim.4
  18.0 5.8 %all-to-all-start.1 = ((bf16[8,16,1280]{2,1,0:T(8,128)(2,1)}), bf16[8,16,1280]{2,1,0:T(8,128)(2,1)S(1)}, u32[]{:S(2)}, u32[]{:S(2)}) async-start(bf16[8,16,1280]{2,1,0:T(8,128)(2,1)} %broadcast_in_dim.4), calls=%async_computation.1 | async-start | bytes 655360 | tf_op jit(solution)/shard_map/all_to_all | solution.py:377
  23.8 0.0 copy-done
  23.8 0.0 copy-done.1
  23.8 0.0 copy-done.6
  23.8 0.0 copy-done.8
  23.9 0.0 copy-done.9
  23.9 0.0 copy-start.2
  23.9 1.3 %copy-done.2 = bf16[512,1152]{1,0:T(8,128)(2,1)S(1)} copy-done((bf16[512,1152]{1,0:T(8,128)(2,1)S(1)}, bf16[512,1152]{1,0:T(8,128)(2,1)}, u32[]{:S(2)}) %copy-start.2) | copy-done | bytes 1179672
  25.1 0.0 copy-start.7
  25.1 0.0 copy-start.11
  25.1 3.7 %forward.1 = (bf16[512,538]{1,0:T(8,128)(2,1)S(1)}, f32[8,2,1152]{2,1,0:T(2,128)S(1)}) custom-call(bf16[512,1152]{1,0:T(8,128)(2,1)S(1)} %copy-done.2, f32[1152]{0:T(1024)S(1)} %copy-done.8, f32[538]{0:T(1024)S(1)} %copy-done.9, f32[1152]{0:T(1024)S(1)} %copy-done.6, bf16[538,1152]{1,0:T(8,128)(2,1)S(1)} %bitcast.8, bf16[538,1152]{1,0:T(8,128)(2,1)S(1)} %copy-done.1), custom_call_target="tpu_custom_call" | custom-call | flops 634650624 | bytes 4760576 | tf_op jit(solution)/shard_map/forward/pallas_call | solution.py:153
  28.9 0.0 copy-start.5
  28.9 0.6 copy-done.5
  29.5 0.8 all-to-all-done.1
  30.3 12.9 %all-to-all-start.2 = ((f32[8,2,1152]{2,1,0:T(2,128)}), f32[8,2,1152]{2,1,0:T(2,128)}, u32[]{:S(2)}, u32[]{:S(2)}) async-start(f32[8,2,1152]{2,1,0:T(2,128)} %copy-done.5), calls=%async_computation.2 | async-start | bytes 147456 | tf_op jit(solution)/shard_map/all_to_all | solution.py:377
  44.5 6.2 %all-to-all-done.2.parts_ref = f32[8,2,1152]{2,1,0:T(2,128)} async-done(((f32[8,2,1152]{2,1,0:T(2,128)}), f32[8,2,1152]{2,1,0:T(2,128)}, u32[]{:S(2)}, u32[]{:S(2)}) %all-to-all-start.2) | async-done | bytes 73760 | tf_op jit(solution)/shard_map/all_to_all | solution.py:377
  50.8 0.0 copy-done.7
  50.8 0.0 copy-done.11
  50.8 3.7 %loss_and_back.1 = (bf16[8,2,1152]{2,1,0:T(2,128)(2,1)}, f32[2,1152]{1,0:T(2,128)S(1)}, bf16[256,1152]{1,0:T(8,128)(2,1)}, bf16[256,1152]{1,0:T(8,128)(2,1)S(1)}) custom-call(s32[1]{0:T(128)} %bitcast.place_ref, s32[2]{0:T(128)S(1)} %copy-done.11, f32[1]{0:T(128)S(6)} %copy.14.sharp_ref, f32[1]{0:T(128)S(6)} %copy.15.shift_ref, ...), custom_call_target="tpu_custom_call" | custom-call | flops 634650624 | bytes 4820480 | tf_op jit(solution)/shard_map/loss_and_back/pallas_call | solution.py:263
  54.5 0.0 copy-start.3
  54.5 0.8 copy-done.3
  55.3 0.0 copy-start.4
  55.3 3.0 %collective-permute-start = (bf16[256,1152]{1,0:T(8,128)(2,1)}, bf16[256,1152]{1,0:T(8,128)(2,1)S(1)}, u32[]{:S(2)}, u32[]{:S(2)}) collective-permute-start(bf16[256,1152]{1,0:T(8,128)(2,1)} %get-tuple-element.32), channel_id=1, source_target_pairs={{0,1},{1,0},{2,3},{3,2},{4,5},{5,4},{6,7},{7,6},{8,9},{9,8},{10,11... | collective-permute-start | bytes 1769480 | tf_op jit(solution)/shard_map/ppermute | solution.py:361
  58.3 0.9 constant_dynamic-slice_fusion.x_ref
  59.3 0.9 collective-permute-done
  60.2 1.0 add_convert_fusion
  61.2 2.1 %collective-permute-start.1 = (bf16[128,1152]{1,0:T(8,128)(2,1)S(1)}, bf16[128,1152]{1,0:T(8,128)(2,1)S(1)}, u32[]{:S(2)}, u32[]{:S(2)}) collective-permute-start(bf16[128,1152]{1,0:T(8,128)(2,1)S(1)} %add_convert_fusion), channel_id=1, source_target_pairs={{0,2},{1,7},{2,0},{3,5},{4,6},{5,3},{6,4},{7,1},{8,10},{9,15},{10,... | collective-permute-start | bytes 884744 | tf_op jit(solution)/shard_map/ppermute | solution.py:361
  63.3 3.8 %all-to-all-start.3 = ((bf16[8,2,1152]{2,1,0:T(2,128)(2,1)}), bf16[8,2,1152]{2,1,0:T(2,128)(2,1)S(1)}, u32[]{:S(2)}, u32[]{:S(2)}) async-start(bf16[8,2,1152]{2,1,0:T(2,128)(2,1)} %get-tuple-element.34), calls=%async_computation.3 | async-start | bytes 73728 | tf_op jit(solution)/shard_map/all_to_all | solution.py:377
  67.1 0.0 copy-done.4
  67.1 0.1 convert_add_fusion
  67.1 5.1 %all-to-all-done.3 = bf16[8,2,1152]{2,1,0:T(2,128)(2,1)S(1)} async-done(((bf16[8,2,1152]{2,1,0:T(2,128)(2,1)}), bf16[8,2,1152]{2,1,0:T(2,128)(2,1)S(1)}, u32[]{:S(2)}, u32[]{:S(2)}) %all-to-all-start.3) | async-done | bytes 36896 | tf_op jit(solution)/shard_map/all_to_all | solution.py:377
  72.2 1.9 %collective-permute-done.1.one_ref = bf16[128,1152]{1,0:T(8,128)(2,1)S(1)} collective-permute-done((bf16[128,1152]{1,0:T(8,128)(2,1)S(1)}, bf16[128,1152]{1,0:T(8,128)(2,1)S(1)}, u32[]{:S(2)}, u32[]{:S(2)}) %collective-permute-start.1) | collective-permute-done | bytes 294944 | tf_op jit(solution)/shard_map/ppermute | solution.py:361
  74.1 2.6 %collective-permute-start.2 = (bf16[64,1152]{1,0:T(8,128)(2,1)S(1)}, bf16[64,1152]{1,0:T(8,128)(2,1)S(1)}, u32[]{:S(2)}, u32[]{:S(2)}) collective-permute-start(bf16[64,1152]{1,0:T(8,128)(2,1)S(1)} %add_convert_fusion.1), channel_id=1, source_target_pairs={{0,6},{1,3},{2,4},{3,1},{4,2},{5,7},{6,0},{7,5},{8,14},{9,11},{10,... | collective-permute-start | bytes 442376 | tf_op jit(solution)/shard_map/ppermute | solution.py:361
  76.7 0.7 broadcast_in_dim.5
  77.4 3.4 %all-to-all-start.4 = ((bf16[8,16,1152]{2,1,0:T(8,128)(2,1)}), bf16[8,16,1152]{2,1,0:T(8,128)(2,1)S(1)}, u32[]{:S(2)}, u32[]{:S(2)}) async-start(bf16[8,16,1152]{2,1,0:T(8,128)(2,1)} %broadcast_in_dim.5), calls=%async_computation.4 | async-start | bytes 589824 | tf_op jit(solution)/shard_map/all_to_all | solution.py:377
  80.9 1.9 %collective-permute-done.2.two_ref = bf16[64,1152]{1,0:T(8,128)(2,1)S(1)} collective-permute-done((bf16[64,1152]{1,0:T(8,128)(2,1)S(1)}, bf16[64,1152]{1,0:T(8,128)(2,1)S(1)}, u32[]{:S(2)}, u32[]{:S(2)}) %collective-permute-start.2) | collective-permute-done | bytes 147488 | tf_op jit(solution)/shard_map/ppermute | solution.py:361
  82.8 0.3 finish.1.own
  83.1 1.9 %collective-permute-start.3 = (bf16[64,1152]{1,0:T(8,128)(2,1)S(1)}, bf16[64,1152]{1,0:T(8,128)(2,1)S(1)}, u32[]{:S(2)}, u32[]{:S(2)}) collective-permute-start(bf16[64,1152]{1,0:T(8,128)(2,1)S(1)} %finish.1.own), channel_id=1, source_target_pairs={{0,6},{1,3},{2,4},{3,1},{4,2},{5,7},{6,0},{7,5},{8,14},{9,11},{10,... | collective-permute-start | bytes 442376 | tf_op jit(solution)/shard_map/ppermute | solution.py:361
  85.1 8.8 %all-to-all-done.4 = bf16[8,16,1152]{2,1,0:T(8,128)(2,1)S(1)} async-done(((bf16[8,16,1152]{2,1,0:T(8,128)(2,1)}), bf16[8,16,1152]{2,1,0:T(8,128)(2,1)S(1)}, u32[]{:S(2)}, u32[]{:S(2)}) %all-to-all-start.4) | async-done | bytes 294944 | tf_op jit(solution)/shard_map/all_to_all | solution.py:377
  93.9 1.7 %text_grad.1 = f32[2,1152]{1,0:T(2,128)} custom-call(s32[2]{0:T(128)S(1)} %copy-done.11, f32[1]{0:T(128)S(6)} %copy.14.sharp_ref, f32[1]{0:T(128)S(6)} %copy.15.shift_ref, f32[2,1152]{1,0:T(2,128)S(1)} %get-tuple-element.40.unit_ref, f32[2,128]{1,0:T(2,128)S(1)} %get-tuple-element.41.len_ref, bf16[128,1152]{1,0:T(8,128)(2,1)S(1)} %bitcast.12, ...), custom_call_target="tpu_custom_call" | custom-call | flops 1000000000 | bytes 600000 | tf_op jit(solution)/shard_map/text_grad/pallas_call | solution.py:297
  95.6 0.0 collective-permute-done.3.two
  95.6 1.9 %collective-permute-start.4 = (bf16[128,1152]{1,0:T(8,128)(2,1)S(1)}, bf16[128,1152]{1,0:T(8,128)(2,1)S(1)}, u32[]{:S(2)}, u32[]{:S(2)}) collective-permute-start(bf16[128,1152]{1,0:T(8,128)(2,1)S(1)} %pad_maximum_fusion), channel_id=1, source_target_pairs={{0,2},{1,7},{2,0},{3,5},{4,6},{5,3},{6,4},{7,1},{8,10},{9,15},{10,... | collective-permute-start | bytes 884744 | tf_op jit(solution)/shard_map/ppermute | solution.py:361
  97.5 4.3 %collective-permute-start.5 = (bf16[128,1152]{1,0:T(8,128)(2,1)S(1)}, bf16[128,1152]{1,0:T(8,128)(2,1)S(1)}, u32[]{:S(2)}, u32[]{:S(2)}) collective-permute-start(bf16[128,1152]{1,0:T(8,128)(2,1)S(1)} %pad_maximum_fusion), channel_id=1, source_target_pairs={{0,1},{1,0},{2,3},{3,2},{4,5},{5,4},{6,7},{7,6},{8,9},{9,8},{10,11... | collective-permute-start | bytes 884744 | tf_op jit(solution)/shard_map/ppermute | solution.py:361
  101.8 3.6 %collective-permute-done.4.one = bf16[128,1152]{1,0:T(8,128)(2,1)S(1)} collective-permute-done((bf16[128,1152]{1,0:T(8,128)(2,1)S(1)}, bf16[128,1152]{1,0:T(8,128)(2,1)S(1)}, u32[]{:S(2)}, u32[]{:S(2)}) %collective-permute-start.4) | collective-permute-done | bytes 294944 | tf_op jit(solution)/shard_map/ppermute | solution.py:361
  105.5 3.5 %collective-permute-start.6 = (bf16[128,1152]{1,0:T(8,128)(2,1)S(1)}, bf16[128,1152]{1,0:T(8,128)(2,1)S(1)}, u32[]{:S(2)}, u32[]{:S(2)}) collective-permute-start(bf16[128,1152]{1,0:T(8,128)(2,1)S(1)} %collective-permute-done.4.one), channel_id=1, source_target_pairs={{0,1},{1,0},{2,3},{3,2},{4,5},{5,4},{6,7},{7,6},{8,9},{9,8},{10,11... | collective-permute-start | bytes 884744 | tf_op jit(solution)/shard_map/ppermute | solution.py:361
  108.9 0.0 collective-permute-done.5.near
  108.9 1.2 %collective-permute-done.6.rest = bf16[128,1152]{1,0:T(8,128)(2,1)S(1)} collective-permute-done((bf16[128,1152]{1,0:T(8,128)(2,1)S(1)}, bf16[128,1152]{1,0:T(8,128)(2,1)S(1)}, u32[]{:S(2)}, u32[]{:S(2)}) %collective-permute-start.6) | collective-permute-done | bytes 294944 | tf_op jit(solution)/shard_map/ppermute | solution.py:361
  110.1 1.1 put_in_place.1
  (6 shorter events, 0.1 us)
Async XLA Ops:
  0.6 0.7 copy-start.10
  1.3 0.7 copy-start.12
  2.0 21.8 %copy-start = (bf16[1152,538]{0,1:T(8,128)(2,1)S(1)}, bf16[1152,538]{0,1:T(8,128)(2,1)}, u32[]{:S(2)}) copy-start(bf16[1152,538]{0,1:T(8,128)(2,1)} %param.13) | copy-start | bytes 3718660
  2.0 21.8 %copy-start.1 = (bf16[538,1152]{1,0:T(8,128)(2,1)S(1)}, bf16[538,1152]{1,0:T(8,128)(2,1)}, u32[]{:S(2)}) copy-start(bf16[538,1152]{1,0:T(8,128)(2,1)} %down_ref.3) | copy-start | bytes 3718660
  2.6 21.2 %copy-start.6 = (f32[1152]{0:T(1024)S(1)}, f32[1152]{0:T(1024)}, u32[]{:S(2)}) copy-start(f32[1152]{0:T(1024)} %b_down_ref.1) | copy-start | bytes 13828
  2.7 21.2 %copy-start.8 = (f32[1152]{0:T(1024)S(1)}, f32[1152]{0:T(1024)}, u32[]{:S(2)}) copy-start(f32[1152]{0:T(1024)} %gain_ref.4) | copy-start | bytes 13828
  2.7 21.2 %copy-start.9 = (f32[538]{0:T(1024)S(1)}, f32[538]{0:T(1024)}, u32[]{:S(2)}) copy-start(f32[538]{0:T(1024)} %bias_ref.1) | copy-start | bytes 6460
  18.0 12.3 %all-to-all-start.1 = ((bf16[8,16,1280]{2,1,0:T(8,128)(2,1)}), bf16[8,16,1280]{2,1,0:T(8,128)(2,1)S(1)}, u32[]{:S(2)}, u32[]{:S(2)}) async-start(bf16[8,16,1280]{2,1,0:T(8,128)(2,1)} %broadcast_in_dim.4), calls=%async_computation.1 | async-start | bytes 655360 | tf_op jit(solution)/shard_map/all_to_all | solution.py:377
  23.9 1.3 %copy-start.2 = (bf16[512,1152]{1,0:T(8,128)(2,1)S(1)}, bf16[512,1152]{1,0:T(8,128)(2,1)}, u32[]{:S(2)}) copy-start(bf16[512,1152]{1,0:T(8,128)(2,1)} %x_ref.1) | copy-start | bytes 3538948
  25.1 25.6 %copy-start.7 = (f32[1152]{0:T(1024)S(1)}, f32[1152]{0:T(1024)}, u32[]{:S(2)}) copy-start(f32[1152]{0:T(1024)} %gain_ref.3) | copy-start | bytes 13828
  25.1 25.6 %copy-start.11 = (s32[2]{0:T(128)S(1)}, s32[2]{0:T(128)}, u32[]{:S(2)}) copy-start(s32[2]{0:T(128)} %ids_ref.5) | copy-start | bytes 28
  28.9 0.6 copy-start.5
  30.3 20.5 %all-to-all-start.2 = ((f32[8,2,1152]{2,1,0:T(2,128)}), f32[8,2,1152]{2,1,0:T(2,128)}, u32[]{:S(2)}, u32[]{:S(2)}) async-start(f32[8,2,1152]{2,1,0:T(2,128)} %copy-done.5), calls=%async_computation.2 | async-start | bytes 147456 | tf_op jit(solution)/shard_map/all_to_all | solution.py:377
  54.5 0.8 copy-start.3
  55.3 11.8 %copy-start.4 = (bf16[256,1152]{1,0:T(8,128)(2,1)S(1)}, bf16[256,1152]{1,0:T(8,128)(2,1)}, u32[]{:S(2)}) copy-start(bf16[256,1152]{1,0:T(8,128)(2,1)} %copy-done.3) | copy-start | bytes 1769476
  55.3 4.9 %collective-permute-start = (bf16[256,1152]{1,0:T(8,128)(2,1)}, bf16[256,1152]{1,0:T(8,128)(2,1)S(1)}, u32[]{:S(2)}, u32[]{:S(2)}) collective-permute-start(bf16[256,1152]{1,0:T(8,128)(2,1)} %get-tuple-element.32), channel_id=1, source_target_pairs={{0,1},{1,0},{2,3},{3,2},{4,5},{5,4},{6,7},{7,6},{8,9},{9,8},{10,11... | collective-permute-start | bytes 1769480 | tf_op jit(solution)/shard_map/ppermute | solution.py:361
  61.2 12.9 %collective-permute-start.1 = (bf16[128,1152]{1,0:T(8,128)(2,1)S(1)}, bf16[128,1152]{1,0:T(8,128)(2,1)S(1)}, u32[]{:S(2)}, u32[]{:S(2)}) collective-permute-start(bf16[128,1152]{1,0:T(8,128)(2,1)S(1)} %add_convert_fusion), channel_id=1, source_target_pairs={{0,2},{1,7},{2,0},{3,5},{4,6},{5,3},{6,4},{7,1},{8,10},{9,15},{10,... | collective-permute-start | bytes 884744 | tf_op jit(solution)/shard_map/ppermute | solution.py:361
  63.3 9.0 %all-to-all-start.3 = ((bf16[8,2,1152]{2,1,0:T(2,128)(2,1)}), bf16[8,2,1152]{2,1,0:T(2,128)(2,1)S(1)}, u32[]{:S(2)}, u32[]{:S(2)}) async-start(bf16[8,2,1152]{2,1,0:T(2,128)(2,1)} %get-tuple-element.34), calls=%async_computation.3 | async-start | bytes 73728 | tf_op jit(solution)/shard_map/all_to_all | solution.py:377
  74.1 8.6 %collective-permute-start.2 = (bf16[64,1152]{1,0:T(8,128)(2,1)S(1)}, bf16[64,1152]{1,0:T(8,128)(2,1)S(1)}, u32[]{:S(2)}, u32[]{:S(2)}) collective-permute-start(bf16[64,1152]{1,0:T(8,128)(2,1)S(1)} %add_convert_fusion.1), channel_id=1, source_target_pairs={{0,6},{1,3},{2,4},{3,1},{4,2},{5,7},{6,0},{7,5},{8,14},{9,11},{10,... | collective-permute-start | bytes 442376 | tf_op jit(solution)/shard_map/ppermute | solution.py:361
  77.4 16.5 %all-to-all-start.4 = ((bf16[8,16,1152]{2,1,0:T(8,128)(2,1)}), bf16[8,16,1152]{2,1,0:T(8,128)(2,1)S(1)}, u32[]{:S(2)}, u32[]{:S(2)}) async-start(bf16[8,16,1152]{2,1,0:T(8,128)(2,1)} %broadcast_in_dim.5), calls=%async_computation.4 | async-start | bytes 589824 | tf_op jit(solution)/shard_map/all_to_all | solution.py:377
  83.1 12.5 %collective-permute-start.3 = (bf16[64,1152]{1,0:T(8,128)(2,1)S(1)}, bf16[64,1152]{1,0:T(8,128)(2,1)S(1)}, u32[]{:S(2)}, u32[]{:S(2)}) collective-permute-start(bf16[64,1152]{1,0:T(8,128)(2,1)S(1)} %finish.1.own), channel_id=1, source_target_pairs={{0,6},{1,3},{2,4},{3,1},{4,2},{5,7},{6,0},{7,5},{8,14},{9,11},{10,... | collective-permute-start | bytes 442376 | tf_op jit(solution)/shard_map/ppermute | solution.py:361
  95.6 9.9 %collective-permute-start.4 = (bf16[128,1152]{1,0:T(8,128)(2,1)S(1)}, bf16[128,1152]{1,0:T(8,128)(2,1)S(1)}, u32[]{:S(2)}, u32[]{:S(2)}) collective-permute-start(bf16[128,1152]{1,0:T(8,128)(2,1)S(1)} %pad_maximum_fusion), channel_id=1, source_target_pairs={{0,2},{1,7},{2,0},{3,5},{4,6},{5,3},{6,4},{7,1},{8,10},{9,15},{10,... | collective-permute-start | bytes 884744 | tf_op jit(solution)/shard_map/ppermute | solution.py:361
  97.5 11.4 %collective-permute-start.5 = (bf16[128,1152]{1,0:T(8,128)(2,1)S(1)}, bf16[128,1152]{1,0:T(8,128)(2,1)S(1)}, u32[]{:S(2)}, u32[]{:S(2)}) collective-permute-start(bf16[128,1152]{1,0:T(8,128)(2,1)S(1)} %pad_maximum_fusion), channel_id=1, source_target_pairs={{0,1},{1,0},{2,3},{3,2},{4,5},{5,4},{6,7},{7,6},{8,9},{9,8},{10,11... | collective-permute-start | bytes 884744 | tf_op jit(solution)/shard_map/ppermute | solution.py:361
  105.5 4.7 %collective-permute-start.6 = (bf16[128,1152]{1,0:T(8,128)(2,1)S(1)}, bf16[128,1152]{1,0:T(8,128)(2,1)S(1)}, u32[]{:S(2)}, u32[]{:S(2)}) collective-permute-start(bf16[128,1152]{1,0:T(8,128)(2,1)S(1)} %collective-permute-done.4.one), channel_id=1, source_target_pairs={{0,1},{1,0},{2,3},{3,2},{4,5},{5,4},{6,7},{7,6},{8,9},{9,8},{10,11... | collective-permute-start | bytes 884744 | tf_op jit(solution)/shard_map/ppermute | solution.py:361

commit v11 on v10

--- a/solution.py
+++ b/solution.py
@@ -461,10 +461,10 @@
         images,
         ids,
     )
-    from_two, grad_text = lax.optimization_barrier((from_two, grad_text))
     pair = jnp.concatenate([done, from_two])
     from_one = swap(pair, "tensor", step_one)
     near = swap_core(pair)
+    from_one, grad_text = lax.optimization_barrier((from_one, grad_text))
     rest = swap_core(from_one)
     grad_patches = put_in_place(
         place, (done, from_two, from_one, near, rest), patches.shape[0]

time: 112 us -> 113 us (level)
  the two profiles are of different devices: /device:TPU:1 before, /device:TPU:65 now
where the time goes in v11:
time: 113 us
  starting transfers between devices  58.2 us (52%)
  waiting for transfers between devices  19.6 us (17%)
  blocking collectives  13.7 us (12%)
  Pallas kernels  11.2 us (10%)
  local copies, waits for them, and re-layouts  6.56 us (6%)
  between operations  2.17 us (2%)
  other arithmetic  1.14 us (1%)
    ppermute x7, starting transfers between devices, swap(): return lax.ppermute(value, axis, [(i, partner(i)) for i in range(size)])  32.7 us
    all_to_all x4, starting transfers between devices, exchange(): lax.all_to_all(copies, axis, split_axis=0, concat_axis=0, axis_index_grou...  25.5 us
    all_to_all x1, blocking collectives, exchange(): lax.all_to_all(copies, axis, split_axis=0, concat_axis=0, axis_index_grou...  13.7 us
    all_to_all x4, waiting for transfers between devices, exchange(): lax.all_to_all(copies, axis, split_axis=0, concat_axis=0, axis_index_grou...  10.2 us
    ppermute x7, waiting for transfers between devices, swap(): return lax.ppermute(value, axis, [(i, partner(i)) for i in range(size)])  9.42 us
    unnamed x26, local copies, waits for them, and re-layouts  4.08 us
    pallas_call x1, Pallas kernels, forward(): pl.pallas_call(functools.partial(forward_kernel, n_tensor), grid=(tokens...  3.73 us
    pallas_call x1, Pallas kernels, loss_and_back(): pl.pallas_call(loss_kernel, in_specs=[SMEM] * 2 + [VMEM] * 8, out_shape=[...  3.67 us
  transfers between devices with their start and end apart: 11, of which 7 were waited for; matrix products, arithmetic and copies ran while one was open for 2% of the time, Pallas kernels for 5%

profile of v11, /device:TPU:65, one launch (start us, length us, event | category | flops | bytes accessed | tf_op | source)
XLA Modules:
  0.0 112.6 jit_solution(18287084328301507189)
XLA Ops:
  0.6 0.0 copy-start.10
  0.6 0.6 copy-done.10
  1.3 0.0 copy-start.12
  1.3 0.7 copy-done.12
  2.0 0.0 copy-start
  2.0 0.0 copy-start.1
  2.0 0.7 pack.1
  2.6 0.0 copy-start.6
  2.7 0.0 copy-start.8
  2.7 0.0 copy-start.9
  2.7 13.7 %all_to_all.25 = bf16[8,2,1280]{2,1,0:T(2,128)(2,1)S(1)} all-to-all(bf16[8,2,1280]{2,1,0:T(2,128)(2,1)S(1)} %get-tuple-element.24), channel_id=1, replica_groups={{0,64,128,192,256,320,384,448},{8,72,136,200,264,328,392,456},{16,80,14..., dimensions={0} | all-to-all | bytes 81920 | tf_op jit(solution)/shard_map/all_to_all | solution.py:377
  16.4 0.7 broadcast_in_dim.4
  17.2 5.2 %all-to-all-start.1 = ((bf16[8,16,1280]{2,1,0:T(8,128)(2,1)}), bf16[8,16,1280]{2,1,0:T(8,128)(2,1)S(1)}, u32[]{:S(2)}, u32[]{:S(2)}) async-start(bf16[8,16,1280]{2,1,0:T(8,128)(2,1)} %broadcast_in_dim.4), calls=%async_computation.1 | async-start | bytes 655360 | tf_op jit(solution)/shard_map/all_to_all | solution.py:377
  22.4 0.0 copy-done
  22.4 0.0 copy-done.1
  22.4 0.0 copy-done.6
  22.4 0.0 copy-done.8
  22.4 0.0 copy-done.9
  22.4 0.0 copy-start.2
  22.4 1.3 %copy-done.2 = bf16[512,1152]{1,0:T(8,128)(2,1)S(1)} copy-done((bf16[512,1152]{1,0:T(8,128)(2,1)S(1)}, bf16[512,1152]{1,0:T(8,128)(2,1)}, u32[]{:S(2)}) %copy-start.2) | copy-done | bytes 1179672
  23.7 0.0 copy-start.7
  23.7 0.0 copy-start.11
  23.7 3.7 %forward.1 = (bf16[512,538]{1,0:T(8,128)(2,1)S(1)}, f32[8,2,1152]{2,1,0:T(2,128)S(1)}) custom-call(bf16[512,1152]{1,0:T(8,128)(2,1)S(1)} %copy-done.2, f32[1152]{0:T(1024)S(1)} %copy-done.8, f32[538]{0:T(1024)S(1)} %copy-done.9, f32[1152]{0:T(1024)S(1)} %copy-done.6, bf16[538,1152]{1,0:T(8,128)(2,1)S(1)} %bitcast.8, bf16[538,1152]{1,0:T(8,128)(2,1)S(1)} %copy-done.1), custom_call_target="tpu_custom_call" | custom-call | flops 634650624 | bytes 4760576 | tf_op jit(solution)/shard_map/forward/pallas_call | solution.py:153
  27.4 0.0 copy-start.5
  27.4 0.6 copy-done.5
  28.1 0.0 all-to-all-done.1
  28.1 12.8 %all-to-all-start.2 = ((f32[8,2,1152]{2,1,0:T(2,128)}), f32[8,2,1152]{2,1,0:T(2,128)}, u32[]{:S(2)}, u32[]{:S(2)}) async-start(f32[8,2,1152]{2,1,0:T(2,128)} %copy-done.5), calls=%async_computation.2 | async-start | bytes 147456 | tf_op jit(solution)/shard_map/all_to_all | solution.py:377
  42.2 6.2 %all-to-all-done.2.parts_ref = f32[8,2,1152]{2,1,0:T(2,128)} async-done(((f32[8,2,1152]{2,1,0:T(2,128)}), f32[8,2,1152]{2,1,0:T(2,128)}, u32[]{:S(2)}, u32[]{:S(2)}) %all-to-all-start.2) | async-done | bytes 73760 | tf_op jit(solution)/shard_map/all_to_all | solution.py:377
  48.4 0.0 copy-done.7
  48.4 0.0 copy-done.11
  48.4 3.7 %loss_and_back.1 = (bf16[8,2,1152]{2,1,0:T(2,128)(2,1)}, f32[2,1152]{1,0:T(2,128)S(1)}, bf16[256,1152]{1,0:T(8,128)(2,1)}, bf16[256,1152]{1,0:T(8,128)(2,1)S(1)}) custom-call(s32[1]{0:T(128)} %bitcast.place_ref, s32[2]{0:T(128)S(1)} %copy-done.11, f32[1]{0:T(128)S(6)} %copy.14.sharp_ref, f32[1]{0:T(128)S(6)} %copy.15.shift_ref, ...), custom_call_target="tpu_custom_call" | custom-call | flops 634650624 | bytes 4820480 | tf_op jit(solution)/shard_map/loss_and_back/pallas_call | solution.py:263
  52.1 0.0 copy-start.3
  52.1 0.8 copy-done.3
  52.9 0.0 copy-start.4
  52.9 3.1 %collective-permute-start = (bf16[256,1152]{1,0:T(8,128)(2,1)}, bf16[256,1152]{1,0:T(8,128)(2,1)S(1)}, u32[]{:S(2)}, u32[]{:S(2)}) collective-permute-start(bf16[256,1152]{1,0:T(8,128)(2,1)} %get-tuple-element.32), channel_id=1, source_target_pairs={{0,1},{1,0},{2,3},{3,2},{4,5},{5,4},{6,7},{7,6},{8,9},{9,8},{10,11... | collective-permute-start | bytes 1769480 | tf_op jit(solution)/shard_map/ppermute | solution.py:361
  56.1 0.9 constant_dynamic-slice_fusion.x_ref
  57.0 0.9 collective-permute-done
  57.9 1.0 add_convert_fusion
  58.9 2.6 %collective-permute-start.1 = (bf16[128,1152]{1,0:T(8,128)(2,1)S(1)}, bf16[128,1152]{1,0:T(8,128)(2,1)S(1)}, u32[]{:S(2)}, u32[]{:S(2)}) collective-permute-start(bf16[128,1152]{1,0:T(8,128)(2,1)S(1)} %add_convert_fusion), channel_id=1, source_target_pairs={{0,2},{1,7},{2,0},{3,5},{4,6},{5,3},{6,4},{7,1},{8,10},{9,15},{10,... | collective-permute-start | bytes 884744 | tf_op jit(solution)/shard_map/ppermute | solution.py:361
  61.5 4.0 %all-to-all-start.3 = ((bf16[8,2,1152]{2,1,0:T(2,128)(2,1)}), bf16[8,2,1152]{2,1,0:T(2,128)(2,1)S(1)}, u32[]{:S(2)}, u32[]{:S(2)}) async-start(bf16[8,2,1152]{2,1,0:T(2,128)(2,1)} %get-tuple-element.34), calls=%async_computation.3 | async-start | bytes 73728 | tf_op jit(solution)/shard_map/all_to_all | solution.py:377
  65.6 0.0 copy-done.4
  65.6 0.1 convert_add_fusion
  65.7 4.0 %all-to-all-done.3 = bf16[8,2,1152]{2,1,0:T(2,128)(2,1)S(1)} async-done(((bf16[8,2,1152]{2,1,0:T(2,128)(2,1)}), bf16[8,2,1152]{2,1,0:T(2,128)(2,1)S(1)}, u32[]{:S(2)}, u32[]{:S(2)}) %all-to-all-start.3) | async-done | bytes 36896 | tf_op jit(solution)/shard_map/all_to_all | solution.py:377
  69.7 1.7 %collective-permute-done.1.one_ref = bf16[128,1152]{1,0:T(8,128)(2,1)S(1)} collective-permute-done((bf16[128,1152]{1,0:T(8,128)(2,1)S(1)}, bf16[128,1152]{1,0:T(8,128)(2,1)S(1)}, u32[]{:S(2)}, u32[]{:S(2)}) %collective-permute-start.1) | collective-permute-done | bytes 294944 | tf_op jit(solution)/shard_map/ppermute | solution.py:361
  71.4 1.9 %collective-permute-start.2 = (bf16[64,1152]{1,0:T(8,128)(2,1)S(1)}, bf16[64,1152]{1,0:T(8,128)(2,1)S(1)}, u32[]{:S(2)}, u32[]{:S(2)}) collective-permute-start(bf16[64,1152]{1,0:T(8,128)(2,1)S(1)} %add_convert_fusion.1), channel_id=1, source_target_pairs={{0,6},{1,3},{2,4},{3,1},{4,2},{5,7},{6,0},{7,5},{8,14},{9,11},{10,... | collective-permute-start | bytes 442376 | tf_op jit(solution)/shard_map/ppermute | solution.py:361
  73.3 5.0 %collective-permute-done.2.two_ref = bf16[64,1152]{1,0:T(8,128)(2,1)S(1)} collective-permute-done((bf16[64,1152]{1,0:T(8,128)(2,1)S(1)}, bf16[64,1152]{1,0:T(8,128)(2,1)S(1)}, u32[]{:S(2)}, u32[]{:S(2)}) %collective-permute-start.2) | collective-permute-done | bytes 147488 | tf_op jit(solution)/shard_map/ppermute | solution.py:361
  78.3 0.3 finish.1.own
  78.6 1.9 %collective-permute-start.3 = (bf16[64,1152]{1,0:T(8,128)(2,1)S(1)}, bf16[64,1152]{1,0:T(8,128)(2,1)S(1)}, u32[]{:S(2)}, u32[]{:S(2)}) collective-permute-start(bf16[64,1152]{1,0:T(8,128)(2,1)S(1)} %finish.1.own), channel_id=1, source_target_pairs={{0,6},{1,3},{2,4},{3,1},{4,2},{5,7},{6,0},{7,5},{8,14},{9,11},{10,... | collective-permute-start | bytes 442376 | tf_op jit(solution)/shard_map/ppermute | solution.py:361
  80.5 0.7 broadcast_in_dim.5
  81.3 3.4 %all-to-all-start.4 = ((bf16[8,16,1152]{2,1,0:T(8,128)(2,1)}), bf16[8,16,1152]{2,1,0:T(8,128)(2,1)S(1)}, u32[]{:S(2)}, u32[]{:S(2)}) async-start(bf16[8,16,1152]{2,1,0:T(8,128)(2,1)} %broadcast_in_dim.5), calls=%async_computation.4 | async-start | bytes 589824 | tf_op jit(solution)/shard_map/all_to_all | solution.py:377
  84.7 0.7 collective-permute-done.3.two
  85.4 6.1 %collective-permute-start.4 = (bf16[128,1152]{1,0:T(8,128)(2,1)S(1)}, bf16[128,1152]{1,0:T(8,128)(2,1)S(1)}, u32[]{:S(2)}, u32[]{:S(2)}) collective-permute-start(bf16[128,1152]{1,0:T(8,128)(2,1)S(1)} %pad_maximum_fusion), channel_id=1, source_target_pairs={{0,2},{1,7},{2,0},{3,5},{4,6},{5,3},{6,4},{7,1},{8,10},{9,15},{10,... | collective-permute-start | bytes 884744 | tf_op jit(solution)/shard_map/ppermute | solution.py:361
  91.5 11.2 %collective-permute-start.5 = (bf16[128,1152]{1,0:T(8,128)(2,1)S(1)}, bf16[128,1152]{1,0:T(8,128)(2,1)S(1)}, u32[]{:S(2)}, u32[]{:S(2)}) collective-permute-start(bf16[128,1152]{1,0:T(8,128)(2,1)S(1)} %pad_maximum_fusion), channel_id=1, source_target_pairs={{0,1},{1,0},{2,3},{3,2},{4,5},{5,4},{6,7},{7,6},{8,9},{9,8},{10,11... | collective-permute-start | bytes 884744 | tf_op jit(solution)/shard_map/ppermute | solution.py:361
  102.8 0.0 all-to-all-done.4
  102.8 1.7 %text_grad.1 = f32[2,1152]{1,0:T(2,128)} custom-call(s32[2]{0:T(128)S(1)} %copy-done.11, f32[1]{0:T(128)S(6)} %copy.14.sharp_ref, f32[1]{0:T(128)S(6)} %copy.15.shift_ref, f32[2,1152]{1,0:T(2,128)S(1)} %get-tuple-element.40.unit_ref, f32[2,128]{1,0:T(2,128)S(1)} %get-tuple-element.41.len_ref, bf16[128,1152]{1,0:T(8,128)(2,1)S(1)} %bitcast.12, ...), custom_call_target="tpu_custom_call" | custom-call | flops 1000000000 | bytes 600000 | tf_op jit(solution)/shard_map/text_grad/pallas_call | solution.py:297
  104.5 0.0 collective-permute-done.4.one
  104.5 5.8 %collective-permute-start.6 = (bf16[128,1152]{1,0:T(8,128)(2,1)S(1)}, bf16[128,1152]{1,0:T(8,128)(2,1)S(1)}, u32[]{:S(2)}, u32[]{:S(2)}) collective-permute-start(bf16[128,1152]{1,0:T(8,128)(2,1)S(1)} %collective-permute-done.4.one), channel_id=1, source_target_pairs={{0,1},{1,0},{2,3},{3,2},{4,5},{5,4},{6,7},{7,6},{8,9},{9,8},{10,11... | collective-permute-start | bytes 884744 | tf_op jit(solution)/shard_map/ppermute | solution.py:361
  110.3 0.0 collective-permute-done.5.near
  110.3 1.2 %collective-permute-done.6.rest = bf16[128,1152]{1,0:T(8,128)(2,1)S(1)} collective-permute-done((bf16[128,1152]{1,0:T(8,128)(2,1)S(1)}, bf16[128,1152]{1,0:T(8,128)(2,1)S(1)}, u32[]{:S(2)}, u32[]{:S(2)}) %collective-permute-start.6) | collective-permute-done | bytes 294944 | tf_op jit(solution)/shard_map/ppermute | solution.py:361
  111.5 1.1 put_in_place.1
  (6 shorter events, 0.1 us)
Async XLA Ops:
  0.6 0.7 copy-start.10
  1.3 0.7 copy-start.12
  2.0 20.4 %copy-start = (bf16[1152,538]{0,1:T(8,128)(2,1)S(1)}, bf16[1152,538]{0,1:T(8,128)(2,1)}, u32[]{:S(2)}) copy-start(bf16[1152,538]{0,1:T(8,128)(2,1)} %param.13) | copy-start | bytes 3718660
  2.0 20.4 %copy-start.1 = (bf16[538,1152]{1,0:T(8,128)(2,1)S(1)}, bf16[538,1152]{1,0:T(8,128)(2,1)}, u32[]{:S(2)}) copy-start(bf16[538,1152]{1,0:T(8,128)(2,1)} %down_ref.3) | copy-start | bytes 3718660
  2.6 19.7 %copy-start.6 = (f32[1152]{0:T(1024)S(1)}, f32[1152]{0:T(1024)}, u32[]{:S(2)}) copy-start(f32[1152]{0:T(1024)} %b_down_ref.1) | copy-start | bytes 13828
  2.7 19.7 %copy-start.8 = (f32[1152]{0:T(1024)S(1)}, f32[1152]{0:T(1024)}, u32[]{:S(2)}) copy-start(f32[1152]{0:T(1024)} %gain_ref.4) | copy-start | bytes 13828
  2.7 19.7 %copy-start.9 = (f32[538]{0:T(1024)S(1)}, f32[538]{0:T(1024)}, u32[]{:S(2)}) copy-start(f32[538]{0:T(1024)} %bias_ref.1) | copy-start | bytes 6460
  17.2 10.9 %all-to-all-start.1 = ((bf16[8,16,1280]{2,1,0:T(8,128)(2,1)}), bf16[8,16,1280]{2,1,0:T(8,128)(2,1)S(1)}, u32[]{:S(2)}, u32[]{:S(2)}) async-start(bf16[8,16,1280]{2,1,0:T(8,128)(2,1)} %broadcast_in_dim.4), calls=%async_computation.1 | async-start | bytes 655360 | tf_op jit(solution)/shard_map/all_to_all | solution.py:377
  22.4 1.3 %copy-start.2 = (bf16[512,1152]{1,0:T(8,128)(2,1)S(1)}, bf16[512,1152]{1,0:T(8,128)(2,1)}, u32[]{:S(2)}) copy-start(bf16[512,1152]{1,0:T(8,128)(2,1)} %x_ref.1) | copy-start | bytes 3538948
  23.7 24.7 %copy-start.7 = (f32[1152]{0:T(1024)S(1)}, f32[1152]{0:T(1024)}, u32[]{:S(2)}) copy-start(f32[1152]{0:T(1024)} %gain_ref.3) | copy-start | bytes 13828
  23.7 24.7 %copy-start.11 = (s32[2]{0:T(128)S(1)}, s32[2]{0:T(128)}, u32[]{:S(2)}) copy-start(s32[2]{0:T(128)} %ids_ref.5) | copy-start | bytes 28
  27.4 0.6 copy-start.5
  28.1 20.4 %all-to-all-start.2 = ((f32[8,2,1152]{2,1,0:T(2,128)}), f32[8,2,1152]{2,1,0:T(2,128)}, u32[]{:S(2)}, u32[]{:S(2)}) async-start(f32[8,2,1152]{2,1,0:T(2,128)} %copy-done.5), calls=%async_computation.2 | async-start | bytes 147456 | tf_op jit(solution)/shard_map/all_to_all | solution.py:377
  52.1 0.8 copy-start.3
  52.9 12.7 %copy-start.4 = (bf16[256,1152]{1,0:T(8,128)(2,1)S(1)}, bf16[256,1152]{1,0:T(8,128)(2,1)}, u32[]{:S(2)}) copy-start(bf16[256,1152]{1,0:T(8,128)(2,1)} %copy-done.3) | copy-start | bytes 1769476
  52.9 5.0 %collective-permute-start = (bf16[256,1152]{1,0:T(8,128)(2,1)}, bf16[256,1152]{1,0:T(8,128)(2,1)S(1)}, u32[]{:S(2)}, u32[]{:S(2)}) collective-permute-start(bf16[256,1152]{1,0:T(8,128)(2,1)} %get-tuple-element.32), channel_id=1, source_target_pairs={{0,1},{1,0},{2,3},{3,2},{4,5},{5,4},{6,7},{7,6},{8,9},{9,8},{10,11... | collective-permute-start | bytes 1769480 | tf_op jit(solution)/shard_map/ppermute | solution.py:361
  58.9 12.5 %collective-permute-start.1 = (bf16[128,1152]{1,0:T(8,128)(2,1)S(1)}, bf16[128,1152]{1,0:T(8,128)(2,1)S(1)}, u32[]{:S(2)}, u32[]{:S(2)}) collective-permute-start(bf16[128,1152]{1,0:T(8,128)(2,1)S(1)} %add_convert_fusion), channel_id=1, source_target_pairs={{0,2},{1,7},{2,0},{3,5},{4,6},{5,3},{6,4},{7,1},{8,10},{9,15},{10,... | collective-permute-start | bytes 884744 | tf_op jit(solution)/shard_map/ppermute | solution.py:361
  61.5 8.1 %all-to-all-start.3 = ((bf16[8,2,1152]{2,1,0:T(2,128)(2,1)}), bf16[8,2,1152]{2,1,0:T(2,128)(2,1)S(1)}, u32[]{:S(2)}, u32[]{:S(2)}) async-start(bf16[8,2,1152]{2,1,0:T(2,128)(2,1)} %get-tuple-element.34), calls=%async_computation.3 | async-start | bytes 73728 | tf_op jit(solution)/shard_map/all_to_all | solution.py:377
  71.4 6.9 %collective-permute-start.2 = (bf16[64,1152]{1,0:T(8,128)(2,1)S(1)}, bf16[64,1152]{1,0:T(8,128)(2,1)S(1)}, u32[]{:S(2)}, u32[]{:S(2)}) collective-permute-start(bf16[64,1152]{1,0:T(8,128)(2,1)S(1)} %add_convert_fusion.1), channel_id=1, source_target_pairs={{0,6},{1,3},{2,4},{3,1},{4,2},{5,7},{6,0},{7,5},{8,14},{9,11},{10,... | collective-permute-start | bytes 442376 | tf_op jit(solution)/shard_map/ppermute | solution.py:361
  78.6 6.8 %collective-permute-start.3 = (bf16[64,1152]{1,0:T(8,128)(2,1)S(1)}, bf16[64,1152]{1,0:T(8,128)(2,1)S(1)}, u32[]{:S(2)}, u32[]{:S(2)}) collective-permute-start(bf16[64,1152]{1,0:T(8,128)(2,1)S(1)} %finish.1.own), channel_id=1, source_target_pairs={{0,6},{1,3},{2,4},{3,1},{4,2},{5,7},{6,0},{7,5},{8,14},{9,11},{10,... | collective-permute-start | bytes 442376 | tf_op jit(solution)/shard_map/ppermute | solution.py:361
  81.3 21.5 %all-to-all-start.4 = ((bf16[8,16,1152]{2,1,0:T(8,128)(2,1)}), bf16[8,16,1152]{2,1,0:T(8,128)(2,1)S(1)}, u32[]{:S(2)}, u32[]{:S(2)}) async-start(bf16[8,16,1152]{2,1,0:T(8,128)(2,1)} %broadcast_in_dim.5), calls=%async_computation.4 | async-start | bytes 589824 | tf_op jit(solution)/shard_map/all_to_all | solution.py:377
  85.4 19.0 %collective-permute-start.4 = (bf16[128,1152]{1,0:T(8,128)(2,1)S(1)}, bf16[128,1152]{1,0:T(8,128)(2,1)S(1)}, u32[]{:S(2)}, u32[]{:S(2)}) collective-permute-start(bf16[128,1152]{1,0:T(8,128)(2,1)S(1)} %pad_maximum_fusion), channel_id=1, source_target_pairs={{0,2},{1,7},{2,0},{3,5},{4,6},{5,3},{6,4},{7,1},{8,10},{9,15},{10,... | collective-permute-start | bytes 884744 | tf_op jit(solution)/shard_map/ppermute | solution.py:361
  91.5 18.7 %collective-permute-start.5 = (bf16[128,1152]{1,0:T(8,128)(2,1)S(1)}, bf16[128,1152]{1,0:T(8,128)(2,1)S(1)}, u32[]{:S(2)}, u32[]{:S(2)}) collective-permute-start(bf16[128,1152]{1,0:T(8,128)(2,1)S(1)} %pad_maximum_fusion), channel_id=1, source_target_pairs={{0,1},{1,0},{2,3},{3,2},{4,5},{5,4},{6,7},{7,6},{8,9},{9,8},{10,11... | collective-permute-start | bytes 884744 | tf_op jit(solution)/shard_map/ppermute | solution.py:361
  104.5 7.0 %collective-permute-start.6 = (bf16[128,1152]{1,0:T(8,128)(2,1)S(1)}, bf16[128,1152]{1,0:T(8,128)(2,1)S(1)}, u32[]{:S(2)}, u32[]{:S(2)}) collective-permute-start(bf16[128,1152]{1,0:T(8,128)(2,1)S(1)} %collective-permute-done.4.one), channel_id=1, source_target_pairs={{0,1},{1,0},{2,3},{3,2},{4,5},{5,4},{6,7},{7,6},{8,9},{9,8},{10,11... | collective-permute-start | bytes 884744 | tf_op jit(solution)/shard_map/ppermute | solution.py:361
